TPU v7x, 128 devices: a whole 4x4x4 slice. The times are simulated.
128 devices in a mesh: dp: 32 (over z, y, core), fsdp: 4 (over x).
Axes of the slice: x: 4, y: 4, z: 4, core: 2. Of those that a mesh axis runs over, the one named last changes fastest.
Arguments:
- enc_hidden: bfloat16 [65536, 2048], P(('dp', 'fsdp')), may hold values from -24 to 24
- kv_weights: bfloat16 [2048, 4096], P('dp', 'fsdp'), may hold values from -0.125 to 0.125
- queries: bfloat16 [65536, 2048], P(('dp', 'fsdp')), may hold values from -1000 to 1000
- cotangent: bfloat16 [65536, 2048], P(('dp', 'fsdp')), may hold values from -6 to 6
- enc_lengths: int32 [128, 4], replicated, may hold values from 1 to 160, as said below
- dec_lengths: int32 [128, 4], replicated, may hold values from 1 to 160, as said below
- dec_partner: int32 [128, 4], replicated, may hold values from 0 to 511, as said below
Outputs:
- context: bfloat16 [65536, 2048], P(('dp', 'fsdp'))
- grad_queries: bfloat16 [65536, 2048], P(('dp', 'fsdp'))
- grad_kv_weights: float32 [2048, 4096], P('dp', 'fsdp')
Inputs may be any that keep to these rules, and one draw needn't show every extreme that they name: `enc_lengths`: each row sums to 512. `dec_lengths`: each row sums to 512. `dec_partner`: every encoder segment id is named exactly once. With device index = dp index * 4 + fsdp index, row b names segments of device b and of the devices with b's fsdp index whose dp index is one lower or one higher than b's, exactly one segment of each such neighbour.
All inputs are finite; a program needn't handle non-finite values.
Results may differ from a plain program's by a relative error of at most 0.034.
The roundings to bfloat16 on the way count: a program that leaves them out, or rounds other values in their place, can miss the bound.
Values may be sent and summed in bfloat16 or wider, within the bound.
No kernel may reach another device: no remote copies, remote signals or barrier semaphores. Data moves between devices by JAX's collectives and lax.ppermute only.
A program may use at most 192 MiB of HBM per device.

v0:
```python
import jax
import jax.numpy as jnp
from jax import lax
from jax.sharding import PartitionSpec as P

HEADS = 8
HEAD_DIM = 256
ENC_MOST = 160
DEC_MOST = 160


def extended(block, sides, width):
    for axis, dim in sides:
        count = lax.axis_size(axis)
        forward = [(i, i + 1) for i in range(count - 1)]
        backward = [(target, source) for source, target in forward]
        low = lax.ppermute(
            lax.slice_in_dim(block, block.shape[dim] - width, None, axis=dim), axis, forward
        )
        high = lax.ppermute(lax.slice_in_dim(block, 0, width, axis=dim), axis, backward)
        block = jnp.concatenate([low, block, high], axis=dim)
    return block


def segment_slots(lengths, token_total):
    seg_ends = jnp.cumsum(lengths)
    places = jnp.arange(token_total, dtype=jnp.int32)
    return jnp.sum((places[:, None] >= seg_ends[None, :]).astype(jnp.int32), axis=1)


def select_entry(table, index):
    index = jnp.asarray(index)
    width = table.shape[-1]
    match = jnp.arange(width, dtype=jnp.int32) == index[..., None]
    return jnp.sum(jnp.where(match, table, 0), axis=-1)


def take_rows(source, start, length, depth, live):
    start = jnp.asarray(start)
    length = jnp.asarray(length)
    live = jnp.asarray(live)
    offsets = jnp.arange(depth, dtype=jnp.int32)
    index = start[..., None] + offsets
    alive = (offsets < length[..., None]) & live[..., None]
    picked = source[jnp.minimum(index, source.shape[0] - 1)]
    picked = jnp.where(alive[..., None], picked, jnp.zeros((), source.dtype))
    return (picked, alive)


def attend(query_rows, upstream, key_rows, key_alive):
    seg_total, row_total, inner_width = query_rows.shape
    key_total = key_rows.shape[1]
    score_scale = HEAD_DIM ** (-0.5)
    query_heads = query_rows.reshape(seg_total, row_total, HEADS, HEAD_DIM)
    key_heads = key_rows[:, :, :inner_width].reshape(seg_total, key_total, HEADS, HEAD_DIM)
    value_heads = key_rows[:, :, inner_width:].reshape(seg_total, key_total, HEADS, HEAD_DIM)
    upstream_heads = upstream.reshape(seg_total, row_total, HEADS, HEAD_DIM)
    scores = (
        jnp.einsum("sqhd,skhd->shqk", query_heads, key_heads, preferred_element_type=jnp.float32)
        * score_scale
    )
    allowed = key_alive[:, None, None, :]
    top_score = jnp.max(jnp.where(allowed, scores, -jnp.inf), axis=3, keepdims=True)
    exponent = jnp.where(allowed, jnp.exp(scores - top_score), 0.0)
    weights = exponent / jnp.sum(exponent, axis=3, keepdims=True)
    weights_low = weights.astype(jnp.bfloat16)
    context = jnp.einsum(
        "shqk,skhd->sqhd", weights_low, value_heads, preferred_element_type=jnp.float32
    )
    grad_weights = jnp.einsum(
        "sqhd,skhd->shqk", upstream_heads, value_heads, preferred_element_type=jnp.float32
    )
    row_delta = jnp.sum(weights * grad_weights, axis=3, keepdims=True)
    grad_scores = (weights * (grad_weights - row_delta) * score_scale).astype(jnp.bfloat16)
    grad_query = jnp.einsum(
        "shqk,skhd->sqhd", grad_scores, key_heads, preferred_element_type=jnp.float32
    )
    grad_key = jnp.einsum(
        "shqk,sqhd->skhd", grad_scores, query_heads, preferred_element_type=jnp.float32
    )
    grad_value = jnp.einsum(
        "shqk,sqhd->skhd", weights_low, upstream_heads, preferred_element_type=jnp.float32
    )
    grad_pair = jnp.concatenate(
        [
            grad_key.reshape(seg_total, key_total, inner_width),
            grad_value.reshape(seg_total, key_total, inner_width),
        ],
        axis=2,
    )
    return (
        context.reshape(seg_total, row_total, inner_width).astype(jnp.bfloat16),
        grad_query.reshape(seg_total, row_total, inner_width).astype(jnp.bfloat16),
        grad_pair.astype(jnp.bfloat16),
    )


def body(enc_hidden, kv_weights, queries, cotangent, enc_lengths, dec_lengths, dec_partner):
    dp_count = lax.axis_size("dp")
    fsdp_count = lax.axis_size("fsdp")
    dp_index = lax.axis_index("dp")
    fsdp_index = lax.axis_index("fsdp")
    device_id = dp_index * fsdp_count + fsdp_index
    device_total = enc_lengths.shape[0]
    seg_count = enc_lengths.shape[1]
    enc_count, model_width = enc_hidden.shape
    dec_count, inner_width = queries.shape
    zero_low = jnp.zeros((), jnp.bfloat16)
    row_panel = lax.all_gather(kv_weights, "dp", axis=0, tiled=True)
    key_values = jnp.dot(
        enc_hidden,
        lax.all_gather(row_panel, "fsdp", axis=1, tiled=True),
        preferred_element_type=jnp.float32,
    ).astype(jnp.bfloat16)
    below_id = jnp.maximum(device_id - fsdp_count, 0)
    above_id = jnp.minimum(device_id + fsdp_count, device_total - 1)
    has_below = dp_index > 0
    has_above = dp_index < dp_count - 1
    enc_own = lax.dynamic_index_in_dim(enc_lengths, device_id, 0, keepdims=False)
    dec_own = lax.dynamic_index_in_dim(dec_lengths, device_id, 0, keepdims=False)
    partner_own = lax.dynamic_index_in_dim(dec_partner, device_id, 0, keepdims=False)
    below_row = lax.dynamic_index_in_dim(dec_partner, below_id, 0, keepdims=False)
    above_row = lax.dynamic_index_in_dim(dec_partner, above_id, 0, keepdims=False)
    enc_starts = jnp.cumsum(enc_own) - enc_own
    dec_starts = jnp.cumsum(dec_own) - dec_own
    seg_range = jnp.arange(seg_count, dtype=jnp.int32)
    hit_down = (below_row // seg_count == device_id) & has_below
    hit_up = (above_row // seg_count == device_id) & has_above
    has_down = jnp.any(hit_down)
    has_up = jnp.any(hit_up)
    down_slot = jnp.sum(jnp.where(hit_down, below_row % seg_count, 0))
    up_slot = jnp.sum(jnp.where(hit_up, above_row % seg_count, 0))
    partner_owner = partner_own // seg_count
    partner_slot = partner_own % seg_count
    from_below = partner_owner == device_id - fsdp_count
    from_above = partner_owner == device_id + fsdp_count
    kept_match = partner_own[None, :] == device_id * seg_count + seg_range[:, None]
    kept_any = jnp.any(kept_match, axis=1)
    kept_pos = jnp.sum(jnp.where(kept_match, seg_range[None, :], 0), axis=1)
    stacked = jnp.concatenate([queries, cotangent], axis=1)
    enc_slot_of = segment_slots(enc_own, enc_count)
    dec_slot_of = segment_slots(dec_own, dec_count)
    enc_places = jnp.arange(enc_count, dtype=jnp.int32)
    dec_places = jnp.arange(dec_count, dtype=jnp.int32)
    always = jnp.asarray(True)
    flat_lengths = enc_lengths.reshape(-1)
    send_down, unused_down = take_rows(
        key_values,
        select_entry(enc_starts, down_slot),
        select_entry(enc_own, down_slot),
        ENC_MOST,
        has_down,
    )
    send_up, unused_up = take_rows(
        key_values,
        select_entry(enc_starts, up_slot),
        select_entry(enc_own, up_slot),
        ENC_MOST,
        has_up,
    )
    padded = extended(jnp.concatenate([send_down, send_up], axis=0), (("dp", 0),), ENC_MOST)
    key_pool = jnp.concatenate([key_values, padded[:ENC_MOST], padded[-ENC_MOST:]], axis=0)
    key_start = jnp.where(
        from_below,
        enc_count,
        jnp.where(from_above, enc_count + ENC_MOST, select_entry(enc_starts, partner_slot)),
    )
    key_length = select_entry(flat_lengths, partner_own)
    key_rows, key_alive = take_rows(key_pool, key_start, key_length, ENC_MOST, always)
    query_rows, unused_alive = take_rows(stacked, dec_starts, dec_own, DEC_MOST, always)
    context_seg, query_grads, pair_grads = attend(
        query_rows[:, :, :inner_width], query_rows[:, :, inner_width:], key_rows, key_alive
    )
    results = jnp.concatenate([context_seg, query_grads], axis=2).reshape(-1, 2 * inner_width)
    dec_home = dec_slot_of * DEC_MOST + dec_places - select_entry(dec_starts, dec_slot_of)
    gathered = results[dec_home]
    back_down = jnp.sum(jnp.where(from_below[:, None, None], pair_grads, zero_low), axis=0)
    back_up = jnp.sum(jnp.where(from_above[:, None, None], pair_grads, zero_low), axis=0)
    returned = extended(jnp.concatenate([back_down, back_up], axis=0), (("dp", 0),), ENC_MOST)
    grad_pool = jnp.concatenate(
        [pair_grads.reshape(-1, 2 * inner_width), returned[:ENC_MOST], returned[-ENC_MOST:]], axis=0
    )
    is_down = (seg_range == down_slot) & has_down
    slot_base = jnp.where(
        kept_any,
        kept_pos * ENC_MOST,
        jnp.where(is_down, seg_count * ENC_MOST, seg_count * ENC_MOST + ENC_MOST),
    )
    enc_home = (
        select_entry(slot_base, enc_slot_of) + enc_places - select_entry(enc_starts, enc_slot_of)
    )
    grad_key_values = grad_pool[enc_home]
    grad_share = lax.psum_scatter(
        lax.dot_general(
            enc_hidden,
            grad_key_values,
            (((0,), (0,)), ((), ())),
            preferred_element_type=jnp.float32,
        ).astype(jnp.bfloat16),
        "dp",
        scatter_dimension=0,
        tiled=True,
    ).astype(jnp.float32)
    grad_kv_weights = lax.psum_scatter(grad_share, "fsdp", scatter_dimension=1, tiled=True)
    context = gathered[:, :inner_width]
    grad_queries = gathered[:, inner_width:]
    return (context, grad_queries, grad_kv_weights)


def solution(mesh):
    in_specs = (
        P(("dp", "fsdp"), None),
        P("dp", "fsdp"),
        P(("dp", "fsdp"), None),
        P(("dp", "fsdp"), None),
        P(),
        P(),
        P(),
    )
    out_specs = (P(("dp", "fsdp"), None), P(("dp", "fsdp"), None), P("dp", "fsdp"))
    return jax.shard_map(body, mesh=mesh, in_specs=in_specs, out_specs=out_specs, check_vma=False)
```

profile of v0, /device:TPU:1, one launch (start us, length us, event | category | flops | bytes accessed | tf_op | source)
XLA Modules:
  0.0 592.7 jit_solution(13131519848824367295)
XLA Ops:
  8.0 52.4 %all-gather.3.cloned.1.call-done = bf16[2048,1024]{1,0:T(8,128)(2,1)} async-done(((bf16[64,1024]{1,0:T(8,128)(2,1)}), bf16[2048,1024]{1,0:T(8,128)(2,1)}) %all-gather.3.cloned.1.call-update) | async-done | bytes 4194320 | tf_op jit(solution)/shard_map/all_gather | solution.py:109
  61.7 4.7 pad_maximum_fusion.3
  66.5 14.4 %gather_fusion.3 = bf16[640,4096]{1,0:T(8,128)(2,1)} fusion(bf16[512,4096]{1,0:T(8,128)(2,1)} %pad_maximum_fusion.3, s32[1024]{0:T(1024)S(1)} %pad_clamp_fusion.2), kind=kCustom, calls=%fused_computation.3 | custom fusion | bytes 10488320 | tf_op jit(solution)/shard_map/gather | solution.py:45
  89.3 5.3 broadcast_select_fusion
  94.6 120.4 %all-gather.5.cloned.1.call-done = bf16[2048,4096]{1,0:T(8,128)(2,1)} async-done(((bf16[2048,1024]{1,0:T(8,128)(2,1)}), bf16[2048,4096]{1,0:T(8,128)(2,1)}) %all-gather.5.cloned.1.call-update) | async-done | bytes 16777232 | tf_op jit(solution)/shard_map/all_gather | solution.py:112
  215.0 14.2 %convolution_convert_fusion = bf16[512,4096]{1,0:T(8,128)(2,1)} fusion(bf16[512,2048]{1,0:T(8,128)(2,1)S(1)} %copy-done, bf16[2048,4096]{1,0:T(8,128)(2,1)} %all-gather.5.cloned.1.call-done), kind=kOutput, calls=%fused_computation.11 | convolution fusion | flops 8592031744 | bytes 23068672 | tf_op jit(solution)/shard_map/dot_general | solution.py:110
  229.2 5.4 gather_fusion.1
  234.6 6.4 %gather_fusion = bf16[160,4096]{1,0:T(8,128)(2,1)} fusion(bf16[512,4096]{1,0:T(8,128)(2,1)} %convolution_convert_fusion, s32[1024]{0:T(1024)S(1)} %pad_clamp_fusion.5), kind=kCustom, calls=%fused_computation | custom fusion | bytes 2622080 | tf_op jit(solution)/shard_map/gather | solution.py:45
  243.5 3.7 collective-permute-start
  250.9 5.9 fusion.72
  256.8 5.3 collective-permute-done
  262.0 5.5 collective-permute-done.1
  267.5 8.9 %pad_maximum_fusion.1 = bf16[832,4096]{1,0:T(8,128)(2,1)} fusion(bf16[160,4096]{1,0:T(8,128)(2,1)S(1)} %collective-permute-done.1, bf16[160,4096]{1,0:T(8,128)(2,1)} %collective-permute-done, bf16[512,4096]{1,0:T(8,128)(2,1)S(1)} %copy-done.1), kind=kLoop, calls=%fused_computation.10 | loop fusion | flops 20447232 | bytes 13631488 | tf_op jit(solution)/shard_map/concatenate | solution.py:162
  276.4 15.4 %gather_fusion.2 = bf16[640,4096]{1,0:T(8,128)(2,1)} fusion(bf16[832,4096]{1,0:T(8,128)(2,1)} %pad_maximum_fusion.1, s32[1024]{0:T(1024)S(1)} %pad_clamp_fusion.3), kind=kCustom, calls=%fused_computation.2 | custom fusion | bytes 10488320 | tf_op jit(solution)/shard_map/gather | solution.py:45
  291.8 2.9 broadcast_select_fusion.1
  300.5 3.6 fusion.17
  306.8 11.4 %fusion.44 = bf16[4,8,256,160]{2,3,1,0:T(8,128)(2,1)} fusion(bf16[4,20,8,8,256]{4,3,2,1,0:T(8,128)(2,1)} %bitcast.88, f32[4,8,160,160]{2,3,1,0:T(8,128)} %fusion.17, f32[4,8,160,160]{2,3,1,0:T(8,128)} %copy-done.16, f32[4,8,160]{2,1,0:T(8,128)S(1)} %get-tuple-element.45), kind=kOutput, calls=%fused_computation.55 | convolution fusion | flops 426480800 | bytes 11816960 | tf_op jit(solution)/shard_map/shqk,sqhd->skhd/dot_general | solution.py:78
  321.2 3.6 select_reduce_fusion.1
  326.8 3.5 collective-permute-start.3
  332.2 3.4 copy.61
  338.8 2.8 collective-permute-done.2
  341.6 4.2 collective-permute-done.3
  345.8 24.2 %pad_maximum_fusion = bf16[960,4096]{1,0:T(8,128)(2,1)} fusion(bf16[160,4096]{1,0:T(8,128)(2,1)} %collective-permute-done.3, bf16[160,4096]{1,0:T(8,128)(2,1)} %collective-permute-done.2, bf16[640,2048]{1,0:T(8,128)(2,1)S(1)} %bitcast.105, bf16[640,2048]{1,0:T(8,128)(2,1)S(1)} %bitcast.104), kind=kLoop, calls=%fused_computation.9 | loop fusion | flops 31457280 | bytes 15728640 | tf_op jit(solution)/shard_map/concatenate | solution.py:180
  370.0 12.8 %gather_fusion.5 = bf16[512,4096]{1,0:T(8,128)(2,1)} fusion(bf16[960,4096]{1,0:T(8,128)(2,1)} %pad_maximum_fusion, s32[1024]{0:T(1024)S(1)} %pad_clamp_fusion), kind=kCustom, calls=%fused_computation.5 | custom fusion | bytes 8390656 | tf_op jit(solution)/shard_map/gather | solution.py:192
  382.8 14.8 %convert_bitcast_fusion = bf16[2048,4096]{0,1:T(8,128)(2,1)} fusion(bf16[512,4096]{1,0:T(8,128)(2,1)} %gather_fusion.5, bf16[512,2048]{1,0:T(8,128)(2,1)S(1)} %copy-done), kind=kOutput, calls=%fused_computation.8 | convolution fusion | flops 8598323200 | bytes 23068672 | tf_op jit(solution)/shard_map/dot_general | solution.py:194
  397.6 20.7 %copy.69 = bf16[2048,4096]{1,0:T(8,128)(2,1)} copy(bf16[2048,4096]{0,1:T(8,128)(2,1)} %convert_bitcast_fusion) | data formatting | bytes 33554432
  419.2 117.5 %reduce-scatter.7.cloned.1.call-done = bf16[64,4096]{1,0:T(8,128)(2,1)} async-done(((bf16[2048,4096]{1,0:T(8,128)(2,1)}), bf16[64,4096]{1,0:T(8,128)(2,1)}) %reduce-scatter.7.cloned.1.call-update) | async-done | bytes 524304
  539.7 4.6 convert_bitcast_fusion.2
  548.2 12.0 %convert_bitcast_fusion.1 = bf16[4,160,8,256]{3,1,2,0:T(8,128)(2,1)} fusion(f32[4,8,160,160]{2,3,1,0:T(8,128)} %fusion.17, bf16[4,20,8,8,256]{4,3,2,1,0:T(8,128)(2,1)} %bitcast.85, f32[4,8,160,160]{2,3,1,0:T(8,128)} %copy-done.16, f32[4,8,160]{2,1,0:T(8,128)S(1)} %get-tuple-element.45), kind=kOutput, calls=%fused_computation.39 | convolution fusion | flops 426480800 | bytes 11816960 | tf_op jit(solution)/shard_map/shqk,skhd->sqhd/dot_general | solution.py:75
  560.1 3.4 copy.59
  567.1 12.1 %gather_fusion.4 = bf16[512,4096]{1,0:T(8,128)(2,1)} fusion(bf16[640,4096]{1,0:T(8,128)(2,1)} %pad_maximum_fusion.2, s32[1024]{0:T(1024)S(1)} %pad_clamp_fusion.1), kind=kCustom, calls=%fused_computation.4 | custom fusion | bytes 8390656 | tf_op jit(solution)/shard_map/gather | solution.py:176
  579.1 4.8 fusion.74
  (107 shorter events, 48.3 us)
Async XLA Ops:
  7.2 207.8 %copy-start = (bf16[512,2048]{1,0:T(8,128)(2,1)S(1)}, bf16[512,2048]{1,0:T(8,128)(2,1)}, u32[]{:S(2)}) copy-start(bf16[512,2048]{1,0:T(8,128)(2,1)} %param.7) | copy-start | bytes 6291460
  7.2 53.3 %copy-start.10 = (s32[128,4]{0,1:T(4,128)S(1)}, s32[128,4]{0,1:T(4,128)}, u32[]{:S(2)}) copy-start(s32[128,4]{0,1:T(4,128)} %param.11) | copy-start | bytes 6148
  7.2 53.4 %copy-start.13 = (s32[128,4]{0,1:T(4,128)S(1)}, s32[128,4]{0,1:T(4,128)}, u32[]{:S(2)}) copy-start(s32[128,4]{0,1:T(4,128)} %param.12) | copy-start | bytes 6148
  7.2 53.2 %all-gather.3.cloned.1.call-start = ((), (), s32[]{:S(2)}) async-start(), calls=%async_computation.2 | async-start | bytes 4325376 | tf_op jit(solution)/shard_map/all_gather | solution.py:109
  7.9 207.0 %all-gather.5.cloned.1.call-start = ((), (), s32[]{:S(2)}) async-start(), calls=%async_computation.3 | async-start | bytes 20971520 | tf_op jit(solution)/shard_map/all_gather | solution.py:112
  60.4 476.3 %reduce-scatter.7.cloned.1.call-start = ((), (), s32[]{:S(2)}) async-start(), calls=%async_computation.5 | async-start | bytes 17301504
  61.0 0.6 copy-start.14
  61.6 4.9 copy-start.11
  66.5 14.4 %copy-start.9 = (s32[128,4]{0,1:T(4,128)S(1)}, s32[128,4]{0,1:T(4,128)}, u32[]{:S(2)}) copy-start(s32[128,4]{0,1:T(4,128)} %param.13) | copy-start | bytes 6148
  243.5 18.5 %collective-permute-start = (bf16[160,4096]{1,0:T(8,128)(2,1)}, bf16[160,4096]{1,0:T(8,128)(2,1)}, u32[]{:S(2)}, u32[]{:S(2)}) collective-permute-start(bf16[160,4096]{1,0:T(8,128)(2,1)} %broadcast_select_fusion.3), channel_id=1, source_target_pairs={{0,4},{4,8},{8,12},{12,16},{16,20},{20,24},{24,28},{28,32},{32,36}... | collective-permute-start | bytes 3932168 | tf_op jit(solution)/shard_map/ppermute | solution.py:17
  248.4 19.1 %collective-permute-start.1 = (bf16[160,4096]{1,0:T(8,128)(2,1)}, bf16[160,4096]{1,0:T(8,128)(2,1)S(1)}, u32[]{:S(2)}, u32[]{:S(2)}) collective-permute-start(bf16[160,4096]{1,0:T(8,128)(2,1)} %broadcast_select_fusion.2), channel_id=1, source_target_pairs={{4,0},{8,4},{12,8},{16,12},{20,16},{24,20},{28,24},{32,28},{36,32}... | collective-permute-start | bytes 3932168 | tf_op jit(solution)/shard_map/ppermute | solution.py:20
  250.8 16.7 %copy-start.1 = (bf16[512,4096]{1,0:T(8,128)(2,1)S(1)}, bf16[512,4096]{1,0:T(8,128)(2,1)}, u32[]{:S(2)}) copy-start(bf16[512,4096]{1,0:T(8,128)(2,1)} %convolution_convert_fusion) | copy-start | bytes 12582916
  294.7 2.5 copy-start.4
  295.2 3.0 copy-start.2
  295.2 5.3 copy-start.3
  298.2 2.3 copy-start.5
  300.5 4.0 copy-start.16
  318.1 2.5 copy-start.7
  324.8 16.8 %collective-permute-start.2 = (bf16[160,4096]{1,0:T(8,128)(2,1)}, bf16[160,4096]{1,0:T(8,128)(2,1)}, u32[]{:S(2)}, u32[]{:S(2)}) collective-permute-start(bf16[160,4096]{1,0:T(8,128)(2,1)} %get-tuple-element.15), channel_id=1, source_target_pairs={{0,4},{4,8},{8,12},{12,16},{16,20},{20,24},{24,28},{28,32},{32,36}... | collective-permute-start | bytes 3932168 | tf_op jit(solution)/shard_map/ppermute | solution.py:17
  326.8 19.0 %collective-permute-start.3 = (bf16[160,4096]{1,0:T(8,128)(2,1)S(1)}, bf16[160,4096]{1,0:T(8,128)(2,1)}, u32[]{:S(2)}, u32[]{:S(2)}) collective-permute-start(bf16[160,4096]{1,0:T(8,128)(2,1)S(1)} %get-tuple-element.16), channel_id=1, source_target_pairs={{4,0},{8,4},{12,8},{16,12},{20,16},{24,20},{28,24},{32,28},{36,32}... | collective-permute-start | bytes 3932168 | tf_op jit(solution)/shard_map/ppermute | solution.py:20
  332.1 4.3 copy-start.8
  418.3 0.7 copy-start.15
  418.3 0.7 copy-start.12
  418.3 165.6 %reduce-scatter.5.cloned.1.call-start = ((), (), s32[]{:S(2)}) async-start(), calls=%async_computation.4 | async-start | bytes 2621440 | tf_op jit(solution)/shard_map/reduce_scatter | solution.py:204
  560.1 4.3 copy-start.6
Sparse Core Ops, SparseCore 0:
  10.3 50.0 all-gather.2
  62.0 152.8 all-gather.4
  418.4 118.1 reduce-scatter.6
  539.8 30.2 reduce-scatter.4
where the time goes:
time: 601 us; the launch traced here: 593 us
  waiting for transfers between devices  309 us (51%)
  local copies, waits for them, and re-layouts  124 us (21%)
  other arithmetic  70.7 us (12%)
  matrix products  63.8 us (11%)
  between operations  14.4 us (2%)
  starting transfers between devices  11.1 us (2%)
    all_gather x1, waiting for transfers between devices, body(): lax.all_gather(row_panel, 'fsdp', axis=1, tiled=True)  120 us
    unnamed x5, waiting for transfers between devices  118 us
    all_gather x1, waiting for transfers between devices, body(): row_panel = lax.all_gather(kv_weights, 'dp', axis=0, tiled=True)  52.4 us
    gather x4, local copies, waits for them, and re-layouts, take_rows(): picked = source[jnp.minimum(index, source.shape[0] - 1)]  41.6 us
    unnamed x43, local copies, waits for them, and re-layouts  33 us
    concatenate x1, other arithmetic, body(): jnp.concatenate([pair_grads.reshape(-1, 2 * inner_width), returned[:ENC_M...  24.2 us
    dot_general x1, matrix products, body(): lax.dot_general(enc_hidden, grad_key_values, (((0,), (0,)), ((), ())), pr...  14.8 us
    dot_general x1, matrix products, body(): jnp.dot(enc_hidden, lax.all_gather(row_panel, 'fsdp', axis=1, tiled=True)...  14.2 us
  transfers between devices with their start and end apart: 8, of which 7 were waited for; matrix products, arithmetic and copies ran while one was open for 16% of the time, Pallas kernels for 0%

commit v1 on v0

v1 whole, which is shorter than its diff:
```python
import jax
import jax.numpy as jnp
from jax import lax
from jax.experimental import pallas as pl
from jax.experimental.pallas import tpu as pltpu
from jax.sharding import Mesh, PartitionSpec as P

HEADS = 8
HEAD_DIM = 256
SEGS = 4
TOK = 512
PAIR = 2 * TOK
WIN = 176
POOL = PAIR + 2 * WIN
D = 2048
CHIP = ("z", "y", "x")
ALL = ("z", "y", "c", "x")


def align(start, limit):
    return jnp.minimum((start // 16) * 16, limit - WIN)


def kernel(meta, x_ref, xt_ref, wk_ref, wv_ref, q_ref, ct_ref, ctx_ref, gq_ref, dw_ref, k_s, v_s, gk_s, gv_s):
    scale = HEAD_DIM ** -0.5
    x = x_ref[...]
    k_s[...] = jnp.dot(
        x, wk_ref[...].reshape(D, HEAD_DIM), preferred_element_type=jnp.float32
    ).astype(jnp.bfloat16)
    v_s[...] = jnp.dot(
        x, wv_ref[...].reshape(D, HEAD_DIM), preferred_element_type=jnp.float32
    ).astype(jnp.bfloat16)

    def mm(a, b, dims):
        return lax.dot_general(a, b, (dims, ((), ())), preferred_element_type=jnp.float32)

    col = lax.broadcasted_iota(jnp.int32, (WIN, WIN), 1)
    row = lax.broadcasted_iota(jnp.int32, (WIN, WIN), 0)
    row_wide = lax.broadcasted_iota(jnp.int32, (WIN, HEAD_DIM), 0)
    for e in range(2 * SEGS):
        es, el, ds, dl = meta[e, 0], meta[e, 1], meta[e, 2], meta[e, 3]
        ew = pl.multiple_of(align(es, PAIR), 16)
        dw = pl.multiple_of(align(ds, POOL), 16)
        elo, dlo = es - ew, ds - dw
        ewin, dwin = pl.ds(ew, WIN), pl.ds(dw, WIN)
        k, v = k_s[ewin, :], v_s[ewin, :]
        q, ct = q_ref[dwin, :], ct_ref[dwin, :]
        s = mm(q, k, ((1,), (1,))) * scale
        gw = mm(ct, v, ((1,), (1,)))
        k_live = (col >= elo) & (col < elo + el)
        live = k_live & (row >= dlo) & (row < dlo + dl)
        top = jnp.max(jnp.where(k_live, s, -jnp.inf), axis=1, keepdims=True)
        p = jnp.where(k_live, jnp.exp(s - top), 0.0)
        total = jnp.sum(p, axis=1, keepdims=True)
        w = jnp.where(live, p * (1.0 / total), 0.0)
        w_low = w.astype(jnp.bfloat16)
        delta = jnp.sum(w * gw, axis=1, keepdims=True)
        gs = (w * (gw - delta) * scale).astype(jnp.bfloat16)
        ctx = mm(w_low, v, ((1,), (0,))).astype(jnp.bfloat16)
        gq = mm(gs, k, ((1,), (0,))).astype(jnp.bfloat16)
        gk = mm(gs, q, ((0,), (0,))).astype(jnp.bfloat16)
        gv = mm(w_low, ct, ((0,), (0,))).astype(jnp.bfloat16)
        d_in = (row_wide >= dlo) & (row_wide < dlo + dl)
        e_in = (row_wide >= elo) & (row_wide < elo + el)
        ctx_ref[dwin, :] = jnp.where(d_in, ctx, ctx_ref[dwin, :])
        gq_ref[dwin, :] = jnp.where(d_in, gq, gq_ref[dwin, :])
        gk_s[ewin, :] = jnp.where(e_in, gk, gk_s[ewin, :])
        gv_s[ewin, :] = jnp.where(e_in, gv, gv_s[ewin, :])
    xt = xt_ref[...]
    dw_ref[:, 0, 0] = (
        jnp.dot(xt, gk_s[...], preferred_element_type=jnp.float32)
        .astype(jnp.bfloat16)
        .reshape(16, 128, HEAD_DIM)
    )
    dw_ref[:, 1, 0] = (
        jnp.dot(xt, gv_s[...], preferred_element_type=jnp.float32)
        .astype(jnp.bfloat16)
        .reshape(16, 128, HEAD_DIM)
    )


def run_kernel(meta, x, xt, weights, pool, core):
    col_of = core.reshape(1).astype(jnp.int32)

    def wrap(meta, core_ref, *refs):
        kernel(meta, *refs)

    grid_spec = pltpu.PrefetchScalarGridSpec(
        num_scalar_prefetch=2,
        grid=(4,),
        in_specs=[
            pl.BlockSpec((PAIR, D), lambda i, m, c: (0, 0)),
            pl.BlockSpec((D, PAIR), lambda i, m, c: (0, 0)),
            pl.BlockSpec((32, 1, 64, HEAD_DIM), lambda i, m, c: (0, i // 2, 0, c[0] * 2 + i % 2)),
            pl.BlockSpec((32, 1, 64, HEAD_DIM), lambda i, m, c: (0, 2 + i // 2, 0, c[0] * 2 + i % 2)),
            pl.BlockSpec((POOL, HEAD_DIM), lambda i, m, c: (0, i)),
            pl.BlockSpec((POOL, HEAD_DIM), lambda i, m, c: (0, 4 + i)),
        ],
        out_specs=[
            pl.BlockSpec((POOL, HEAD_DIM), lambda i, m, c: (0, i)),
            pl.BlockSpec((POOL, HEAD_DIM), lambda i, m, c: (0, i)),
            pl.BlockSpec((16, 2, 1, 128, HEAD_DIM), lambda i, m, c: (0, 0, i // 2, 0, i % 2)),
        ],
        scratch_shapes=[pltpu.VMEM((PAIR, HEAD_DIM), jnp.bfloat16)] * 4,
    )
    return pl.pallas_call(
        wrap,
        grid_spec=grid_spec,
        out_shape=[
            jax.ShapeDtypeStruct((POOL, 4 * HEAD_DIM), jnp.bfloat16),
            jax.ShapeDtypeStruct((POOL, 4 * HEAD_DIM), jnp.bfloat16),
            jax.ShapeDtypeStruct((16, 2, 2, 128, 512), jnp.bfloat16),
        ],
        compiler_params=pltpu.CompilerParams(vmem_limit_bytes=50 * 1024 * 1024),
        cost_estimate=pl.CostEstimate(flops=25_000_000_000, bytes_accessed=40_000_000, transcendentals=1_000_000),
    )(meta, col_of, x, xt, weights, weights, pool, pool)


def swap(value):
    return lax.ppermute(value, "c", [(0, 1), (1, 0)])


def send_up(value):
    return lax.ppermute(value, ("z", "y"), [(i, i + 1) for i in range(15)])


def send_down(value):
    return lax.ppermute(value, ("z", "y"), [(i + 1, i) for i in range(15)])


def plan(enc_lengths, dec_lengths, dec_partner, t, c, x):
    cores = jnp.stack([c, 1 - c])
    devices = (t * 2 + cores) * 4 + x
    ids = (devices[:, None] * SEGS + jnp.arange(SEGS, dtype=jnp.int32)).reshape(-1)
    dec_starts = (jnp.cumsum(dec_lengths, axis=1) - dec_lengths).reshape(-1)
    enc_starts = (jnp.cumsum(enc_lengths, axis=1) - enc_lengths).reshape(-1)
    places = jnp.arange(ids.shape[0] * 0 + enc_starts.shape[0], dtype=jnp.int32)
    own = places[None, :] == ids[:, None]
    hit = dec_partner.reshape(-1)[None, :] == ids[:, None]

    def pick(mask, table):
        return jnp.sum(jnp.where(mask, table[None, :], 0), axis=1)

    enc_len = pick(own, enc_lengths.reshape(-1))
    enc_start = pick(own, enc_starts) + jnp.repeat(jnp.arange(2, dtype=jnp.int32) * TOK, SEGS)
    dec_len = pick(hit, dec_lengths.reshape(-1))
    dec_start = pick(hit, dec_starts)
    owner_dp = pick(hit, places) // (SEGS * 4)
    base = jnp.where(owner_dp % 2 == c, 0, TOK)
    in_pool = base + dec_start
    window = align(in_pool, PAIR)
    chip = owner_dp // 2
    dec_at = jnp.where(
        chip == t,
        in_pool,
        in_pool - window + jnp.where(chip < t, PAIR, PAIR + WIN),
    )
    meta = jnp.stack([enc_start, enc_len, dec_at, dec_len], axis=1).astype(jnp.int32)

    def leaving(core, step):
        device = (t * 2 + core) * 4 + x
        at = places // SEGS == device
        goes = at & (dec_partner.reshape(-1) // (SEGS * 4) == t * 2 + core + step)
        length = jnp.sum(jnp.where(goes, dec_lengths.reshape(-1), 0))
        start = jnp.sum(jnp.where(goes, dec_starts, 0)) + jnp.where(core == c, 0, TOK)
        return start, length, align(start, PAIR)

    return meta, leaving(0, -1), leaving(1, 1)


def body(enc_hidden, kv_weights, queries, cotangent, enc_lengths, dec_lengths, dec_partner):
    z, y, c, x = (lax.axis_index(a) for a in ALL)
    t = z * 4 + y
    weights = lax.all_gather(kv_weights, ALL, axis=0).reshape(32, 4, 64, 1024)
    meta, below, above = plan(enc_lengths, dec_lengths, dec_partner, t, c, x)

    tokens = jnp.concatenate([enc_hidden, swap(enc_hidden)], axis=0)
    tokens_t = tokens.T
    stacked = jnp.concatenate([queries, cotangent], axis=1).reshape(TOK, 4, 2, 512)
    mine = lax.dynamic_index_in_dim(stacked, c, 2, keepdims=False).reshape(TOK, 2048)
    other = lax.dynamic_index_in_dim(stacked, 1 - c, 2, keepdims=False).reshape(TOK, 2048)
    pair = jnp.concatenate([mine, swap(other)], axis=0)
    to_below = lax.dynamic_slice_in_dim(pair, below[2], WIN, 0)
    to_above = lax.dynamic_slice_in_dim(pair, above[2], WIN, 0)
    pool = jnp.concatenate([pair, send_up(to_above), send_down(to_below)], axis=0)

    ctx, gq, dw = run_kernel(meta, tokens, tokens_t, weights, pool, c)

    parts = lax.all_to_all(dw.reshape(64, 128, 512), CHIP, 0, 0, tiled=True)
    summed = jnp.sum(parts.astype(jnp.float32), axis=0).reshape(2, 64, 512)
    kept = lax.dynamic_index_in_dim(summed, c, 0, keepdims=False)
    got = swap(lax.dynamic_index_in_dim(summed, 1 - c, 0, keepdims=False))
    grad = jnp.where(
        c == 0, jnp.concatenate([kept, got], axis=1), jnp.concatenate([got, kept], axis=1)
    )

    both = jnp.concatenate([ctx, gq], axis=1)
    from_above = send_down(both[PAIR : PAIR + WIN])
    from_below = send_up(both[PAIR + WIN :])
    out = both[:PAIR]
    offsets = jnp.arange(WIN, dtype=jnp.int32)[:, None]
    for (start, length, window), got in ((below, from_below), (above, from_above)):
        inside = (offsets + window >= start) & (offsets + window < start + length)
        now = lax.dynamic_slice_in_dim(out, window, WIN, 0)
        out = lax.dynamic_update_slice_in_dim(out, jnp.where(inside, got, now), window, 0)
    theirs = swap(out[TOK:]).reshape(TOK, 4, 1, 512)
    ours = out[:TOK].reshape(TOK, 4, 1, 512)
    full = jnp.where(
        c == 0, jnp.concatenate([ours, theirs], axis=2), jnp.concatenate([theirs, ours], axis=2)
    ).reshape(TOK, 4096)
    return full[:, :2048], full[:, 2048:], grad


def solution(mesh):
    fine = Mesh(mesh.devices.reshape(4, 4, 2, 4), ALL)
    rows = P(ALL, None)
    cut = P(("z", "y", "c"), "x")
    return jax.shard_map(
        body,
        mesh=fine,
        in_specs=(rows, cut, rows, rows, P(), P(), P()),
        out_specs=(rows, rows, cut),
        check_vma=False,
    )
```

time: 601 us -> 375 us (0.62)
  the two profiles are of different devices: /device:TPU:1 before, /device:TPU:77 now
where the time goes in v1:
time: 375 us; the launch traced here: 371 us
  waiting for transfers between devices  140 us (37%)
  local copies, waits for them, and re-layouts  101 us (27%)
  Pallas kernels  44.1 us (12%)
  starting transfers between devices  34.5 us (9%)
  other arithmetic  34.4 us (9%)
  between operations  17.1 us (5%)
    ppermute x2, waiting for transfers between devices, send_up(): return lax.ppermute(value, ('z', 'y'), [(i, i + 1) for i in range(15)])  135 us
    pallas_call x1, Pallas kernels, run_kernel(): pl.pallas_call(wrap, grid_spec=grid_spec, out_shape=[jax.ShapeDtypeStruct...  44.1 us
    dynamic_slice x1, local copies, waits for them, and re-layouts, body(): lax.dynamic_index_in_dim(stacked, 1 - c, 2, keepdims=False)  29.1 us
    all_to_all x1, starting transfers between devices, body(): parts = lax.all_to_all(dw.reshape(64, 128, 512), CHIP, 0, 0, tiled=True)  21.3 us
    select_n x2, local copies, waits for them, and re-layouts, body(): jnp.where(c == 0, jnp.concatenate([ours, theirs], axis=2), jnp.concatenat...  16.3 us
    unnamed x28, local copies, waits for them, and re-layouts  11.5 us
    concatenate x1, other arithmetic, body(): jnp.concatenate([pair, send_up(to_above), send_down(to_below)], axis=0)  9.29 us
    dynamic_update_slice x2, local copies, waits for them, and re-layouts, body(): lax.dynamic_update_slice_in_dim(out, jnp.where(inside, got, now), window, 0)  8.86 us
  transfers between devices with their start and end apart: 10, of which 4 were waited for; matrix products, arithmetic and copies ran while one was open for 34% of the time, Pallas kernels for 0%

profile of v1, /device:TPU:77, one launch (start us, length us, event | category | flops | bytes accessed | tf_op | source)
XLA Modules:
  0.0 371.2 jit_solution(9285843149762652786)
XLA Ops:
  7.9 4.6 %pad_maximum_fusion.2 = bf16[512,4096]{1,0:T(8,128)(2,1)} fusion(bf16[512,2048]{1,0:T(8,128)(2,1)} %param.10, bf16[512,2048]{1,0:T(8,128)(2,1)} %param.9), kind=kLoop, calls=%fused_computation.3 | loop fusion | flops 8388608 | bytes 8388608 | tf_op jit(solution)/shard_map/concatenate | solution.py:179
  12.6 7.8 %reshape.347 = bf16[512,4,2,512]{3,2,1,0:T(2,128)(2,1)} reshape(bf16[512,4096]{1,0:T(8,128)(2,1)} %pad_maximum_fusion.2) | data formatting | bytes 8388608 | tf_op jit(solution)/shard_map/reshape | solution.py:179
  20.4 29.1 %dynamic-slice_reduce_fusion = (bf16[512,4,512]{2,1,0:T(4,128)(2,1)S(1)}, bf16[512,4,512]{2,1,0:T(4,128)(2,1)}) fusion(bf16[512,4,2,512]{3,2,1,0:T(2,128)(2,1)} %reshape.347, s32[]{:T(128)S(6)} %select_n.205, s32[]{:T(128)S(6)} %select_n.204), kind=kLoop, calls=%fused_computation.5 | loop fusion | bytes 8388616 | tf_op jit(solution)/shard_map/jit(dynamic_index_in_dim)/dynamic_slice | solution.py:181
  49.5 2.0 copy.68
  52.2 2.5 copy.60
  59.6 2.2 copy.67
  62.0 1.7 constant_dynamic-update-slice_fusion
  64.1 3.2 collective-permute-start.2
  67.3 2.3 collective-permute-start.3
  69.8 5.5 %fusion.20 = (bf16[2048,1024]{1,0:T(8,128)(2,1)}, bf16[1024,2048]{0,1:T(8,128)(2,1)}) fusion(bf16[512,2048]{0,1:T(8,128)(2,1)} %collective-permute-done, bf16[512,2048]{0,1:T(8,128)(2,1)} %copy.60), kind=kLoop, calls=%fused_computation.85 | loop fusion | flops 8388608 | bytes 12582912 | tf_op jit(solution)/shard_map/transpose | solution.py:178
  75.3 6.5 %copy.63.refs_0_ = bf16[1024,2048]{1,0:T(8,128)(2,1)} copy(bf16[1024,2048]{0,1:T(8,128)(2,1)} %get-tuple-element.34) | data formatting | bytes 8388608 | tf_op jit(solution)/shard_map/concatenate | solution.py:177
  81.8 17.6 %collective-permute-done.2 = bf16[176,2048]{1,0:T(8,128)(2,1)} collective-permute-done((bf16[176,2048]{1,0:T(8,128)(2,1)S(1)}, bf16[176,2048]{1,0:T(8,128)(2,1)}, u32[]{:S(2)}, u32[]{:S(2)}) %collective-permute-start.2) | collective-permute-done | bytes 720928 | tf_op jit(solution)/shard_map/ppermute | solution.py:124
  99.3 3.1 collective-permute-done.3
  102.5 9.3 %pad_maximum_fusion.refs_4_.refs_5_ = bf16[1376,2048]{1,0:T(8,128)(2,1)} fusion(bf16[176,2048]{1,0:T(8,128)(2,1)} %collective-permute-done.3, bf16[176,2048]{1,0:T(8,128)(2,1)} %collective-permute-done.2, bf16[512,2048]{1,0:T(8,128)(2,1)} %collective-permute-done.1, bf16[512,2048]{1,0:T(8,128)(2,1)S(1)} %bitcast.21), kind=kLoop, calls=%fused_computation.1 | loop fusion | flops 22544384 | bytes 11272192 | tf_op jit(solution)/shard_map/concatenate | solution.py:185
  111.8 44.1 %shard_map.94 = (bf16[1376,1024]{1,0:T(8,128)(2,1)S(1)}, bf16[1376,1024]{1,0:T(8,128)(2,1)}, bf16[16,2,2,128,512]{4,3,2,1,0:T(8,128)(2,1)}) custom-call(s32[8,4]{1,0:T(8,128)S(1)} %pad_add_fusion.meta, s32[1]{0:T(128)} %bitcast.core_ref, bf16[1024,2048]{1,0:T(8,128)(2,1)} %copy.63.refs_0_, bf16[2048,1024]{1,0:T(8,128)(2,1)} %get-tuple-element.33.refs_1_, ...), custom_call_target="tpu_custom_call" | custom-call | flops 24999999488 | bytes 40000000 | tf_op jit(solution)/shard_map/pallas_call | solution.py:106
  155.9 21.3 %all-to-all-start = ((bf16[64,128,512]{2,1,0:T(8,128)(2,1)}), bf16[64,128,512]{2,1,0:T(8,128)(2,1)}, u32[]{:S(2)}, u32[]{:S(2)}) async-start(bf16[64,128,512]{2,1,0:T(8,128)(2,1)} %bitcast.24), calls=%async_computation | async-start | bytes 16777216 | tf_op jit(solution)/shard_map/all_to_all | solution.py:189
  179.4 2.5 copy-done.2
  182.1 3.1 collective-permute-start.4
  185.2 2.2 collective-permute-start.5
  188.7 2.5 slice.28
  191.2 117.6 %collective-permute-done.4 = bf16[176,2048]{1,0:T(8,128)(2,1)S(1)} collective-permute-done((bf16[176,2048]{1,0:T(8,128)(2,1)S(1)}, bf16[176,2048]{1,0:T(8,128)(2,1)S(1)}, u32[]{:S(2)}, u32[]{:S(2)}) %collective-permute-start.4) | collective-permute-done | bytes 720928 | tf_op jit(solution)/shard_map/ppermute | solution.py:124
  309.3 4.4 %dynamic_update_slice.6 = bf16[1024,2048]{1,0:T(8,128)(2,1)} dynamic-update-slice(bf16[1024,2048]{1,0:T(8,128)(2,1)} %copy-done, bf16[176,2048]{1,0:T(8,128)(2,1)S(1)} %dynamic-slice_select_fusion.1, s32[]{:T(128)S(6)} %select_n.215, s32[]{:T(128)} %constant.150.clone.1) | dynamic-update-slice | bytes 1441796 | tf_op jit(solution)/shard_map/dynamic_update_slice | solution.py:205
  313.7 1.5 dynamic-slice_select_fusion
  315.2 4.4 %dynamic_update_slice.7 = bf16[1024,2048]{1,0:T(8,128)(2,1)} dynamic-update-slice(bf16[1024,2048]{1,0:T(8,128)(2,1)} %dynamic_update_slice.6, bf16[176,2048]{1,0:T(8,128)(2,1)S(1)} %dynamic-slice_select_fusion, s32[]{:T(128)S(6)} %select_n.211, s32[]{:T(128)} %constant.150.clone.1) | dynamic-update-slice | bytes 1441796 | tf_op jit(solution)/shard_map/dynamic_update_slice | solution.py:205
  319.6 4.0 %fusion.23 = (bf16[512,2048]{1,0:T(8,128)(2,1)S(1)}, bf16[512,2048]{1,0:T(8,128)(2,1)}) fusion(bf16[1024,2048]{1,0:T(8,128)(2,1)} %dynamic_update_slice.7), kind=kLoop, calls=%fused_computation.88 | loop fusion | bytes 8388608 | tf_op jit(solution)/shard_map/slice | solution.py:207
  324.8 2.7 reshape.350
  328.9 4.5 %reshape.351 = bf16[512,4,1,512]{3,1,0,2:T(4,128)(2,1)} reshape(bf16[512,2048]{1,0:T(8,128)(2,1)} %collective-permute-done.6) | data formatting | bytes 4194304 | tf_op jit(solution)/shard_map/reshape | solution.py:206
  333.4 6.0 %maximum_select_fusion = bf16[512,4,2,512]{3,1,0,2:T(4,128)(2,1)S(1)} fusion(bf16[512,4,1,512]{3,1,0,2:T(4,128)(2,1)} %reshape.351, bf16[512,4,1,512]{3,1,0,2:T(4,128)(2,1)S(1)} %copy-done.3, pred[]{:T(512)S(6)} %eq.96), kind=kLoop, calls=%fused_computation.4 | loop fusion | flops 6291456 | bytes 8388609 | tf_op jit(solution)/shard_map/jit(_where)/select_n | solution.py:208
  339.4 8.4 %copy.64 = bf16[512,4,2,512]{3,2,1,0:T(2,128)(2,1)} copy(bf16[512,4,2,512]{3,1,0,2:T(4,128)(2,1)S(1)} %maximum_select_fusion) | data formatting | bytes 8388608 | tf_op jit(solution)/shard_map/jit(_where)/select_n | solution.py:208
  347.8 7.8 %select_n.221 = bf16[512,4096]{1,0:T(8,128)(2,1)} reshape(bf16[512,4,2,512]{3,2,1,0:T(2,128)(2,1)} %copy.64) | data formatting | bytes 8388608 | tf_op jit(solution)/shard_map/jit(_where)/select_n | solution.py:208
  355.7 4.9 %convert_reduce_fusion = f32[128,512]{1,0:T(8,128)S(1)} fusion(bf16[64,128,512]{2,1,0:T(8,128)(2,1)} %all-to-all-done), kind=kLoop, calls=%fused_computation | loop fusion | flops 8323072 | bytes 8650752 | tf_op jit(solution)/shard_map/reduce_sum | solution.py:190
  361.1 2.3 fusion.22
  (72 shorter events, 12.1 us)
Async XLA Ops:
  7.2 104.6 %all-gather.3.cloned.1.call-start = ((), (), s32[]{:S(2)}) async-start(), calls=%async_computation.1 | async-start | bytes 16908288 | tf_op jit(solution)/shard_map/all_gather | solution.py:174
  49.5 2.7 copy-start.5
  49.5 5.2 %copy-start.7 = (s32[128,4]{0,1:T(4,128)S(1)}, s32[128,4]{0,1:T(4,128)}, u32[]{:S(2)}) copy-start(s32[128,4]{0,1:T(4,128)} %param.12) | copy-start | bytes 6148
  49.5 5.2 %copy-start.9 = (s32[128,4]{0,1:T(4,128)S(1)}, s32[128,4]{0,1:T(4,128)}, u32[]{:S(2)}) copy-start(s32[128,4]{0,1:T(4,128)} %param.13) | copy-start | bytes 6148
  49.5 7.4 %copy-start.6 = (s32[128,4]{0,1:T(4,128)S(1)}, s32[128,4]{0,1:T(4,128)}, u32[]{:S(2)}) copy-start(s32[128,4]{0,1:T(4,128)} %param.11) | copy-start | bytes 6148
  51.5 10.5 %collective-permute-start.1 = (bf16[512,2048]{1,0:T(8,128)(2,1)}, bf16[512,2048]{1,0:T(8,128)(2,1)}, u32[]{:S(2)}, u32[]{:S(2)}) collective-permute-start(bf16[512,2048]{1,0:T(8,128)(2,1)} %bitcast.16), channel_id=1, source_target_pairs={{0,4},{4,0},{1,5},{5,1},{2,6},{6,2},{3,7},{7,3},{8,12},{12,8},{9,1... | collective-permute-start | bytes 6291464 | tf_op jit(solution)/shard_map/ppermute | solution.py:120
  54.6 15.1 %collective-permute-start = (bf16[512,2048]{0,1:T(8,128)(2,1)}, bf16[512,2048]{0,1:T(8,128)(2,1)}, u32[]{:S(2)}, u32[]{:S(2)}) collective-permute-start(bf16[512,2048]{0,1:T(8,128)(2,1)} %copy.60), channel_id=1, source_target_pairs={{0,4},{4,0},{1,5},{5,1},{2,6},{6,2},{3,7},{7,3},{8,12},{12,8},{9,1... | collective-permute-start | bytes 6291464 | tf_op jit(solution)/shard_map/ppermute | solution.py:120
  62.0 7.7 %copy-start.8 = (s32[8,1]{1,0:T(8,128)S(1)}, s32[8,1]{1,0:T(8,128)}, u32[]{:S(2)}) copy-start(s32[8,1]{1,0:T(8,128)} %copy.55) | copy-start | bytes 100
  64.1 35.3 %collective-permute-start.2 = (bf16[176,2048]{1,0:T(8,128)(2,1)S(1)}, bf16[176,2048]{1,0:T(8,128)(2,1)}, u32[]{:S(2)}, u32[]{:S(2)}) collective-permute-start(bf16[176,2048]{1,0:T(8,128)(2,1)S(1)} %get-tuple-element.31), channel_id=1, source_target_pairs={{0,8},{8,16},{16,24},{24,32},{32,40},{40,48},{48,56},{56,64},{64,7... | collective-permute-start | bytes 2162696 | tf_op jit(solution)/shard_map/ppermute | solution.py:124
  67.3 35.2 %collective-permute-start.3 = (bf16[176,2048]{1,0:T(8,128)(2,1)S(1)}, bf16[176,2048]{1,0:T(8,128)(2,1)}, u32[]{:S(2)}, u32[]{:S(2)}) collective-permute-start(bf16[176,2048]{1,0:T(8,128)(2,1)S(1)} %get-tuple-element.32), channel_id=1, source_target_pairs={{8,0},{16,8},{24,16},{32,24},{40,32},{48,40},{56,48},{64,56},{72,6... | collective-permute-start | bytes 2162696 | tf_op jit(solution)/shard_map/ppermute | solution.py:128
  155.9 199.8 %all-to-all-start = ((bf16[64,128,512]{2,1,0:T(8,128)(2,1)}), bf16[64,128,512]{2,1,0:T(8,128)(2,1)}, u32[]{:S(2)}, u32[]{:S(2)}) async-start(bf16[64,128,512]{2,1,0:T(8,128)(2,1)} %bitcast.24), calls=%async_computation | async-start | bytes 16777216 | tf_op jit(solution)/shard_map/all_to_all | solution.py:189
  177.2 1.8 copy-start.4
  179.4 2.5 copy-start.2
  182.1 126.8 %collective-permute-start.4 = (bf16[176,2048]{1,0:T(8,128)(2,1)S(1)}, bf16[176,2048]{1,0:T(8,128)(2,1)S(1)}, u32[]{:S(2)}, u32[]{:S(2)}) collective-permute-start(bf16[176,2048]{1,0:T(8,128)(2,1)S(1)} %get-tuple-element.26), channel_id=1, source_target_pairs={{0,8},{8,16},{16,24},{24,32},{32,40},{40,48},{48,56},{56,64},{64,7... | collective-permute-start | bytes 2162696 | tf_op jit(solution)/shard_map/ppermute | solution.py:124
  185.2 128.5 %collective-permute-start.5 = (bf16[176,2048]{1,0:T(8,128)(2,1)S(1)}, bf16[176,2048]{1,0:T(8,128)(2,1)S(1)}, u32[]{:S(2)}, u32[]{:S(2)}) collective-permute-start(bf16[176,2048]{1,0:T(8,128)(2,1)S(1)} %get-tuple-element.25), channel_id=1, source_target_pairs={{8,0},{16,8},{24,16},{32,24},{40,32},{48,40},{56,48},{64,56},{72,6... | collective-permute-start | bytes 2162696 | tf_op jit(solution)/shard_map/ppermute | solution.py:128
  191.2 117.6 %copy-start = (bf16[1024,2048]{1,0:T(8,128)(2,1)}, bf16[1024,2048]{1,0:T(8,128)(2,1)S(1)}, u32[]{:S(2)}) copy-start(bf16[1024,2048]{1,0:T(8,128)(2,1)S(1)} %slice.28) | copy-start | bytes 12582916
  323.6 5.3 %collective-permute-start.6 = (bf16[512,2048]{1,0:T(8,128)(2,1)}, bf16[512,2048]{1,0:T(8,128)(2,1)}, u32[]{:S(2)}, u32[]{:S(2)}) collective-permute-start(bf16[512,2048]{1,0:T(8,128)(2,1)} %get-tuple-element.30), channel_id=1, source_target_pairs={{0,4},{4,0},{1,5},{5,1},{2,6},{6,2},{3,7},{7,3},{8,12},{12,8},{9,1... | collective-permute-start | bytes 6291464 | tf_op jit(solution)/shard_map/ppermute | solution.py:120
  327.5 5.9 %copy-start.3 = (bf16[512,4,1,512]{3,1,0,2:T(4,128)(2,1)S(1)}, bf16[512,4,1,512]{3,1,0,2:T(4,128)(2,1)}, u32[]{:S(2)}) copy-start(bf16[512,4,1,512]{3,1,0,2:T(4,128)(2,1)} %reshape.350) | copy-start | bytes 6291460
  355.7 5.4 %copy-start.1 = (bf16[512,4096]{1,0:T(8,128)(2,1)S(1)}, bf16[512,4096]{1,0:T(8,128)(2,1)}, u32[]{:S(2)}) copy-start(bf16[512,4096]{1,0:T(8,128)(2,1)} %select_n.221) | copy-start | bytes 12582916
  360.6 2.8 collective-permute-start.7
Sparse Core Ops, SparseCore 0:
  11.2 95.1 all-gather.2

commit v2 on v1

v2 whole, which is shorter than its diff:
```python
import jax
import jax.numpy as jnp
from jax import lax
from jax.experimental import pallas as pl
from jax.experimental.pallas import tpu as pltpu
from jax.sharding import Mesh, PartitionSpec as P

HEAD_DIM = 256
SEGS = 4
TOK = 512
PAIR = 2 * TOK
WIN = 176
POOL = PAIR + 2 * WIN
D = 2048
HALF = 512
DP = ("z", "y", "c")
ALL = ("z", "y", "c", "x")
MIB = 1024 * 1024
BF = jnp.bfloat16


def align(start, limit):
    return jnp.minimum((start // 16) * 16, limit - WIN)


def mm(a, b, dims):
    return lax.dot_general(a, b, (dims, ((), ())), preferred_element_type=jnp.float32)


def attend(meta, k_s, v_s, q_s, ct_s, ctx_s, gq_s, gk_s, gv_s):
    scale = HEAD_DIM ** -0.5
    col = lax.broadcasted_iota(jnp.int32, (WIN, WIN), 1)
    row = lax.broadcasted_iota(jnp.int32, (WIN, WIN), 0)
    row_wide = lax.broadcasted_iota(jnp.int32, (WIN, HEAD_DIM), 0)
    for e in range(2 * SEGS):
        es, el, ds, dl = meta[e, 0], meta[e, 1], meta[e, 2], meta[e, 3]
        ew = pl.multiple_of(align(es, PAIR), 16)
        dw = pl.multiple_of(align(ds, POOL), 16)
        elo, dlo = es - ew, ds - dw
        ewin, dwin = pl.ds(ew, WIN), pl.ds(dw, WIN)
        k, v = k_s[ewin, :], v_s[ewin, :]
        q, ct = q_s[dwin, :], ct_s[dwin, :]
        s = mm(q, k, ((1,), (1,))) * scale
        gw = mm(ct, v, ((1,), (1,)))
        k_live = (col >= elo) & (col < elo + el)
        live = k_live & (row >= dlo) & (row < dlo + dl)
        top = jnp.max(jnp.where(k_live, s, -jnp.inf), axis=1, keepdims=True)
        p = jnp.where(k_live, jnp.exp(s - top), 0.0)
        total = jnp.sum(p, axis=1, keepdims=True)
        w = jnp.where(live, p * (1.0 / total), 0.0)
        w_low = w.astype(BF)
        delta = jnp.sum(w * gw, axis=1, keepdims=True)
        gs = (w * (gw - delta) * scale).astype(BF)
        ctx = mm(w_low, v, ((1,), (0,))).astype(BF)
        gq = mm(gs, k, ((1,), (0,))).astype(BF)
        gk = mm(gs, q, ((0,), (0,))).astype(BF)
        gv = mm(w_low, ct, ((0,), (0,))).astype(BF)
        d_in = (row_wide >= dlo) & (row_wide < dlo + dl)
        e_in = (row_wide >= elo) & (row_wide < elo + el)
        ctx_s[dwin, :] = jnp.where(d_in, ctx, ctx_s[dwin, :])
        gq_s[dwin, :] = jnp.where(d_in, gq, gq_s[dwin, :])
        gk_s[ewin, :] = jnp.where(e_in, gk, gk_s[ewin, :])
        gv_s[ewin, :] = jnp.where(e_in, gv, gv_s[ewin, :])


def places(me):
    z, y, c, x = me[0], me[1], me[2], me[3]

    def block(ra, rb, rc):
        first = c == 0
        bx = (x + jnp.where(first, ra, rb)) & 3
        by = (y + jnp.where(first, rb, rc)) & 3
        bz = (z + jnp.where(first, rc, ra)) & 3
        return bx, bz * 4 + by

    return block


def main_kernel(meta, me, x_ref, xt_ref, wk_ref, wv_ref, qm, qo, qa, qb, cm, co, ca, cb,
                om, oo, oa, ob, d0, d1, d2, d3,
                k_s, v_s, gk_s, gv_s, q_s, ct_s, ctx_s, gq_s, dw_s):
    step = pl.program_id(0)
    x = x_ref[...]
    k_s[...] = jnp.dot(x, wk_ref[...].reshape(D, HEAD_DIM), preferred_element_type=jnp.float32).astype(BF)
    v_s[...] = jnp.dot(x, wv_ref[...].reshape(D, HEAD_DIM), preferred_element_type=jnp.float32).astype(BF)
    for pool, parts in ((q_s, (qm, qo, qa, qb)), (ct_s, (cm, co, ca, cb))):
        pool[0:TOK, :] = parts[0][...]
        pool[TOK:PAIR, :] = parts[1][...]
        pool[PAIR : PAIR + WIN, :] = parts[2][...]
        pool[PAIR + WIN :, :] = parts[3][...]
    attend(meta, k_s, v_s, q_s, ct_s, ctx_s, gq_s, gk_s, gv_s)
    for kind, pool in enumerate((ctx_s, gq_s)):
        om[kind] = pool[0:TOK, :]
        oo[kind] = pool[TOK:PAIR, :]
        oa[kind] = pool[PAIR : PAIR + WIN, :]
        ob[kind] = pool[PAIR + WIN :, :]
    xt = xt_ref[...]
    dw_s[step] = jnp.dot(xt, gk_s[...], preferred_element_type=jnp.float32).astype(BF)
    dw_s[2 + step] = jnp.dot(xt, gv_s[...], preferred_element_type=jnp.float32).astype(BF)

    @pl.when(step == 1)
    def _():
        block = places(me)

        def put(n, carry):
            rb, rc = n // 4, n % 4
            for ra, out in enumerate((d0, d1, d2, d3)):
                bx, bzy = block(ra, rb, rc)
                out[rb, rc] = dw_s[bx, pl.ds(pl.multiple_of(bzy * 128, 128), 128), :]
            return carry

        lax.fori_loop(0, 16, put, 0)


def run_main(chunk, meta, me, x, xt, weights, q, q_other, ct, ct_other, sent_a, sent_b):
    def fixed(*shape):
        return pl.BlockSpec(shape, lambda i, m, e: (0,) * len(shape), pipeline_mode=pl.Buffered(1))

    def wide(rows):
        return pl.BlockSpec((rows, HEAD_DIM), lambda i, m, e: (0, i * 4 + e[2] * 2 + chunk))

    def narrow(kind):
        return pl.BlockSpec((WIN, HEAD_DIM), lambda i, m, e: (0, kind * 4 + i * 2 + chunk))

    def weight(kind):
        return pl.BlockSpec((32, 1, 64, HEAD_DIM), lambda i, m, e: (0, kind * 2 + i, 0, e[2] * 2 + chunk))

    def out(rows):
        return pl.BlockSpec((2, rows, HEAD_DIM), lambda i, m, e: (0, 0, i))

    part = pl.BlockSpec((4, 4, 128, HEAD_DIM), lambda i, m, e: (0, 0, 0, 0))
    pair = pltpu.VMEM((PAIR, HEAD_DIM), BF)
    pool = pltpu.VMEM((POOL, HEAD_DIM), BF)
    return pl.pallas_call(
        main_kernel,
        grid_spec=pltpu.PrefetchScalarGridSpec(
            num_scalar_prefetch=2,
            grid=(2,),
            in_specs=[fixed(PAIR, D), fixed(D, PAIR), weight(0), weight(1),
                      wide(TOK), wide(TOK), narrow(0), narrow(0),
                      wide(TOK), wide(TOK), narrow(1), narrow(1)],
            out_specs=[out(TOK), out(TOK), out(WIN), out(WIN), part, part, part, part],
            scratch_shapes=[pair, pair, pair, pair, pool, pool, pool, pool,
                            pltpu.VMEM((4, D, HEAD_DIM), BF)],
        ),
        out_shape=[jax.ShapeDtypeStruct((2, rows, HALF), BF) for rows in (TOK, TOK, WIN, WIN)]
        + [jax.ShapeDtypeStruct((4, 4, 128, HEAD_DIM), BF)] * 4,
        compiler_params=pltpu.CompilerParams(vmem_limit_bytes=52 * MIB),
        cost_estimate=pl.CostEstimate(flops=12_000_000_000, bytes_accessed=24_000_000, transcendentals=500_000),
    )(meta, me, x, xt, weights, weights, q, q_other, sent_a, sent_b, ct, ct_other, sent_a, sent_b)


def add_kernel(*refs):
    ins, outs = refs[:4], refs[-4:]
    total = sum(ref[...].astype(jnp.float32) for ref in ins).astype(BF)
    for n, out in enumerate(outs):
        out[...] = total[n]


def add_parts(parts, after=None):
    extra = [] if after is None else [after]
    shape = parts[0].shape
    rank = len(shape)
    if rank == 4:
        grid = (4,)
        source = pl.BlockSpec((4, 1, 128, HEAD_DIM), lambda i: (0, i, 0, 0))
        target = pl.BlockSpec((1, 128, HEAD_DIM), lambda i: (i, 0, 0))
    else:
        grid = (1,)
        source = pl.BlockSpec(shape, lambda i: (0, 0, 0))
        target = pl.BlockSpec(shape[1:], lambda i: (0, 0))
    return pl.pallas_call(
        add_kernel,
        grid=grid,
        in_specs=[source] * 4 + [pl.BlockSpec(memory_space=pl.ANY)] * len(extra),
        out_specs=[target] * 4,
        out_shape=[jax.ShapeDtypeStruct(shape[1:], BF)] * 4,
        compiler_params=pltpu.CompilerParams(vmem_limit_bytes=16 * MIB),
    )(*parts, *extra)


def depart_kernel(info, q_ref, ct_ref, a_ref, b_ref):
    rows = pl.ds(pl.multiple_of(info[0], 16), WIN)
    core = info[1]
    for n in range(4):
        source = (q_ref, ct_ref)[n // 2]
        for side, out in ((core, a_ref), (1 - core, b_ref)):
            start = pl.multiple_of((n % 2) * 1024 + side * HALF, HALF)
            out[:, n * HALF : (n + 1) * HALF] = source[rows, pl.ds(start, HALF)]


def depart(info, q, ct):
    whole = pl.BlockSpec(memory_space=pltpu.VMEM)
    return pl.pallas_call(
        depart_kernel,
        in_specs=[pl.BlockSpec(memory_space=pltpu.SMEM), whole, whole],
        out_specs=[whole, whole],
        out_shape=[jax.ShapeDtypeStruct((WIN, 2048), BF)] * 2,
        compiler_params=pltpu.CompilerParams(vmem_limit_bytes=16 * MIB),
    )(info, q, ct)


def finish_kernel(info, *refs):
    ins, outs = refs[:8], refs[8:]
    win = pl.multiple_of(info[0], 16)
    core, start, length = info[1], info[2] - info[0], info[3]
    rows = pl.ds(win, WIN)
    place = lax.broadcasted_iota(jnp.int32, (WIN, HEAD_DIM), 0)
    inside = (place >= start) & (place < start + length)
    for chunk in range(2):
        mine, theirs, back_a, back_b = ins[chunk * 4 : chunk * 4 + 4]
        for side, base, back in ((core, mine, back_a), (1 - core, theirs, back_b)):
            cols = pl.ds(pl.multiple_of(side * HALF + chunk * HEAD_DIM, HEAD_DIM), HEAD_DIM)
            for kind, out in enumerate(outs):
                out[:, cols] = base[kind]
                out[rows, cols] = jnp.where(inside, back[kind], out[rows, cols])


def finish(info, pieces):
    def source(rows):
        return pl.BlockSpec((2, rows, HEAD_DIM), lambda i, e: (0, 0, i))

    out = pl.BlockSpec((TOK, 1024), lambda i, e: (0, i))
    return pl.pallas_call(
        finish_kernel,
        grid_spec=pltpu.PrefetchScalarGridSpec(
            num_scalar_prefetch=1,
            grid=(2,),
            in_specs=[source(TOK), source(TOK), source(WIN), source(WIN)] * 2,
            out_specs=[out, out],
        ),
        out_shape=[jax.ShapeDtypeStruct((TOK, 2048), BF)] * 2,
        compiler_params=pltpu.CompilerParams(vmem_limit_bytes=32 * MIB),
    )(info, *pieces)


def swap(value):
    return lax.ppermute(value, "c", [(0, 1), (1, 0)])


SEND_A = [(2 * t, 2 * t - 2) for t in range(1, 16)] + [(2 * t + 1, 2 * t + 3) for t in range(15)]
SEND_B = [(2 * t, 2 * t - 1) for t in range(1, 16)] + [(2 * t + 1, 2 * t + 2) for t in range(15)]


def back(pairs):
    return [(b, a) for a, b in pairs]


def shift(phase, amount):
    pairs = []
    for z in range(4):
        for y in range(4):
            for c in range(2):
                for x in range(4):
                    to = {"z": z, "y": y, "x": x}
                    axis = ("xyz", "zxy")[c][phase]
                    to[axis] = (to[axis] + amount) % 4
                    pairs.append((((z * 4 + y) * 2 + c) * 4 + x, ((to["z"] * 4 + to["y"]) * 2 + c) * 4 + to["x"]))
    return pairs


def exchange(parts, phase):
    return [parts[0]] + [lax.ppermute(parts[r], ALL, shift(phase, r)) for r in (1, 3, 2)]


def plan(enc_lengths, dec_lengths, dec_partner, t, c, x):
    device = (t * 2 + c) * 4 + x
    cores = jnp.stack([c, 1 - c])
    devices = (t * 2 + cores) * 4 + x
    ids = (devices[:, None] * SEGS + jnp.arange(SEGS, dtype=jnp.int32)).reshape(-1)
    dec_starts = (jnp.cumsum(dec_lengths, axis=1) - dec_lengths).reshape(-1)
    enc_starts = (jnp.cumsum(enc_lengths, axis=1) - enc_lengths).reshape(-1)
    flat_dec = dec_lengths.reshape(-1)
    flat_partner = dec_partner.reshape(-1)
    entries = jnp.arange(enc_starts.shape[0], dtype=jnp.int32)
    own = entries[None, :] == ids[:, None]
    hit = flat_partner[None, :] == ids[:, None]

    def pick(mask, table):
        return jnp.sum(jnp.where(mask, table[None, :], 0), axis=1)

    enc_len = pick(own, enc_lengths.reshape(-1))
    enc_start = pick(own, enc_starts) + jnp.repeat(jnp.arange(2, dtype=jnp.int32) * TOK, SEGS)
    dec_len = pick(hit, flat_dec)
    dec_start = pick(hit, dec_starts)
    owner = pick(hit, entries) // (SEGS * 4)
    same = owner % 2 == c
    dec_at = jnp.where(
        owner // 2 == t,
        dec_start + jnp.where(same, 0, TOK),
        dec_start - align(dec_start, TOK) + PAIR + jnp.where(same, 0, WIN),
    )
    meta = jnp.stack([enc_start, enc_len, dec_at, dec_len], axis=1).astype(jnp.int32)

    goes = (entries // SEGS == device) & (flat_partner // (SEGS * 4) == t * 2 + c + jnp.where(c == 0, -1, 1))
    length = jnp.sum(jnp.where(goes, flat_dec, 0))
    start = jnp.sum(jnp.where(goes, dec_starts, 0))
    info = jnp.stack([align(start, TOK), c, start, length]).astype(jnp.int32)
    return meta, info


def body(enc_hidden, kv_weights, queries, cotangent, enc_lengths, dec_lengths, dec_partner):
    z, y, c, x = (lax.axis_index(a) for a in ALL)
    me = jnp.stack([z, y, c, x]).astype(jnp.int32)
    weights = lax.all_gather(kv_weights, ALL, axis=0).reshape(32, 4, 64, 1024)
    meta, info = plan(enc_lengths, dec_lengths, dec_partner, z * 4 + y, c, x)
    leave_a, leave_b = depart(info, queries, cotangent)
    sent_a = lax.ppermute(leave_a, DP, SEND_A)
    sent_b = lax.ppermute(leave_b, DP, SEND_B)
    tokens = jnp.concatenate([enc_hidden, swap(enc_hidden)], axis=0)
    tokens_t = tokens.T
    q_other, ct_other = swap(queries), swap(cotangent)

    pieces, grads = [], []
    for chunk in range(2):
        mine, other, far_a, far_b, *parts = run_main(
            chunk, meta, me, tokens, tokens_t, weights, queries, q_other, cotangent, ct_other, sent_a, sent_b
        )
        grads.append(exchange(parts, 0))
        pieces += [mine, swap(other), lax.ppermute(far_a, DP, back(SEND_A)), lax.ppermute(far_b, DP, back(SEND_B))]

    last = []
    for chunk, parts in enumerate(grads):
        after = grads[1][0] if chunk == 0 else None
        second = exchange(add_parts(parts, after), 1)
        last.append(exchange(add_parts(second), 2))
    summed = jnp.concatenate(
        [sum(part.astype(jnp.float32) for part in parts) for parts in last], axis=1
    )
    low, high = summed[:64], summed[64:]
    got = swap(jnp.where(c == 0, high, low))
    kept = jnp.where(c == 0, low, high)
    grad = jnp.concatenate([jnp.where(c == 0, kept, got), jnp.where(c == 0, got, kept)], axis=1)
    context, grad_queries = finish(info, pieces)
    return context, grad_queries, grad


def solution(mesh):
    fine = Mesh(mesh.devices.reshape(4, 4, 2, 4), ALL)
    rows = P(ALL, None)
    cut = P(DP, "x")
    return jax.shard_map(
        body,
        mesh=fine,
        in_specs=(rows, cut, rows, rows, P(), P(), P()),
        out_specs=(rows, rows, cut),
        check_vma=False,
    )
```

time: 375 us -> 244 us (0.65)
  the two profiles are of different devices: /device:TPU:77 before, /device:TPU:1 now
where the time goes in v2:
time: 244 us; the launch traced here: 241 us
  waiting for transfers between devices  68.9 us (28%)
  Pallas kernels  60.2 us (25%)
  starting transfers between devices  52.4 us (21%)
  local copies, waits for them, and re-layouts  29.2 us (12%)
  between operations  16.9 us (7%)
  other arithmetic  13.4 us (5%)
    pallas_call x2, Pallas kernels, run_main(): pl.pallas_call(main_kernel, grid_spec=pltpu.PrefetchScalarGridSpec(num_sc...  53.2 us
    all_gather x1, waiting for transfers between devices, body(): weights = lax.all_gather(kv_weights, ALL, axis=0).reshape(32, 4, 64, 1024)  34.2 us
    ppermute x18, waiting for transfers between devices, exchange(): lax.ppermute(parts[r], ALL, shift(phase, r))  29.2 us
    ppermute x18, starting transfers between devices, exchange(): lax.ppermute(parts[r], ALL, shift(phase, r))  21.7 us
    ppermute x6, starting transfers between devices, swap(): return lax.ppermute(value, 'c', [(0, 1), (1, 0)])  14.6 us
    ppermute x2, starting transfers between devices, body(): lax.ppermute(far_b, DP, back(SEND_B))  8.02 us
    unnamed x26, local copies, waits for them, and re-layouts  7.9 us
    concatenate x1, local copies, waits for them, and re-layouts, body(): tokens = jnp.concatenate([enc_hidden, swap(enc_hidden)], axis=0)  6.61 us
  transfers between devices with their start and end apart: 31, of which 8 were waited for; matrix products, arithmetic and copies ran while one was open for 17% of the time, Pallas kernels for 14%

profile of v2, /device:TPU:1, one launch (start us, length us, event | category | flops | bytes accessed | tf_op | source)
XLA Modules:
  0.0 241.0 jit_solution(8023292134093763423)
XLA Ops:
  7.9 4.1 %copy.71 = bf16[512,2048]{0,1:T(8,128)(2,1)} copy(bf16[512,2048]{1,0:T(8,128)(2,1)} %param.7) | data formatting | bytes 4194304 | tf_op args[0]
  12.0 1.4 collective-permute-start
  19.2 1.6 copy-done.1
  20.8 1.5 shard_map.94
  22.3 3.3 %collective-permute-start.2 = (bf16[176,2048]{1,0:T(8,128)(2,1)}, bf16[176,2048]{1,0:T(8,128)(2,1)S(1)}, u32[]{:S(2)}, u32[]{:S(2)}) collective-permute-start(bf16[176,2048]{1,0:T(8,128)(2,1)} %get-tuple-element.39), channel_id=1, source_target_pairs={{8,0},{16,8},{24,16},{32,24},{40,32},{48,40},{56,48},{64,56},{72,6... | collective-permute-start | bytes 2162696 | tf_op jit(solution)/shard_map/ppermute | solution.py:308
  25.6 2.1 collective-permute-start.3
  36.2 1.5 eq.87
  37.8 1.5 broadcast_in_dim.66
  39.3 1.5 broadcast_in_dim.72
  40.8 1.5 fusion.1
  49.2 5.4 %fusion.27 = (bf16[2048,1024]{1,0:T(8,128)(2,1)}, bf16[1024,2048]{0,1:T(8,128)(2,1)}) fusion(bf16[512,2048]{0,1:T(8,128)(2,1)} %collective-permute-done, bf16[512,2048]{0,1:T(8,128)(2,1)} %copy.71), kind=kLoop, calls=%fused_computation.80 | loop fusion | flops 8388608 | bytes 12582912 | tf_op jit(solution)/shard_map/transpose | solution.py:311
  54.6 6.6 %copy.72.x_ref = bf16[1024,2048]{1,0:T(8,128)(2,1)} copy(bf16[1024,2048]{0,1:T(8,128)(2,1)} %get-tuple-element.84) | data formatting | bytes 8388608 | tf_op jit(solution)/shard_map/concatenate | solution.py:310
  61.2 34.2 %all-gather.3.cloned.1.call-done = bf16[8192,1024]{1,0:T(8,128)(2,1)} async-done(((bf16[64,1024]{1,0:T(8,128)(2,1)}), bf16[8192,1024]{1,0:T(8,128)(2,1)}) %all-gather.3.cloned.1.call-update) | async-done | bytes 16777232 | tf_op jit(solution)/shard_map/all_gather | solution.py:305
  95.4 26.6 %shard_map.96 = (bf16[2,512,512]{2,1,0:T(8,128)(2,1)}, bf16[2,512,512]{2,1,0:T(8,128)(2,1)}, bf16[2,176,512]{2,1,0:T(8,128)(2,1)S(1)}, bf16[2,176,512]{2,1,0:T(8...) custom-call(s32[8,4]{1,0:T(8,128)S(1)} %pad_add_fusion.meta, ...), custom_call_target="tpu_custom_call" | custom-call | flops 12000000000 | bytes 24000000 | tf_op jit(solution)/shard_map/pallas_call | solution.py:134
  122.9 1.8 collective-permute-start.21
  126.0 26.7 %shard_map.95 = (bf16[2,512,512]{2,1,0:T(8,128)(2,1)}, bf16[2,512,512]{2,1,0:T(8,128)(2,1)}, bf16[2,176,512]{2,1,0:T(8,128)(2,1)S(1)}, bf16[2,176,512]{2,1,0:T(8...) custom-call(s32[8,4]{1,0:T(8,128)S(1)} %pad_add_fusion.meta, ...), custom_call_target="tpu_custom_call" | custom-call | flops 12000000000 | bytes 24000000 | tf_op jit(solution)/shard_map/pallas_call | solution.py:134
  153.1 2.3 collective-permute-start.12
  158.2 1.5 collective-permute-start.24
  159.6 19.7 %collective-permute-done.11.refs_1_ = bf16[4,4,128,256]{3,2,1,0:T(8,128)(2,1)S(1)} collective-permute-done((bf16[4,4,128,256]{3,2,1,0:T(8,128)(2,1)}, bf16[4,4,128,256]{3,2,1,0:T(8,128)(2,1)S(1)}, u32[]{:S(2)}, u32[]{:S(2)}) %collective-permute-start.11) | collective-permute-done | bytes 1048608 | tf_op jit(solution)/shard_map/ppermute | solution.py:263
  179.3 1.9 collective-permute-start.25
  184.1 2.1 collective-permute-start.15
  186.3 10.6 %collective-permute-start.8 = (bf16[2,512,512]{2,1,0:T(8,128)(2,1)S(1)}, bf16[2,512,512]{2,1,0:T(8,128)(2,1)S(1)}, u32[]{:S(2)}, u32[]{:S(2)}) collective-permute-start(bf16[2,512,512]{2,1,0:T(8,128)(2,1)S(1)} %copy-done.9), channel_id=1, source_target_pairs={{0,4},{4,0},{1,5},{5,1},{2,6},{6,2},{3,7},{7,3},{8,12},{12,8},{9,1... | collective-permute-start | bytes 3145736 | tf_op jit(solution)/shard_map/ppermute | solution.py:238
  197.0 1.8 collective-permute-start.16
  199.0 5.2 %collective-permute-done.16.refs_3_ = bf16[4,128,256]{2,1,0:T(8,128)(2,1)S(1)} collective-permute-done((bf16[4,128,256]{2,1,0:T(8,128)(2,1)S(1)}, bf16[4,128,256]{2,1,0:T(8,128)(2,1)S(1)}, u32[]{:S(2)}, u32[]{:S(2)}) %collective-permute-start.16) | collective-permute-done | bytes 262176 | tf_op jit(solution)/shard_map/ppermute | solution.py:263
  204.2 1.6 collective-permute-start.27
  207.3 6.1 %collective-permute-start.10 = (bf16[2,176,512]{2,1,0:T(8,128)(2,1)S(1)}, bf16[2,176,512]{2,1,0:T(8,128)(2,1)S(1)}, u32[]{:S(2)}, u32[]{:S(2)}) collective-permute-start(bf16[2,176,512]{2,1,0:T(8,128)(2,1)S(1)} %get-tuple-element.48), channel_id=1, source_target_pairs={{4,8},{12,16},{20,24},{28,32},{36,40},{44,48},{52,56},{60,64},{68,... | collective-permute-start | bytes 1081352 | tf_op jit(solution)/shard_map/ppermute | solution.py:320
  213.4 2.9 %collective-permute-start.18 = (bf16[128,256]{1,0:T(8,128)(2,1)S(1)}, bf16[128,256]{1,0:T(8,128)(2,1)S(1)}, u32[]{:S(2)}, u32[]{:S(2)}) collective-permute-start(bf16[128,256]{1,0:T(8,128)(2,1)S(1)} %get-tuple-element.62), channel_id=1, source_target_pairs={{0,96},{1,97},{2,98},{3,99},{4,28},{5,29},{6,30},{7,31},{8,104},{9... | collective-permute-start | bytes 196616 | tf_op jit(solution)/shard_map/ppermute | solution.py:263
  219.0 2.3 collective-permute-done.19
  221.3 1.9 collective-permute-start.7
  223.3 2.0 collective-permute-start.29
  225.9 4.2 %collective-permute-done.7.refs_3_ = bf16[2,176,512]{2,1,0:T(8,128)(2,1)S(1)} collective-permute-done((bf16[2,176,512]{2,1,0:T(8,128)(2,1)S(1)}, bf16[2,176,512]{2,1,0:T(8,128)(2,1)S(1)}, u32[]{:S(2)}, u32[]{:S(2)}) %collective-permute-start.7) | collective-permute-done | bytes 360480 | tf_op jit(solution)/shard_map/ppermute | solution.py:320
  230.1 3.4 %shard_map.97 = (bf16[512,2048]{1,0:T(8,128)(2,1)}, bf16[512,2048]{1,0:T(8,128)(2,1)}) custom-call(s32[4]{0:T(128)S(1)} %pad_add_fusion.1.info, bf16[2,512,512]{2,1,0:T(8,128)(2,1)S(1)} %copy-done.5, bf16[2,512,512]{2,1,0:T(8,128)(2,1)S(1)} %collective-permute-done.5.refs_1_, bf16[2,176,512]{2,1,0:T(8,128)(2,1)S(1)} %collective-permute-done.6.refs_2_, ...), custom_call_target="tpu_custom_call" | custom-call | tf_op jit(solution)/shard_map/pallas_call | solution.py:224
  (100 shorter events, 33.2 us)
Async XLA Ops:
  7.2 88.3 %all-gather.3.cloned.1.call-start = ((), (), s32[]{:S(2)}) async-start(), calls=%async_computation | async-start | bytes 16908288 | tf_op jit(solution)/shard_map/all_gather | solution.py:305
  12.0 37.2 %collective-permute-start = (bf16[512,2048]{0,1:T(8,128)(2,1)}, bf16[512,2048]{0,1:T(8,128)(2,1)}, u32[]{:S(2)}, u32[]{:S(2)}) collective-permute-start(bf16[512,2048]{0,1:T(8,128)(2,1)} %copy.71), channel_id=1, source_target_pairs={{0,4},{4,0},{1,5},{5,1},{2,6},{6,2},{3,7},{7,3},{8,12},{12,8},{9,1... | collective-permute-start | bytes 6291464 | tf_op jit(solution)/shard_map/ppermute | solution.py:238
  13.4 47.8 %collective-permute-start.1 = (bf16[512,2048]{1,0:T(8,128)(2,1)S(1)}, bf16[512,2048]{1,0:T(8,128)(2,1)}, u32[]{:S(2)}, u32[]{:S(2)}) collective-permute-start(bf16[512,2048]{1,0:T(8,128)(2,1)S(1)} %copy-done), channel_id=1, source_target_pairs={{0,4},{4,0},{1,5},{5,1},{2,6},{6,2},{3,7},{7,3},{8,12},{12,8},{9,1... | collective-permute-start | bytes 6291464 | tf_op jit(solution)/shard_map/ppermute | solution.py:238
  13.4 47.8 %collective-permute-start.4 = (bf16[512,2048]{1,0:T(8,128)(2,1)}, bf16[512,2048]{1,0:T(8,128)(2,1)}, u32[]{:S(2)}, u32[]{:S(2)}) collective-permute-start(bf16[512,2048]{1,0:T(8,128)(2,1)} %cm.3), channel_id=1, source_target_pairs={{0,4},{4,0},{1,5},{5,1},{2,6},{6,2},{3,7},{7,3},{8,12},{12,8},{9,1... | collective-permute-start | bytes 6291464 | tf_op jit(solution)/shard_map/ppermute | solution.py:238
  22.3 38.9 %collective-permute-start.2 = (bf16[176,2048]{1,0:T(8,128)(2,1)}, bf16[176,2048]{1,0:T(8,128)(2,1)S(1)}, u32[]{:S(2)}, u32[]{:S(2)}) collective-permute-start(bf16[176,2048]{1,0:T(8,128)(2,1)} %get-tuple-element.39), channel_id=1, source_target_pairs={{8,0},{16,8},{24,16},{32,24},{40,32},{48,40},{56,48},{64,56},{72,6... | collective-permute-start | bytes 2162696 | tf_op jit(solution)/shard_map/ppermute | solution.py:308
  25.6 35.6 %collective-permute-start.3 = (bf16[176,2048]{1,0:T(8,128)(2,1)S(1)}, bf16[176,2048]{1,0:T(8,128)(2,1)}, u32[]{:S(2)}, u32[]{:S(2)}) collective-permute-start(bf16[176,2048]{1,0:T(8,128)(2,1)S(1)} %get-tuple-element.40), channel_id=1, source_target_pairs={{8,4},{16,12},{24,20},{32,28},{40,36},{48,44},{56,52},{64,60},{72,... | collective-permute-start | bytes 2162696 | tf_op jit(solution)/shard_map/ppermute | solution.py:309
  122.0 33.4 %collective-permute-start.20 = (bf16[4,4,128,256]{3,2,1,0:T(8,128)(2,1)}, bf16[4,4,128,256]{3,2,1,0:T(8,128)(2,1)S(1)}, u32[]{:S(2)}, u32[]{:S(2)}) collective-permute-start(bf16[4,4,128,256]{3,2,1,0:T(8,128)(2,1)} %get-tuple-element.64), channel_id=1, source_target_pairs={{0,1},{1,2},{2,3},{3,0},{4,36},{5,37},{6,38},{7,39},{8,9},{9,10},{... | collective-permute-start | bytes 3145736 | tf_op jit(solution)/shard_map/ppermute | solution.py:263
  122.9 33.0 %collective-permute-start.21 = (bf16[4,4,128,256]{3,2,1,0:T(8,128)(2,1)}, bf16[4,4,128,256]{3,2,1,0:T(8,128)(2,1)S(1)}, u32[]{:S(2)}, u32[]{:S(2)}) collective-permute-start(bf16[4,4,128,256]{3,2,1,0:T(8,128)(2,1)} %get-tuple-element.65), channel_id=1, source_target_pairs={{0,3},{1,0},{2,1},{3,2},{4,100},{5,101},{6,102},{7,103},{8,11},{9,... | collective-permute-start | bytes 3145736 | tf_op jit(solution)/shard_map/ppermute | solution.py:263
  124.8 31.2 %collective-permute-start.22 = (bf16[4,4,128,256]{3,2,1,0:T(8,128)(2,1)}, bf16[4,4,128,256]{3,2,1,0:T(8,128)(2,1)S(1)}, u32[]{:S(2)}, u32[]{:S(2)}) collective-permute-start(bf16[4,4,128,256]{3,2,1,0:T(8,128)(2,1)} %get-tuple-element.66), channel_id=1, source_target_pairs={{0,2},{1,3},{2,0},{3,1},{4,68},{5,69},{6,70},{7,71},{8,10},{9,11},... | collective-permute-start | bytes 3145736 | tf_op jit(solution)/shard_map/ppermute | solution.py:263
  152.6 26.7 %collective-permute-start.11 = (bf16[4,4,128,256]{3,2,1,0:T(8,128)(2,1)}, bf16[4,4,128,256]{3,2,1,0:T(8,128)(2,1)S(1)}, u32[]{:S(2)}, u32[]{:S(2)}) collective-permute-start(bf16[4,4,128,256]{3,2,1,0:T(8,128)(2,1)} %get-tuple-element.52), channel_id=1, source_target_pairs={{0,1},{1,2},{2,3},{3,0},{4,36},{5,37},{6,38},{7,39},{8,9},{9,10},{... | collective-permute-start | bytes 3145736 | tf_op jit(solution)/shard_map/ppermute | solution.py:263
  153.1 28.1 %collective-permute-start.12 = (bf16[4,4,128,256]{3,2,1,0:T(8,128)(2,1)}, bf16[4,4,128,256]{3,2,1,0:T(8,128)(2,1)S(1)}, u32[]{:S(2)}, u32[]{:S(2)}) collective-permute-start(bf16[4,4,128,256]{3,2,1,0:T(8,128)(2,1)} %get-tuple-element.53), channel_id=1, source_target_pairs={{0,3},{1,0},{2,1},{3,2},{4,100},{5,101},{6,102},{7,103},{8,11},{9,... | collective-permute-start | bytes 3145736 | tf_op jit(solution)/shard_map/ppermute | solution.py:263
  155.4 25.8 %collective-permute-start.13 = (bf16[4,4,128,256]{3,2,1,0:T(8,128)(2,1)}, bf16[4,4,128,256]{3,2,1,0:T(8,128)(2,1)S(1)}, u32[]{:S(2)}, u32[]{:S(2)}) collective-permute-start(bf16[4,4,128,256]{3,2,1,0:T(8,128)(2,1)} %get-tuple-element.54), channel_id=1, source_target_pairs={{0,2},{1,3},{2,0},{3,1},{4,68},{5,69},{6,70},{7,71},{8,10},{9,11},... | collective-permute-start | bytes 3145736 | tf_op jit(solution)/shard_map/ppermute | solution.py:263
  156.9 27.2 %collective-permute-start.23 = (bf16[4,128,256]{2,1,0:T(8,128)(2,1)S(1)}, bf16[4,128,256]{2,1,0:T(8,128)(2,1)S(1)}, u32[]{:S(2)}, u32[]{:S(2)}) collective-permute-start(bf16[4,128,256]{2,1,0:T(8,128)(2,1)S(1)} %get-tuple-element.68), channel_id=1, source_target_pairs={{0,8},{1,9},{2,10},{3,11},{4,5},{5,6},{6,7},{7,4},{8,16},{9,17},{1... | collective-permute-start | bytes 786440 | tf_op jit(solution)/shard_map/ppermute | solution.py:263
  158.2 28.1 %collective-permute-start.24 = (bf16[4,128,256]{2,1,0:T(8,128)(2,1)S(1)}, bf16[4,128,256]{2,1,0:T(8,128)(2,1)S(1)}, u32[]{:S(2)}, u32[]{:S(2)}) collective-permute-start(bf16[4,128,256]{2,1,0:T(8,128)(2,1)S(1)} %get-tuple-element.69), channel_id=1, source_target_pairs={{0,24},{1,25},{2,26},{3,27},{4,7},{5,4},{6,5},{7,6},{8,0},{9,1},{1... | collective-permute-start | bytes 786440 | tf_op jit(solution)/shard_map/ppermute | solution.py:263
  179.3 17.5 %collective-permute-start.25 = (bf16[4,128,256]{2,1,0:T(8,128)(2,1)S(1)}, bf16[4,128,256]{2,1,0:T(8,128)(2,1)S(1)}, u32[]{:S(2)}, u32[]{:S(2)}) collective-permute-start(bf16[4,128,256]{2,1,0:T(8,128)(2,1)S(1)} %get-tuple-element.70), channel_id=1, source_target_pairs={{0,16},{1,17},{2,18},{3,19},{4,6},{5,7},{6,4},{7,5},{8,24},{9,25},... | collective-permute-start | bytes 786440 | tf_op jit(solution)/shard_map/ppermute | solution.py:263
  182.1 47.9 %copy-start.4 = (bf16[2,512,512]{2,1,0:T(8,128)(2,1)S(1)}, bf16[2,512,512]{2,1,0:T(8,128)(2,1)}, u32[]{:S(2)}) copy-start(bf16[2,512,512]{2,1,0:T(8,128)(2,1)} %get-tuple-element.45.refs_4_) | copy-start | bytes 3145732
  182.2 14.8 %collective-permute-start.14 = (bf16[4,128,256]{2,1,0:T(8,128)(2,1)S(1)}, bf16[4,128,256]{2,1,0:T(8,128)(2,1)S(1)}, u32[]{:S(2)}, u32[]{:S(2)}) collective-permute-start(bf16[4,128,256]{2,1,0:T(8,128)(2,1)S(1)} %get-tuple-element.57), channel_id=1, source_target_pairs={{0,8},{1,9},{2,10},{3,11},{4,5},{5,6},{6,7},{7,4},{8,16},{9,17},{1... | collective-permute-start | bytes 786440 | tf_op jit(solution)/shard_map/ppermute | solution.py:263
  182.7 23.2 %collective-permute-start.9 = (bf16[2,176,512]{2,1,0:T(8,128)(2,1)S(1)}, bf16[2,176,512]{2,1,0:T(8,128)(2,1)S(1)}, u32[]{:S(2)}, u32[]{:S(2)}) collective-permute-start(bf16[2,176,512]{2,1,0:T(8,128)(2,1)S(1)} %get-tuple-element.47), channel_id=1, source_target_pairs={{0,8},{8,16},{16,24},{24,32},{32,40},{40,48},{48,56},{56,64},{64,7... | collective-permute-start | bytes 1081352 | tf_op jit(solution)/shard_map/ppermute | solution.py:320
  184.1 14.8 %collective-permute-start.15 = (bf16[4,128,256]{2,1,0:T(8,128)(2,1)S(1)}, bf16[4,128,256]{2,1,0:T(8,128)(2,1)S(1)}, u32[]{:S(2)}, u32[]{:S(2)}) collective-permute-start(bf16[4,128,256]{2,1,0:T(8,128)(2,1)S(1)} %get-tuple-element.58), channel_id=1, source_target_pairs={{0,24},{1,25},{2,26},{3,27},{4,7},{5,4},{6,5},{7,6},{8,0},{9,1},{1... | collective-permute-start | bytes 786440 | tf_op jit(solution)/shard_map/ppermute | solution.py:263
  186.3 43.8 %collective-permute-start.8 = (bf16[2,512,512]{2,1,0:T(8,128)(2,1)S(1)}, bf16[2,512,512]{2,1,0:T(8,128)(2,1)S(1)}, u32[]{:S(2)}, u32[]{:S(2)}) collective-permute-start(bf16[2,512,512]{2,1,0:T(8,128)(2,1)S(1)} %copy-done.9), channel_id=1, source_target_pairs={{0,4},{4,0},{1,5},{5,1},{2,6},{6,2},{3,7},{7,3},{8,12},{12,8},{9,1... | collective-permute-start | bytes 3145736 | tf_op jit(solution)/shard_map/ppermute | solution.py:238
  196.9 33.2 %collective-permute-start.5 = (bf16[2,512,512]{2,1,0:T(8,128)(2,1)S(1)}, bf16[2,512,512]{2,1,0:T(8,128)(2,1)S(1)}, u32[]{:S(2)}, u32[]{:S(2)}) collective-permute-start(bf16[2,512,512]{2,1,0:T(8,128)(2,1)S(1)} %copy-done.10), channel_id=1, source_target_pairs={{0,4},{4,0},{1,5},{5,1},{2,6},{6,2},{3,7},{7,3},{8,12},{12,8},{9,1... | collective-permute-start | bytes 3145736 | tf_op jit(solution)/shard_map/ppermute | solution.py:238
  197.0 7.2 %collective-permute-start.16 = (bf16[4,128,256]{2,1,0:T(8,128)(2,1)S(1)}, bf16[4,128,256]{2,1,0:T(8,128)(2,1)S(1)}, u32[]{:S(2)}, u32[]{:S(2)}) collective-permute-start(bf16[4,128,256]{2,1,0:T(8,128)(2,1)S(1)} %get-tuple-element.59), channel_id=1, source_target_pairs={{0,16},{1,17},{2,18},{3,19},{4,6},{5,7},{6,4},{7,5},{8,24},{9,25},... | collective-permute-start | bytes 786440 | tf_op jit(solution)/shard_map/ppermute | solution.py:263
  198.9 7.2 %collective-permute-start.26 = (bf16[128,256]{1,0:T(8,128)(2,1)S(1)}, bf16[128,256]{1,0:T(8,128)(2,1)S(1)}, u32[]{:S(2)}, u32[]{:S(2)}) collective-permute-start(bf16[128,256]{1,0:T(8,128)(2,1)S(1)} %get-tuple-element.72), channel_id=1, source_target_pairs={{0,32},{1,33},{2,34},{3,35},{4,12},{5,13},{6,14},{7,15},{8,40},{9,... | collective-permute-start | bytes 196616 | tf_op jit(solution)/shard_map/ppermute | solution.py:263
  204.2 3.1 %collective-permute-start.27 = (bf16[128,256]{1,0:T(8,128)(2,1)S(1)}, bf16[128,256]{1,0:T(8,128)(2,1)S(1)}, u32[]{:S(2)}, u32[]{:S(2)}) collective-permute-start(bf16[128,256]{1,0:T(8,128)(2,1)S(1)} %get-tuple-element.73), channel_id=1, source_target_pairs={{0,96},{1,97},{2,98},{3,99},{4,28},{5,29},{6,30},{7,31},{8,104},{9... | collective-permute-start | bytes 196616 | tf_op jit(solution)/shard_map/ppermute | solution.py:263
  206.0 7.5 %collective-permute-start.28 = (bf16[128,256]{1,0:T(8,128)(2,1)S(1)}, bf16[128,256]{1,0:T(8,128)(2,1)S(1)}, u32[]{:S(2)}, u32[]{:S(2)}) collective-permute-start(bf16[128,256]{1,0:T(8,128)(2,1)S(1)} %get-tuple-element.74), channel_id=1, source_target_pairs={{0,64},{1,65},{2,66},{3,67},{4,20},{5,21},{6,22},{7,23},{8,72},{9,... | collective-permute-start | bytes 196616 | tf_op jit(solution)/shard_map/ppermute | solution.py:263
  206.1 10.3 %collective-permute-start.17 = (bf16[128,256]{1,0:T(8,128)(2,1)S(1)}, bf16[128,256]{1,0:T(8,128)(2,1)S(1)}, u32[]{:S(2)}, u32[]{:S(2)}) collective-permute-start(bf16[128,256]{1,0:T(8,128)(2,1)S(1)} %get-tuple-element.61), channel_id=1, source_target_pairs={{0,32},{1,33},{2,34},{3,35},{4,12},{5,13},{6,14},{7,15},{8,40},{9,... | collective-permute-start | bytes 196616 | tf_op jit(solution)/shard_map/ppermute | solution.py:263
  207.3 16.0 %collective-permute-start.10 = (bf16[2,176,512]{2,1,0:T(8,128)(2,1)S(1)}, bf16[2,176,512]{2,1,0:T(8,128)(2,1)S(1)}, u32[]{:S(2)}, u32[]{:S(2)}) collective-permute-start(bf16[2,176,512]{2,1,0:T(8,128)(2,1)S(1)} %get-tuple-element.48), channel_id=1, source_target_pairs={{4,8},{12,16},{20,24},{28,32},{36,40},{44,48},{52,56},{60,64},{68,... | collective-permute-start | bytes 1081352 | tf_op jit(solution)/shard_map/ppermute | solution.py:320
  213.4 4.3 %collective-permute-start.18 = (bf16[128,256]{1,0:T(8,128)(2,1)S(1)}, bf16[128,256]{1,0:T(8,128)(2,1)S(1)}, u32[]{:S(2)}, u32[]{:S(2)}) collective-permute-start(bf16[128,256]{1,0:T(8,128)(2,1)S(1)} %get-tuple-element.62), channel_id=1, source_target_pairs={{0,96},{1,97},{2,98},{3,99},{4,28},{5,29},{6,30},{7,31},{8,104},{9... | collective-permute-start | bytes 196616 | tf_op jit(solution)/shard_map/ppermute | solution.py:263
  216.4 4.9 %collective-permute-start.19 = (bf16[128,256]{1,0:T(8,128)(2,1)S(1)}, bf16[128,256]{1,0:T(8,128)(2,1)S(1)}, u32[]{:S(2)}, u32[]{:S(2)}) collective-permute-start(bf16[128,256]{1,0:T(8,128)(2,1)S(1)} %get-tuple-element.63), channel_id=1, source_target_pairs={{0,64},{1,65},{2,66},{3,67},{4,20},{5,21},{6,22},{7,23},{8,72},{9,... | collective-permute-start | bytes 196616 | tf_op jit(solution)/shard_map/ppermute | solution.py:263
  217.7 8.2 %collective-permute-start.6 = (bf16[2,176,512]{2,1,0:T(8,128)(2,1)S(1)}, bf16[2,176,512]{2,1,0:T(8,128)(2,1)S(1)}, u32[]{:S(2)}, u32[]{:S(2)}) collective-permute-start(bf16[2,176,512]{2,1,0:T(8,128)(2,1)S(1)} %get-tuple-element.43), channel_id=1, source_target_pairs={{0,8},{8,16},{16,24},{24,32},{32,40},{40,48},{48,56},{56,64},{64,7... | collective-permute-start | bytes 1081352 | tf_op jit(solution)/shard_map/ppermute | solution.py:320
  221.3 8.7 %collective-permute-start.7 = (bf16[2,176,512]{2,1,0:T(8,128)(2,1)S(1)}, bf16[2,176,512]{2,1,0:T(8,128)(2,1)S(1)}, u32[]{:S(2)}, u32[]{:S(2)}) collective-permute-start(bf16[2,176,512]{2,1,0:T(8,128)(2,1)S(1)} %get-tuple-element.44), channel_id=1, source_target_pairs={{4,8},{12,16},{20,24},{28,32},{36,40},{44,48},{52,56},{60,64},{68,... | collective-permute-start | bytes 1081352 | tf_op jit(solution)/shard_map/ppermute | solution.py:320
  223.3 10.2 %collective-permute-start.29 = (f32[64,512]{1,0:T(8,128)S(1)}, f32[64,512]{1,0:T(8,128)S(1)}, u32[]{:S(2)}, u32[]{:S(2)}) collective-permute-start(f32[64,512]{1,0:T(8,128)S(1)} %broadcast_select_fusion.2), channel_id=1, source_target_pairs={{0,4},{4,0},{1,5},{5,1},{2,6},{6,2},{3,7},{7,3},{8,12},{12,8},{9,1... | collective-permute-start | bytes 393224 | tf_op jit(solution)/shard_map/ppermute | solution.py:238
  (10 other events, 152.0 us)
Sparse Core Ops, SparseCore 0:
  11.2 84.2 all-gather.2

commit v3 on v2

--- a/solution.py
+++ b/solution.py
@@ -13,6 +13,7 @@
 POOL = PAIR + 2 * WIN
 D = 2048
 HALF = 512
+GROUP = 4
 DP = ("z", "y", "c")
 ALL = ("z", "y", "c", "x")
 MIB = 1024 * 1024
@@ -32,35 +33,42 @@
     col = lax.broadcasted_iota(jnp.int32, (WIN, WIN), 1)
     row = lax.broadcasted_iota(jnp.int32, (WIN, WIN), 0)
     row_wide = lax.broadcasted_iota(jnp.int32, (WIN, HEAD_DIM), 0)
-    for e in range(2 * SEGS):
-        es, el, ds, dl = meta[e, 0], meta[e, 1], meta[e, 2], meta[e, 3]
-        ew = pl.multiple_of(align(es, PAIR), 16)
-        dw = pl.multiple_of(align(ds, POOL), 16)
-        elo, dlo = es - ew, ds - dw
-        ewin, dwin = pl.ds(ew, WIN), pl.ds(dw, WIN)
-        k, v = k_s[ewin, :], v_s[ewin, :]
-        q, ct = q_s[dwin, :], ct_s[dwin, :]
-        s = mm(q, k, ((1,), (1,))) * scale
-        gw = mm(ct, v, ((1,), (1,)))
-        k_live = (col >= elo) & (col < elo + el)
-        live = k_live & (row >= dlo) & (row < dlo + dl)
-        top = jnp.max(jnp.where(k_live, s, -jnp.inf), axis=1, keepdims=True)
-        p = jnp.where(k_live, jnp.exp(s - top), 0.0)
-        total = jnp.sum(p, axis=1, keepdims=True)
-        w = jnp.where(live, p * (1.0 / total), 0.0)
-        w_low = w.astype(BF)
-        delta = jnp.sum(w * gw, axis=1, keepdims=True)
-        gs = (w * (gw - delta) * scale).astype(BF)
-        ctx = mm(w_low, v, ((1,), (0,))).astype(BF)
-        gq = mm(gs, k, ((1,), (0,))).astype(BF)
-        gk = mm(gs, q, ((0,), (0,))).astype(BF)
-        gv = mm(w_low, ct, ((0,), (0,))).astype(BF)
-        d_in = (row_wide >= dlo) & (row_wide < dlo + dl)
-        e_in = (row_wide >= elo) & (row_wide < elo + el)
-        ctx_s[dwin, :] = jnp.where(d_in, ctx, ctx_s[dwin, :])
-        gq_s[dwin, :] = jnp.where(d_in, gq, gq_s[dwin, :])
-        gk_s[ewin, :] = jnp.where(e_in, gk, gk_s[ewin, :])
-        gv_s[ewin, :] = jnp.where(e_in, gv, gv_s[ewin, :])
+    for first in range(0, 2 * SEGS, GROUP):
+        spots, loaded, scores = [], [], []
+        for e in range(first, first + GROUP):
+            es, el, ds, dl = meta[e, 0], meta[e, 1], meta[e, 2], meta[e, 3]
+            ew = pl.multiple_of(align(es, PAIR), 16)
+            dw = pl.multiple_of(align(ds, POOL), 16)
+            spots.append((pl.ds(ew, WIN), pl.ds(dw, WIN), es - ew, el, ds - dw, dl))
+        for ewin, dwin, *_ in spots:
+            k, v, q, ct = k_s[ewin, :], v_s[ewin, :], q_s[dwin, :], ct_s[dwin, :]
+            loaded.append((k, v, q, ct))
+            scores.append((mm(q, k, ((1,), (1,))), mm(ct, v, ((1,), (1,)))))
+        weights = []
+        for (_, _, elo, el, dlo, dl), (s, gw) in zip(spots, scores):
+            k_live = (col >= elo) & (col < elo + el)
+            q_live = (row[:, :1] >= dlo) & (row[:, :1] < dlo + dl)
+            s = jnp.where(k_live, s * scale, -jnp.inf)
+            p = jnp.exp(s - jnp.max(s, axis=1, keepdims=True))
+            share = jnp.where(q_live, 1.0 / jnp.sum(p, axis=1, keepdims=True), 0.0)
+            w = p * share
+            delta = jnp.sum(w * gw, axis=1, keepdims=True)
+            weights.append((w.astype(BF), (w * (gw - delta) * scale).astype(BF)))
+        results = []
+        for (k, v, q, ct), (w_low, gs) in zip(loaded, weights):
+            results.append((
+                mm(w_low, v, ((1,), (0,))).astype(BF),
+                mm(gs, k, ((1,), (0,))).astype(BF),
+                mm(gs, q, ((0,), (0,))).astype(BF),
+                mm(w_low, ct, ((0,), (0,))).astype(BF),
+            ))
+        for (ewin, dwin, elo, el, dlo, dl), (ctx, gq, gk, gv) in zip(spots, results):
+            d_in = (row_wide >= dlo) & (row_wide < dlo + dl)
+            e_in = (row_wide >= elo) & (row_wide < elo + el)
+            ctx_s[dwin, :] = jnp.where(d_in, ctx, ctx_s[dwin, :])
+            gq_s[dwin, :] = jnp.where(d_in, gq, gq_s[dwin, :])
+            gk_s[ewin, :] = jnp.where(e_in, gk, gk_s[ewin, :])
+            gv_s[ewin, :] = jnp.where(e_in, gv, gv_s[ewin, :])
 
 
 def places(me):
@@ -76,13 +84,27 @@
     return block
 
 
-def main_kernel(meta, me, x_ref, xt_ref, wk_ref, wv_ref, qm, qo, qa, qb, cm, co, ca, cb,
+def main_kernel(meta, me, x_ref, xt_ref, w0, w1, w3, w2a, w2b, qm, qo, qa, qb, cm, co, ca, cb,
                 om, oo, oa, ob, d0, d1, d2, d3,
-                k_s, v_s, gk_s, gv_s, q_s, ct_s, ctx_s, gq_s, dw_s):
+                k_s, v_s, gk_s, gv_s, q_s, ct_s, ctx_s, gq_s, dw_s, w_s):
     step = pl.program_id(0)
+    block = places(me)
+
+    @pl.when(step == 0)
+    def _():
+        def take(rc, carry):
+            for rb in range(4):
+                far = w2a[rb, rc] if rb < 2 else w2b[rb - 2, rc]
+                for ra, value in enumerate((w0[rb, rc], w1[rb, rc], far, w3[rb, rc])):
+                    bx, bzy = block(ra, rb, rc)
+                    w_s[bx, pl.ds(pl.multiple_of(bzy * 128, 128), 128), :] = value
+            return carry
+
+        lax.fori_loop(0, 4, take, 0)
+
     x = x_ref[...]
-    k_s[...] = jnp.dot(x, wk_ref[...].reshape(D, HEAD_DIM), preferred_element_type=jnp.float32).astype(BF)
-    v_s[...] = jnp.dot(x, wv_ref[...].reshape(D, HEAD_DIM), preferred_element_type=jnp.float32).astype(BF)
+    k_s[...] = jnp.dot(x, w_s[step], preferred_element_type=jnp.float32).astype(BF)
+    v_s[...] = jnp.dot(x, w_s[2 + step], preferred_element_type=jnp.float32).astype(BF)
     for pool, parts in ((q_s, (qm, qo, qa, qb)), (ct_s, (cm, co, ca, cb))):
         pool[0:TOK, :] = parts[0][...]
         pool[TOK:PAIR, :] = parts[1][...]
@@ -100,8 +122,6 @@
 
     @pl.when(step == 1)
     def _():
-        block = places(me)
-
         def put(n, carry):
             rb, rc = n // 4, n % 4
             for ra, out in enumerate((d0, d1, d2, d3)):
@@ -122,9 +142,6 @@
     def narrow(kind):
         return pl.BlockSpec((WIN, HEAD_DIM), lambda i, m, e: (0, kind * 4 + i * 2 + chunk))
 
-    def weight(kind):
-        return pl.BlockSpec((32, 1, 64, HEAD_DIM), lambda i, m, e: (0, kind * 2 + i, 0, e[2] * 2 + chunk))
-
     def out(rows):
         return pl.BlockSpec((2, rows, HEAD_DIM), lambda i, m, e: (0, 0, i))
 
@@ -136,18 +153,18 @@
         grid_spec=pltpu.PrefetchScalarGridSpec(
             num_scalar_prefetch=2,
             grid=(2,),
-            in_specs=[fixed(PAIR, D), fixed(D, PAIR), weight(0), weight(1),
+            in_specs=[fixed(PAIR, D), fixed(D, PAIR), *[fixed(*w.shape) for w in weights],
                       wide(TOK), wide(TOK), narrow(0), narrow(0),
                       wide(TOK), wide(TOK), narrow(1), narrow(1)],
             out_specs=[out(TOK), out(TOK), out(WIN), out(WIN), part, part, part, part],
             scratch_shapes=[pair, pair, pair, pair, pool, pool, pool, pool,
-                            pltpu.VMEM((4, D, HEAD_DIM), BF)],
+                            pltpu.VMEM((4, D, HEAD_DIM), BF)] + [pltpu.VMEM((4, D, HEAD_DIM), BF)],
         ),
         out_shape=[jax.ShapeDtypeStruct((2, rows, HALF), BF) for rows in (TOK, TOK, WIN, WIN)]
         + [jax.ShapeDtypeStruct((4, 4, 128, HEAD_DIM), BF)] * 4,
         compiler_params=pltpu.CompilerParams(vmem_limit_bytes=52 * MIB),
         cost_estimate=pl.CostEstimate(flops=12_000_000_000, bytes_accessed=24_000_000, transcendentals=500_000),
-    )(meta, me, x, xt, weights, weights, q, q_other, sent_a, sent_b, ct, ct_other, sent_a, sent_b)
+    )(meta, me, x, xt, *weights, q, q_other, sent_a, sent_b, ct, ct_other, sent_a, sent_b)
 
 
 def add_kernel(*refs):
@@ -179,25 +196,90 @@
     )(*parts, *extra)
 
 
-def depart_kernel(info, q_ref, ct_ref, a_ref, b_ref):
+def depart_kernel(me, enc_len, dec_len, partner, q_ref, ct_ref, meta, info, a_ref, b_ref):
+    core, x = me[2], me[3]
+    t = me[0] * 4 + me[1]
+
+    for side in range(2):
+        device = (t * 2 + (core if side == 0 else 1 - core)) * 4 + x
+        start = jnp.int32(side * TOK)
+        for slot in range(SEGS):
+            meta[side * SEGS + slot, 0] = start
+            meta[side * SEGS + slot, 1] = enc_len[device, slot]
+            start = start + enc_len[device, slot]
+    for n in range(4):
+        info[n] = jnp.int32(0)
+    info[1] = core
+    for near in range(4):
+        dp = t * 2 - 1 + near
+        device = jnp.clip(dp, 0, 31) * 4 + x
+        real = (dp >= 0) & (dp < 32)
+        same = (dp & 1) == core
+        start = jnp.int32(0)
+        for slot in range(SEGS):
+            begin, length = start, dec_len[device, slot]
+            owner = partner[device, slot] >> 4
+            here = real & ((owner >> 1) == t)
+            window = align(begin, TOK)
+            if near in (1, 2):
+                at = begin + jnp.where(same, 0, TOK)
+            else:
+                at = begin - window + PAIR + jnp.where(same, 0, WIN)
+
+            @pl.when(here)
+            def _():
+                entry = jnp.where((owner & 1) == core, 0, SEGS) + (partner[device, slot] & 3)
+                meta[entry, 2] = at
+                meta[entry, 3] = length
+
+            if near in (1, 2):
+
+                @pl.when(same & jnp.logical_not(here))
+                def _():
+                    info[0] = window
+                    info[2] = begin
+                    info[3] = length
+
+            start = start + length
+
     rows = pl.ds(pl.multiple_of(info[0], 16), WIN)
-    core = info[1]
     for n in range(4):
         source = (q_ref, ct_ref)[n // 2]
         for side, out in ((core, a_ref), (1 - core, b_ref)):
-            start = pl.multiple_of((n % 2) * 1024 + side * HALF, HALF)
-            out[:, n * HALF : (n + 1) * HALF] = source[rows, pl.ds(start, HALF)]
-
-
-def depart(info, q, ct):
+            begin = pl.multiple_of((n % 2) * 1024 + side * HALF, HALF)
+            out[:, n * HALF : (n + 1) * HALF] = source[rows, pl.ds(begin, HALF)]
+
+
+def depart(me, enc_lengths, dec_lengths, dec_partner, q, ct):
     whole = pl.BlockSpec(memory_space=pltpu.VMEM)
+    scalar = pl.BlockSpec(memory_space=pltpu.SMEM)
     return pl.pallas_call(
         depart_kernel,
-        in_specs=[pl.BlockSpec(memory_space=pltpu.SMEM), whole, whole],
-        out_specs=[whole, whole],
-        out_shape=[jax.ShapeDtypeStruct((WIN, 2048), BF)] * 2,
+        in_specs=[scalar, scalar, scalar, scalar, whole, whole],
+        out_specs=[scalar, scalar, whole, whole],
+        out_shape=[jax.ShapeDtypeStruct((2 * SEGS, 4), jnp.int32), jax.ShapeDtypeStruct((4,), jnp.int32)]
+        + [jax.ShapeDtypeStruct((WIN, 2048), BF)] * 2,
         compiler_params=pltpu.CompilerParams(vmem_limit_bytes=16 * MIB),
-    )(info, q, ct)
+    )(me, enc_lengths, dec_lengths, dec_partner, q, ct)
+
+
+def turn_kernel(a_ref, b_ref, x_ref, xt_ref):
+    for n, ref in enumerate((a_ref, b_ref)):
+        value = ref[...]
+        x_ref[n * TOK : (n + 1) * TOK, :] = value
+        xt_ref[:, n * TOK : (n + 1) * TOK] = value.T
+
+
+def turn(a, b):
+    part = pl.BlockSpec((TOK, 512), lambda i: (0, i))
+    return pl.pallas_call(
+        turn_kernel,
+        grid=(D // 512,),
+        in_specs=[part, part],
+        out_specs=[pl.BlockSpec((PAIR, 512), lambda i: (0, i)), pl.BlockSpec((512, PAIR), lambda i: (i, 0))],
+        out_shape=[jax.ShapeDtypeStruct((PAIR, D), BF), jax.ShapeDtypeStruct((D, PAIR), BF)],
+        compiler_params=pltpu.CompilerParams(vmem_limit_bytes=16 * MIB),
+    )(a, b)
 
 
 def finish_kernel(info, *refs):
@@ -263,58 +345,56 @@
     return [parts[0]] + [lax.ppermute(parts[r], ALL, shift(phase, r)) for r in (1, 3, 2)]
 
 
-def plan(enc_lengths, dec_lengths, dec_partner, t, c, x):
-    device = (t * 2 + c) * 4 + x
-    cores = jnp.stack([c, 1 - c])
-    devices = (t * 2 + cores) * 4 + x
-    ids = (devices[:, None] * SEGS + jnp.arange(SEGS, dtype=jnp.int32)).reshape(-1)
-    dec_starts = (jnp.cumsum(dec_lengths, axis=1) - dec_lengths).reshape(-1)
-    enc_starts = (jnp.cumsum(enc_lengths, axis=1) - enc_lengths).reshape(-1)
-    flat_dec = dec_lengths.reshape(-1)
-    flat_partner = dec_partner.reshape(-1)
-    entries = jnp.arange(enc_starts.shape[0], dtype=jnp.int32)
-    own = entries[None, :] == ids[:, None]
-    hit = flat_partner[None, :] == ids[:, None]
-
-    def pick(mask, table):
-        return jnp.sum(jnp.where(mask, table[None, :], 0), axis=1)
-
-    enc_len = pick(own, enc_lengths.reshape(-1))
-    enc_start = pick(own, enc_starts) + jnp.repeat(jnp.arange(2, dtype=jnp.int32) * TOK, SEGS)
-    dec_len = pick(hit, flat_dec)
-    dec_start = pick(hit, dec_starts)
-    owner = pick(hit, entries) // (SEGS * 4)
-    same = owner % 2 == c
-    dec_at = jnp.where(
-        owner // 2 == t,
-        dec_start + jnp.where(same, 0, TOK),
-        dec_start - align(dec_start, TOK) + PAIR + jnp.where(same, 0, WIN),
-    )
-    meta = jnp.stack([enc_start, enc_len, dec_at, dec_len], axis=1).astype(jnp.int32)
-
-    goes = (entries // SEGS == device) & (flat_partner // (SEGS * 4) == t * 2 + c + jnp.where(c == 0, -1, 1))
-    length = jnp.sum(jnp.where(goes, flat_dec, 0))
-    start = jnp.sum(jnp.where(goes, dec_starts, 0))
-    info = jnp.stack([align(start, TOK), c, start, length]).astype(jnp.int32)
-    return meta, info
+def join_kernel(*refs):
+    for n in range(4):
+        refs[-1][n] = refs[n][...]
+
+
+def join(parts, after):
+    whole = pl.BlockSpec(memory_space=pltpu.VMEM)
+    return pl.pallas_call(
+        join_kernel,
+        in_specs=[whole] * 4 + [pl.BlockSpec(memory_space=pl.ANY)] * len(after),
+        out_specs=whole,
+        out_shape=jax.ShapeDtypeStruct((4,) + parts[0].shape, BF),
+        compiler_params=pltpu.CompilerParams(vmem_limit_bytes=16 * MIB),
+    )(*parts, *after)
+
+
+def ring(value, phase, amount):
+    return lax.ppermute(value, ALL, shift(phase, -amount))
+
+
+def gather(kv_weights, c):
+    low, high = kv_weights[:, :HALF], kv_weights[:, HALF:]
+    mine, got = jnp.where(c == 0, low, high), swap(jnp.where(c == 0, high, low))
+    own = jnp.where(c == 0, jnp.concatenate([mine, got]), jnp.concatenate([got, mine]))
+    first = [own] + [ring(own, 2, n) for n in (1, 2, 3)]
+    chunks = []
+    for chunk in range(2):
+        cols = slice(chunk * HEAD_DIM, (chunk + 1) * HEAD_DIM)
+        part = jnp.stack([piece[:, cols] for piece in first])
+        part = join([part] + [ring(part, 1, n) for n in (1, 2, 3)], chunks[0][1:3] if chunk else [])
+        ahead, behind = ring(part, 0, 1), ring(part, 0, -1)
+        far_a, far_b = ring(behind[:2], 0, -1), ring(ahead[2:], 0, 1)
+        chunks.append([part, ahead, behind, far_a, far_b])
+    return chunks
 
 
 def body(enc_hidden, kv_weights, queries, cotangent, enc_lengths, dec_lengths, dec_partner):
     z, y, c, x = (lax.axis_index(a) for a in ALL)
     me = jnp.stack([z, y, c, x]).astype(jnp.int32)
-    weights = lax.all_gather(kv_weights, ALL, axis=0).reshape(32, 4, 64, 1024)
-    meta, info = plan(enc_lengths, dec_lengths, dec_partner, z * 4 + y, c, x)
-    leave_a, leave_b = depart(info, queries, cotangent)
+    weights = gather(kv_weights, c)
+    meta, info, leave_a, leave_b = depart(me, enc_lengths, dec_lengths, dec_partner, queries, cotangent)
     sent_a = lax.ppermute(leave_a, DP, SEND_A)
     sent_b = lax.ppermute(leave_b, DP, SEND_B)
-    tokens = jnp.concatenate([enc_hidden, swap(enc_hidden)], axis=0)
-    tokens_t = tokens.T
+    tokens, tokens_t = turn(enc_hidden, swap(enc_hidden))
     q_other, ct_other = swap(queries), swap(cotangent)
 
     pieces, grads = [], []
     for chunk in range(2):
         mine, other, far_a, far_b, *parts = run_main(
-            chunk, meta, me, tokens, tokens_t, weights, queries, q_other, cotangent, ct_other, sent_a, sent_b
+            chunk, meta, me, tokens, tokens_t, weights[chunk], queries, q_other, cotangent, ct_other, sent_a, sent_b
         )
         grads.append(exchange(parts, 0))
         pieces += [mine, swap(other), lax.ppermute(far_a, DP, back(SEND_A)), lax.ppermute(far_b, DP, back(SEND_B))]

time: 244 us -> 220 us (0.902)
  starting transfers between devices: 52.4 us -> 82.4 us
  local copies, waits for them, and re-layouts: 29.2 us -> 9.28 us
  between operations: 16.9 us -> 1.15 us
  other arithmetic: 13.4 us -> 1.89 us
  waiting for transfers between devices: 68.9 us -> 60.1 us
    all_gather x1 -> x0, waiting for transfers between devices: 34.2 us -> none  [body(): weights = lax.all_gather(kv_weights, ALL, axis=0).reshape(32, 4, 64, 1024)]
    ppermute x0 -> x17, starting transfers between devices: none -> 28.9 us  [ring(): return lax.ppermute(value, ALL, shift(phase, -amount))]
    ppermute x0 -> x17, waiting for transfers between devices: none -> 25.8 us  [ring(): return lax.ppermute(value, ALL, shift(phase, -amount))]
    pallas_call x1 -> x4, Pallas kernels: 1.53 us -> 10.1 us  [the longest x1 4.74 us: depart(): pl.pallas_call(depart_kernel, in_specs=[scalar, scalar, scalar, scalar, w...]
    ppermute x18, starting transfers between devices: 21.7 us -> 29.2 us  [exchange(): lax.ppermute(parts[r], ALL, shift(phase, r))]
    ppermute x18, waiting for transfers between devices: 29.2 us -> 22.5 us  [exchange(): lax.ppermute(parts[r], ALL, shift(phase, r))]
    concatenate x1 -> x0, local copies, waits for them, and re-layouts: 6.61 us -> none  [body(): tokens = jnp.concatenate([enc_hidden, swap(enc_hidden)], axis=0)]
    pallas_call x2, Pallas kernels: 53.2 us -> 46.8 us  [run_main(): pl.pallas_call(main_kernel, grid_spec=pltpu.PrefetchScalarGridSpec(num_sc...]
  transfers between devices with their start and end apart: 31 -> 48, of which waited for: 8 -> 16; matrix products, arithmetic and copies ran while one was open for 17% -> 1% of each run, Pallas kernels for 14% -> 29%
where the time goes in v3:
time: 220 us; the launch traced here: 217 us
  starting transfers between devices  82.4 us (37%)
  Pallas kernels  62.3 us (28%)
  waiting for transfers between devices  60.1 us (27%)
  local copies, waits for them, and re-layouts  9.28 us (4%)
    pallas_call x2, Pallas kernels, run_main(): pl.pallas_call(main_kernel, grid_spec=pltpu.PrefetchScalarGridSpec(num_sc...  46.8 us
    ppermute x18, starting transfers between devices, exchange(): lax.ppermute(parts[r], ALL, shift(phase, r))  29.2 us
    ppermute x17, starting transfers between devices, ring(): return lax.ppermute(value, ALL, shift(phase, -amount))  28.9 us
    ppermute x17, waiting for transfers between devices, ring(): return lax.ppermute(value, ALL, shift(phase, -amount))  25.8 us
    ppermute x18, waiting for transfers between devices, exchange(): lax.ppermute(parts[r], ALL, shift(phase, r))  22.5 us
    ppermute x7, starting transfers between devices, swap(): return lax.ppermute(value, 'c', [(0, 1), (1, 0)])  10.8 us
    unnamed x49, local copies, waits for them, and re-layouts  9.1 us
    ppermute x2, starting transfers between devices, body(): lax.ppermute(far_b, DP, back(SEND_B))  5.66 us
  transfers between devices with their start and end apart: 48, of which 16 were waited for; matrix products, arithmetic and copies ran while one was open for 1% of the time, Pallas kernels for 29%

profile of v3, /device:TPU:1, one launch (start us, length us, event | category | flops | bytes accessed | tf_op | source)
XLA Modules:
  0.0 217.1 jit_solution(1643148946289338408)
XLA Ops:
  5.4 2.6 %collective-permute-start.3 = (bf16[128,512]{1,0:T(8,128)(2,1)S(1)}, bf16[128,512]{1,0:T(8,128)(2,1)S(1)}, u32[]{:S(2)}, u32[]{:S(2)}) collective-permute-start(bf16[128,512]{1,0:T(8,128)(2,1)S(1)} %maximum_select_fusion), channel_id=1, source_target_pairs={{0,64},{1,65},{2,66},{3,67},{4,20},{5,21},{6,22},{7,23},{8,72},{9,... | collective-permute-start | bytes 393224 | tf_op jit(solution)/shard_map/ppermute | solution.py:365
  9.2 2.6 %collective-permute-done.3 = bf16[128,512]{1,0:T(8,128)(2,1)S(1)} collective-permute-done((bf16[128,512]{1,0:T(8,128)(2,1)S(1)}, bf16[128,512]{1,0:T(8,128)(2,1)S(1)}, u32[]{:S(2)}, u32[]{:S(2)}) %collective-permute-start.3) | collective-permute-done | bytes 131104 | tf_op jit(solution)/shard_map/ppermute | solution.py:365
  13.2 2.5 %collective-permute-start.6 = (bf16[4,128,256]{2,1,0:T(8,128)(2,1)S(1)}, bf16[4,128,256]{2,1,0:T(8,128)(2,1)S(1)}, u32[]{:S(2)}, u32[]{:S(2)}) collective-permute-start(bf16[4,128,256]{2,1,0:T(8,128)(2,1)S(1)} %pad_maximum_fusion.refs_0_), channel_id=1, source_target_pairs={{0,16},{1,17},{2,18},{3,19},{4,6},{5,7},{6,4},{7,5},{8,24},{9,25},... | collective-permute-start | bytes 786440 | tf_op jit(solution)/shard_map/ppermute | solution.py:365
  18.4 3.8 %collective-permute-done.6.refs_2_ = bf16[4,128,256]{2,1,0:T(8,128)(2,1)S(1)} collective-permute-done((bf16[4,128,256]{2,1,0:T(8,128)(2,1)S(1)}, bf16[4,128,256]{2,1,0:T(8,128)(2,1)S(1)}, u32[]{:S(2)}, u32[]{:S(2)}) %collective-permute-start.6) | collective-permute-done | bytes 262176 | tf_op jit(solution)/shard_map/ppermute | solution.py:365
  22.3 2.3 %collective-permute-start.9 = (bf16[4,4,128,256]{3,2,1,0:T(8,128)(2,1)S(1)}, bf16[4,4,128,256]{3,2,1,0:T(8,128)(2,1)S(1)}, u32[]{:S(2)}, u32[]{:S(2)}) collective-permute-start(bf16[4,4,128,256]{3,2,1,0:T(8,128)(2,1)S(1)} %shard_map.96.w0), channel_id=1, source_target_pairs={{0,1},{1,2},{2,3},{3,0},{4,36},{5,37},{6,38},{7,39},{8,9},{9,10},{... | collective-permute-start | bytes 3145736 | tf_op jit(solution)/shard_map/ppermute | solution.py:365
  24.6 3.8 %collective-permute-start = (bf16[512,2048]{1,0:T(8,128)(2,1)}, bf16[512,2048]{1,0:T(8,128)(2,1)}, u32[]{:S(2)}, u32[]{:S(2)}) collective-permute-start(bf16[512,2048]{1,0:T(8,128)(2,1)} %a_ref.1), channel_id=1, source_target_pairs={{0,4},{4,0},{1,5},{5,1},{2,6},{6,2},{3,7},{7,3},{8,12},{12,8},{9,1... | collective-permute-start | bytes 6291464 | tf_op jit(solution)/shard_map/ppermute | solution.py:320
  34.0 4.1 %collective-permute-done.21.refs_3_ = bf16[4,128,256]{2,1,0:T(8,128)(2,1)} collective-permute-done((bf16[4,128,256]{2,1,0:T(8,128)(2,1)S(1)}, bf16[4,128,256]{2,1,0:T(8,128)(2,1)}, u32[]{:S(2)}, u32[]{:S(2)}) %collective-permute-start.21) | collective-permute-done | bytes 262176 | tf_op jit(solution)/shard_map/ppermute | solution.py:365
  39.3 4.7 %shard_map.94 = (s32[8,4]{1,0:T(8,128)S(1)}, s32[4]{0:T(128)S(1)}, bf16[176,2048]{1,0:T(8,128)(2,1)S(1)}, bf16[176,2048]{1,0:T(8,128)(2,1)S(1)}) custom-call(s32[4]{0:T(128)S(1)} %pad_add_fusion.me, s32[128,4]{1,0:T(8,128)S(1)} %copy.10.enc_len, s32[128,4]{1,0:T(8,128)S(1)} %copy.11.dec_len, s32[128,4]{1,0:T(8,128)S(1)} %copy-done.9, bf16[512,2048]{1,0:T(8,128)(2,1)} %qm.3, ...), custom_call_target="tpu_custom_call" | custom-call | tf_op jit(solution)/shard_map/pallas_call | solution.py:256
  44.1 3.3 %collective-permute-start.13 = (bf16[176,2048]{1,0:T(8,128)(2,1)S(1)}, bf16[176,2048]{1,0:T(8,128)(2,1)S(1)}, u32[]{:S(2)}, u32[]{:S(2)}) collective-permute-start(bf16[176,2048]{1,0:T(8,128)(2,1)S(1)} %get-tuple-element.47), channel_id=1, source_target_pairs={{8,0},{16,8},{24,16},{32,24},{40,32},{48,40},{56,48},{64,56},{72,6... | collective-permute-start | bytes 2162696 | tf_op jit(solution)/shard_map/ppermute | solution.py:389
  50.7 4.9 %collective-permute-done.13.qa.ca = bf16[176,2048]{1,0:T(8,128)(2,1)S(1)} collective-permute-done((bf16[176,2048]{1,0:T(8,128)(2,1)S(1)}, bf16[176,2048]{1,0:T(8,128)(2,1)S(1)}, u32[]{:S(2)}, u32[]{:S(2)}) %collective-permute-start.13) | collective-permute-done | bytes 720928 | tf_op jit(solution)/shard_map/ppermute | solution.py:389
  55.5 4.7 %collective-permute-start.22 = (bf16[4,4,128,256]{3,2,1,0:T(8,128)(2,1)S(1)}, bf16[4,4,128,256]{3,2,1,0:T(8,128)(2,1)S(1)}, u32[]{:S(2)}, u32[]{:S(2)}) collective-permute-start(bf16[4,4,128,256]{3,2,1,0:T(8,128)(2,1)S(1)} %shard_map.98.w0), channel_id=1, source_target_pairs={{0,3},{1,0},{2,1},{3,2},{4,100},{5,101},{6,102},{7,103},{8,11},{9,... | collective-permute-start | bytes 3145736 | tf_op jit(solution)/shard_map/ppermute | solution.py:365
  62.3 13.6 %collective-permute-done.23.w3 = bf16[4,4,128,256]{3,2,1,0:T(8,128)(2,1)S(1)} collective-permute-done((bf16[4,4,128,256]{3,2,1,0:T(8,128)(2,1)S(1)}, bf16[4,4,128,256]{3,2,1,0:T(8,128)(2,1)S(1)}, u32[]{:S(2)}, u32[]{:S(2)}) %collective-permute-start.23) | collective-permute-done | bytes 1048608 | tf_op jit(solution)/shard_map/ppermute | solution.py:365
  75.9 2.2 %collective-permute-start.10 = (bf16[2,4,128,256]{3,2,1,0:T(8,128)(2,1)S(1)}, bf16[2,4,128,256]{3,2,1,0:T(8,128)(2,1)S(1)}, u32[]{:S(2)}, u32[]{:S(2)}) collective-permute-start(bf16[2,4,128,256]{3,2,1,0:T(8,128)(2,1)S(1)} %slice.68), channel_id=1, source_target_pairs={{0,1},{1,2},{2,3},{3,0},{4,36},{5,37},{6,38},{7,39},{8,9},{9,10},{... | collective-permute-start | bytes 1572872 | tf_op jit(solution)/shard_map/ppermute | solution.py:365
  79.5 3.9 %shard_map.95 = (bf16[1024,2048]{1,0:T(8,128)(2,1)S(1)}, bf16[2048,1024]{1,0:T(8,128)(2,1)S(1)}) custom-call(bf16[512,2048]{1,0:T(8,128)(2,1)} %a_ref.1, bf16[512,2048]{1,0:T(8,128)(2,1)} %collective-permute-done.b_ref), custom_call_target="tpu_custom_call" | custom-call | tf_op jit(solution)/shard_map/pallas_call | solution.py:275
  83.4 2.0 copy-done.10
  85.4 2.0 copy-done.11
  87.7 2.6 %collective-permute-start.25 = (bf16[2,4,128,256]{3,2,1,0:T(8,128)(2,1)S(1)}, bf16[2,4,128,256]{3,2,1,0:T(8,128)(2,1)S(1)}, u32[]{:S(2)}, u32[]{:S(2)}) collective-permute-start(bf16[2,4,128,256]{3,2,1,0:T(8,128)(2,1)S(1)} %slice.75), channel_id=1, source_target_pairs={{0,3},{1,0},{2,1},{3,2},{4,100},{5,101},{6,102},{7,103},{8,11},{9,... | collective-permute-start | bytes 1572872 | tf_op jit(solution)/shard_map/ppermute | solution.py:365
  92.3 23.5 %shard_map.97 = (bf16[2,512,512]{2,1,0:T(8,128)(2,1)}, bf16[2,512,512]{2,1,0:T(8,128)(2,1)}, bf16[2,176,512]{2,1,0:T(8,128)(2,1)S(1)}, bf16[2,176,512]{2,1,0:T(8...) custom-call(s32[8,4]{1,0:T(8,128)S(1)} %get-tuple-element.44.meta, ...), custom_call_target="tpu_custom_call" | custom-call | flops 12000000000 | bytes 24000000 | tf_op jit(solution)/shard_map/pallas_call | solution.py:151
  115.8 2.7 %collective-permute-start.30 = (bf16[4,4,128,256]{3,2,1,0:T(8,128)(2,1)}, bf16[4,4,128,256]{3,2,1,0:T(8,128)(2,1)S(1)}, u32[]{:S(2)}, u32[]{:S(2)}) collective-permute-start(bf16[4,4,128,256]{3,2,1,0:T(8,128)(2,1)} %get-tuple-element.61), channel_id=1, source_target_pairs={{0,3},{1,0},{2,1},{3,2},{4,100},{5,101},{6,102},{7,103},{8,11},{9,... | collective-permute-start | bytes 3145736 | tf_op jit(solution)/shard_map/ppermute | solution.py:345
  118.5 23.3 %shard_map.99 = (bf16[2,512,512]{2,1,0:T(8,128)(2,1)}, bf16[2,512,512]{2,1,0:T(8,128)(2,1)}, bf16[2,176,512]{2,1,0:T(8,128)(2,1)S(1)}, bf16[2,176,512]{2,1,0:T(8...) custom-call(s32[8,4]{1,0:T(8,128)S(1)} %get-tuple-element.44.meta, ...), custom_call_target="tpu_custom_call" | custom-call | flops 12000000000 | bytes 24000000 | tf_op jit(solution)/shard_map/pallas_call | solution.py:151
  142.6 2.0 collective-permute-start.39
  151.3 6.0 %collective-permute-done.38.refs_1_ = bf16[4,4,128,256]{3,2,1,0:T(8,128)(2,1)S(1)} collective-permute-done((bf16[4,4,128,256]{3,2,1,0:T(8,128)(2,1)}, bf16[4,4,128,256]{3,2,1,0:T(8,128)(2,1)S(1)}, u32[]{:S(2)}, u32[]{:S(2)}) %collective-permute-start.38) | collective-permute-done | bytes 1048608 | tf_op jit(solution)/shard_map/ppermute | solution.py:345
  158.9 10.0 %collective-permute-done.40.refs_3_ = bf16[4,4,128,256]{3,2,1,0:T(8,128)(2,1)S(1)} collective-permute-done((bf16[4,4,128,256]{3,2,1,0:T(8,128)(2,1)}, bf16[4,4,128,256]{3,2,1,0:T(8,128)(2,1)S(1)}, u32[]{:S(2)}, u32[]{:S(2)}) %collective-permute-start.40) | collective-permute-done | bytes 1048608 | tf_op jit(solution)/shard_map/ppermute | solution.py:345
  173.9 3.5 %collective-permute-start.16 = (bf16[2,512,512]{2,1,0:T(8,128)(2,1)S(1)}, bf16[2,512,512]{2,1,0:T(8,128)(2,1)S(1)}, u32[]{:S(2)}, u32[]{:S(2)}) collective-permute-start(bf16[2,512,512]{2,1,0:T(8,128)(2,1)S(1)} %copy-done.19), channel_id=1, source_target_pairs={{0,4},{4,0},{1,5},{5,1},{2,6},{6,2},{3,7},{7,3},{8,12},{12,8},{9,1... | collective-permute-start | bytes 3145736 | tf_op jit(solution)/shard_map/ppermute | solution.py:320
  177.5 4.4 %collective-permute-start.43 = (bf16[4,128,256]{2,1,0:T(8,128)(2,1)S(1)}, bf16[4,128,256]{2,1,0:T(8,128)(2,1)S(1)}, u32[]{:S(2)}, u32[]{:S(2)}) collective-permute-start(bf16[4,128,256]{2,1,0:T(8,128)(2,1)S(1)} %get-tuple-element.78), channel_id=1, source_target_pairs={{0,16},{1,17},{2,18},{3,19},{4,6},{5,7},{6,4},{7,5},{8,24},{9,25},... | collective-permute-start | bytes 786440 | tf_op jit(solution)/shard_map/ppermute | solution.py:345
  182.0 2.3 %collective-permute-start.35 = (bf16[128,256]{1,0:T(8,128)(2,1)S(1)}, bf16[128,256]{1,0:T(8,128)(2,1)S(1)}, u32[]{:S(2)}, u32[]{:S(2)}) collective-permute-start(bf16[128,256]{1,0:T(8,128)(2,1)S(1)} %get-tuple-element.69), channel_id=1, source_target_pairs={{0,32},{1,33},{2,34},{3,35},{4,12},{5,13},{6,14},{7,15},{8,40},{9,... | collective-permute-start | bytes 196616 | tf_op jit(solution)/shard_map/ppermute | solution.py:345
  186.0 4.1 %collective-permute-start.36 = (bf16[128,256]{1,0:T(8,128)(2,1)S(1)}, bf16[128,256]{1,0:T(8,128)(2,1)S(1)}, u32[]{:S(2)}, u32[]{:S(2)}) collective-permute-start(bf16[128,256]{1,0:T(8,128)(2,1)S(1)} %get-tuple-element.70), channel_id=1, source_target_pairs={{0,96},{1,97},{2,98},{3,99},{4,28},{5,29},{6,30},{7,31},{8,104},{9... | collective-permute-start | bytes 196616 | tf_op jit(solution)/shard_map/ppermute | solution.py:345
  191.4 3.8 %collective-permute-start.18 = (bf16[2,176,512]{2,1,0:T(8,128)(2,1)S(1)}, bf16[2,176,512]{2,1,0:T(8,128)(2,1)S(1)}, u32[]{:S(2)}, u32[]{:S(2)}) collective-permute-start(bf16[2,176,512]{2,1,0:T(8,128)(2,1)S(1)} %get-tuple-element.52), channel_id=1, source_target_pairs={{4,8},{12,16},{20,24},{28,32},{36,40},{44,48},{52,56},{60,64},{68,... | collective-permute-start | bytes 1081352 | tf_op jit(solution)/shard_map/ppermute | solution.py:400
  195.2 2.8 %collective-permute-start.45 = (bf16[128,256]{1,0:T(8,128)(2,1)S(1)}, bf16[128,256]{1,0:T(8,128)(2,1)S(1)}, u32[]{:S(2)}, u32[]{:S(2)}) collective-permute-start(bf16[128,256]{1,0:T(8,128)(2,1)S(1)} %get-tuple-element.81), channel_id=1, source_target_pairs={{0,96},{1,97},{2,98},{3,99},{4,28},{5,29},{6,30},{7,31},{8,104},{9... | collective-permute-start | bytes 196616 | tf_op jit(solution)/shard_map/ppermute | solution.py:345
  200.6 3.6 %collective-permute-done.46 = bf16[128,256]{1,0:T(8,128)(2,1)S(1)} collective-permute-done((bf16[128,256]{1,0:T(8,128)(2,1)S(1)}, bf16[128,256]{1,0:T(8,128)(2,1)S(1)}, u32[]{:S(2)}, u32[]{:S(2)}) %collective-permute-start.46) | collective-permute-done | bytes 65568 | tf_op jit(solution)/shard_map/ppermute | solution.py:345
  207.6 5.4 %collective-permute-done.28.refs_7_ = bf16[2,176,512]{2,1,0:T(8,128)(2,1)S(1)} collective-permute-done((bf16[2,176,512]{2,1,0:T(8,128)(2,1)S(1)}, bf16[2,176,512]{2,1,0:T(8,128)(2,1)S(1)}, u32[]{:S(2)}, u32[]{:S(2)}) %collective-permute-start.28) | collective-permute-done | bytes 360480 | tf_op jit(solution)/shard_map/ppermute | solution.py:400
  213.0 3.4 %shard_map.100 = (bf16[512,2048]{1,0:T(8,128)(2,1)}, bf16[512,2048]{1,0:T(8,128)(2,1)}) custom-call(s32[4]{0:T(128)S(1)} %get-tuple-element.43.info, bf16[2,512,512]{2,1,0:T(8,128)(2,1)S(1)} %copy-done.6, bf16[2,512,512]{2,1,0:T(8,128)(2,1)S(1)} %collective-permute-done.16.refs_1_, bf16[2,176,512]{2,1,0:T(8,128)(2,1)S(1)} %collective-permute-done.17.refs_2_, ...), custom_call_target="tpu_custom_call" | custom-call | tf_op jit(solution)/shard_map/pallas_call | solution.py:306
  (142 shorter events, 49.9 us)
Async XLA Ops:
  13.2 9.0 %collective-permute-start.6 = (bf16[4,128,256]{2,1,0:T(8,128)(2,1)S(1)}, bf16[4,128,256]{2,1,0:T(8,128)(2,1)S(1)}, u32[]{:S(2)}, u32[]{:S(2)}) collective-permute-start(bf16[4,128,256]{2,1,0:T(8,128)(2,1)S(1)} %pad_maximum_fusion.refs_0_), channel_id=1, source_target_pairs={{0,16},{1,17},{2,18},{3,19},{4,6},{5,7},{6,4},{7,5},{8,24},{9,25},... | collective-permute-start | bytes 786440 | tf_op jit(solution)/shard_map/ppermute | solution.py:365
  22.3 25.2 %collective-permute-start.9 = (bf16[4,4,128,256]{3,2,1,0:T(8,128)(2,1)S(1)}, bf16[4,4,128,256]{3,2,1,0:T(8,128)(2,1)S(1)}, u32[]{:S(2)}, u32[]{:S(2)}) collective-permute-start(bf16[4,4,128,256]{3,2,1,0:T(8,128)(2,1)S(1)} %shard_map.96.w0), channel_id=1, source_target_pairs={{0,1},{1,2},{2,3},{3,0},{4,36},{5,37},{6,38},{7,39},{8,9},{9,10},{... | collective-permute-start | bytes 3145736 | tf_op jit(solution)/shard_map/ppermute | solution.py:365
  24.6 35.6 %collective-permute-start = (bf16[512,2048]{1,0:T(8,128)(2,1)}, bf16[512,2048]{1,0:T(8,128)(2,1)}, u32[]{:S(2)}, u32[]{:S(2)}) collective-permute-start(bf16[512,2048]{1,0:T(8,128)(2,1)} %a_ref.1), channel_id=1, source_target_pairs={{0,4},{4,0},{1,5},{5,1},{2,6},{6,2},{3,7},{7,3},{8,12},{12,8},{9,1... | collective-permute-start | bytes 6291464 | tf_op jit(solution)/shard_map/ppermute | solution.py:320
  28.4 9.8 %collective-permute-start.21 = (bf16[4,128,256]{2,1,0:T(8,128)(2,1)S(1)}, bf16[4,128,256]{2,1,0:T(8,128)(2,1)}, u32[]{:S(2)}, u32[]{:S(2)}) collective-permute-start(bf16[4,128,256]{2,1,0:T(8,128)(2,1)S(1)} %pad_maximum_fusion.1.refs_0_), channel_id=1, source_target_pairs={{0,8},{1,9},{2,10},{3,11},{4,5},{5,6},{6,7},{7,4},{8,16},{9,17},{1... | collective-permute-start | bytes 786440 | tf_op jit(solution)/shard_map/ppermute | solution.py:365
  29.7 18.8 %collective-permute-start.8 = (bf16[4,4,128,256]{3,2,1,0:T(8,128)(2,1)S(1)}, bf16[4,4,128,256]{3,2,1,0:T(8,128)(2,1)S(1)}, u32[]{:S(2)}, u32[]{:S(2)}) collective-permute-start(bf16[4,4,128,256]{3,2,1,0:T(8,128)(2,1)S(1)} %shard_map.96.w0), channel_id=1, source_target_pairs={{0,3},{1,0},{2,1},{3,2},{4,100},{5,101},{6,102},{7,103},{8,11},{9,... | collective-permute-start | bytes 3145736 | tf_op jit(solution)/shard_map/ppermute | solution.py:365
  31.6 12.4 %collective-permute-start.20 = (bf16[4,128,256]{2,1,0:T(8,128)(2,1)S(1)}, bf16[4,128,256]{2,1,0:T(8,128)(2,1)}, u32[]{:S(2)}, u32[]{:S(2)}) collective-permute-start(bf16[4,128,256]{2,1,0:T(8,128)(2,1)S(1)} %pad_maximum_fusion.1.refs_0_), channel_id=1, source_target_pairs={{0,16},{1,17},{2,18},{3,19},{4,6},{5,7},{6,4},{7,5},{8,24},{9,25},... | collective-permute-start | bytes 786440 | tf_op jit(solution)/shard_map/ppermute | solution.py:365
  38.2 9.2 %collective-permute-start.19 = (bf16[4,128,256]{2,1,0:T(8,128)(2,1)S(1)}, bf16[4,128,256]{2,1,0:T(8,128)(2,1)S(1)}, u32[]{:S(2)}, u32[]{:S(2)}) collective-permute-start(bf16[4,128,256]{2,1,0:T(8,128)(2,1)S(1)} %pad_maximum_fusion.1.refs_0_), channel_id=1, source_target_pairs={{0,24},{1,25},{2,26},{3,27},{4,7},{5,4},{6,5},{7,6},{8,0},{9,1},{1... | collective-permute-start | bytes 786440 | tf_op jit(solution)/shard_map/ppermute | solution.py:365
  44.1 11.5 %collective-permute-start.13 = (bf16[176,2048]{1,0:T(8,128)(2,1)S(1)}, bf16[176,2048]{1,0:T(8,128)(2,1)S(1)}, u32[]{:S(2)}, u32[]{:S(2)}) collective-permute-start(bf16[176,2048]{1,0:T(8,128)(2,1)S(1)} %get-tuple-element.47), channel_id=1, source_target_pairs={{8,0},{16,8},{24,16},{32,24},{40,32},{48,40},{56,48},{64,56},{72,6... | collective-permute-start | bytes 2162696 | tf_op jit(solution)/shard_map/ppermute | solution.py:389
  47.4 42.9 %collective-permute-start.12 = (bf16[512,2048]{1,0:T(8,128)(2,1)}, bf16[512,2048]{1,0:T(8,128)(2,1)S(1)}, u32[]{:S(2)}, u32[]{:S(2)}) collective-permute-start(bf16[512,2048]{1,0:T(8,128)(2,1)} %qm.3), channel_id=1, source_target_pairs={{0,4},{4,0},{1,5},{5,1},{2,6},{6,2},{3,7},{7,3},{8,12},{12,8},{9,1... | collective-permute-start | bytes 6291464 | tf_op jit(solution)/shard_map/ppermute | solution.py:320
  47.5 42.8 %collective-permute-start.15 = (bf16[512,2048]{1,0:T(8,128)(2,1)}, bf16[512,2048]{1,0:T(8,128)(2,1)S(1)}, u32[]{:S(2)}, u32[]{:S(2)}) collective-permute-start(bf16[512,2048]{1,0:T(8,128)(2,1)} %cm.3), channel_id=1, source_target_pairs={{0,4},{4,0},{1,5},{5,1},{2,6},{6,2},{3,7},{7,3},{8,12},{12,8},{9,1... | collective-permute-start | bytes 6291464 | tf_op jit(solution)/shard_map/ppermute | solution.py:320
  50.0 25.9 %collective-permute-start.23 = (bf16[4,4,128,256]{3,2,1,0:T(8,128)(2,1)S(1)}, bf16[4,4,128,256]{3,2,1,0:T(8,128)(2,1)S(1)}, u32[]{:S(2)}, u32[]{:S(2)}) collective-permute-start(bf16[4,4,128,256]{3,2,1,0:T(8,128)(2,1)S(1)} %shard_map.98.w0), channel_id=1, source_target_pairs={{0,1},{1,2},{2,3},{3,0},{4,36},{5,37},{6,38},{7,39},{8,9},{9,10},{... | collective-permute-start | bytes 3145736 | tf_op jit(solution)/shard_map/ppermute | solution.py:365
  55.5 22.5 %collective-permute-start.22 = (bf16[4,4,128,256]{3,2,1,0:T(8,128)(2,1)S(1)}, bf16[4,4,128,256]{3,2,1,0:T(8,128)(2,1)S(1)}, u32[]{:S(2)}, u32[]{:S(2)}) collective-permute-start(bf16[4,4,128,256]{3,2,1,0:T(8,128)(2,1)S(1)} %shard_map.98.w0), channel_id=1, source_target_pairs={{0,3},{1,0},{2,1},{3,2},{4,100},{5,101},{6,102},{7,103},{8,11},{9,... | collective-permute-start | bytes 3145736 | tf_op jit(solution)/shard_map/ppermute | solution.py:365
  60.2 27.3 %collective-permute-start.14 = (bf16[176,2048]{1,0:T(8,128)(2,1)S(1)}, bf16[176,2048]{1,0:T(8,128)(2,1)S(1)}, u32[]{:S(2)}, u32[]{:S(2)}) collective-permute-start(bf16[176,2048]{1,0:T(8,128)(2,1)S(1)} %get-tuple-element.48), channel_id=1, source_target_pairs={{8,4},{16,12},{24,20},{32,28},{40,36},{48,44},{56,52},{64,60},{72,... | collective-permute-start | bytes 2162696 | tf_op jit(solution)/shard_map/ppermute | solution.py:390
  75.9 11.8 %collective-permute-start.10 = (bf16[2,4,128,256]{3,2,1,0:T(8,128)(2,1)S(1)}, bf16[2,4,128,256]{3,2,1,0:T(8,128)(2,1)S(1)}, u32[]{:S(2)}, u32[]{:S(2)}) collective-permute-start(bf16[2,4,128,256]{3,2,1,0:T(8,128)(2,1)S(1)} %slice.68), channel_id=1, source_target_pairs={{0,1},{1,2},{2,3},{3,0},{4,36},{5,37},{6,38},{7,39},{8,9},{9,10},{... | collective-permute-start | bytes 1572872 | tf_op jit(solution)/shard_map/ppermute | solution.py:365
  78.1 12.2 %collective-permute-start.11 = (bf16[2,4,128,256]{3,2,1,0:T(8,128)(2,1)S(1)}, bf16[2,4,128,256]{3,2,1,0:T(8,128)(2,1)S(1)}, u32[]{:S(2)}, u32[]{:S(2)}) collective-permute-start(bf16[2,4,128,256]{3,2,1,0:T(8,128)(2,1)S(1)} %slice.69), channel_id=1, source_target_pairs={{0,3},{1,0},{2,1},{3,2},{4,100},{5,101},{6,102},{7,103},{8,11},{9,... | collective-permute-start | bytes 1572872 | tf_op jit(solution)/shard_map/ppermute | solution.py:365
  87.5 31.0 %collective-permute-start.24 = (bf16[2,4,128,256]{3,2,1,0:T(8,128)(2,1)S(1)}, bf16[2,4,128,256]{3,2,1,0:T(8,128)(2,1)S(1)}, u32[]{:S(2)}, u32[]{:S(2)}) collective-permute-start(bf16[2,4,128,256]{3,2,1,0:T(8,128)(2,1)S(1)} %slice.74), channel_id=1, source_target_pairs={{0,1},{1,2},{2,3},{3,0},{4,36},{5,37},{6,38},{7,39},{8,9},{9,10},{... | collective-permute-start | bytes 1572872 | tf_op jit(solution)/shard_map/ppermute | solution.py:365
  87.7 30.8 %collective-permute-start.25 = (bf16[2,4,128,256]{3,2,1,0:T(8,128)(2,1)S(1)}, bf16[2,4,128,256]{3,2,1,0:T(8,128)(2,1)S(1)}, u32[]{:S(2)}, u32[]{:S(2)}) collective-permute-start(bf16[2,4,128,256]{3,2,1,0:T(8,128)(2,1)S(1)} %slice.75), channel_id=1, source_target_pairs={{0,3},{1,0},{2,1},{3,2},{4,100},{5,101},{6,102},{7,103},{8,11},{9,... | collective-permute-start | bytes 1572872 | tf_op jit(solution)/shard_map/ppermute | solution.py:365
  115.8 28.8 %collective-permute-start.29 = (bf16[4,4,128,256]{3,2,1,0:T(8,128)(2,1)}, bf16[4,4,128,256]{3,2,1,0:T(8,128)(2,1)S(1)}, u32[]{:S(2)}, u32[]{:S(2)}) collective-permute-start(bf16[4,4,128,256]{3,2,1,0:T(8,128)(2,1)} %get-tuple-element.60), channel_id=1, source_target_pairs={{0,1},{1,2},{2,3},{3,0},{4,36},{5,37},{6,38},{7,39},{8,9},{9,10},{... | collective-permute-start | bytes 3145736 | tf_op jit(solution)/shard_map/ppermute | solution.py:345
  115.8 30.6 %collective-permute-start.30 = (bf16[4,4,128,256]{3,2,1,0:T(8,128)(2,1)}, bf16[4,4,128,256]{3,2,1,0:T(8,128)(2,1)S(1)}, u32[]{:S(2)}, u32[]{:S(2)}) collective-permute-start(bf16[4,4,128,256]{3,2,1,0:T(8,128)(2,1)} %get-tuple-element.61), channel_id=1, source_target_pairs={{0,3},{1,0},{2,1},{3,2},{4,100},{5,101},{6,102},{7,103},{8,11},{9,... | collective-permute-start | bytes 3145736 | tf_op jit(solution)/shard_map/ppermute | solution.py:345
  118.5 27.9 %collective-permute-start.31 = (bf16[4,4,128,256]{3,2,1,0:T(8,128)(2,1)}, bf16[4,4,128,256]{3,2,1,0:T(8,128)(2,1)S(1)}, u32[]{:S(2)}, u32[]{:S(2)}) collective-permute-start(bf16[4,4,128,256]{3,2,1,0:T(8,128)(2,1)} %get-tuple-element.62), channel_id=1, source_target_pairs={{0,2},{1,3},{2,0},{3,1},{4,68},{5,69},{6,70},{7,71},{8,10},{9,11},... | collective-permute-start | bytes 3145736 | tf_op jit(solution)/shard_map/ppermute | solution.py:345
  141.8 15.4 %collective-permute-start.38 = (bf16[4,4,128,256]{3,2,1,0:T(8,128)(2,1)}, bf16[4,4,128,256]{3,2,1,0:T(8,128)(2,1)S(1)}, u32[]{:S(2)}, u32[]{:S(2)}) collective-permute-start(bf16[4,4,128,256]{3,2,1,0:T(8,128)(2,1)} %get-tuple-element.72), channel_id=1, source_target_pairs={{0,1},{1,2},{2,3},{3,0},{4,36},{5,37},{6,38},{7,39},{8,9},{9,10},{... | collective-permute-start | bytes 3145736 | tf_op jit(solution)/shard_map/ppermute | solution.py:345
  142.6 16.3 %collective-permute-start.39 = (bf16[4,4,128,256]{3,2,1,0:T(8,128)(2,1)}, bf16[4,4,128,256]{3,2,1,0:T(8,128)(2,1)S(1)}, u32[]{:S(2)}, u32[]{:S(2)}) collective-permute-start(bf16[4,4,128,256]{3,2,1,0:T(8,128)(2,1)} %get-tuple-element.73), channel_id=1, source_target_pairs={{0,3},{1,0},{2,1},{3,2},{4,100},{5,101},{6,102},{7,103},{8,11},{9,... | collective-permute-start | bytes 3145736 | tf_op jit(solution)/shard_map/ppermute | solution.py:345
  144.6 24.3 %collective-permute-start.40 = (bf16[4,4,128,256]{3,2,1,0:T(8,128)(2,1)}, bf16[4,4,128,256]{3,2,1,0:T(8,128)(2,1)S(1)}, u32[]{:S(2)}, u32[]{:S(2)}) collective-permute-start(bf16[4,4,128,256]{3,2,1,0:T(8,128)(2,1)} %get-tuple-element.74), channel_id=1, source_target_pairs={{0,2},{1,3},{2,0},{3,1},{4,68},{5,69},{6,70},{7,71},{8,10},{9,11},... | collective-permute-start | bytes 3145736 | tf_op jit(solution)/shard_map/ppermute | solution.py:345
  148.5 23.6 %collective-permute-start.32 = (bf16[4,128,256]{2,1,0:T(8,128)(2,1)S(1)}, bf16[4,128,256]{2,1,0:T(8,128)(2,1)S(1)}, u32[]{:S(2)}, u32[]{:S(2)}) collective-permute-start(bf16[4,128,256]{2,1,0:T(8,128)(2,1)S(1)} %get-tuple-element.65), channel_id=1, source_target_pairs={{0,8},{1,9},{2,10},{3,11},{4,5},{5,6},{6,7},{7,4},{8,16},{9,17},{1... | collective-permute-start | bytes 786440 | tf_op jit(solution)/shard_map/ppermute | solution.py:345
  149.9 24.0 %collective-permute-start.33 = (bf16[4,128,256]{2,1,0:T(8,128)(2,1)S(1)}, bf16[4,128,256]{2,1,0:T(8,128)(2,1)S(1)}, u32[]{:S(2)}, u32[]{:S(2)}) collective-permute-start(bf16[4,128,256]{2,1,0:T(8,128)(2,1)S(1)} %get-tuple-element.66), channel_id=1, source_target_pairs={{0,24},{1,25},{2,26},{3,27},{4,7},{5,4},{6,5},{7,6},{8,0},{9,1},{1... | collective-permute-start | bytes 786440 | tf_op jit(solution)/shard_map/ppermute | solution.py:345
  157.3 20.1 %collective-permute-start.34 = (bf16[4,128,256]{2,1,0:T(8,128)(2,1)S(1)}, bf16[4,128,256]{2,1,0:T(8,128)(2,1)S(1)}, u32[]{:S(2)}, u32[]{:S(2)}) collective-permute-start(bf16[4,128,256]{2,1,0:T(8,128)(2,1)S(1)} %get-tuple-element.67), channel_id=1, source_target_pairs={{0,16},{1,17},{2,18},{3,19},{4,6},{5,7},{6,4},{7,5},{8,24},{9,25},... | collective-permute-start | bytes 786440 | tf_op jit(solution)/shard_map/ppermute | solution.py:345
  170.9 19.3 %collective-permute-start.17 = (bf16[2,176,512]{2,1,0:T(8,128)(2,1)S(1)}, bf16[2,176,512]{2,1,0:T(8,128)(2,1)S(1)}, u32[]{:S(2)}, u32[]{:S(2)}) collective-permute-start(bf16[2,176,512]{2,1,0:T(8,128)(2,1)S(1)} %get-tuple-element.51), channel_id=1, source_target_pairs={{0,8},{8,16},{16,24},{24,32},{32,40},{40,48},{48,56},{56,64},{64,7... | collective-permute-start | bytes 1081352 | tf_op jit(solution)/shard_map/ppermute | solution.py:400
  172.2 9.9 %collective-permute-start.42 = (bf16[4,128,256]{2,1,0:T(8,128)(2,1)S(1)}, bf16[4,128,256]{2,1,0:T(8,128)(2,1)S(1)}, u32[]{:S(2)}, u32[]{:S(2)}) collective-permute-start(bf16[4,128,256]{2,1,0:T(8,128)(2,1)S(1)} %get-tuple-element.77), channel_id=1, source_target_pairs={{0,24},{1,25},{2,26},{3,27},{4,7},{5,4},{6,5},{7,6},{8,0},{9,1},{1... | collective-permute-start | bytes 786440 | tf_op jit(solution)/shard_map/ppermute | solution.py:345
  173.9 33.1 %collective-permute-start.16 = (bf16[2,512,512]{2,1,0:T(8,128)(2,1)S(1)}, bf16[2,512,512]{2,1,0:T(8,128)(2,1)S(1)}, u32[]{:S(2)}, u32[]{:S(2)}) collective-permute-start(bf16[2,512,512]{2,1,0:T(8,128)(2,1)S(1)} %copy-done.19), channel_id=1, source_target_pairs={{0,4},{4,0},{1,5},{5,1},{2,6},{6,2},{3,7},{7,3},{8,12},{12,8},{9,1... | collective-permute-start | bytes 3145736 | tf_op jit(solution)/shard_map/ppermute | solution.py:320
  177.4 35.5 %collective-permute-start.26 = (bf16[2,512,512]{2,1,0:T(8,128)(2,1)S(1)}, bf16[2,512,512]{2,1,0:T(8,128)(2,1)S(1)}, u32[]{:S(2)}, u32[]{:S(2)}) collective-permute-start(bf16[2,512,512]{2,1,0:T(8,128)(2,1)S(1)} %copy-done.20), channel_id=1, source_target_pairs={{0,4},{4,0},{1,5},{5,1},{2,6},{6,2},{3,7},{7,3},{8,12},{12,8},{9,1... | collective-permute-start | bytes 3145736 | tf_op jit(solution)/shard_map/ppermute | solution.py:320
  191.4 14.8 %collective-permute-start.18 = (bf16[2,176,512]{2,1,0:T(8,128)(2,1)S(1)}, bf16[2,176,512]{2,1,0:T(8,128)(2,1)S(1)}, u32[]{:S(2)}, u32[]{:S(2)}) collective-permute-start(bf16[2,176,512]{2,1,0:T(8,128)(2,1)S(1)} %get-tuple-element.52), channel_id=1, source_target_pairs={{4,8},{12,16},{20,24},{28,32},{36,40},{44,48},{52,56},{60,64},{68,... | collective-permute-start | bytes 1081352 | tf_op jit(solution)/shard_map/ppermute | solution.py:400
  206.2 10.1 %collective-permute-start.47 = (f32[64,512]{1,0:T(8,128)S(1)}, f32[64,512]{1,0:T(8,128)S(1)}, u32[]{:S(2)}, u32[]{:S(2)}) collective-permute-start(f32[64,512]{1,0:T(8,128)S(1)} %broadcast_select_fusion.2), channel_id=1, source_target_pairs={{0,4},{4,0},{1,5},{5,1},{2,6},{6,2},{3,7},{7,3},{8,12},{12,8},{9,1... | collective-permute-start | bytes 393224 | tf_op jit(solution)/shard_map/ppermute | solution.py:320
  (39 other events, 494.7 us)

commit v4 on v3

--- a/solution.py
+++ b/solution.py
@@ -1,3 +1,5 @@
+import functools
+
 import jax
 import jax.numpy as jnp
 from jax import lax
@@ -84,9 +86,10 @@
     return block
 
 
-def main_kernel(meta, me, x_ref, xt_ref, w0, w1, w3, w2a, w2b, qm, qo, qa, qb, cm, co, ca, cb,
-                om, oo, oa, ob, d0, d1, d2, d3,
-                k_s, v_s, gk_s, gv_s, q_s, ct_s, ctx_s, gq_s, dw_s, w_s):
+def main_kernel(extra, meta, me, x_ref, xt_ref, w0, w1, w3, w2a, w2b,
+                qm, qo, qa, qb, cm, co, ca, cb, *refs):
+    om, oo, oa, ob, d0, d1, d2, d3 = refs[extra : extra + 8]
+    k_s, v_s, gk_s, gv_s, q_s, ct_s, ctx_s, gq_s, dw_s, w_s = refs[extra + 8 :]
     step = pl.program_id(0)
     block = places(me)
 
@@ -132,39 +135,43 @@
         lax.fori_loop(0, 16, put, 0)
 
 
-def run_main(chunk, meta, me, x, xt, weights, q, q_other, ct, ct_other, sent_a, sent_b):
+def run_main(chunk, meta, me, x, xt, weights, q, ct, given, sent_a, sent_b, before=(), after=()):
     def fixed(*shape):
         return pl.BlockSpec(shape, lambda i, m, e: (0,) * len(shape), pipeline_mode=pl.Buffered(1))
 
-    def wide(rows):
-        return pl.BlockSpec((rows, HEAD_DIM), lambda i, m, e: (0, i * 4 + e[2] * 2 + chunk))
-
-    def narrow(kind):
-        return pl.BlockSpec((WIN, HEAD_DIM), lambda i, m, e: (0, kind * 4 + i * 2 + chunk))
+    def wide():
+        return pl.BlockSpec((TOK, HEAD_DIM), lambda i, m, e: (0, i * 4 + e[2] * 2 + chunk))
+
+    def narrow(rows, kind):
+        return pl.BlockSpec((rows, HEAD_DIM), lambda i, m, e: (0, kind * 4 + i * 2 + chunk))
 
     def out(rows):
-        return pl.BlockSpec((2, rows, HEAD_DIM), lambda i, m, e: (0, 0, i))
+        return pl.BlockSpec((2, rows, HEAD_DIM), lambda i, m, e: (0, 0, i * 2 + chunk))
 
     part = pl.BlockSpec((4, 4, 128, HEAD_DIM), lambda i, m, e: (0, 0, 0, 0))
+    anywhere = pl.BlockSpec(memory_space=pl.ANY)
     pair = pltpu.VMEM((PAIR, HEAD_DIM), BF)
     pool = pltpu.VMEM((POOL, HEAD_DIM), BF)
-    return pl.pallas_call(
-        main_kernel,
+    extra = [*before, *after]
+    return pl.pallas_call(
+        functools.partial(main_kernel, len(extra)),
         grid_spec=pltpu.PrefetchScalarGridSpec(
             num_scalar_prefetch=2,
             grid=(2,),
             in_specs=[fixed(PAIR, D), fixed(D, PAIR), *[fixed(*w.shape) for w in weights],
-                      wide(TOK), wide(TOK), narrow(0), narrow(0),
-                      wide(TOK), wide(TOK), narrow(1), narrow(1)],
+                      wide(), narrow(TOK, 0), narrow(WIN, 0), narrow(WIN, 0),
+                      wide(), narrow(TOK, 1), narrow(WIN, 1), narrow(WIN, 1)]
+            + [anywhere] * len(extra),
             out_specs=[out(TOK), out(TOK), out(WIN), out(WIN), part, part, part, part],
             scratch_shapes=[pair, pair, pair, pair, pool, pool, pool, pool,
-                            pltpu.VMEM((4, D, HEAD_DIM), BF)] + [pltpu.VMEM((4, D, HEAD_DIM), BF)],
+                            pltpu.VMEM((4, D, HEAD_DIM), BF), pltpu.VMEM((4, D, HEAD_DIM), BF)],
         ),
-        out_shape=[jax.ShapeDtypeStruct((2, rows, HALF), BF) for rows in (TOK, TOK, WIN, WIN)]
+        out_shape=[jax.ShapeDtypeStruct((2, rows, 2 * HALF), BF) for rows in (TOK, TOK, WIN, WIN)]
         + [jax.ShapeDtypeStruct((4, 4, 128, HEAD_DIM), BF)] * 4,
+        input_output_aliases={17 + n: n for n in range(len(before))},
         compiler_params=pltpu.CompilerParams(vmem_limit_bytes=52 * MIB),
         cost_estimate=pl.CostEstimate(flops=12_000_000_000, bytes_accessed=24_000_000, transcendentals=500_000),
-    )(meta, me, x, xt, *weights, q, q_other, sent_a, sent_b, ct, ct_other, sent_a, sent_b)
+    )(meta, me, x, xt, *weights, q, given, sent_a, sent_b, ct, given, sent_a, sent_b, *extra)
 
 
 def add_kernel(*refs):
@@ -174,8 +181,8 @@
         out[...] = total[n]
 
 
-def add_parts(parts, after=None):
-    extra = [] if after is None else [after]
+def add_parts(parts, after=()):
+    extra = list(after)
     shape = parts[0].shape
     rank = len(shape)
     if rank == 4:
@@ -196,7 +203,7 @@
     )(*parts, *extra)
 
 
-def depart_kernel(me, enc_len, dec_len, partner, q_ref, ct_ref, meta, info, a_ref, b_ref):
+def depart_kernel(me, enc_len, dec_len, partner, q_ref, ct_ref, meta, info, a_ref, b_ref, give_ref):
     core, x = me[2], me[3]
     t = me[0] * 4 + me[1]
 
@@ -248,6 +255,7 @@
         for side, out in ((core, a_ref), (1 - core, b_ref)):
             begin = pl.multiple_of((n % 2) * 1024 + side * HALF, HALF)
             out[:, n * HALF : (n + 1) * HALF] = source[rows, pl.ds(begin, HALF)]
+        give_ref[:, n * HALF : (n + 1) * HALF] = source[:, pl.ds(begin, HALF)]
 
 
 def depart(me, enc_lengths, dec_lengths, dec_partner, q, ct):
@@ -256,9 +264,9 @@
     return pl.pallas_call(
         depart_kernel,
         in_specs=[scalar, scalar, scalar, scalar, whole, whole],
-        out_specs=[scalar, scalar, whole, whole],
+        out_specs=[scalar, scalar, whole, whole, whole],
         out_shape=[jax.ShapeDtypeStruct((2 * SEGS, 4), jnp.int32), jax.ShapeDtypeStruct((4,), jnp.int32)]
-        + [jax.ShapeDtypeStruct((WIN, 2048), BF)] * 2,
+        + [jax.ShapeDtypeStruct((rows, 2048), BF) for rows in (WIN, WIN, TOK)],
         compiler_params=pltpu.CompilerParams(vmem_limit_bytes=16 * MIB),
     )(me, enc_lengths, dec_lengths, dec_partner, q, ct)
 
@@ -283,24 +291,23 @@
 
 
 def finish_kernel(info, *refs):
-    ins, outs = refs[:8], refs[8:]
+    ins, outs = refs[:4], refs[4:]
     win = pl.multiple_of(info[0], 16)
     core, start, length = info[1], info[2] - info[0], info[3]
     rows = pl.ds(win, WIN)
-    place = lax.broadcasted_iota(jnp.int32, (WIN, HEAD_DIM), 0)
+    place = lax.broadcasted_iota(jnp.int32, (WIN, HALF), 0)
     inside = (place >= start) & (place < start + length)
-    for chunk in range(2):
-        mine, theirs, back_a, back_b = ins[chunk * 4 : chunk * 4 + 4]
-        for side, base, back in ((core, mine, back_a), (1 - core, theirs, back_b)):
-            cols = pl.ds(pl.multiple_of(side * HALF + chunk * HEAD_DIM, HEAD_DIM), HEAD_DIM)
-            for kind, out in enumerate(outs):
-                out[:, cols] = base[kind]
-                out[rows, cols] = jnp.where(inside, back[kind], out[rows, cols])
+    mine, theirs, back_a, back_b = ins
+    for side, base, back in ((core, mine, back_a), (1 - core, theirs, back_b)):
+        cols = pl.ds(pl.multiple_of(side * HALF, HALF), HALF)
+        for kind, out in enumerate(outs):
+            out[:, cols] = base[kind]
+            out[rows, cols] = jnp.where(inside, back[kind], out[rows, cols])
 
 
 def finish(info, pieces):
     def source(rows):
-        return pl.BlockSpec((2, rows, HEAD_DIM), lambda i, e: (0, 0, i))
+        return pl.BlockSpec((2, rows, HALF), lambda i, e: (0, 0, i))
 
     out = pl.BlockSpec((TOK, 1024), lambda i, e: (0, i))
     return pl.pallas_call(
@@ -308,7 +315,7 @@
         grid_spec=pltpu.PrefetchScalarGridSpec(
             num_scalar_prefetch=1,
             grid=(2,),
-            in_specs=[source(TOK), source(TOK), source(WIN), source(WIN)] * 2,
+            in_specs=[source(TOK), source(TOK), source(WIN), source(WIN)],
             out_specs=[out, out],
         ),
         out_shape=[jax.ShapeDtypeStruct((TOK, 2048), BF)] * 2,
@@ -345,18 +352,18 @@
     return [parts[0]] + [lax.ppermute(parts[r], ALL, shift(phase, r)) for r in (1, 3, 2)]
 
 
-def join_kernel(*refs):
+def join_kernel(cols, *refs):
     for n in range(4):
-        refs[-1][n] = refs[n][...]
-
-
-def join(parts, after):
+        refs[-1][n] = refs[n][..., cols]
+
+
+def join(parts, after, cols=slice(0, HEAD_DIM)):
     whole = pl.BlockSpec(memory_space=pltpu.VMEM)
     return pl.pallas_call(
-        join_kernel,
+        functools.partial(join_kernel, cols),
         in_specs=[whole] * 4 + [pl.BlockSpec(memory_space=pl.ANY)] * len(after),
         out_specs=whole,
-        out_shape=jax.ShapeDtypeStruct((4,) + parts[0].shape, BF),
+        out_shape=jax.ShapeDtypeStruct((4,) + parts[0].shape[:-1] + (HEAD_DIM,), BF),
         compiler_params=pltpu.CompilerParams(vmem_limit_bytes=16 * MIB),
     )(*parts, *after)
 
@@ -365,7 +372,7 @@
     return lax.ppermute(value, ALL, shift(phase, -amount))
 
 
-def gather(kv_weights, c):
+def gather(kv_weights, c, ready, turned):
     low, high = kv_weights[:, :HALF], kv_weights[:, HALF:]
     mine, got = jnp.where(c == 0, low, high), swap(jnp.where(c == 0, high, low))
     own = jnp.where(c == 0, jnp.concatenate([mine, got]), jnp.concatenate([got, mine]))
@@ -373,8 +380,8 @@
     chunks = []
     for chunk in range(2):
         cols = slice(chunk * HEAD_DIM, (chunk + 1) * HEAD_DIM)
-        part = jnp.stack([piece[:, cols] for piece in first])
-        part = join([part] + [ring(part, 1, n) for n in (1, 2, 3)], chunks[0][1:3] if chunk else [])
+        part = join(first, chunks[0][:1] if chunk else [ready], cols)
+        part = join([part] + [ring(part, 1, n) for n in (1, 2, 3)], [] if chunk else [turned])
         ahead, behind = ring(part, 0, 1), ring(part, 0, -1)
         far_a, far_b = ring(behind[:2], 0, -1), ring(ahead[2:], 0, 1)
         chunks.append([part, ahead, behind, far_a, far_b])
@@ -384,26 +391,29 @@
 def body(enc_hidden, kv_weights, queries, cotangent, enc_lengths, dec_lengths, dec_partner):
     z, y, c, x = (lax.axis_index(a) for a in ALL)
     me = jnp.stack([z, y, c, x]).astype(jnp.int32)
-    weights = gather(kv_weights, c)
-    meta, info, leave_a, leave_b = depart(me, enc_lengths, dec_lengths, dec_partner, queries, cotangent)
+    meta, info, leave_a, leave_b, give = depart(me, enc_lengths, dec_lengths, dec_partner, queries, cotangent)
+    tokens, tokens_t = turn(enc_hidden, swap(enc_hidden))
+    weights = gather(kv_weights, c, leave_a, tokens_t)
     sent_a = lax.ppermute(leave_a, DP, SEND_A)
     sent_b = lax.ppermute(leave_b, DP, SEND_B)
-    tokens, tokens_t = turn(enc_hidden, swap(enc_hidden))
-    q_other, ct_other = swap(queries), swap(cotangent)
-
-    pieces, grads = [], []
+    shared = (meta, me, tokens, tokens_t)
+    inputs = (queries, cotangent, swap(give), sent_a, sent_b)
+
+    results, parts = [], []
     for chunk in range(2):
-        mine, other, far_a, far_b, *parts = run_main(
-            chunk, meta, me, tokens, tokens_t, weights[chunk], queries, q_other, cotangent, ct_other, sent_a, sent_b
-        )
-        grads.append(exchange(parts, 0))
-        pieces += [mine, swap(other), lax.ppermute(far_a, DP, back(SEND_A)), lax.ppermute(far_b, DP, back(SEND_B))]
-
-    last = []
-    for chunk, parts in enumerate(grads):
-        after = grads[1][0] if chunk == 0 else None
-        second = exchange(add_parts(parts, after), 1)
-        last.append(exchange(add_parts(second), 2))
+        done = run_main(chunk, *shared, weights[chunk], *inputs, before=results, after=() if chunk else weights[1][1:3])
+        results = done[:4]
+        parts.append(exchange(done[4:], 0))
+    mine, other, far_a, far_b = results
+    context, grad_queries = finish(
+        info,
+        [mine, swap(other), lax.ppermute(far_a, DP, back(SEND_A)), lax.ppermute(far_b, DP, back(SEND_B))],
+    )
+
+    second = add_parts(exchange(add_parts(parts[0], [mine]), 1))
+    last = [exchange(second, 2)]
+    second = add_parts(exchange(add_parts(parts[1], [second[0]]), 1), [context])
+    last.append(exchange(second, 2))
     summed = jnp.concatenate(
         [sum(part.astype(jnp.float32) for part in parts) for parts in last], axis=1
     )
@@ -411,7 +421,6 @@
     got = swap(jnp.where(c == 0, high, low))
     kept = jnp.where(c == 0, low, high)
     grad = jnp.concatenate([jnp.where(c == 0, kept, got), jnp.where(c == 0, got, kept)], axis=1)
-    context, grad_queries = finish(info, pieces)
     return context, grad_queries, grad
 
 

time: 220 us -> 220 us (level)
  local copies, waits for them, and re-layouts: 9.28 us -> 12.8 us
  Pallas kernels: 62.3 us -> 59.3 us
  starting transfers between devices: 82.4 us -> 79.7 us
  waiting for transfers between devices: 60.1 us -> 62.8 us
    ppermute x2 -> x1, starting transfers between devices: 5.66 us -> 13.1 us  [body(): lax.ppermute(far_b, DP, back(SEND_B))]
    ppermute x18, starting transfers between devices: 29.2 us -> 22.3 us  [exchange(): lax.ppermute(parts[r], ALL, shift(phase, r))]
    ppermute x17, waiting for transfers between devices: 25.8 us -> 30.8 us  [ring(): return lax.ppermute(value, ALL, shift(phase, -amount))]
    ppermute x1, waiting for transfers between devices: 4.89 us -> 0.01 us  [body(): sent_a = lax.ppermute(leave_a, DP, SEND_A)]
    unnamed x49 -> x43, local copies, waits for them, and re-layouts: 9.1 us -> 12.7 us
    ppermute x7 -> x5, waiting for transfers between devices: 0.92 us -> 3.88 us  [swap(): return lax.ppermute(value, 'c', [(0, 1), (1, 0)])]
    ppermute x1, starting transfers between devices: 1.91 us -> 4.36 us  [body(): sent_b = lax.ppermute(leave_b, DP, SEND_B)]
    pallas_call x4 -> x6, Pallas kernels: 48.3 us -> 47 us  [the longest x2 46.9 us: run_main(): pl.pallas_call(functools.partial(main_kernel, len(extra)), grid_spec=pltp...]
  transfers between devices with their start and end apart: 48 -> 44, of which waited for: 16 -> 13; matrix products, arithmetic and copies ran while one was open for 1% -> 2% of each run, Pallas kernels for 29% -> 27%
where the time goes in v4:
time: 220 us; the launch traced here: 217 us
  starting transfers between devices  79.7 us (36%)
  waiting for transfers between devices  62.8 us (29%)
  Pallas kernels  59.3 us (27%)
  local copies, waits for them, and re-layouts  12.8 us (6%)
    pallas_call x2, Pallas kernels, run_main(): pl.pallas_call(functools.partial(main_kernel, len(extra)), grid_spec=pltp...  46.9 us
    ppermute x17, waiting for transfers between devices, ring(): return lax.ppermute(value, ALL, shift(phase, -amount))  30.8 us
    ppermute x17, starting transfers between devices, ring(): return lax.ppermute(value, ALL, shift(phase, -amount))  27.5 us
    ppermute x18, waiting for transfers between devices, exchange(): lax.ppermute(parts[r], ALL, shift(phase, r))  23.3 us
    ppermute x18, starting transfers between devices, exchange(): lax.ppermute(parts[r], ALL, shift(phase, r))  22.3 us
    ppermute x1, starting transfers between devices, body(): lax.ppermute(far_b, DP, back(SEND_B))  13.1 us
    unnamed x43, local copies, waits for them, and re-layouts  12.7 us
    ppermute x5, starting transfers between devices, swap(): return lax.ppermute(value, 'c', [(0, 1), (1, 0)])  9.87 us
  transfers between devices with their start and end apart: 44, of which 13 were waited for; matrix products, arithmetic and copies ran while one was open for 2% of the time, Pallas kernels for 27%

profile of v4, /device:TPU:1, one launch (start us, length us, event | category | flops | bytes accessed | tf_op | source)
XLA Modules:
  0.0 217.5 jit_solution(15540958800617583128)
XLA Ops:
  3.1 2.9 %collective-permute-done.1 = bf16[64,512]{1,0:T(8,128)(2,1)S(1)} collective-permute-done((bf16[64,512]{1,0:T(8,128)(2,1)S(1)}, bf16[64,512]{1,0:T(8,128)(2,1)S(1)}, u32[]{:S(2)}, u32[]{:S(2)}) %collective-permute-start.1) | collective-permute-done | bytes 65568 | tf_op jit(solution)/shard_map/ppermute | solution.py:327
  7.5 2.6 %collective-permute-start.3 = (bf16[128,512]{1,0:T(8,128)(2,1)S(1)}, bf16[128,512]{1,0:T(8,128)(2,1)S(1)}, u32[]{:S(2)}, u32[]{:S(2)}) collective-permute-start(bf16[128,512]{1,0:T(8,128)(2,1)S(1)} %maximum_select_fusion.refs_0_), channel_id=1, source_target_pairs={{0,64},{1,65},{2,66},{3,67},{4,20},{5,21},{6,22},{7,23},{8,72},{9,... | collective-permute-start | bytes 393224 | tf_op jit(solution)/shard_map/ppermute | solution.py:372
  16.8 4.9 %shard_map.94 = (s32[8,4]{1,0:T(8,128)S(1)}, s32[4]{0:T(128)S(1)}, bf16[176,2048]{1,0:T(8,128)(2,1)S(1)}, bf16[176,2048]{1,0:T(8,128)(2,1)S(1)}, bf16[512,2048]{1,0:T(8,128)(2,1)S(1)}) custom-call(s32[4]{0:T(128)S(1)} %pad_add_fusion.me, s32[128,4]{1,0:T(8,128)S(1)} %copy.14.enc_len, s32[128,4]{1,0:T(8,128)S(1)} %copy.15.dec_len, ...), custom_call_target="tpu_custom_call" | custom-call | tf_op jit(solution)/shard_map/pallas_call | solution.py:264
  23.0 2.5 %collective-permute-start.6 = (bf16[4,128,256]{2,1,0:T(8,128)(2,1)S(1)}, bf16[4,128,256]{2,1,0:T(8,128)(2,1)S(1)}, u32[]{:S(2)}, u32[]{:S(2)}) collective-permute-start(bf16[4,128,256]{2,1,0:T(8,128)(2,1)S(1)} %shard_map.96.refs_0_), channel_id=1, source_target_pairs={{0,16},{1,17},{2,18},{3,19},{4,6},{5,7},{6,4},{7,5},{8,24},{9,25},... | collective-permute-start | bytes 786440 | tf_op jit(solution)/shard_map/ppermute | solution.py:372
  26.6 2.9 %collective-permute-start.15 = (bf16[512,2048]{1,0:T(8,128)(2,1)S(1)}, bf16[512,2048]{1,0:T(8,128)(2,1)S(1)}, u32[]{:S(2)}, u32[]{:S(2)}) collective-permute-start(bf16[512,2048]{1,0:T(8,128)(2,1)S(1)} %get-tuple-element.49), channel_id=1, source_target_pairs={{0,4},{4,0},{1,5},{5,1},{2,6},{6,2},{3,7},{7,3},{8,12},{12,8},{9,1... | collective-permute-start | bytes 6291464 | tf_op jit(solution)/shard_map/ppermute | solution.py:327
  29.5 2.1 shard_map.95
  31.7 2.0 copy-done.11
  33.7 1.9 copy-done.2
  37.0 2.5 %collective-permute-start.9 = (bf16[4,128,256]{2,1,0:T(8,128)(2,1)S(1)}, bf16[4,128,256]{2,1,0:T(8,128)(2,1)S(1)}, u32[]{:S(2)}, u32[]{:S(2)}) collective-permute-start(bf16[4,128,256]{2,1,0:T(8,128)(2,1)S(1)} %shard_map.98.refs_0_), channel_id=1, source_target_pairs={{0,16},{1,17},{2,18},{3,19},{4,6},{5,7},{6,4},{7,5},{8,24},{9,25},... | collective-permute-start | bytes 786440 | tf_op jit(solution)/shard_map/ppermute | solution.py:372
  42.5 3.7 %collective-permute-start.18 = (bf16[4,4,128,256]{3,2,1,0:T(8,128)(2,1)S(1)}, bf16[4,4,128,256]{3,2,1,0:T(8,128)(2,1)S(1)}, u32[]{:S(2)}, u32[]{:S(2)}) collective-permute-start(bf16[4,4,128,256]{3,2,1,0:T(8,128)(2,1)S(1)} %shard_map.97.refs_4_.w0), channel_id=1, source_target_pairs={{0,3},{1,0},{2,1},{3,2},{4,100},{5,101},{6,102},{7,103},{8,11},{9,... | collective-permute-start | bytes 3145736 | tf_op jit(solution)/shard_map/ppermute | solution.py:372
  47.0 2.0 collective-permute-start.11
  49.0 6.7 %collective-permute-done.19.w3 = bf16[4,4,128,256]{3,2,1,0:T(8,128)(2,1)S(1)} collective-permute-done((bf16[4,4,128,256]{3,2,1,0:T(8,128)(2,1)S(1)}, bf16[4,4,128,256]{3,2,1,0:T(8,128)(2,1)S(1)}, u32[]{:S(2)}, u32[]{:S(2)}) %collective-permute-start.19) | collective-permute-done | bytes 1048608 | tf_op jit(solution)/shard_map/ppermute | solution.py:372
  55.7 4.4 %collective-permute-start.17 = (bf16[176,2048]{1,0:T(8,128)(2,1)S(1)}, bf16[176,2048]{1,0:T(8,128)(2,1)S(1)}, u32[]{:S(2)}, u32[]{:S(2)}) collective-permute-start(bf16[176,2048]{1,0:T(8,128)(2,1)S(1)} %get-tuple-element.50), channel_id=1, source_target_pairs={{8,4},{16,12},{24,20},{32,28},{40,36},{48,44},{56,52},{64,60},{72,... | collective-permute-start | bytes 2162696 | tf_op jit(solution)/shard_map/ppermute | solution.py:398
  61.6 18.2 %collective-permute-done.12.refs_1_.w3 = bf16[4,4,128,256]{3,2,1,0:T(8,128)(2,1)S(1)} collective-permute-done((bf16[4,4,128,256]{3,2,1,0:T(8,128)(2,1)S(1)}, bf16[4,4,128,256]{3,2,1,0:T(8,128)(2,1)S(1)}, u32[]{:S(2)}, u32[]{:S(2)}) %collective-permute-start.12) | collective-permute-done | bytes 1048608 | tf_op jit(solution)/shard_map/ppermute | solution.py:372
  79.7 2.2 %collective-permute-start.20 = (bf16[2,4,128,256]{3,2,1,0:T(8,128)(2,1)S(1)}, bf16[2,4,128,256]{3,2,1,0:T(8,128)(2,1)S(1)}, u32[]{:S(2)}, u32[]{:S(2)}) collective-permute-start(bf16[2,4,128,256]{3,2,1,0:T(8,128)(2,1)S(1)} %slice.34), channel_id=1, source_target_pairs={{0,1},{1,2},{2,3},{3,0},{4,36},{5,37},{6,38},{7,39},{8,9},{9,10},{... | collective-permute-start | bytes 1572872 | tf_op jit(solution)/shard_map/ppermute | solution.py:372
  85.3 3.7 %collective-permute-done.20.w2a = bf16[2,4,128,256]{3,2,1,0:T(8,128)(2,1)S(1)} collective-permute-done((bf16[2,4,128,256]{3,2,1,0:T(8,128)(2,1)S(1)}, bf16[2,4,128,256]{3,2,1,0:T(8,128)(2,1)S(1)}, u32[]{:S(2)}, u32[]{:S(2)}) %collective-permute-start.20) | collective-permute-done | bytes 524320 | tf_op jit(solution)/shard_map/ppermute | solution.py:372
  90.0 23.5 %shard_map.100 = (bf16[2,512,1024]{2,1,0:T(8,128)(2,1)}, bf16[2,512,1024]{2,1,0:T(8,128)(2,1)}, bf16[2,176,1024]{2,1,0:T(8,128)(2,1)S(1)}, bf16[2,176,1024]{2,1,...) custom-call(s32[8,4]{1,0:T(8,128)S(1)} %get-tuple-element.45.meta, ...), custom_call_target="tpu_custom_call" | custom-call | flops 12000000000 | bytes 24000000 | tf_op jit(solution)/shard_map/pallas_call | solution.py:156
  113.7 2.6 %collective-permute-start.26 = (bf16[4,4,128,256]{3,2,1,0:T(8,128)(2,1)}, bf16[4,4,128,256]{3,2,1,0:T(8,128)(2,1)S(1)}, u32[]{:S(2)}, u32[]{:S(2)}) collective-permute-start(bf16[4,4,128,256]{3,2,1,0:T(8,128)(2,1)} %get-tuple-element.63), channel_id=1, source_target_pairs={{0,3},{1,0},{2,1},{3,2},{4,100},{5,101},{6,102},{7,103},{8,11},{9,... | collective-permute-start | bytes 3145736 | tf_op jit(solution)/shard_map/ppermute | solution.py:352
  116.4 23.4 %shard_map.101 = (bf16[2,512,1024]{2,1,0:T(8,128)(2,1)}, bf16[2,512,1024]{2,1,0:T(8,128)(2,1)}, bf16[2,176,1024]{2,1,0:T(8,128)(2,1)S(1)}, bf16[2,176,1024]{2,1,...) custom-call(s32[8,4]{1,0:T(8,128)S(1)} %get-tuple-element.45.meta, ...), custom_call_target="tpu_custom_call", output_to_operand_aliasing={{0}: (17, {}), {1}: (18, {}), {2}: (19, {}), {3}: (20, {})} | custom-call | flops 12000000000 | bytes 24000000 | tf_op jit(solution)/shard_map/pallas_call | solution.py:156
  140.8 1.8 collective-permute-start.35
  147.0 8.2 %collective-permute-done.34.refs_1_ = bf16[4,4,128,256]{3,2,1,0:T(8,128)(2,1)S(1)} collective-permute-done((bf16[4,4,128,256]{3,2,1,0:T(8,128)(2,1)}, bf16[4,4,128,256]{3,2,1,0:T(8,128)(2,1)S(1)}, u32[]{:S(2)}, u32[]{:S(2)}) %collective-permute-start.34) | collective-permute-done | bytes 1048608 | tf_op jit(solution)/shard_map/ppermute | solution.py:352
  155.3 6.5 %collective-permute-done.28.refs_1_ = bf16[4,128,256]{2,1,0:T(8,128)(2,1)S(1)} collective-permute-done((bf16[4,128,256]{2,1,0:T(8,128)(2,1)S(1)}, bf16[4,128,256]{2,1,0:T(8,128)(2,1)S(1)}, u32[]{:S(2)}, u32[]{:S(2)}) %collective-permute-start.28) | collective-permute-done | bytes 262176 | tf_op jit(solution)/shard_map/ppermute | solution.py:352
  164.6 4.1 %collective-permute-done.30.refs_3_ = bf16[4,128,256]{2,1,0:T(8,128)(2,1)S(1)} collective-permute-done((bf16[4,128,256]{2,1,0:T(8,128)(2,1)S(1)}, bf16[4,128,256]{2,1,0:T(8,128)(2,1)S(1)}, u32[]{:S(2)}, u32[]{:S(2)}) %collective-permute-start.30) | collective-permute-done | bytes 262176 | tf_op jit(solution)/shard_map/ppermute | solution.py:352
  168.8 13.1 %collective-permute-start.24 = (bf16[2,176,1024]{2,1,0:T(8,128)(2,1)S(1)}, bf16[2,176,1024]{2,1,0:T(8,128)(2,1)S(1)}, u32[]{:S(2)}, u32[]{:S(2)}) collective-permute-start(bf16[2,176,1024]{2,1,0:T(8,128)(2,1)S(1)} %copy-done.19), channel_id=1, source_target_pairs={{4,8},{12,16},{20,24},{28,32},{36,40},{44,48},{52,56},{60,64},{68,... | collective-permute-start | bytes 2162696 | tf_op jit(solution)/shard_map/ppermute | solution.py:410
  183.1 2.7 %collective-permute-start.38 = (bf16[4,128,256]{2,1,0:T(8,128)(2,1)S(1)}, bf16[4,128,256]{2,1,0:T(8,128)(2,1)S(1)}, u32[]{:S(2)}, u32[]{:S(2)}) collective-permute-start(bf16[4,128,256]{2,1,0:T(8,128)(2,1)S(1)} %get-tuple-element.79), channel_id=1, source_target_pairs={{0,24},{1,25},{2,26},{3,27},{4,7},{5,4},{6,5},{7,6},{8,0},{9,1},{1... | collective-permute-start | bytes 786440 | tf_op jit(solution)/shard_map/ppermute | solution.py:352
  185.7 4.7 %collective-permute-start.39 = (bf16[4,128,256]{2,1,0:T(8,128)(2,1)S(1)}, bf16[4,128,256]{2,1,0:T(8,128)(2,1)S(1)}, u32[]{:S(2)}, u32[]{:S(2)}) collective-permute-start(bf16[4,128,256]{2,1,0:T(8,128)(2,1)S(1)} %get-tuple-element.80), channel_id=1, source_target_pairs={{0,16},{1,17},{2,18},{3,19},{4,6},{5,7},{6,4},{7,5},{8,24},{9,25},... | collective-permute-start | bytes 786440 | tf_op jit(solution)/shard_map/ppermute | solution.py:352
  190.5 4.9 %collective-permute-done.24.refs_3_ = bf16[2,176,1024]{2,1,0:T(8,128)(2,1)S(1)} collective-permute-done((bf16[2,176,1024]{2,1,0:T(8,128)(2,1)S(1)}, bf16[2,176,1024]{2,1,0:T(8,128)(2,1)S(1)}, u32[]{:S(2)}, u32[]{:S(2)}) %collective-permute-start.24) | collective-permute-done | bytes 720928 | tf_op jit(solution)/shard_map/ppermute | solution.py:410
  195.3 2.7 %collective-permute-start.32 = (bf16[128,256]{1,0:T(8,128)(2,1)S(1)}, bf16[128,256]{1,0:T(8,128)(2,1)S(1)}, u32[]{:S(2)}, u32[]{:S(2)}) collective-permute-start(bf16[128,256]{1,0:T(8,128)(2,1)S(1)} %get-tuple-element.71), channel_id=1, source_target_pairs={{0,96},{1,97},{2,98},{3,99},{4,28},{5,29},{6,30},{7,31},{8,104},{9... | collective-permute-start | bytes 196616 | tf_op jit(solution)/shard_map/ppermute | solution.py:352
  198.0 3.2 %shard_map.102 = (bf16[512,2048]{1,0:T(8,128)(2,1)}, bf16[512,2048]{1,0:T(8,128)(2,1)}) custom-call(s32[4]{0:T(128)S(1)} %get-tuple-element.44.info, bf16[2,512,1024]{2,1,0:T(8,128)(2,1)S(1)} %copy-done.1, bf16[2,512,1024]{2,1,0:T(8,128)(2,1)S(1)} %collective-permute-done.22.refs_1_, bf16[2,176,1024]{2,1,0:T(8,128)(2,1)S(1)} %collective-permute-done.23.refs_2_, ...), custom_call_target="tpu_custom_call" | custom-call | tf_op jit(solution)/shard_map/pallas_call | solution.py:313
  203.7 2.0 collective-permute-start.41
  207.5 2.8 %collective-permute-done.42 = bf16[128,256]{1,0:T(8,128)(2,1)S(1)} collective-permute-done((bf16[128,256]{1,0:T(8,128)(2,1)S(1)}, bf16[128,256]{1,0:T(8,128)(2,1)S(1)}, u32[]{:S(2)}, u32[]{:S(2)}) %collective-permute-start.42) | collective-permute-done | bytes 65568 | tf_op jit(solution)/shard_map/ppermute | solution.py:352
  210.4 5.4 %collective-permute-start.43 = (f32[64,512]{1,0:T(8,128)S(1)}, f32[64,512]{1,0:T(8,128)S(1)}, u32[]{:S(2)}, u32[]{:S(2)}) collective-permute-start(f32[64,512]{1,0:T(8,128)S(1)} %broadcast_select_fusion.2), channel_id=1, source_target_pairs={{0,4},{4,0},{1,5},{5,1},{2,6},{6,2},{3,7},{7,3},{8,12},{12,8},{9,1... | collective-permute-start | bytes 393224 | tf_op jit(solution)/shard_map/ppermute | solution.py:327
  (124 shorter events, 39.9 us)
Async XLA Ops:
  0.6 28.9 %collective-permute-start = (bf16[512,2048]{1,0:T(8,128)(2,1)}, bf16[512,2048]{1,0:T(8,128)(2,1)S(1)}, u32[]{:S(2)}, u32[]{:S(2)}) collective-permute-start(bf16[512,2048]{1,0:T(8,128)(2,1)} %a_ref.1), channel_id=1, source_target_pairs={{0,4},{4,0},{1,5},{5,1},{2,6},{6,2},{3,7},{7,3},{8,12},{12,8},{9,1... | collective-permute-start | bytes 6291464 | tf_op jit(solution)/shard_map/ppermute | solution.py:327
  6.0 15.6 %collective-permute-start.4 = (bf16[128,512]{1,0:T(8,128)(2,1)S(1)}, bf16[128,512]{1,0:T(8,128)(2,1)S(1)}, u32[]{:S(2)}, u32[]{:S(2)}) collective-permute-start(bf16[128,512]{1,0:T(8,128)(2,1)S(1)} %maximum_select_fusion.refs_0_), channel_id=1, source_target_pairs={{0,32},{1,33},{2,34},{3,35},{4,12},{5,13},{6,14},{7,15},{8,40},{9,... | collective-permute-start | bytes 393224 | tf_op jit(solution)/shard_map/ppermute | solution.py:372
  7.5 14.2 %collective-permute-start.3 = (bf16[128,512]{1,0:T(8,128)(2,1)S(1)}, bf16[128,512]{1,0:T(8,128)(2,1)S(1)}, u32[]{:S(2)}, u32[]{:S(2)}) collective-permute-start(bf16[128,512]{1,0:T(8,128)(2,1)S(1)} %maximum_select_fusion.refs_0_), channel_id=1, source_target_pairs={{0,64},{1,65},{2,66},{3,67},{4,20},{5,21},{6,22},{7,23},{8,72},{9,... | collective-permute-start | bytes 393224 | tf_op jit(solution)/shard_map/ppermute | solution.py:372
  10.1 11.6 %collective-permute-start.2 = (bf16[128,512]{1,0:T(8,128)(2,1)S(1)}, bf16[128,512]{1,0:T(8,128)(2,1)S(1)}, u32[]{:S(2)}, u32[]{:S(2)}) collective-permute-start(bf16[128,512]{1,0:T(8,128)(2,1)S(1)} %maximum_select_fusion.refs_0_), channel_id=1, source_target_pairs={{0,96},{1,97},{2,98},{3,99},{4,28},{5,29},{6,30},{7,31},{8,104},{9... | collective-permute-start | bytes 393224 | tf_op jit(solution)/shard_map/ppermute | solution.py:372
  21.7 11.9 %collective-permute-start.7 = (bf16[4,128,256]{2,1,0:T(8,128)(2,1)S(1)}, bf16[4,128,256]{2,1,0:T(8,128)(2,1)S(1)}, u32[]{:S(2)}, u32[]{:S(2)}) collective-permute-start(bf16[4,128,256]{2,1,0:T(8,128)(2,1)S(1)} %shard_map.96.refs_0_), channel_id=1, source_target_pairs={{0,8},{1,9},{2,10},{3,11},{4,5},{5,6},{6,7},{7,4},{8,16},{9,17},{1... | collective-permute-start | bytes 786440 | tf_op jit(solution)/shard_map/ppermute | solution.py:372
  23.0 10.6 %collective-permute-start.6 = (bf16[4,128,256]{2,1,0:T(8,128)(2,1)S(1)}, bf16[4,128,256]{2,1,0:T(8,128)(2,1)S(1)}, u32[]{:S(2)}, u32[]{:S(2)}) collective-permute-start(bf16[4,128,256]{2,1,0:T(8,128)(2,1)S(1)} %shard_map.96.refs_0_), channel_id=1, source_target_pairs={{0,16},{1,17},{2,18},{3,19},{4,6},{5,7},{6,4},{7,5},{8,24},{9,25},... | collective-permute-start | bytes 786440 | tf_op jit(solution)/shard_map/ppermute | solution.py:372
  26.6 58.7 %collective-permute-start.15 = (bf16[512,2048]{1,0:T(8,128)(2,1)S(1)}, bf16[512,2048]{1,0:T(8,128)(2,1)S(1)}, u32[]{:S(2)}, u32[]{:S(2)}) collective-permute-start(bf16[512,2048]{1,0:T(8,128)(2,1)S(1)} %get-tuple-element.49), channel_id=1, source_target_pairs={{0,4},{4,0},{1,5},{5,1},{2,6},{6,2},{3,7},{7,3},{8,12},{12,8},{9,1... | collective-permute-start | bytes 6291464 | tf_op jit(solution)/shard_map/ppermute | solution.py:327
  40.6 15.2 %collective-permute-start.19 = (bf16[4,4,128,256]{3,2,1,0:T(8,128)(2,1)S(1)}, bf16[4,4,128,256]{3,2,1,0:T(8,128)(2,1)S(1)}, u32[]{:S(2)}, u32[]{:S(2)}) collective-permute-start(bf16[4,4,128,256]{3,2,1,0:T(8,128)(2,1)S(1)} %shard_map.97.refs_4_.w0), channel_id=1, source_target_pairs={{0,1},{1,2},{2,3},{3,0},{4,36},{5,37},{6,38},{7,39},{8,9},{9,10},{... | collective-permute-start | bytes 3145736 | tf_op jit(solution)/shard_map/ppermute | solution.py:372
  42.5 17.6 %collective-permute-start.18 = (bf16[4,4,128,256]{3,2,1,0:T(8,128)(2,1)S(1)}, bf16[4,4,128,256]{3,2,1,0:T(8,128)(2,1)S(1)}, u32[]{:S(2)}, u32[]{:S(2)}) collective-permute-start(bf16[4,4,128,256]{3,2,1,0:T(8,128)(2,1)S(1)} %shard_map.97.refs_4_.w0), channel_id=1, source_target_pairs={{0,3},{1,0},{2,1},{3,2},{4,100},{5,101},{6,102},{7,103},{8,11},{9,... | collective-permute-start | bytes 3145736 | tf_op jit(solution)/shard_map/ppermute | solution.py:372
  46.3 33.5 %collective-permute-start.12 = (bf16[4,4,128,256]{3,2,1,0:T(8,128)(2,1)S(1)}, bf16[4,4,128,256]{3,2,1,0:T(8,128)(2,1)S(1)}, u32[]{:S(2)}, u32[]{:S(2)}) collective-permute-start(bf16[4,4,128,256]{3,2,1,0:T(8,128)(2,1)S(1)} %shard_map.99.w0), channel_id=1, source_target_pairs={{0,1},{1,2},{2,3},{3,0},{4,36},{5,37},{6,38},{7,39},{8,9},{9,10},{... | collective-permute-start | bytes 3145736 | tf_op jit(solution)/shard_map/ppermute | solution.py:372
  47.0 35.0 %collective-permute-start.11 = (bf16[4,4,128,256]{3,2,1,0:T(8,128)(2,1)S(1)}, bf16[4,4,128,256]{3,2,1,0:T(8,128)(2,1)S(1)}, u32[]{:S(2)}, u32[]{:S(2)}) collective-permute-start(bf16[4,4,128,256]{3,2,1,0:T(8,128)(2,1)S(1)} %shard_map.99.w0), channel_id=1, source_target_pairs={{0,3},{1,0},{2,1},{3,2},{4,100},{5,101},{6,102},{7,103},{8,11},{9,... | collective-permute-start | bytes 3145736 | tf_op jit(solution)/shard_map/ppermute | solution.py:372
  55.7 26.8 %collective-permute-start.17 = (bf16[176,2048]{1,0:T(8,128)(2,1)S(1)}, bf16[176,2048]{1,0:T(8,128)(2,1)S(1)}, u32[]{:S(2)}, u32[]{:S(2)}) collective-permute-start(bf16[176,2048]{1,0:T(8,128)(2,1)S(1)} %get-tuple-element.50), channel_id=1, source_target_pairs={{8,4},{16,12},{24,20},{32,28},{40,36},{48,44},{56,52},{64,60},{72,... | collective-permute-start | bytes 2162696 | tf_op jit(solution)/shard_map/ppermute | solution.py:398
  60.1 23.5 %collective-permute-start.16 = (bf16[176,2048]{1,0:T(8,128)(2,1)S(1)}, bf16[176,2048]{1,0:T(8,128)(2,1)S(1)}, u32[]{:S(2)}, u32[]{:S(2)}) collective-permute-start(bf16[176,2048]{1,0:T(8,128)(2,1)S(1)} %get-tuple-element.48.refs_4_), channel_id=1, source_target_pairs={{8,0},{16,8},{24,16},{32,24},{40,32},{48,40},{56,48},{64,56},{72,6... | collective-permute-start | bytes 2162696 | tf_op jit(solution)/shard_map/ppermute | solution.py:397
  79.7 9.2 %collective-permute-start.20 = (bf16[2,4,128,256]{3,2,1,0:T(8,128)(2,1)S(1)}, bf16[2,4,128,256]{3,2,1,0:T(8,128)(2,1)S(1)}, u32[]{:S(2)}, u32[]{:S(2)}) collective-permute-start(bf16[2,4,128,256]{3,2,1,0:T(8,128)(2,1)S(1)} %slice.34), channel_id=1, source_target_pairs={{0,1},{1,2},{2,3},{3,0},{4,36},{5,37},{6,38},{7,39},{8,9},{9,10},{... | collective-permute-start | bytes 1572872 | tf_op jit(solution)/shard_map/ppermute | solution.py:372
  82.5 33.9 %collective-permute-start.13 = (bf16[2,4,128,256]{3,2,1,0:T(8,128)(2,1)S(1)}, bf16[2,4,128,256]{3,2,1,0:T(8,128)(2,1)S(1)}, u32[]{:S(2)}, u32[]{:S(2)}) collective-permute-start(bf16[2,4,128,256]{3,2,1,0:T(8,128)(2,1)S(1)} %slice.32), channel_id=1, source_target_pairs={{0,1},{1,2},{2,3},{3,0},{4,36},{5,37},{6,38},{7,39},{8,9},{9,10},{... | collective-permute-start | bytes 1572872 | tf_op jit(solution)/shard_map/ppermute | solution.py:372
  83.6 32.8 %collective-permute-start.14 = (bf16[2,4,128,256]{3,2,1,0:T(8,128)(2,1)S(1)}, bf16[2,4,128,256]{3,2,1,0:T(8,128)(2,1)S(1)}, u32[]{:S(2)}, u32[]{:S(2)}) collective-permute-start(bf16[2,4,128,256]{3,2,1,0:T(8,128)(2,1)S(1)} %slice.33), channel_id=1, source_target_pairs={{0,3},{1,0},{2,1},{3,2},{4,100},{5,101},{6,102},{7,103},{8,11},{9,... | collective-permute-start | bytes 1572872 | tf_op jit(solution)/shard_map/ppermute | solution.py:372
  113.5 27.3 %collective-permute-start.25 = (bf16[4,4,128,256]{3,2,1,0:T(8,128)(2,1)}, bf16[4,4,128,256]{3,2,1,0:T(8,128)(2,1)S(1)}, u32[]{:S(2)}, u32[]{:S(2)}) collective-permute-start(bf16[4,4,128,256]{3,2,1,0:T(8,128)(2,1)} %get-tuple-element.62), channel_id=1, source_target_pairs={{0,1},{1,2},{2,3},{3,0},{4,36},{5,37},{6,38},{7,39},{8,9},{9,10},{... | collective-permute-start | bytes 3145736 | tf_op jit(solution)/shard_map/ppermute | solution.py:352
  113.7 28.9 %collective-permute-start.26 = (bf16[4,4,128,256]{3,2,1,0:T(8,128)(2,1)}, bf16[4,4,128,256]{3,2,1,0:T(8,128)(2,1)S(1)}, u32[]{:S(2)}, u32[]{:S(2)}) collective-permute-start(bf16[4,4,128,256]{3,2,1,0:T(8,128)(2,1)} %get-tuple-element.63), channel_id=1, source_target_pairs={{0,3},{1,0},{2,1},{3,2},{4,100},{5,101},{6,102},{7,103},{8,11},{9,... | collective-permute-start | bytes 3145736 | tf_op jit(solution)/shard_map/ppermute | solution.py:352
  116.2 27.9 %collective-permute-start.27 = (bf16[4,4,128,256]{3,2,1,0:T(8,128)(2,1)}, bf16[4,4,128,256]{3,2,1,0:T(8,128)(2,1)S(1)}, u32[]{:S(2)}, u32[]{:S(2)}) collective-permute-start(bf16[4,4,128,256]{3,2,1,0:T(8,128)(2,1)} %get-tuple-element.64), channel_id=1, source_target_pairs={{0,2},{1,3},{2,0},{3,1},{4,68},{5,69},{6,70},{7,71},{8,10},{9,11},... | collective-permute-start | bytes 3145736 | tf_op jit(solution)/shard_map/ppermute | solution.py:352
  139.8 15.4 %collective-permute-start.34 = (bf16[4,4,128,256]{3,2,1,0:T(8,128)(2,1)}, bf16[4,4,128,256]{3,2,1,0:T(8,128)(2,1)S(1)}, u32[]{:S(2)}, u32[]{:S(2)}) collective-permute-start(bf16[4,4,128,256]{3,2,1,0:T(8,128)(2,1)} %get-tuple-element.74), channel_id=1, source_target_pairs={{0,1},{1,2},{2,3},{3,0},{4,36},{5,37},{6,38},{7,39},{8,9},{9,10},{... | collective-permute-start | bytes 3145736 | tf_op jit(solution)/shard_map/ppermute | solution.py:352
  140.8 57.2 %collective-permute-start.22 = (bf16[2,512,1024]{2,1,0:T(8,128)(2,1)}, bf16[2,512,1024]{2,1,0:T(8,128)(2,1)S(1)}, u32[]{:S(2)}, u32[]{:S(2)}) collective-permute-start(bf16[2,512,1024]{2,1,0:T(8,128)(2,1)} %get-tuple-element.56), channel_id=1, source_target_pairs={{0,4},{4,0},{1,5},{5,1},{2,6},{6,2},{3,7},{7,3},{8,12},{12,8},{9,1... | collective-permute-start | bytes 6291464 | tf_op jit(solution)/shard_map/ppermute | solution.py:327
  140.8 41.2 %collective-permute-start.35 = (bf16[4,4,128,256]{3,2,1,0:T(8,128)(2,1)}, bf16[4,4,128,256]{3,2,1,0:T(8,128)(2,1)S(1)}, u32[]{:S(2)}, u32[]{:S(2)}) collective-permute-start(bf16[4,4,128,256]{3,2,1,0:T(8,128)(2,1)} %get-tuple-element.75), channel_id=1, source_target_pairs={{0,3},{1,0},{2,1},{3,2},{4,100},{5,101},{6,102},{7,103},{8,11},{9,... | collective-permute-start | bytes 3145736 | tf_op jit(solution)/shard_map/ppermute | solution.py:352
  142.6 39.5 %collective-permute-start.36 = (bf16[4,4,128,256]{3,2,1,0:T(8,128)(2,1)}, bf16[4,4,128,256]{3,2,1,0:T(8,128)(2,1)S(1)}, u32[]{:S(2)}, u32[]{:S(2)}) collective-permute-start(bf16[4,4,128,256]{3,2,1,0:T(8,128)(2,1)} %get-tuple-element.76), channel_id=1, source_target_pairs={{0,2},{1,3},{2,0},{3,1},{4,68},{5,69},{6,70},{7,71},{8,10},{9,11},... | collective-permute-start | bytes 3145736 | tf_op jit(solution)/shard_map/ppermute | solution.py:352
  146.7 15.1 %collective-permute-start.28 = (bf16[4,128,256]{2,1,0:T(8,128)(2,1)S(1)}, bf16[4,128,256]{2,1,0:T(8,128)(2,1)S(1)}, u32[]{:S(2)}, u32[]{:S(2)}) collective-permute-start(bf16[4,128,256]{2,1,0:T(8,128)(2,1)S(1)} %get-tuple-element.66), channel_id=1, source_target_pairs={{0,8},{1,9},{2,10},{3,11},{4,5},{5,6},{6,7},{7,4},{8,16},{9,17},{1... | collective-permute-start | bytes 786440 | tf_op jit(solution)/shard_map/ppermute | solution.py:352
  163.4 22.4 %collective-permute-start.23 = (bf16[2,176,1024]{2,1,0:T(8,128)(2,1)S(1)}, bf16[2,176,1024]{2,1,0:T(8,128)(2,1)S(1)}, u32[]{:S(2)}, u32[]{:S(2)}) collective-permute-start(bf16[2,176,1024]{2,1,0:T(8,128)(2,1)S(1)} %get-tuple-element.57), channel_id=1, source_target_pairs={{0,8},{8,16},{16,24},{24,32},{32,40},{40,48},{48,56},{56,64},{64,7... | collective-permute-start | bytes 2162696 | tf_op jit(solution)/shard_map/ppermute | solution.py:410
  168.8 26.5 %collective-permute-start.24 = (bf16[2,176,1024]{2,1,0:T(8,128)(2,1)S(1)}, bf16[2,176,1024]{2,1,0:T(8,128)(2,1)S(1)}, u32[]{:S(2)}, u32[]{:S(2)}) collective-permute-start(bf16[2,176,1024]{2,1,0:T(8,128)(2,1)S(1)} %copy-done.19), channel_id=1, source_target_pairs={{4,8},{12,16},{20,24},{28,32},{36,40},{44,48},{52,56},{60,64},{68,... | collective-permute-start | bytes 2162696 | tf_op jit(solution)/shard_map/ppermute | solution.py:410
  183.0 12.3 %collective-permute-start.37 = (bf16[4,128,256]{2,1,0:T(8,128)(2,1)S(1)}, bf16[4,128,256]{2,1,0:T(8,128)(2,1)S(1)}, u32[]{:S(2)}, u32[]{:S(2)}) collective-permute-start(bf16[4,128,256]{2,1,0:T(8,128)(2,1)S(1)} %get-tuple-element.78), channel_id=1, source_target_pairs={{0,8},{1,9},{2,10},{3,11},{4,5},{5,6},{6,7},{7,4},{8,16},{9,17},{1... | collective-permute-start | bytes 786440 | tf_op jit(solution)/shard_map/ppermute | solution.py:352
  183.1 18.2 %collective-permute-start.38 = (bf16[4,128,256]{2,1,0:T(8,128)(2,1)S(1)}, bf16[4,128,256]{2,1,0:T(8,128)(2,1)S(1)}, u32[]{:S(2)}, u32[]{:S(2)}) collective-permute-start(bf16[4,128,256]{2,1,0:T(8,128)(2,1)S(1)} %get-tuple-element.79), channel_id=1, source_target_pairs={{0,24},{1,25},{2,26},{3,27},{4,7},{5,4},{6,5},{7,6},{8,0},{9,1},{1... | collective-permute-start | bytes 786440 | tf_op jit(solution)/shard_map/ppermute | solution.py:352
  185.7 15.5 %collective-permute-start.39 = (bf16[4,128,256]{2,1,0:T(8,128)(2,1)S(1)}, bf16[4,128,256]{2,1,0:T(8,128)(2,1)S(1)}, u32[]{:S(2)}, u32[]{:S(2)}) collective-permute-start(bf16[4,128,256]{2,1,0:T(8,128)(2,1)S(1)} %get-tuple-element.80), channel_id=1, source_target_pairs={{0,16},{1,17},{2,18},{3,19},{4,6},{5,7},{6,4},{7,5},{8,24},{9,25},... | collective-permute-start | bytes 786440 | tf_op jit(solution)/shard_map/ppermute | solution.py:352
  195.3 10.4 %collective-permute-start.31 = (bf16[128,256]{1,0:T(8,128)(2,1)S(1)}, bf16[128,256]{1,0:T(8,128)(2,1)S(1)}, u32[]{:S(2)}, u32[]{:S(2)}) collective-permute-start(bf16[128,256]{1,0:T(8,128)(2,1)S(1)} %get-tuple-element.70), channel_id=1, source_target_pairs={{0,32},{1,33},{2,34},{3,35},{4,12},{5,13},{6,14},{7,15},{8,40},{9,... | collective-permute-start | bytes 196616 | tf_op jit(solution)/shard_map/ppermute | solution.py:352
  195.3 12.1 %collective-permute-start.32 = (bf16[128,256]{1,0:T(8,128)(2,1)S(1)}, bf16[128,256]{1,0:T(8,128)(2,1)S(1)}, u32[]{:S(2)}, u32[]{:S(2)}) collective-permute-start(bf16[128,256]{1,0:T(8,128)(2,1)S(1)} %get-tuple-element.71), channel_id=1, source_target_pairs={{0,96},{1,97},{2,98},{3,99},{4,28},{5,29},{6,30},{7,31},{8,104},{9... | collective-permute-start | bytes 196616 | tf_op jit(solution)/shard_map/ppermute | solution.py:352
  198.0 9.5 %collective-permute-start.33 = (bf16[128,256]{1,0:T(8,128)(2,1)S(1)}, bf16[128,256]{1,0:T(8,128)(2,1)S(1)}, u32[]{:S(2)}, u32[]{:S(2)}) collective-permute-start(bf16[128,256]{1,0:T(8,128)(2,1)S(1)} %get-tuple-element.72), channel_id=1, source_target_pairs={{0,64},{1,65},{2,66},{3,67},{4,20},{5,21},{6,22},{7,23},{8,72},{9,... | collective-permute-start | bytes 196616 | tf_op jit(solution)/shard_map/ppermute | solution.py:352
  (32 other events, 358.2 us)

commit v5 on v4

--- a/solution.py
+++ b/solution.py
@@ -86,10 +86,11 @@
     return block
 
 
-def main_kernel(extra, meta, me, x_ref, xt_ref, w0, w1, w3, w2a, w2b,
-                qm, qo, qa, qb, cm, co, ca, cb, *refs):
-    om, oo, oa, ob, d0, d1, d2, d3 = refs[extra : extra + 8]
-    k_s, v_s, gk_s, gv_s, q_s, ct_s, ctx_s, gq_s, dw_s, w_s = refs[extra + 8 :]
+def main_kernel(weights, extra, meta, me, x_ref, xt_ref, *refs):
+    w0, w1, w3, *w2 = refs[:weights]
+    qm, qo, qa, qb, cm, co, ca, cb = refs[weights : weights + 8]
+    om, oo, oa, ob, d0, d1, d3, *d2 = refs[weights + 8 + extra : -10]
+    k_s, v_s, gk_s, gv_s, q_s, ct_s, ctx_s, gq_s, dw_s, w_s = refs[-10:]
     step = pl.program_id(0)
     block = places(me)
 
@@ -97,7 +98,7 @@
     def _():
         def take(rc, carry):
             for rb in range(4):
-                far = w2a[rb, rc] if rb < 2 else w2b[rb - 2, rc]
+                far = w2[rb * len(w2) // 4][rb % (4 // len(w2)), rc]
                 for ra, value in enumerate((w0[rb, rc], w1[rb, rc], far, w3[rb, rc])):
                     bx, bzy = block(ra, rb, rc)
                     w_s[bx, pl.ds(pl.multiple_of(bzy * 128, 128), 128), :] = value
@@ -125,17 +126,18 @@
 
     @pl.when(step == 1)
     def _():
-        def put(n, carry):
-            rb, rc = n // 4, n % 4
-            for ra, out in enumerate((d0, d1, d2, d3)):
-                bx, bzy = block(ra, rb, rc)
-                out[rb, rc] = dw_s[bx, pl.ds(pl.multiple_of(bzy * 128, 128), 128), :]
+        def put(rc, carry):
+            for rb in range(4):
+                for ra, out in ((0, d0), (1, d1), (3, d3), (2, d2[rb * len(d2) // 4])):
+                    bx, bzy = block(ra, rb, rc)
+                    at = rb % (4 // len(d2)) if ra == 2 else rb
+                    out[at, rc] = dw_s[bx, pl.ds(pl.multiple_of(bzy * 128, 128), 128), :]
             return carry
 
-        lax.fori_loop(0, 16, put, 0)
-
-
-def run_main(chunk, meta, me, x, xt, weights, q, ct, given, sent_a, sent_b, before=(), after=()):
+        lax.fori_loop(0, 4, put, 0)
+
+
+def run_main(chunk, meta, me, x, xt, weights, q, ct, given, sent_a, sent_b, before=()):
     def fixed(*shape):
         return pl.BlockSpec(shape, lambda i, m, e: (0,) * len(shape), pipeline_mode=pl.Buffered(1))
 
@@ -148,34 +150,36 @@
     def out(rows):
         return pl.BlockSpec((2, rows, HEAD_DIM), lambda i, m, e: (0, 0, i * 2 + chunk))
 
-    part = pl.BlockSpec((4, 4, 128, HEAD_DIM), lambda i, m, e: (0, 0, 0, 0))
+    def part(shape):
+        return pl.BlockSpec(shape, lambda i, m, e: (0, 0, 0, 0))
+
+    parts = [(4, 4, 128, HEAD_DIM)] * 4 if chunk == 0 else [(4, 4, 128, HEAD_DIM)] * 3 + [(2, 4, 128, HEAD_DIM)] * 2
     anywhere = pl.BlockSpec(memory_space=pl.ANY)
     pair = pltpu.VMEM((PAIR, HEAD_DIM), BF)
     pool = pltpu.VMEM((POOL, HEAD_DIM), BF)
-    extra = [*before, *after]
-    return pl.pallas_call(
-        functools.partial(main_kernel, len(extra)),
+    return pl.pallas_call(
+        functools.partial(main_kernel, len(weights), len(before)),
         grid_spec=pltpu.PrefetchScalarGridSpec(
             num_scalar_prefetch=2,
             grid=(2,),
             in_specs=[fixed(PAIR, D), fixed(D, PAIR), *[fixed(*w.shape) for w in weights],
                       wide(), narrow(TOK, 0), narrow(WIN, 0), narrow(WIN, 0),
                       wide(), narrow(TOK, 1), narrow(WIN, 1), narrow(WIN, 1)]
-            + [anywhere] * len(extra),
-            out_specs=[out(TOK), out(TOK), out(WIN), out(WIN), part, part, part, part],
+            + [anywhere] * len(before),
+            out_specs=[out(TOK), out(TOK), out(WIN), out(WIN), *[part(shape) for shape in parts]],
             scratch_shapes=[pair, pair, pair, pair, pool, pool, pool, pool,
                             pltpu.VMEM((4, D, HEAD_DIM), BF), pltpu.VMEM((4, D, HEAD_DIM), BF)],
         ),
         out_shape=[jax.ShapeDtypeStruct((2, rows, 2 * HALF), BF) for rows in (TOK, TOK, WIN, WIN)]
-        + [jax.ShapeDtypeStruct((4, 4, 128, HEAD_DIM), BF)] * 4,
-        input_output_aliases={17 + n: n for n in range(len(before))},
+        + [jax.ShapeDtypeStruct(shape, BF) for shape in parts],
+        input_output_aliases={12 + len(weights) + n: n for n in range(len(before))},
         compiler_params=pltpu.CompilerParams(vmem_limit_bytes=52 * MIB),
         cost_estimate=pl.CostEstimate(flops=12_000_000_000, bytes_accessed=24_000_000, transcendentals=500_000),
-    )(meta, me, x, xt, *weights, q, given, sent_a, sent_b, ct, given, sent_a, sent_b, *extra)
-
-
-def add_kernel(*refs):
-    ins, outs = refs[:4], refs[-4:]
+    )(meta, me, x, xt, *weights, q, given, sent_a, sent_b, ct, given, sent_a, sent_b, *before)
+
+
+def add_kernel(count, *refs):
+    ins, outs = refs[:count], refs[-4:]
     total = sum(ref[...].astype(jnp.float32) for ref in ins).astype(BF)
     for n, out in enumerate(outs):
         out[...] = total[n]
@@ -194,16 +198,16 @@
         source = pl.BlockSpec(shape, lambda i: (0, 0, 0))
         target = pl.BlockSpec(shape[1:], lambda i: (0, 0))
     return pl.pallas_call(
-        add_kernel,
+        functools.partial(add_kernel, len(parts)),
         grid=grid,
-        in_specs=[source] * 4 + [pl.BlockSpec(memory_space=pl.ANY)] * len(extra),
+        in_specs=[source] * len(parts) + [pl.BlockSpec(memory_space=pl.ANY)] * len(extra),
         out_specs=[target] * 4,
         out_shape=[jax.ShapeDtypeStruct(shape[1:], BF)] * 4,
         compiler_params=pltpu.CompilerParams(vmem_limit_bytes=16 * MIB),
     )(*parts, *extra)
 
 
-def depart_kernel(me, enc_len, dec_len, partner, q_ref, ct_ref, meta, info, a_ref, b_ref, give_ref):
+def depart_kernel(me, enc_len, dec_len, partner, q_ref, ct_ref, meta, info, a_ref, b_ref, give_ref, sems):
     core, x = me[2], me[3]
     t = me[0] * 4 + me[1]
 
@@ -250,44 +254,53 @@
             start = start + length
 
     rows = pl.ds(pl.multiple_of(info[0], 16), WIN)
+    copies = []
     for n in range(4):
         source = (q_ref, ct_ref)[n // 2]
+        cols = pl.ds(n * HALF, HALF)
         for side, out in ((core, a_ref), (1 - core, b_ref)):
-            begin = pl.multiple_of((n % 2) * 1024 + side * HALF, HALF)
-            out[:, n * HALF : (n + 1) * HALF] = source[rows, pl.ds(begin, HALF)]
-        give_ref[:, n * HALF : (n + 1) * HALF] = source[:, pl.ds(begin, HALF)]
+            begin = pl.ds(pl.multiple_of((n % 2) * 1024 + side * HALF, HALF), HALF)
+            copies.append((source.at[rows, begin], out.at[:, cols]))
+        copies.append((source.at[:, begin], give_ref.at[:, cols]))
+    copies = [pltpu.make_async_copy(a, b, sems.at[n]) for n, (a, b) in enumerate(copies)]
+    for copy in copies:
+        copy.start()
+    for copy in copies:
+        copy.wait()
 
 
 def depart(me, enc_lengths, dec_lengths, dec_partner, q, ct):
-    whole = pl.BlockSpec(memory_space=pltpu.VMEM)
+    whole = pl.BlockSpec(memory_space=pl.ANY)
     scalar = pl.BlockSpec(memory_space=pltpu.SMEM)
     return pl.pallas_call(
         depart_kernel,
         in_specs=[scalar, scalar, scalar, scalar, whole, whole],
         out_specs=[scalar, scalar, whole, whole, whole],
+        scratch_shapes=[pltpu.SemaphoreType.DMA((12,))],
         out_shape=[jax.ShapeDtypeStruct((2 * SEGS, 4), jnp.int32), jax.ShapeDtypeStruct((4,), jnp.int32)]
         + [jax.ShapeDtypeStruct((rows, 2048), BF) for rows in (WIN, WIN, TOK)],
         compiler_params=pltpu.CompilerParams(vmem_limit_bytes=16 * MIB),
     )(me, enc_lengths, dec_lengths, dec_partner, q, ct)
 
 
-def turn_kernel(a_ref, b_ref, x_ref, xt_ref):
+def turn_kernel(a_ref, b_ref, *refs):
+    x_ref, xt_ref = refs[-2:]
     for n, ref in enumerate((a_ref, b_ref)):
         value = ref[...]
         x_ref[n * TOK : (n + 1) * TOK, :] = value
         xt_ref[:, n * TOK : (n + 1) * TOK] = value.T
 
 
-def turn(a, b):
+def turn(a, b, after):
     part = pl.BlockSpec((TOK, 512), lambda i: (0, i))
     return pl.pallas_call(
         turn_kernel,
         grid=(D // 512,),
-        in_specs=[part, part],
+        in_specs=[part, part] + [pl.BlockSpec(memory_space=pl.ANY)] * len(after),
         out_specs=[pl.BlockSpec((PAIR, 512), lambda i: (0, i)), pl.BlockSpec((512, PAIR), lambda i: (i, 0))],
         out_shape=[jax.ShapeDtypeStruct((PAIR, D), BF), jax.ShapeDtypeStruct((D, PAIR), BF)],
         compiler_params=pltpu.CompilerParams(vmem_limit_bytes=16 * MIB),
-    )(a, b)
+    )(a, b, *after)
 
 
 def finish_kernel(info, *refs):
@@ -357,62 +370,107 @@
         refs[-1][n] = refs[n][..., cols]
 
 
-def join(parts, after, cols=slice(0, HEAD_DIM)):
+def join(parts, after, cols):
     whole = pl.BlockSpec(memory_space=pltpu.VMEM)
     return pl.pallas_call(
         functools.partial(join_kernel, cols),
         in_specs=[whole] * 4 + [pl.BlockSpec(memory_space=pl.ANY)] * len(after),
         out_specs=whole,
-        out_shape=jax.ShapeDtypeStruct((4,) + parts[0].shape[:-1] + (HEAD_DIM,), BF),
+        out_shape=jax.ShapeDtypeStruct((4,) + parts[0].shape[:-1] + (cols.stop - cols.start,), BF),
         compiler_params=pltpu.CompilerParams(vmem_limit_bytes=16 * MIB),
     )(*parts, *after)
 
 
+def pick_kernel(me, w_ref, got_ref, *refs):
+    mine = w_ref[:, pl.ds(pl.multiple_of(me[2] * HALF, HALF), HALF)]
+    for core in range(2):
+
+        @pl.when(me[2] == core)
+        def _():
+            refs[-1][core * 64 : core * 64 + 64, :] = mine
+            refs[-1][64 - core * 64 : 128 - core * 64, :] = got_ref[...]
+
+
+def pick(me, weights, got, after):
+    whole = pl.BlockSpec(memory_space=pltpu.VMEM)
+    return pl.pallas_call(
+        pick_kernel,
+        in_specs=[pl.BlockSpec(memory_space=pltpu.SMEM), whole, whole]
+        + [pl.BlockSpec(memory_space=pl.ANY)] * len(after),
+        out_specs=whole,
+        out_shape=jax.ShapeDtypeStruct((128, HALF), BF),
+    )(me, weights, got, *after)
+
+
 def ring(value, phase, amount):
     return lax.ppermute(value, ALL, shift(phase, -amount))
 
 
-def gather(kv_weights, c, ready, turned):
-    low, high = kv_weights[:, :HALF], kv_weights[:, HALF:]
-    mine, got = jnp.where(c == 0, low, high), swap(jnp.where(c == 0, high, low))
-    own = jnp.where(c == 0, jnp.concatenate([mine, got]), jnp.concatenate([got, mine]))
-    first = [own] + [ring(own, 2, n) for n in (1, 2, 3)]
-    chunks = []
-    for chunk in range(2):
-        cols = slice(chunk * HEAD_DIM, (chunk + 1) * HEAD_DIM)
-        part = join(first, chunks[0][:1] if chunk else [ready], cols)
-        part = join([part] + [ring(part, 1, n) for n in (1, 2, 3)], [] if chunk else [turned])
-        ahead, behind = ring(part, 0, 1), ring(part, 0, -1)
-        far_a, far_b = ring(behind[:2], 0, -1), ring(ahead[2:], 0, 1)
-        chunks.append([part, ahead, behind, far_a, far_b])
-    return chunks
+def fold_kernel(a_ref, b_ref, got_a, got_b, after, out_a, out_b):
+    for ref, got, out in ((a_ref, got_a, out_a), (b_ref, got_b, out_b)):
+        out[...] = (ref[...].astype(jnp.float32) + got[...].astype(jnp.float32)).astype(BF)
+
+
+def fold(ahead, behind, got_a, got_b, after):
+    def block(start):
+        return pl.BlockSpec((1, 4, 128, HEAD_DIM), lambda i: (i + start, 0, 0, 0))
+
+    whole = jax.ShapeDtypeStruct(ahead.shape, BF)
+    return pl.pallas_call(
+        fold_kernel,
+        grid=(2,),
+        in_specs=[block(0), block(2), block(0), block(0), pl.BlockSpec(memory_space=pl.ANY)],
+        out_specs=[block(0), block(2)],
+        out_shape=[whole, whole],
+        input_output_aliases={0: 0, 1: 1},
+        compiler_params=pltpu.CompilerParams(vmem_limit_bytes=16 * MIB),
+    )(ahead, behind, got_a, got_b, after)
+
+
+def scatter_ring(own, ahead, behind, far_a, far_b, after):
+    got_a = lax.ppermute(far_a, ALL, shift(0, 1))
+    got_b = lax.ppermute(far_b, ALL, shift(0, -1))
+    ahead, behind = fold(ahead, behind, got_a, got_b, after)
+    return [own, lax.ppermute(ahead, ALL, shift(0, 1)), lax.ppermute(behind, ALL, shift(0, -1))]
 
 
 def body(enc_hidden, kv_weights, queries, cotangent, enc_lengths, dec_lengths, dec_partner):
     z, y, c, x = (lax.axis_index(a) for a in ALL)
     me = jnp.stack([z, y, c, x]).astype(jnp.int32)
+    swapped = swap(enc_hidden)
     meta, info, leave_a, leave_b, give = depart(me, enc_lengths, dec_lengths, dec_partner, queries, cotangent)
-    tokens, tokens_t = turn(enc_hidden, swap(enc_hidden))
-    weights = gather(kv_weights, c, leave_a, tokens_t)
     sent_a = lax.ppermute(leave_a, DP, SEND_A)
     sent_b = lax.ppermute(leave_b, DP, SEND_B)
+
+    got = swap(jnp.where(c == 0, kv_weights[:, HALF:], kv_weights[:, :HALF]))
+    own = pick(me, kv_weights, got, [leave_a, swapped])
+    first = [own] + [ring(own, 2, n) for n in (1, 2, 3)]
+    part = join(first, [], slice(0, HALF))
+    second = [part] + [ring(part, 1, n) for n in (1, 2, 3)]
+    part = join(second, [], slice(0, HEAD_DIM))
+    tokens, tokens_t = turn(enc_hidden, swapped, [part])
+    ahead, behind = ring(part, 0, 1), ring(part, 0, -1)
+    weights = [[part, ahead, behind, ring(behind[:2], 0, -1), ring(ahead[2:], 0, 1)]]
+    part = join(second, [ahead, behind, sent_a, sent_b], slice(HEAD_DIM, HALF))
+    weights.append([part, ring(part, 0, 1), ring(part, 0, -1), ring(part, 0, 2)])
+
     shared = (meta, me, tokens, tokens_t)
     inputs = (queries, cotangent, swap(give), sent_a, sent_b)
 
-    results, parts = [], []
-    for chunk in range(2):
-        done = run_main(chunk, *shared, weights[chunk], *inputs, before=results, after=() if chunk else weights[1][1:3])
-        results = done[:4]
-        parts.append(exchange(done[4:], 0))
-    mine, other, far_a, far_b = results
+    *results, d0, d1, d3, d2 = run_main(0, *shared, weights[0], *inputs)
+    parts = exchange([d0, d1, d2, d3], 0)
+    *results, d0, d1, d3, far_a, far_b = run_main(1, *shared, weights[1], *inputs, before=results)
+    mine, other, back_a, back_b = results
     context, grad_queries = finish(
         info,
-        [mine, swap(other), lax.ppermute(far_a, DP, back(SEND_A)), lax.ppermute(far_b, DP, back(SEND_B))],
+        [mine, swap(other), lax.ppermute(back_a, DP, back(SEND_A)), lax.ppermute(back_b, DP, back(SEND_B))],
     )
 
-    second = add_parts(exchange(add_parts(parts[0], [mine]), 1))
+    first = add_parts(parts, [mine])
+    parts = scatter_ring(d0, d1, d3, far_a, far_b, first[0])
+    second = add_parts(exchange(first, 1))
     last = [exchange(second, 2)]
-    second = add_parts(exchange(add_parts(parts[1], [second[0]]), 1), [context])
+    second = add_parts(exchange(add_parts(parts, [second[0]]), 1), [context])
     last.append(exchange(second, 2))
     summed = jnp.concatenate(
         [sum(part.astype(jnp.float32) for part in parts) for parts in last], axis=1

time: 220 us -> 212 us (0.964); the launches traced: 217 us -> 212 us
  starting transfers between devices: 79.7 us -> 68.9 us
  local copies, waits for them, and re-layouts: 12.8 us -> 19.2 us
  waiting for transfers between devices: 62.8 us -> 59.7 us
    ppermute x2 -> x6, waiting for transfers between devices: 4.86 us -> 15.3 us  [the longest x1 10.9 us: body(): lax.ppermute(back_b, DP, back(SEND_B))]
    unnamed x43 -> x67, local copies, waits for them, and re-layouts: 12.7 us -> 19.1 us
    ppermute x18 -> x15, starting transfers between devices: 22.3 us -> 16.2 us  [exchange(): lax.ppermute(parts[r], ALL, shift(phase, r))]
    ppermute x2 -> x6, starting transfers between devices: 14.4 us -> 8.81 us  [the longest x1 2.22 us: scatter_ring(): got_b = lax.ppermute(far_b, ALL, shift(0, -1))]
    ppermute x18 -> x15, waiting for transfers between devices: 23.3 us -> 17.8 us  [exchange(): lax.ppermute(parts[r], ALL, shift(phase, r))]
    ppermute x17 -> x13, starting transfers between devices: 27.5 us -> 22.3 us  [ring(): return lax.ppermute(value, ALL, shift(phase, -amount))]
    ppermute x17 -> x13, waiting for transfers between devices: 30.8 us -> 25.6 us  [ring(): return lax.ppermute(value, ALL, shift(phase, -amount))]
    ppermute x5, waiting for transfers between devices: 3.88 us -> 1 us  [swap(): return lax.ppermute(value, 'c', [(0, 1), (1, 0)])]
  transfers between devices with their start and end apart: 44 -> 41, of which waited for: 13 -> 14; matrix products, arithmetic and copies ran while one was open for 2% -> 2% of each run, Pallas kernels for 27% -> 28%
where the time goes in v5:
time: 212 us
  starting transfers between devices  68.9 us (33%)
  Pallas kernels  61.1 us (29%)
  waiting for transfers between devices  59.7 us (28%)
  local copies, waits for them, and re-layouts  19.2 us (9%)
    pallas_call x2, Pallas kernels, run_main(): pl.pallas_call(functools.partial(main_kernel, len(weights), len(before)),...  46.5 us
    ppermute x13, waiting for transfers between devices, ring(): return lax.ppermute(value, ALL, shift(phase, -amount))  25.6 us
    ppermute x13, starting transfers between devices, ring(): return lax.ppermute(value, ALL, shift(phase, -amount))  22.3 us
    unnamed x67, local copies, waits for them, and re-layouts  19.1 us
    ppermute x15, waiting for transfers between devices, exchange(): lax.ppermute(parts[r], ALL, shift(phase, r))  17.8 us
    ppermute x15, starting transfers between devices, exchange(): lax.ppermute(parts[r], ALL, shift(phase, r))  16.2 us
    ppermute x5, starting transfers between devices, swap(): return lax.ppermute(value, 'c', [(0, 1), (1, 0)])  12.2 us
    ppermute x1, waiting for transfers between devices, body(): lax.ppermute(back_b, DP, back(SEND_B))  10.9 us
  transfers between devices with their start and end apart: 41, of which 14 were waited for; matrix products, arithmetic and copies ran while one was open for 2% of the time, Pallas kernels for 28%

profile of v5, /device:TPU:1, one launch (start us, length us, event | category | flops | bytes accessed | tf_op | source)
XLA Modules:
  0.0 211.7 jit_solution(17740335014441377910)
XLA Ops:
  8.7 5.3 %shard_map.94 = (s32[8,4]{1,0:T(8,128)S(1)}, s32[4]{0:T(128)S(1)}, bf16[176,2048]{1,0:T(8,128)(2,1)S(1)}, bf16[176,2048]{1,0:T(8,128)(2,1)S(1)}, bf16[512,2048]{1,0:T(8,128)(2,1)S(1)}) custom-call(s32[4]{0:T(128)S(1)} %pad_add_fusion.me, s32[128,4]{1,0:T(8,128)S(1)} %copy.16.enc_len, s32[128,4]{1,0:T(8,128)S(1)} %copy.17.dec_len, ...), custom_call_target="tpu_custom_call" | custom-call | tf_op jit(solution)/shard_map/pallas_call | solution.py:275
  20.7 2.6 %collective-permute-start.3 = (bf16[128,512]{1,0:T(8,128)(2,1)}, bf16[128,512]{1,0:T(8,128)(2,1)S(1)}, u32[]{:S(2)}, u32[]{:S(2)}) collective-permute-start(bf16[128,512]{1,0:T(8,128)(2,1)} %shard_map.95.refs_0_), channel_id=1, source_target_pairs={{0,64},{1,65},{2,66},{3,67},{4,20},{5,21},{6,22},{7,23},{8,72},{9,... | collective-permute-start | bytes 393224 | tf_op jit(solution)/shard_map/ppermute | solution.py:406
  24.7 2.6 %collective-permute-done.3.refs_2_ = bf16[128,512]{1,0:T(8,128)(2,1)S(1)} collective-permute-done((bf16[128,512]{1,0:T(8,128)(2,1)}, bf16[128,512]{1,0:T(8,128)(2,1)S(1)}, u32[]{:S(2)}, u32[]{:S(2)}) %collective-permute-start.3) | collective-permute-done | bytes 131104 | tf_op jit(solution)/shard_map/ppermute | solution.py:406
  29.5 2.5 %collective-permute-start.6 = (bf16[4,128,512]{2,1,0:T(8,128)(2,1)S(1)}, bf16[4,128,512]{2,1,0:T(8,128)(2,1)S(1)}, u32[]{:S(2)}, u32[]{:S(2)}) collective-permute-start(bf16[4,128,512]{2,1,0:T(8,128)(2,1)S(1)} %shard_map.96.refs_0_), channel_id=1, source_target_pairs={{0,16},{1,17},{2,18},{3,19},{4,6},{5,7},{6,4},{7,5},{8,24},{9,25},... | collective-permute-start | bytes 1572872 | tf_op jit(solution)/shard_map/ppermute | solution.py:406
  33.1 4.2 %collective-permute-start.15 = (bf16[512,2048]{1,0:T(8,128)(2,1)}, bf16[512,2048]{1,0:T(8,128)(2,1)S(1)}, u32[]{:S(2)}, u32[]{:S(2)}) collective-permute-start(bf16[512,2048]{1,0:T(8,128)(2,1)} %copy-done.25), channel_id=1, source_target_pairs={{0,4},{4,0},{1,5},{5,1},{2,6},{6,2},{3,7},{7,3},{8,12},{12,8},{9,1... | collective-permute-start | bytes 6291464 | tf_op jit(solution)/shard_map/ppermute | solution.py:340
  37.9 6.6 %collective-permute-done.6.refs_2_ = bf16[4,128,512]{2,1,0:T(8,128)(2,1)S(1)} collective-permute-done((bf16[4,128,512]{2,1,0:T(8,128)(2,1)S(1)}, bf16[4,128,512]{2,1,0:T(8,128)(2,1)S(1)}, u32[]{:S(2)}, u32[]{:S(2)}) %collective-permute-start.6) | collective-permute-done | bytes 524320 | tf_op jit(solution)/shard_map/ppermute | solution.py:406
  44.6 2.0 collective-permute-start.9
  46.6 2.2 %collective-permute-start.8 = (bf16[4,4,128,256]{3,2,1,0:T(8,128)(2,1)S(1)}, bf16[4,4,128,256]{3,2,1,0:T(8,128)(2,1)S(1)}, u32[]{:S(2)}, u32[]{:S(2)}) collective-permute-start(bf16[4,4,128,256]{3,2,1,0:T(8,128)(2,1)S(1)} %shard_map.97.refs_0_), channel_id=1, source_target_pairs={{0,3},{1,0},{2,1},{3,2},{4,100},{5,101},{6,102},{7,103},{8,11},{9,... | collective-permute-start | bytes 3145736 | tf_op jit(solution)/shard_map/ppermute | solution.py:406
  48.8 6.6 %collective-permute-start.11 = (bf16[176,2048]{1,0:T(8,128)(2,1)S(1)}, bf16[176,2048]{1,0:T(8,128)(2,1)S(1)}, u32[]{:S(2)}, u32[]{:S(2)}) collective-permute-start(bf16[176,2048]{1,0:T(8,128)(2,1)S(1)} %get-tuple-element.52), channel_id=1, source_target_pairs={{8,4},{16,12},{24,20},{32,28},{40,36},{48,44},{56,52},{64,60},{72,... | collective-permute-start | bytes 2162696 | tf_op jit(solution)/shard_map/ppermute | solution.py:443
  55.4 2.8 %collective-permute-start.10 = (bf16[176,2048]{1,0:T(8,128)(2,1)S(1)}, bf16[176,2048]{1,0:T(8,128)(2,1)S(1)}, u32[]{:S(2)}, u32[]{:S(2)}) collective-permute-start(bf16[176,2048]{1,0:T(8,128)(2,1)S(1)} %copy-done.19), channel_id=1, source_target_pairs={{8,0},{16,8},{24,16},{32,24},{40,32},{48,40},{56,48},{64,56},{72,6... | collective-permute-start | bytes 2162696 | tf_op jit(solution)/shard_map/ppermute | solution.py:442
  58.2 15.5 %collective-permute-done.9.refs_5_.refs_2_ = bf16[4,4,128,256]{3,2,1,0:T(8,128)(2,1)S(1)} collective-permute-done((bf16[4,4,128,256]{3,2,1,0:T(8,128)(2,1)S(1)}, bf16[4,4,128,256]{3,2,1,0:T(8,128)(2,1)S(1)}, u32[]{:S(2)}, u32[]{:S(2)}) %collective-permute-start.9) | collective-permute-done | bytes 1048608 | tf_op jit(solution)/shard_map/ppermute | solution.py:406
  73.8 2.0 collective-permute-start.16
  75.8 2.2 %collective-permute-start.17 = (bf16[2,4,128,256]{3,2,1,0:T(8,128)(2,1)S(1)}, bf16[2,4,128,256]{3,2,1,0:T(8,128)(2,1)S(1)}, u32[]{:S(2)}, u32[]{:S(2)}) collective-permute-start(bf16[2,4,128,256]{3,2,1,0:T(8,128)(2,1)S(1)} %slice.25), channel_id=1, source_target_pairs={{0,3},{1,0},{2,1},{3,2},{4,100},{5,101},{6,102},{7,103},{8,11},{9,... | collective-permute-start | bytes 1572872 | tf_op jit(solution)/shard_map/ppermute | solution.py:406
  78.0 2.1 %shard_map.98 = (bf16[1024,2048]{1,0:T(8,128)(2,1)S(1)}, bf16[2048,1024]{1,0:T(8,128)(2,1)S(1)}) custom-call(bf16[512,2048]{1,0:T(8,128)(2,1)S(1)} %copy-done.8, bf16[512,2048]{1,0:T(8,128)(2,1)S(1)} %copy-done.3, bf16[4,4,128,256]{3,2,1,0:T(8,128)(2,1)S(1)} %shard_map.97.refs_0_), custom_call_target="tpu_custom_call" | custom-call | tf_op jit(solution)/shard_map/pallas_call | solution.py:296
  80.2 2.0 copy-done.24
  86.6 1.9 collective-permute-start.12
  88.6 23.2 %shard_map.100 = (bf16[2,512,1024]{2,1,0:T(8,128)(2,1)}, bf16[2,512,1024]{2,1,0:T(8,128)(2,1)}, bf16[2,176,1024]{2,1,0:T(8,128)(2,1)S(1)}, bf16[2,176,1024]{2,1,...) custom-call(s32[8,4]{1,0:T(8,128)S(1)} %get-tuple-element.48.meta, ...), custom_call_target="tpu_custom_call" | custom-call | flops 12000000000 | bytes 24000000 | tf_op jit(solution)/shard_map/pallas_call | solution.py:160
  111.9 2.7 %collective-permute-start.22 = (bf16[4,4,128,256]{3,2,1,0:T(8,128)(2,1)}, bf16[4,4,128,256]{3,2,1,0:T(8,128)(2,1)S(1)}, u32[]{:S(2)}, u32[]{:S(2)}) collective-permute-start(bf16[4,4,128,256]{3,2,1,0:T(8,128)(2,1)} %get-tuple-element.66), channel_id=1, source_target_pairs={{0,3},{1,0},{2,1},{3,2},{4,100},{5,101},{6,102},{7,103},{8,11},{9,... | collective-permute-start | bytes 3145736 | tf_op jit(solution)/shard_map/ppermute | solution.py:365
  116.3 23.3 %shard_map.101 = (bf16[2,512,1024]{2,1,0:T(8,128)(2,1)}, bf16[2,512,1024]{2,1,0:T(8,128)(2,1)}, bf16[2,176,1024]{2,1,0:T(8,128)(2,1)S(1)}, bf16[2,176,1024]{2,1,...) custom-call(s32[8,4]{1,0:T(8,128)S(1)} %get-tuple-element.48.meta, ...), custom_call_target="tpu_custom_call", output_to_operand_aliasing={{0}: (16, {}), {1}: (17, {}), {2}: (18, {}), {3}: (19, {})} | custom-call | flops 12000000000 | bytes 24000000 | tf_op jit(solution)/shard_map/pallas_call | solution.py:160
  140.2 2.2 %collective-permute-start.31 = (bf16[2,4,128,256]{3,2,1,0:T(8,128)(2,1)S(1)}, bf16[2,4,128,256]{3,2,1,0:T(8,128)(2,1)S(1)}, u32[]{:S(2)}, u32[]{:S(2)}) collective-permute-start(bf16[2,4,128,256]{3,2,1,0:T(8,128)(2,1)S(1)} %get-tuple-element.80), channel_id=1, source_target_pairs={{0,3},{1,0},{2,1},{3,2},{4,100},{5,101},{6,102},{7,103},{8,11},{9,... | collective-permute-start | bytes 1572872 | tf_op jit(solution)/shard_map/ppermute | solution.py:432
  144.9 4.3 %collective-permute-done.30.got_a = bf16[2,4,128,256]{3,2,1,0:T(8,128)(2,1)S(1)} collective-permute-done((bf16[2,4,128,256]{3,2,1,0:T(8,128)(2,1)S(1)}, bf16[2,4,128,256]{3,2,1,0:T(8,128)(2,1)S(1)}, u32[]{:S(2)}, u32[]{:S(2)}) %collective-permute-start.30) | collective-permute-done | bytes 524320 | tf_op jit(solution)/shard_map/ppermute | solution.py:431
  152.9 2.1 collective-permute-start.25
  155.0 6.8 %collective-permute-done.24.refs_1_ = bf16[4,128,256]{2,1,0:T(8,128)(2,1)S(1)} collective-permute-done((bf16[4,128,256]{2,1,0:T(8,128)(2,1)S(1)}, bf16[4,128,256]{2,1,0:T(8,128)(2,1)S(1)}, u32[]{:S(2)}, u32[]{:S(2)}) %collective-permute-start.24) | collective-permute-done | bytes 262176 | tf_op jit(solution)/shard_map/ppermute | solution.py:365
  164.0 7.5 %collective-permute-done.26.refs_3_ = bf16[4,128,256]{2,1,0:T(8,128)(2,1)S(1)} collective-permute-done((bf16[4,128,256]{2,1,0:T(8,128)(2,1)S(1)}, bf16[4,128,256]{2,1,0:T(8,128)(2,1)S(1)}, u32[]{:S(2)}, u32[]{:S(2)}) %collective-permute-start.26) | collective-permute-done | bytes 262176 | tf_op jit(solution)/shard_map/ppermute | solution.py:365
  171.5 2.0 collective-permute-start.20
  174.5 2.7 %collective-permute-start.35 = (bf16[4,128,256]{2,1,0:T(8,128)(2,1)S(1)}, bf16[4,128,256]{2,1,0:T(8,128)(2,1)S(1)}, u32[]{:S(2)}, u32[]{:S(2)}) collective-permute-start(bf16[4,128,256]{2,1,0:T(8,128)(2,1)S(1)} %get-tuple-element.85), channel_id=1, source_target_pairs={{0,24},{1,25},{2,26},{3,27},{4,7},{5,4},{6,5},{7,6},{8,0},{9,1},{1... | collective-permute-start | bytes 786440 | tf_op jit(solution)/shard_map/ppermute | solution.py:365
  177.2 10.9 %collective-permute-done.20.refs_3_ = bf16[2,176,1024]{2,1,0:T(8,128)(2,1)S(1)} collective-permute-done((bf16[2,176,1024]{2,1,0:T(8,128)(2,1)S(1)}, bf16[2,176,1024]{2,1,0:T(8,128)(2,1)S(1)}, u32[]{:S(2)}, u32[]{:S(2)}) %collective-permute-start.20) | collective-permute-done | bytes 720928 | tf_op jit(solution)/shard_map/ppermute | solution.py:466
  188.1 2.7 %collective-permute-start.28 = (bf16[128,256]{1,0:T(8,128)(2,1)S(1)}, bf16[128,256]{1,0:T(8,128)(2,1)S(1)}, u32[]{:S(2)}, u32[]{:S(2)}) collective-permute-start(bf16[128,256]{1,0:T(8,128)(2,1)S(1)} %get-tuple-element.74), channel_id=1, source_target_pairs={{0,96},{1,97},{2,98},{3,99},{4,28},{5,29},{6,30},{7,31},{8,104},{9... | collective-permute-start | bytes 196616 | tf_op jit(solution)/shard_map/ppermute | solution.py:365
  191.4 3.2 %shard_map.102 = (bf16[512,2048]{1,0:T(8,128)(2,1)}, bf16[512,2048]{1,0:T(8,128)(2,1)}) custom-call(s32[4]{0:T(128)S(1)} %get-tuple-element.47.info, bf16[2,512,1024]{2,1,0:T(8,128)(2,1)S(1)} %copy-done.1, bf16[2,512,1024]{2,1,0:T(8,128)(2,1)S(1)} %collective-permute-done.18.refs_1_, bf16[2,176,1024]{2,1,0:T(8,128)(2,1)S(1)} %collective-permute-done.19.refs_2_, ...), custom_call_target="tpu_custom_call" | custom-call | tf_op jit(solution)/shard_map/pallas_call | solution.py:326
  196.7 2.3 %collective-permute-start.38 = (bf16[128,256]{1,0:T(8,128)(2,1)S(1)}, bf16[128,256]{1,0:T(8,128)(2,1)S(1)}, u32[]{:S(2)}, u32[]{:S(2)}) collective-permute-start(bf16[128,256]{1,0:T(8,128)(2,1)S(1)} %get-tuple-element.89), channel_id=1, source_target_pairs={{0,96},{1,97},{2,98},{3,99},{4,28},{5,29},{6,30},{7,31},{8,104},{9... | collective-permute-start | bytes 196616 | tf_op jit(solution)/shard_map/ppermute | solution.py:365
  201.0 2.7 %collective-permute-done.39 = bf16[128,256]{1,0:T(8,128)(2,1)S(1)} collective-permute-done((bf16[128,256]{1,0:T(8,128)(2,1)S(1)}, bf16[128,256]{1,0:T(8,128)(2,1)S(1)}, u32[]{:S(2)}, u32[]{:S(2)}) %collective-permute-start.39) | collective-permute-done | bytes 65568 | tf_op jit(solution)/shard_map/ppermute | solution.py:365
  203.8 6.2 %collective-permute-start.40 = (f32[64,512]{1,0:T(8,128)S(1)}, f32[64,512]{1,0:T(8,128)S(1)}, u32[]{:S(2)}, u32[]{:S(2)}) collective-permute-start(f32[64,512]{1,0:T(8,128)S(1)} %broadcast_select_fusion.2), channel_id=1, source_target_pairs={{0,4},{4,0},{1,5},{5,1},{2,6},{6,2},{3,7},{7,3},{8,12},{12,8},{9,1... | collective-permute-start | bytes 393224 | tf_op jit(solution)/shard_map/ppermute | solution.py:340
  (140 shorter events, 42.4 us)
Async XLA Ops:
  0.6 15.7 %collective-permute-start = (bf16[512,2048]{1,0:T(8,128)(2,1)}, bf16[512,2048]{1,0:T(8,128)(2,1)S(1)}, u32[]{:S(2)}, u32[]{:S(2)}) collective-permute-start(bf16[512,2048]{1,0:T(8,128)(2,1)} %a_ref.1), channel_id=1, source_target_pairs={{0,4},{4,0},{1,5},{5,1},{2,6},{6,2},{3,7},{7,3},{8,12},{12,8},{9,1... | collective-permute-start | bytes 6291464 | tf_op jit(solution)/shard_map/ppermute | solution.py:340
  3.0 13.3 %collective-permute-start.1 = (bf16[64,512]{1,0:T(8,128)(2,1)S(1)}, bf16[64,512]{1,0:T(8,128)(2,1)S(1)}, u32[]{:S(2)}, u32[]{:S(2)}) collective-permute-start(bf16[64,512]{1,0:T(8,128)(2,1)S(1)} %slice_select_fusion), channel_id=1, source_target_pairs={{0,4},{4,0},{1,5},{5,1},{2,6},{6,2},{3,7},{7,3},{8,12},{12,8},{9,1... | collective-permute-start | bytes 196616 | tf_op jit(solution)/shard_map/ppermute | solution.py:340
  28.3 9.6 %collective-permute-start.7 = (bf16[4,128,512]{2,1,0:T(8,128)(2,1)S(1)}, bf16[4,128,512]{2,1,0:T(8,128)(2,1)S(1)}, u32[]{:S(2)}, u32[]{:S(2)}) collective-permute-start(bf16[4,128,512]{2,1,0:T(8,128)(2,1)S(1)} %shard_map.96.refs_0_), channel_id=1, source_target_pairs={{0,8},{1,9},{2,10},{3,11},{4,5},{5,6},{6,7},{7,4},{8,16},{9,17},{1... | collective-permute-start | bytes 1572872 | tf_op jit(solution)/shard_map/ppermute | solution.py:406
  29.5 14.9 %collective-permute-start.6 = (bf16[4,128,512]{2,1,0:T(8,128)(2,1)S(1)}, bf16[4,128,512]{2,1,0:T(8,128)(2,1)S(1)}, u32[]{:S(2)}, u32[]{:S(2)}) collective-permute-start(bf16[4,128,512]{2,1,0:T(8,128)(2,1)S(1)} %shard_map.96.refs_0_), channel_id=1, source_target_pairs={{0,16},{1,17},{2,18},{3,19},{4,6},{5,7},{6,4},{7,5},{8,24},{9,25},... | collective-permute-start | bytes 1572872 | tf_op jit(solution)/shard_map/ppermute | solution.py:406
  32.0 12.5 %collective-permute-start.5 = (bf16[4,128,512]{2,1,0:T(8,128)(2,1)S(1)}, bf16[4,128,512]{2,1,0:T(8,128)(2,1)S(1)}, u32[]{:S(2)}, u32[]{:S(2)}) collective-permute-start(bf16[4,128,512]{2,1,0:T(8,128)(2,1)S(1)} %shard_map.96.refs_0_), channel_id=1, source_target_pairs={{0,24},{1,25},{2,26},{3,27},{4,7},{5,4},{6,5},{7,6},{8,0},{9,1},{1... | collective-permute-start | bytes 1572872 | tf_op jit(solution)/shard_map/ppermute | solution.py:406
  33.1 53.5 %collective-permute-start.15 = (bf16[512,2048]{1,0:T(8,128)(2,1)}, bf16[512,2048]{1,0:T(8,128)(2,1)S(1)}, u32[]{:S(2)}, u32[]{:S(2)}) collective-permute-start(bf16[512,2048]{1,0:T(8,128)(2,1)} %copy-done.25), channel_id=1, source_target_pairs={{0,4},{4,0},{1,5},{5,1},{2,6},{6,2},{3,7},{7,3},{8,12},{12,8},{9,1... | collective-permute-start | bytes 6291464 | tf_op jit(solution)/shard_map/ppermute | solution.py:340
  44.6 29.2 %collective-permute-start.9 = (bf16[4,4,128,256]{3,2,1,0:T(8,128)(2,1)S(1)}, bf16[4,4,128,256]{3,2,1,0:T(8,128)(2,1)S(1)}, u32[]{:S(2)}, u32[]{:S(2)}) collective-permute-start(bf16[4,4,128,256]{3,2,1,0:T(8,128)(2,1)S(1)} %shard_map.97.refs_0_), channel_id=1, source_target_pairs={{0,1},{1,2},{2,3},{3,0},{4,36},{5,37},{6,38},{7,39},{8,9},{9,10},{... | collective-permute-start | bytes 3145736 | tf_op jit(solution)/shard_map/ppermute | solution.py:406
  46.6 29.2 %collective-permute-start.8 = (bf16[4,4,128,256]{3,2,1,0:T(8,128)(2,1)S(1)}, bf16[4,4,128,256]{3,2,1,0:T(8,128)(2,1)S(1)}, u32[]{:S(2)}, u32[]{:S(2)}) collective-permute-start(bf16[4,4,128,256]{3,2,1,0:T(8,128)(2,1)S(1)} %shard_map.97.refs_0_), channel_id=1, source_target_pairs={{0,3},{1,0},{2,1},{3,2},{4,100},{5,101},{6,102},{7,103},{8,11},{9,... | collective-permute-start | bytes 3145736 | tf_op jit(solution)/shard_map/ppermute | solution.py:406
  48.8 33.5 %collective-permute-start.11 = (bf16[176,2048]{1,0:T(8,128)(2,1)S(1)}, bf16[176,2048]{1,0:T(8,128)(2,1)S(1)}, u32[]{:S(2)}, u32[]{:S(2)}) collective-permute-start(bf16[176,2048]{1,0:T(8,128)(2,1)S(1)} %get-tuple-element.52), channel_id=1, source_target_pairs={{8,4},{16,12},{24,20},{32,28},{40,36},{48,44},{56,52},{64,60},{72,... | collective-permute-start | bytes 2162696 | tf_op jit(solution)/shard_map/ppermute | solution.py:443
  55.4 26.9 %collective-permute-start.10 = (bf16[176,2048]{1,0:T(8,128)(2,1)S(1)}, bf16[176,2048]{1,0:T(8,128)(2,1)S(1)}, u32[]{:S(2)}, u32[]{:S(2)}) collective-permute-start(bf16[176,2048]{1,0:T(8,128)(2,1)S(1)} %copy-done.19), channel_id=1, source_target_pairs={{8,0},{16,8},{24,16},{32,24},{40,32},{48,40},{56,48},{64,56},{72,6... | collective-permute-start | bytes 2162696 | tf_op jit(solution)/shard_map/ppermute | solution.py:442
  73.8 14.8 %collective-permute-start.16 = (bf16[2,4,128,256]{3,2,1,0:T(8,128)(2,1)S(1)}, bf16[2,4,128,256]{3,2,1,0:T(8,128)(2,1)S(1)}, u32[]{:S(2)}, u32[]{:S(2)}) collective-permute-start(bf16[2,4,128,256]{3,2,1,0:T(8,128)(2,1)S(1)} %slice.24), channel_id=1, source_target_pairs={{0,1},{1,2},{2,3},{3,0},{4,36},{5,37},{6,38},{7,39},{8,9},{9,10},{... | collective-permute-start | bytes 1572872 | tf_op jit(solution)/shard_map/ppermute | solution.py:406
  75.8 12.8 %collective-permute-start.17 = (bf16[2,4,128,256]{3,2,1,0:T(8,128)(2,1)S(1)}, bf16[2,4,128,256]{3,2,1,0:T(8,128)(2,1)S(1)}, u32[]{:S(2)}, u32[]{:S(2)}) collective-permute-start(bf16[2,4,128,256]{3,2,1,0:T(8,128)(2,1)S(1)} %slice.25), channel_id=1, source_target_pairs={{0,3},{1,0},{2,1},{3,2},{4,100},{5,101},{6,102},{7,103},{8,11},{9,... | collective-permute-start | bytes 1572872 | tf_op jit(solution)/shard_map/ppermute | solution.py:406
  84.6 30.0 %collective-permute-start.14 = (bf16[4,4,128,256]{3,2,1,0:T(8,128)(2,1)S(1)}, bf16[4,4,128,256]{3,2,1,0:T(8,128)(2,1)S(1)}, u32[]{:S(2)}, u32[]{:S(2)}) collective-permute-start(bf16[4,4,128,256]{3,2,1,0:T(8,128)(2,1)S(1)} %shard_map.99.refs_0_), channel_id=1, source_target_pairs={{0,2},{1,3},{2,0},{3,1},{4,68},{5,69},{6,70},{7,71},{8,10},{9,11},... | collective-permute-start | bytes 3145736 | tf_op jit(solution)/shard_map/ppermute | solution.py:406
  85.9 28.8 %collective-permute-start.13 = (bf16[4,4,128,256]{3,2,1,0:T(8,128)(2,1)S(1)}, bf16[4,4,128,256]{3,2,1,0:T(8,128)(2,1)S(1)}, u32[]{:S(2)}, u32[]{:S(2)}) collective-permute-start(bf16[4,4,128,256]{3,2,1,0:T(8,128)(2,1)S(1)} %shard_map.99.refs_0_), channel_id=1, source_target_pairs={{0,1},{1,2},{2,3},{3,0},{4,36},{5,37},{6,38},{7,39},{8,9},{9,10},{... | collective-permute-start | bytes 3145736 | tf_op jit(solution)/shard_map/ppermute | solution.py:406
  86.6 28.1 %collective-permute-start.12 = (bf16[4,4,128,256]{3,2,1,0:T(8,128)(2,1)S(1)}, bf16[4,4,128,256]{3,2,1,0:T(8,128)(2,1)S(1)}, u32[]{:S(2)}, u32[]{:S(2)}) collective-permute-start(bf16[4,4,128,256]{3,2,1,0:T(8,128)(2,1)S(1)} %shard_map.99.refs_0_), channel_id=1, source_target_pairs={{0,3},{1,0},{2,1},{3,2},{4,100},{5,101},{6,102},{7,103},{8,11},{9,... | collective-permute-start | bytes 3145736 | tf_op jit(solution)/shard_map/ppermute | solution.py:406
  111.8 28.3 %collective-permute-start.21 = (bf16[4,4,128,256]{3,2,1,0:T(8,128)(2,1)}, bf16[4,4,128,256]{3,2,1,0:T(8,128)(2,1)S(1)}, u32[]{:S(2)}, u32[]{:S(2)}) collective-permute-start(bf16[4,4,128,256]{3,2,1,0:T(8,128)(2,1)} %get-tuple-element.65), channel_id=1, source_target_pairs={{0,1},{1,2},{2,3},{3,0},{4,36},{5,37},{6,38},{7,39},{8,9},{9,10},{... | collective-permute-start | bytes 3145736 | tf_op jit(solution)/shard_map/ppermute | solution.py:365
  111.9 30.5 %collective-permute-start.22 = (bf16[4,4,128,256]{3,2,1,0:T(8,128)(2,1)}, bf16[4,4,128,256]{3,2,1,0:T(8,128)(2,1)S(1)}, u32[]{:S(2)}, u32[]{:S(2)}) collective-permute-start(bf16[4,4,128,256]{3,2,1,0:T(8,128)(2,1)} %get-tuple-element.66), channel_id=1, source_target_pairs={{0,3},{1,0},{2,1},{3,2},{4,100},{5,101},{6,102},{7,103},{8,11},{9,... | collective-permute-start | bytes 3145736 | tf_op jit(solution)/shard_map/ppermute | solution.py:365
  114.6 27.8 %collective-permute-start.23 = (bf16[4,4,128,256]{3,2,1,0:T(8,128)(2,1)}, bf16[4,4,128,256]{3,2,1,0:T(8,128)(2,1)S(1)}, u32[]{:S(2)}, u32[]{:S(2)}) collective-permute-start(bf16[4,4,128,256]{3,2,1,0:T(8,128)(2,1)} %get-tuple-element.67), channel_id=1, source_target_pairs={{0,2},{1,3},{2,0},{3,1},{4,68},{5,69},{6,70},{7,71},{8,10},{9,11},... | collective-permute-start | bytes 3145736 | tf_op jit(solution)/shard_map/ppermute | solution.py:365
  139.6 51.2 %collective-permute-start.18 = (bf16[2,512,1024]{2,1,0:T(8,128)(2,1)}, bf16[2,512,1024]{2,1,0:T(8,128)(2,1)S(1)}, u32[]{:S(2)}, u32[]{:S(2)}) collective-permute-start(bf16[2,512,1024]{2,1,0:T(8,128)(2,1)} %get-tuple-element.59), channel_id=1, source_target_pairs={{0,4},{4,0},{1,5},{5,1},{2,6},{6,2},{3,7},{7,3},{8,12},{12,8},{9,1... | collective-permute-start | bytes 6291464 | tf_op jit(solution)/shard_map/ppermute | solution.py:340
  139.7 9.6 %collective-permute-start.30 = (bf16[2,4,128,256]{3,2,1,0:T(8,128)(2,1)S(1)}, bf16[2,4,128,256]{3,2,1,0:T(8,128)(2,1)S(1)}, u32[]{:S(2)}, u32[]{:S(2)}) collective-permute-start(bf16[2,4,128,256]{3,2,1,0:T(8,128)(2,1)S(1)} %get-tuple-element.79), channel_id=1, source_target_pairs={{0,1},{1,2},{2,3},{3,0},{4,36},{5,37},{6,38},{7,39},{8,9},{9,10},{... | collective-permute-start | bytes 1572872 | tf_op jit(solution)/shard_map/ppermute | solution.py:431
  149.6 24.1 %collective-permute-start.32 = (bf16[4,4,128,256]{3,2,1,0:T(8,128)(2,1)S(1)}, bf16[4,4,128,256]{3,2,1,0:T(8,128)(2,1)S(1)}, u32[]{:S(2)}, u32[]{:S(2)}) collective-permute-start(bf16[4,4,128,256]{3,2,1,0:T(8,128)(2,1)S(1)} %get-tuple-element.81), channel_id=1, source_target_pairs={{0,1},{1,2},{2,3},{3,0},{4,36},{5,37},{6,38},{7,39},{8,9},{9,10},{... | collective-permute-start | bytes 3145736 | tf_op jit(solution)/shard_map/ppermute | solution.py:434
  150.7 23.0 %collective-permute-start.33 = (bf16[4,4,128,256]{3,2,1,0:T(8,128)(2,1)S(1)}, bf16[4,4,128,256]{3,2,1,0:T(8,128)(2,1)S(1)}, u32[]{:S(2)}, u32[]{:S(2)}) collective-permute-start(bf16[4,4,128,256]{3,2,1,0:T(8,128)(2,1)S(1)} %get-tuple-element.82), channel_id=1, source_target_pairs={{0,3},{1,0},{2,1},{3,2},{4,100},{5,101},{6,102},{7,103},{8,11},{9,... | collective-permute-start | bytes 3145736 | tf_op jit(solution)/shard_map/ppermute | solution.py:434
  152.4 9.5 %collective-permute-start.24 = (bf16[4,128,256]{2,1,0:T(8,128)(2,1)S(1)}, bf16[4,128,256]{2,1,0:T(8,128)(2,1)S(1)}, u32[]{:S(2)}, u32[]{:S(2)}) collective-permute-start(bf16[4,128,256]{2,1,0:T(8,128)(2,1)S(1)} %get-tuple-element.69), channel_id=1, source_target_pairs={{0,8},{1,9},{2,10},{3,11},{4,5},{5,6},{6,7},{7,4},{8,16},{9,17},{1... | collective-permute-start | bytes 786440 | tf_op jit(solution)/shard_map/ppermute | solution.py:365
  152.9 9.8 %collective-permute-start.25 = (bf16[4,128,256]{2,1,0:T(8,128)(2,1)S(1)}, bf16[4,128,256]{2,1,0:T(8,128)(2,1)S(1)}, u32[]{:S(2)}, u32[]{:S(2)}) collective-permute-start(bf16[4,128,256]{2,1,0:T(8,128)(2,1)S(1)} %get-tuple-element.70), channel_id=1, source_target_pairs={{0,24},{1,25},{2,26},{3,27},{4,7},{5,4},{6,5},{7,6},{8,0},{9,1},{1... | collective-permute-start | bytes 786440 | tf_op jit(solution)/shard_map/ppermute | solution.py:365
  161.9 9.6 %collective-permute-start.26 = (bf16[4,128,256]{2,1,0:T(8,128)(2,1)S(1)}, bf16[4,128,256]{2,1,0:T(8,128)(2,1)S(1)}, u32[]{:S(2)}, u32[]{:S(2)}) collective-permute-start(bf16[4,128,256]{2,1,0:T(8,128)(2,1)S(1)} %get-tuple-element.71), channel_id=1, source_target_pairs={{0,16},{1,17},{2,18},{3,19},{4,6},{5,7},{6,4},{7,5},{8,24},{9,25},... | collective-permute-start | bytes 786440 | tf_op jit(solution)/shard_map/ppermute | solution.py:365
  162.7 14.5 %collective-permute-start.19 = (bf16[2,176,1024]{2,1,0:T(8,128)(2,1)S(1)}, bf16[2,176,1024]{2,1,0:T(8,128)(2,1)S(1)}, u32[]{:S(2)}, u32[]{:S(2)}) collective-permute-start(bf16[2,176,1024]{2,1,0:T(8,128)(2,1)S(1)} %get-tuple-element.60), channel_id=1, source_target_pairs={{0,8},{8,16},{16,24},{24,32},{32,40},{40,48},{48,56},{56,64},{64,7... | collective-permute-start | bytes 2162696 | tf_op jit(solution)/shard_map/ppermute | solution.py:466
  171.5 16.6 %collective-permute-start.20 = (bf16[2,176,1024]{2,1,0:T(8,128)(2,1)S(1)}, bf16[2,176,1024]{2,1,0:T(8,128)(2,1)S(1)}, u32[]{:S(2)}, u32[]{:S(2)}) collective-permute-start(bf16[2,176,1024]{2,1,0:T(8,128)(2,1)S(1)} %copy-done.31), channel_id=1, source_target_pairs={{4,8},{12,16},{20,24},{28,32},{36,40},{44,48},{52,56},{60,64},{68,... | collective-permute-start | bytes 2162696 | tf_op jit(solution)/shard_map/ppermute | solution.py:466
  174.4 13.7 %collective-permute-start.34 = (bf16[4,128,256]{2,1,0:T(8,128)(2,1)S(1)}, bf16[4,128,256]{2,1,0:T(8,128)(2,1)S(1)}, u32[]{:S(2)}, u32[]{:S(2)}) collective-permute-start(bf16[4,128,256]{2,1,0:T(8,128)(2,1)S(1)} %get-tuple-element.84), channel_id=1, source_target_pairs={{0,8},{1,9},{2,10},{3,11},{4,5},{5,6},{6,7},{7,4},{8,16},{9,17},{1... | collective-permute-start | bytes 786440 | tf_op jit(solution)/shard_map/ppermute | solution.py:365
  174.5 20.1 %collective-permute-start.35 = (bf16[4,128,256]{2,1,0:T(8,128)(2,1)S(1)}, bf16[4,128,256]{2,1,0:T(8,128)(2,1)S(1)}, u32[]{:S(2)}, u32[]{:S(2)}) collective-permute-start(bf16[4,128,256]{2,1,0:T(8,128)(2,1)S(1)} %get-tuple-element.85), channel_id=1, source_target_pairs={{0,24},{1,25},{2,26},{3,27},{4,7},{5,4},{6,5},{7,6},{8,0},{9,1},{1... | collective-permute-start | bytes 786440 | tf_op jit(solution)/shard_map/ppermute | solution.py:365
  177.2 17.4 %collective-permute-start.36 = (bf16[4,128,256]{2,1,0:T(8,128)(2,1)S(1)}, bf16[4,128,256]{2,1,0:T(8,128)(2,1)S(1)}, u32[]{:S(2)}, u32[]{:S(2)}) collective-permute-start(bf16[4,128,256]{2,1,0:T(8,128)(2,1)S(1)} %get-tuple-element.86), channel_id=1, source_target_pairs={{0,16},{1,17},{2,18},{3,19},{4,6},{5,7},{6,4},{7,5},{8,24},{9,25},... | collective-permute-start | bytes 786440 | tf_op jit(solution)/shard_map/ppermute | solution.py:365
  188.1 11.0 %collective-permute-start.27 = (bf16[128,256]{1,0:T(8,128)(2,1)S(1)}, bf16[128,256]{1,0:T(8,128)(2,1)S(1)}, u32[]{:S(2)}, u32[]{:S(2)}) collective-permute-start(bf16[128,256]{1,0:T(8,128)(2,1)S(1)} %get-tuple-element.73), channel_id=1, source_target_pairs={{0,32},{1,33},{2,34},{3,35},{4,12},{5,13},{6,14},{7,15},{8,40},{9,... | collective-permute-start | bytes 196616 | tf_op jit(solution)/shard_map/ppermute | solution.py:365
  188.1 12.1 %collective-permute-start.28 = (bf16[128,256]{1,0:T(8,128)(2,1)S(1)}, bf16[128,256]{1,0:T(8,128)(2,1)S(1)}, u32[]{:S(2)}, u32[]{:S(2)}) collective-permute-start(bf16[128,256]{1,0:T(8,128)(2,1)S(1)} %get-tuple-element.74), channel_id=1, source_target_pairs={{0,96},{1,97},{2,98},{3,99},{4,28},{5,29},{6,30},{7,31},{8,104},{9... | collective-permute-start | bytes 196616 | tf_op jit(solution)/shard_map/ppermute | solution.py:365
  (41 other events, 403.7 us)

commit v6 on v5

--- a/solution.py
+++ b/solution.py
@@ -147,8 +147,14 @@
     def narrow(rows, kind):
         return pl.BlockSpec((rows, HEAD_DIM), lambda i, m, e: (0, kind * 4 + i * 2 + chunk))
 
+    def handed(kind):
+        return pl.BlockSpec((TOK, HEAD_DIM), lambda i, m, e: (0, i * 4 + kind * 2 + chunk))
+
     def out(rows):
         return pl.BlockSpec((2, rows, HEAD_DIM), lambda i, m, e: (0, 0, i * 2 + chunk))
+
+    def out_far():
+        return pl.BlockSpec((2, WIN, HEAD_DIM), lambda i, m, e: (0, 0, i))
 
     def part(shape):
         return pl.BlockSpec(shape, lambda i, m, e: (0, 0, 0, 0))
@@ -163,14 +169,15 @@
             num_scalar_prefetch=2,
             grid=(2,),
             in_specs=[fixed(PAIR, D), fixed(D, PAIR), *[fixed(*w.shape) for w in weights],
-                      wide(), narrow(TOK, 0), narrow(WIN, 0), narrow(WIN, 0),
-                      wide(), narrow(TOK, 1), narrow(WIN, 1), narrow(WIN, 1)]
+                      wide(), handed(0), narrow(WIN, 0), narrow(WIN, 0),
+                      wide(), handed(1), narrow(WIN, 1), narrow(WIN, 1)]
             + [anywhere] * len(before),
-            out_specs=[out(TOK), out(TOK), out(WIN), out(WIN), *[part(shape) for shape in parts]],
+            out_specs=[out(TOK), out(TOK), out_far(), out_far(), *[part(shape) for shape in parts]],
             scratch_shapes=[pair, pair, pair, pair, pool, pool, pool, pool,
                             pltpu.VMEM((4, D, HEAD_DIM), BF), pltpu.VMEM((4, D, HEAD_DIM), BF)],
         ),
-        out_shape=[jax.ShapeDtypeStruct((2, rows, 2 * HALF), BF) for rows in (TOK, TOK, WIN, WIN)]
+        out_shape=[jax.ShapeDtypeStruct((2, TOK, 2 * HALF), BF)] * 2
+        + [jax.ShapeDtypeStruct((2, WIN, HALF), BF)] * 2
         + [jax.ShapeDtypeStruct(shape, BF) for shape in parts],
         input_output_aliases={12 + len(weights) + n: n for n in range(len(before))},
         compiler_params=pltpu.CompilerParams(vmem_limit_bytes=52 * MIB),
@@ -178,38 +185,93 @@
     )(meta, me, x, xt, *weights, q, given, sent_a, sent_b, ct, given, sent_a, sent_b, *before)
 
 
+def add(refs):
+    return sum(ref[...].astype(jnp.float32) for ref in refs)
+
+
 def add_kernel(count, *refs):
-    ins, outs = refs[:count], refs[-4:]
-    total = sum(ref[...].astype(jnp.float32) for ref in ins).astype(BF)
-    for n, out in enumerate(outs):
+    total = add(refs[:count]).astype(BF)
+    for n, out in enumerate(refs[-4:]):
         out[...] = total[n]
 
 
-def add_parts(parts, after=()):
-    extra = list(after)
-    shape = parts[0].shape
-    rank = len(shape)
-    if rank == 4:
-        grid = (4,)
-        source = pl.BlockSpec((4, 1, 128, HEAD_DIM), lambda i: (0, i, 0, 0))
-        target = pl.BlockSpec((1, 128, HEAD_DIM), lambda i: (i, 0, 0))
-    else:
-        grid = (1,)
-        source = pl.BlockSpec(shape, lambda i: (0, 0, 0))
-        target = pl.BlockSpec(shape[1:], lambda i: (0, 0))
+def add_parts(parts, after):
     return pl.pallas_call(
         functools.partial(add_kernel, len(parts)),
-        grid=grid,
-        in_specs=[source] * len(parts) + [pl.BlockSpec(memory_space=pl.ANY)] * len(extra),
-        out_specs=[target] * 4,
-        out_shape=[jax.ShapeDtypeStruct(shape[1:], BF)] * 4,
-        compiler_params=pltpu.CompilerParams(vmem_limit_bytes=16 * MIB),
-    )(*parts, *extra)
-
-
-def depart_kernel(me, enc_len, dec_len, partner, q_ref, ct_ref, meta, info, a_ref, b_ref, give_ref, sems):
+        grid=(4,),
+        in_specs=[pl.BlockSpec((4, 1, 128, HEAD_DIM), lambda i: (0, i, 0, 0))] * len(parts)
+        + [pl.BlockSpec(memory_space=pl.ANY)] * len(after),
+        out_specs=[pl.BlockSpec((1, 128, HEAD_DIM), lambda i: (i, 0, 0))] * 4,
+        out_shape=[jax.ShapeDtypeStruct((4, 128, HEAD_DIM), BF)] * 4,
+        compiler_params=pltpu.CompilerParams(vmem_limit_bytes=16 * MIB),
+    )(*parts, *after)
+
+
+def add_both_kernel(*refs):
+    for chunk in range(2):
+        total = add(refs[chunk * 4 : chunk * 4 + 4]).astype(BF)
+        for n, out in enumerate(refs[8:]):
+            out[:, chunk * HEAD_DIM : (chunk + 1) * HEAD_DIM] = total[n]
+
+
+def add_both(first, second):
+    whole = pl.BlockSpec(memory_space=pltpu.VMEM)
+    return pl.pallas_call(
+        add_both_kernel,
+        in_specs=[whole] * 8,
+        out_specs=[whole] * 4,
+        out_shape=[jax.ShapeDtypeStruct((128, HALF), BF)] * 4,
+        compiler_params=pltpu.CompilerParams(vmem_limit_bytes=16 * MIB),
+    )(*first, *second)
+
+
+def add_last_kernel(me, *refs):
+    kept, given = refs[-2:]
+    for row, out in ((me[2], kept), (1 - me[2], given)):
+        rows = pl.ds(pl.multiple_of(row * 64, 64), 64)
+        out[...] = sum(ref[rows, :].astype(jnp.float32) for ref in refs[:4])
+
+
+def add_last(me, parts, after):
+    whole = pl.BlockSpec(memory_space=pltpu.VMEM)
+    return pl.pallas_call(
+        add_last_kernel,
+        in_specs=[pl.BlockSpec(memory_space=pltpu.SMEM)] + [whole] * 4
+        + [pl.BlockSpec(memory_space=pl.ANY)] * len(after),
+        out_specs=[whole] * 2,
+        out_shape=[jax.ShapeDtypeStruct((64, HALF), jnp.float32)] * 2,
+        compiler_params=pltpu.CompilerParams(vmem_limit_bytes=16 * MIB),
+    )(me, *parts, *after)
+
+
+def depart_kernel(me, enc_len, dec_len, partner, q_ref, ct_ref, meta, info, a_ref, b_ref, sems):
     core, x = me[2], me[3]
     t = me[0] * 4 + me[1]
+
+    info[0], info[1], info[2], info[3] = jnp.int32(0), core, jnp.int32(0), jnp.int32(0)
+    device = (t * 2 + core) * 4 + x
+    start = jnp.int32(0)
+    for slot in range(SEGS):
+        begin, length = start, dec_len[device, slot]
+
+        @pl.when((partner[device, slot] >> 5) != t)
+        def _():
+            info[0] = align(begin, TOK)
+            info[2] = begin
+            info[3] = length
+
+        start = start + length
+
+    rows = pl.ds(pl.multiple_of(info[0], 16), WIN)
+    copies = []
+    for n in range(4):
+        source = (q_ref, ct_ref)[n // 2]
+        for side, out in ((core, a_ref), (1 - core, b_ref)):
+            begin = pl.ds(pl.multiple_of((n % 2) * 1024 + side * HALF, HALF), HALF)
+            copies.append((source.at[rows, begin], out.at[:, pl.ds(n * HALF, HALF)]))
+    copies = [pltpu.make_async_copy(a, b, sems.at[n]) for n, (a, b) in enumerate(copies)]
+    for copy in copies:
+        copy.start()
 
     for side in range(2):
         device = (t * 2 + (core if side == 0 else 1 - core)) * 4 + x
@@ -218,9 +280,6 @@
             meta[side * SEGS + slot, 0] = start
             meta[side * SEGS + slot, 1] = enc_len[device, slot]
             start = start + enc_len[device, slot]
-    for n in range(4):
-        info[n] = jnp.int32(0)
-    info[1] = core
     for near in range(4):
         dp = t * 2 - 1 + near
         device = jnp.clip(dp, 0, 31) * 4 + x
@@ -230,41 +289,18 @@
         for slot in range(SEGS):
             begin, length = start, dec_len[device, slot]
             owner = partner[device, slot] >> 4
-            here = real & ((owner >> 1) == t)
-            window = align(begin, TOK)
             if near in (1, 2):
                 at = begin + jnp.where(same, 0, TOK)
             else:
-                at = begin - window + PAIR + jnp.where(same, 0, WIN)
-
-            @pl.when(here)
+                at = begin - align(begin, TOK) + PAIR + jnp.where(same, 0, WIN)
+
+            @pl.when(real & ((owner >> 1) == t))
             def _():
                 entry = jnp.where((owner & 1) == core, 0, SEGS) + (partner[device, slot] & 3)
                 meta[entry, 2] = at
                 meta[entry, 3] = length
 
-            if near in (1, 2):
-
-                @pl.when(same & jnp.logical_not(here))
-                def _():
-                    info[0] = window
-                    info[2] = begin
-                    info[3] = length
-
             start = start + length
-
-    rows = pl.ds(pl.multiple_of(info[0], 16), WIN)
-    copies = []
-    for n in range(4):
-        source = (q_ref, ct_ref)[n // 2]
-        cols = pl.ds(n * HALF, HALF)
-        for side, out in ((core, a_ref), (1 - core, b_ref)):
-            begin = pl.ds(pl.multiple_of((n % 2) * 1024 + side * HALF, HALF), HALF)
-            copies.append((source.at[rows, begin], out.at[:, cols]))
-        copies.append((source.at[:, begin], give_ref.at[:, cols]))
-    copies = [pltpu.make_async_copy(a, b, sems.at[n]) for n, (a, b) in enumerate(copies)]
-    for copy in copies:
-        copy.start()
     for copy in copies:
         copy.wait()
 
@@ -275,12 +311,35 @@
     return pl.pallas_call(
         depart_kernel,
         in_specs=[scalar, scalar, scalar, scalar, whole, whole],
-        out_specs=[scalar, scalar, whole, whole, whole],
-        scratch_shapes=[pltpu.SemaphoreType.DMA((12,))],
+        out_specs=[scalar, scalar, whole, whole],
+        scratch_shapes=[pltpu.SemaphoreType.DMA((8,))],
         out_shape=[jax.ShapeDtypeStruct((2 * SEGS, 4), jnp.int32), jax.ShapeDtypeStruct((4,), jnp.int32)]
-        + [jax.ShapeDtypeStruct((rows, 2048), BF) for rows in (WIN, WIN, TOK)],
-        compiler_params=pltpu.CompilerParams(vmem_limit_bytes=16 * MIB),
+        + [jax.ShapeDtypeStruct((WIN, 2048), BF)] * 2,
+        compiler_params=pltpu.CompilerParams(vmem_limit_bytes=60 * MIB),
     )(me, enc_lengths, dec_lengths, dec_partner, q, ct)
+
+
+def hand_kernel(me, q_ref, ct_ref, *refs):
+    refs[-1][:, :HALF] = q_ref[...]
+    refs[-1][:, HALF:] = ct_ref[...]
+
+
+def hand(me, q, ct, after):
+    def half(i, me):
+        return (0, i * 2 + 1 - me[2])
+
+    part = pl.BlockSpec((TOK, HALF), half)
+    return pl.pallas_call(
+        hand_kernel,
+        grid_spec=pltpu.PrefetchScalarGridSpec(
+            num_scalar_prefetch=1,
+            grid=(2,),
+            in_specs=[part, part] + [pl.BlockSpec(memory_space=pl.ANY)] * len(after),
+            out_specs=pl.BlockSpec((TOK, 2 * HALF), lambda i, me: (0, i)),
+        ),
+        out_shape=jax.ShapeDtypeStruct((TOK, 2048), BF),
+        compiler_params=pltpu.CompilerParams(vmem_limit_bytes=16 * MIB),
+    )(me, q, ct, *after)
 
 
 def turn_kernel(a_ref, b_ref, *refs):
@@ -304,23 +363,24 @@
 
 
 def finish_kernel(info, *refs):
-    ins, outs = refs[:4], refs[4:]
+    ins, outs = refs[:6], refs[6:]
     win = pl.multiple_of(info[0], 16)
     core, start, length = info[1], info[2] - info[0], info[3]
     rows = pl.ds(win, WIN)
-    place = lax.broadcasted_iota(jnp.int32, (WIN, HALF), 0)
+    place = lax.broadcasted_iota(jnp.int32, (WIN, HEAD_DIM), 0)
     inside = (place >= start) & (place < start + length)
-    mine, theirs, back_a, back_b = ins
-    for side, base, back in ((core, mine, back_a), (1 - core, theirs, back_b)):
-        cols = pl.ds(pl.multiple_of(side * HALF, HALF), HALF)
-        for kind, out in enumerate(outs):
-            out[:, cols] = base[kind]
-            out[rows, cols] = jnp.where(inside, back[kind], out[rows, cols])
+    mine, theirs, *returned = ins
+    for side, base, first in ((core, mine, 0), (1 - core, theirs, 1)):
+        for chunk in range(2):
+            cols = pl.ds(pl.multiple_of(side * HALF + chunk * HEAD_DIM, HEAD_DIM), HEAD_DIM)
+            for kind, out in enumerate(outs):
+                out[:, cols] = base[kind, :, chunk * HEAD_DIM : (chunk + 1) * HEAD_DIM]
+                out[rows, cols] = jnp.where(inside, returned[chunk * 2 + first][kind], out[rows, cols])
 
 
 def finish(info, pieces):
-    def source(rows):
-        return pl.BlockSpec((2, rows, HALF), lambda i, e: (0, 0, i))
+    def source(rows, cols):
+        return pl.BlockSpec((2, rows, cols), lambda i, e: (0, 0, i))
 
     out = pl.BlockSpec((TOK, 1024), lambda i, e: (0, i))
     return pl.pallas_call(
@@ -328,7 +388,7 @@
         grid_spec=pltpu.PrefetchScalarGridSpec(
             num_scalar_prefetch=1,
             grid=(2,),
-            in_specs=[source(TOK), source(TOK), source(WIN), source(WIN)],
+            in_specs=[source(TOK, HALF)] * 2 + [source(WIN, HEAD_DIM)] * 4,
             out_specs=[out, out],
         ),
         out_shape=[jax.ShapeDtypeStruct((TOK, 2048), BF)] * 2,
@@ -399,6 +459,7 @@
         + [pl.BlockSpec(memory_space=pl.ANY)] * len(after),
         out_specs=whole,
         out_shape=jax.ShapeDtypeStruct((128, HALF), BF),
+        compiler_params=pltpu.CompilerParams(vmem_limit_bytes=16 * MIB),
     )(me, weights, got, *after)
 
 
@@ -438,46 +499,41 @@
     z, y, c, x = (lax.axis_index(a) for a in ALL)
     me = jnp.stack([z, y, c, x]).astype(jnp.int32)
     swapped = swap(enc_hidden)
-    meta, info, leave_a, leave_b, give = depart(me, enc_lengths, dec_lengths, dec_partner, queries, cotangent)
+    meta, info, leave_a, leave_b = depart(me, enc_lengths, dec_lengths, dec_partner, queries, cotangent)
     sent_a = lax.ppermute(leave_a, DP, SEND_A)
     sent_b = lax.ppermute(leave_b, DP, SEND_B)
 
     got = swap(jnp.where(c == 0, kv_weights[:, HALF:], kv_weights[:, :HALF]))
     own = pick(me, kv_weights, got, [leave_a, swapped])
     first = [own] + [ring(own, 2, n) for n in (1, 2, 3)]
-    part = join(first, [], slice(0, HALF))
+    part = join(first, [sent_a], slice(0, HALF))
     second = [part] + [ring(part, 1, n) for n in (1, 2, 3)]
-    part = join(second, [], slice(0, HEAD_DIM))
-    tokens, tokens_t = turn(enc_hidden, swapped, [part])
+    tokens, tokens_t = turn(enc_hidden, swapped, [second[1]])
+    given = hand(me, queries, cotangent, [tokens_t])
+    part = join(second, [given], slice(0, HEAD_DIM))
     ahead, behind = ring(part, 0, 1), ring(part, 0, -1)
     weights = [[part, ahead, behind, ring(behind[:2], 0, -1), ring(ahead[2:], 0, 1)]]
-    part = join(second, [ahead, behind, sent_a, sent_b], slice(HEAD_DIM, HALF))
+    part = join(second, [ahead, behind], slice(HEAD_DIM, HALF))
     weights.append([part, ring(part, 0, 1), ring(part, 0, -1), ring(part, 0, 2)])
 
     shared = (meta, me, tokens, tokens_t)
-    inputs = (queries, cotangent, swap(give), sent_a, sent_b)
+    inputs = (queries, cotangent, swap(given), sent_a, sent_b)
+    home = [back(SEND_A), back(SEND_B)]
 
     *results, d0, d1, d3, d2 = run_main(0, *shared, weights[0], *inputs)
+    returned = [lax.ppermute(part, DP, pairs) for part, pairs in zip(results[2:], home)]
     parts = exchange([d0, d1, d2, d3], 0)
-    *results, d0, d1, d3, far_a, far_b = run_main(1, *shared, weights[1], *inputs, before=results)
-    mine, other, back_a, back_b = results
-    context, grad_queries = finish(
-        info,
-        [mine, swap(other), lax.ppermute(back_a, DP, back(SEND_A)), lax.ppermute(back_b, DP, back(SEND_B))],
-    )
-
-    first = add_parts(parts, [mine])
+    *results, d0, d1, d3, far_a, far_b = run_main(1, *shared, weights[1], *inputs, before=results[:2])
+    mine, other = results[:2]
+    late = [lax.ppermute(part, DP, pairs) for part, pairs in zip(results[2:], home)]
+
+    first = add_parts(parts, [mine, *returned])
     parts = scatter_ring(d0, d1, d3, far_a, far_b, first[0])
-    second = add_parts(exchange(first, 1))
-    last = [exchange(second, 2)]
-    second = add_parts(exchange(add_parts(parts, [second[0]]), 1), [context])
-    last.append(exchange(second, 2))
-    summed = jnp.concatenate(
-        [sum(part.astype(jnp.float32) for part in parts) for parts in last], axis=1
-    )
-    low, high = summed[:64], summed[64:]
-    got = swap(jnp.where(c == 0, high, low))
-    kept = jnp.where(c == 0, low, high)
+    first = exchange(first, 1)
+    second = exchange(add_parts(parts, late), 1)
+    context, grad_queries = finish(info, [mine, swap(other), *returned, *late])
+    kept, given = add_last(me, exchange(add_both(first, second), 2), [context])
+    got = swap(given)
     grad = jnp.concatenate([jnp.where(c == 0, kept, got), jnp.where(c == 0, got, kept)], axis=1)
     return context, grad_queries, grad
 

time: 212 us -> 260 us (1.23)
  Pallas kernels: 61.1 us -> 106 us
  waiting for transfers between devices: 59.7 us -> 67.3 us
  local copies, waits for them, and re-layouts: 19.2 us -> 13.2 us
    pallas_call x1, Pallas kernels: 5.35 us -> 49.5 us  [depart(): pl.pallas_call(depart_kernel, in_specs=[scalar, scalar, scalar, scalar, w...]
    ppermute x13, waiting for transfers between devices: 25.6 us -> 37.1 us  [ring(): return lax.ppermute(value, ALL, shift(phase, -amount))]
    ppermute x15 -> x12, waiting for transfers between devices: 17.8 us -> 9.04 us  [exchange(): lax.ppermute(parts[r], ALL, shift(phase, r))]
    ppermute x2 -> x4, starting transfers between devices: 3.32 us -> 11.9 us  [body(): lax.ppermute(part, DP, pairs)]
    ppermute x5, starting transfers between devices: 12.2 us -> 4.92 us  [swap(): return lax.ppermute(value, 'c', [(0, 1), (1, 0)])]
    ppermute x15 -> x12, starting transfers between devices: 16.2 us -> 22.9 us  [exchange(): lax.ppermute(parts[r], ALL, shift(phase, r))]
    unnamed x67 -> x59, local copies, waits for them, and re-layouts: 19.1 us -> 13.2 us
    ppermute x1, starting transfers between devices: 6.57 us -> 1.91 us  [body(): sent_b = lax.ppermute(leave_b, DP, SEND_B)]
  transfers between devices with their start and end apart: 41 -> 40, of which waited for: 14 -> 17; matrix products, arithmetic and copies ran while one was open for 2% -> 2% of each run, Pallas kernels for 28% -> 41%
where the time goes in v6:
time: 260 us; the launch traced here: 259 us
  Pallas kernels  106 us (41%)
  starting transfers between devices  70.5 us (27%)
  waiting for transfers between devices  67.3 us (26%)
  local copies, waits for them, and re-layouts  13.2 us (5%)
    pallas_call x1, Pallas kernels, depart(): pl.pallas_call(depart_kernel, in_specs=[scalar, scalar, scalar, scalar, w...  49.5 us
    pallas_call x2, Pallas kernels, run_main(): pl.pallas_call(functools.partial(main_kernel, len(weights), len(before)),...  46.3 us
    ppermute x13, waiting for transfers between devices, ring(): return lax.ppermute(value, ALL, shift(phase, -amount))  37.1 us
    ppermute x12, starting transfers between devices, exchange(): lax.ppermute(parts[r], ALL, shift(phase, r))  22.9 us
    ppermute x13, starting transfers between devices, ring(): return lax.ppermute(value, ALL, shift(phase, -amount))  20.1 us
    unnamed x59, local copies, waits for them, and re-layouts  13.2 us
    ppermute x4, starting transfers between devices, body(): lax.ppermute(part, DP, pairs)  11.9 us
    ppermute x12, waiting for transfers between devices, exchange(): lax.ppermute(parts[r], ALL, shift(phase, r))  9.04 us
  transfers between devices with their start and end apart: 40, of which 17 were waited for; matrix products, arithmetic and copies ran while one was open for 2% of the time, Pallas kernels for 41%

profile of v6, /device:TPU:1, one launch (start us, length us, event | category | flops | bytes accessed | tf_op | source)
XLA Modules:
  0.0 259.4 jit_solution(3167445096261947089)
XLA Ops:
  7.0 49.5 %shard_map.94 = (s32[8,4]{1,0:T(8,128)}, s32[4]{0:T(128)}, bf16[176,2048]{1,0:T(8,128)(2,1)}, bf16[176,2048]{1,0:T(8,128)(2,1)}) custom-call(s32[4]{0:T(128)} %pad_add_fusion.me, s32[128,4]{1,0:T(8,128)} %copy.14.enc_len, s32[128,4]{1,0:T(8,128)} %copy.15.dec_len, s32[128,4]{1,0:T(8,128)} %copy.16.partner, bf16[512,2048]{1,0:T(8,128)(2,1)} %refs_4_.1, ...), custom_call_target="tpu_custom_call" | custom-call | tf_op jit(solution)/shard_map/pallas_call | solution.py:311
  56.5 3.3 %collective-permute-start.5 = (bf16[176,2048]{1,0:T(8,128)(2,1)}, bf16[176,2048]{1,0:T(8,128)(2,1)S(1)}, u32[]{:S(2)}, u32[]{:S(2)}) collective-permute-start(bf16[176,2048]{1,0:T(8,128)(2,1)} %get-tuple-element.46.refs_0_), channel_id=1, source_target_pairs={{8,0},{16,8},{24,16},{32,24},{40,32},{48,40},{56,48},{64,56},{72,6... | collective-permute-start | bytes 2162696 | tf_op jit(solution)/shard_map/ppermute | solution.py:503
  64.2 2.6 %collective-permute-start.3 = (bf16[128,512]{1,0:T(8,128)(2,1)S(1)}, bf16[128,512]{1,0:T(8,128)(2,1)S(1)}, u32[]{:S(2)}, u32[]{:S(2)}) collective-permute-start(bf16[128,512]{1,0:T(8,128)(2,1)S(1)} %shard_map.95.refs_0_), channel_id=1, source_target_pairs={{0,64},{1,65},{2,66},{3,67},{4,20},{5,21},{6,22},{7,23},{8,72},{9,... | collective-permute-start | bytes 393224 | tf_op jit(solution)/shard_map/ppermute | solution.py:467
  68.3 5.9 %collective-permute-done.4.refs_3_ = bf16[128,512]{1,0:T(8,128)(2,1)S(1)} collective-permute-done((bf16[128,512]{1,0:T(8,128)(2,1)S(1)}, bf16[128,512]{1,0:T(8,128)(2,1)S(1)}, u32[]{:S(2)}, u32[]{:S(2)}) %collective-permute-start.4) | collective-permute-done | bytes 131104 | tf_op jit(solution)/shard_map/ppermute | solution.py:467
  74.3 2.5 collective-permute-start.6
  76.8 1.7 collective-permute-start.7
  78.6 10.0 %collective-permute-done.6.refs_0_.refs_1_ = bf16[4,128,512]{2,1,0:T(8,128)(2,1)S(1)} collective-permute-done((bf16[4,128,512]{2,1,0:T(8,128)(2,1)S(1)}, bf16[4,128,512]{2,1,0:T(8,128)(2,1)S(1)}, u32[]{:S(2)}, u32[]{:S(2)}) %collective-permute-start.6) | collective-permute-done | bytes 524320 | tf_op jit(solution)/shard_map/ppermute | solution.py:467
  88.6 2.1 shard_map.97
  94.3 3.5 %collective-permute-start.10 = (bf16[4,4,128,256]{3,2,1,0:T(8,128)(2,1)S(1)}, bf16[4,4,128,256]{3,2,1,0:T(8,128)(2,1)S(1)}, u32[]{:S(2)}, u32[]{:S(2)}) collective-permute-start(bf16[4,4,128,256]{3,2,1,0:T(8,128)(2,1)S(1)} %shard_map.99.refs_0_), channel_id=1, source_target_pairs={{0,1},{1,2},{2,3},{3,0},{4,36},{5,37},{6,38},{7,39},{8,9},{9,10},{... | collective-permute-start | bytes 3145736 | tf_op jit(solution)/shard_map/ppermute | solution.py:467
  98.0 1.9 collective-permute-start.15
  99.9 17.3 %collective-permute-done.10.refs_5_.refs_2_ = bf16[4,4,128,256]{3,2,1,0:T(8,128)(2,1)S(1)} collective-permute-done((bf16[4,4,128,256]{3,2,1,0:T(8,128)(2,1)S(1)}, bf16[4,4,128,256]{3,2,1,0:T(8,128)(2,1)S(1)}, u32[]{:S(2)}, u32[]{:S(2)}) %collective-permute-start.10) | collective-permute-done | bytes 1048608 | tf_op jit(solution)/shard_map/ppermute | solution.py:467
  117.3 2.3 collective-permute-start.16
  120.6 2.7 %collective-permute-start.13 = (bf16[4,4,128,256]{3,2,1,0:T(8,128)(2,1)S(1)}, bf16[4,4,128,256]{3,2,1,0:T(8,128)(2,1)S(1)}, u32[]{:S(2)}, u32[]{:S(2)}) collective-permute-start(bf16[4,4,128,256]{3,2,1,0:T(8,128)(2,1)S(1)} %shard_map.100.refs_0_), channel_id=1, source_target_pairs={{0,2},{1,3},{2,0},{3,1},{4,68},{5,69},{6,70},{7,71},{8,10},{9,11},... | collective-permute-start | bytes 3145736 | tf_op jit(solution)/shard_map/ppermute | solution.py:467
  123.3 3.9 %collective-permute-done.16.refs_3_ = bf16[2,4,128,256]{3,2,1,0:T(8,128)(2,1)S(1)} collective-permute-done((bf16[2,4,128,256]{3,2,1,0:T(8,128)(2,1)S(1)}, bf16[2,4,128,256]{3,2,1,0:T(8,128)(2,1)S(1)}, u32[]{:S(2)}, u32[]{:S(2)}) %collective-permute-start.16) | collective-permute-done | bytes 524320 | tf_op jit(solution)/shard_map/ppermute | solution.py:467
  130.0 23.1 %shard_map.101 = (bf16[2,512,1024]{2,1,0:T(8,128)(2,1)}, bf16[2,512,1024]{2,1,0:T(8,128)(2,1)}, bf16[2,176,512]{2,1,0:T(8,128)(2,1)S(1)}, bf16[2,176,512]{2,1,0:...) custom-call(s32[8,4]{1,0:T(8,128)S(1)} %copy-done.21, ...), custom_call_target="tpu_custom_call" | custom-call | flops 12000000000 | bytes 24000000 | tf_op jit(solution)/shard_map/pallas_call | solution.py:166
  154.4 7.4 %collective-permute-start.20 = (bf16[2,176,512]{2,1,0:T(8,128)(2,1)S(1)}, bf16[2,176,512]{2,1,0:T(8,128)(2,1)S(1)}, u32[]{:S(2)}, u32[]{:S(2)}) collective-permute-start(bf16[2,176,512]{2,1,0:T(8,128)(2,1)S(1)} %get-tuple-element.55), channel_id=1, source_target_pairs={{4,8},{12,16},{20,24},{28,32},{36,40},{44,48},{52,56},{60,64},{68,... | collective-permute-start | bytes 1081352 | tf_op jit(solution)/shard_map/ppermute | solution.py:524
  161.9 7.4 %collective-permute-start.23 = (bf16[4,4,128,256]{3,2,1,0:T(8,128)(2,1)}, bf16[4,4,128,256]{3,2,1,0:T(8,128)(2,1)S(1)}, u32[]{:S(2)}, u32[]{:S(2)}) collective-permute-start(bf16[4,4,128,256]{3,2,1,0:T(8,128)(2,1)} %get-tuple-element.61), channel_id=1, source_target_pairs={{0,1},{1,2},{2,3},{3,0},{4,36},{5,37},{6,38},{7,39},{8,9},{9,10},{... | collective-permute-start | bytes 3145736 | tf_op jit(solution)/shard_map/ppermute | solution.py:425
  170.9 5.7 %collective-permute-start.25 = (bf16[4,4,128,256]{3,2,1,0:T(8,128)(2,1)}, bf16[4,4,128,256]{3,2,1,0:T(8,128)(2,1)S(1)}, u32[]{:S(2)}, u32[]{:S(2)}) collective-permute-start(bf16[4,4,128,256]{3,2,1,0:T(8,128)(2,1)} %get-tuple-element.63), channel_id=1, source_target_pairs={{0,2},{1,3},{2,0},{3,1},{4,68},{5,69},{6,70},{7,71},{8,10},{9,11},... | collective-permute-start | bytes 3145736 | tf_op jit(solution)/shard_map/ppermute | solution.py:425
  176.6 23.2 %shard_map.102 = (bf16[2,512,1024]{2,1,0:T(8,128)(2,1)}, bf16[2,512,1024]{2,1,0:T(8,128)(2,1)}, bf16[2,176,512]{2,1,0:T(8,128)(2,1)S(1)}, bf16[2,176,512]{2,1,0:...) custom-call(s32[8,4]{1,0:T(8,128)S(1)} %copy-done.21, ...), custom_call_target="tpu_custom_call", output_to_operand_aliasing={{0}: (16, {}), {1}: (17, {})} | custom-call | flops 12000000000 | bytes 24000000 | tf_op jit(solution)/shard_map/pallas_call | solution.py:166
  199.9 2.7 %collective-permute-start.30 = (bf16[2,4,128,256]{3,2,1,0:T(8,128)(2,1)S(1)}, bf16[2,4,128,256]{3,2,1,0:T(8,128)(2,1)S(1)}, u32[]{:S(2)}, u32[]{:S(2)}) collective-permute-start(bf16[2,4,128,256]{3,2,1,0:T(8,128)(2,1)S(1)} %get-tuple-element.72), channel_id=1, source_target_pairs={{0,3},{1,0},{2,1},{3,2},{4,100},{5,101},{6,102},{7,103},{8,11},{9,... | collective-permute-start | bytes 1572872 | tf_op jit(solution)/shard_map/ppermute | solution.py:493
  205.1 4.3 %collective-permute-done.29.got_a = bf16[2,4,128,256]{3,2,1,0:T(8,128)(2,1)S(1)} collective-permute-done((bf16[2,4,128,256]{3,2,1,0:T(8,128)(2,1)S(1)}, bf16[2,4,128,256]{3,2,1,0:T(8,128)(2,1)S(1)}, u32[]{:S(2)}, u32[]{:S(2)}) %collective-permute-start.29) | collective-permute-done | bytes 524320 | tf_op jit(solution)/shard_map/ppermute | solution.py:492
  214.9 1.9 collective-permute-start.22
  216.8 7.2 %collective-permute-done.21.refs_4_.refs_3_ = bf16[2,176,512]{2,1,0:T(8,128)(2,1)S(1)} collective-permute-done((bf16[2,176,512]{2,1,0:T(8,128)(2,1)S(1)}, bf16[2,176,512]{2,1,0:T(8,128)(2,1)S(1)}, u32[]{:S(2)}, u32[]{:S(2)}) %collective-permute-start.21) | collective-permute-done | bytes 360480 | tf_op jit(solution)/shard_map/ppermute | solution.py:528
  227.5 4.1 %collective-permute-done.31.refs_1_ = bf16[4,4,128,256]{3,2,1,0:T(8,128)(2,1)S(1)} collective-permute-done((bf16[4,4,128,256]{3,2,1,0:T(8,128)(2,1)S(1)}, bf16[4,4,128,256]{3,2,1,0:T(8,128)(2,1)S(1)}, u32[]{:S(2)}, u32[]{:S(2)}) %collective-permute-start.31) | collective-permute-done | bytes 1048608 | tf_op jit(solution)/shard_map/ppermute | solution.py:495
  234.1 2.3 collective-permute-start.34
  236.8 1.8 collective-permute-done.28.refs_3_
  238.6 2.5 collective-permute-done.33.refs_5_
  244.2 2.7 %collective-permute-start.37 = (bf16[128,512]{1,0:T(8,128)(2,1)S(1)}, bf16[128,512]{1,0:T(8,128)(2,1)S(1)}, u32[]{:S(2)}, u32[]{:S(2)}) collective-permute-start(bf16[128,512]{1,0:T(8,128)(2,1)S(1)} %get-tuple-element.81), channel_id=1, source_target_pairs={{0,96},{1,97},{2,98},{3,99},{4,28},{5,29},{6,30},{7,31},{8,104},{9... | collective-permute-start | bytes 393224 | tf_op jit(solution)/shard_map/ppermute | solution.py:425
  246.9 3.4 %shard_map.103 = (bf16[512,2048]{1,0:T(8,128)(2,1)}, bf16[512,2048]{1,0:T(8,128)(2,1)}) custom-call(s32[4]{0:T(128)S(1)} %copy-done.19, bf16[2,512,1024]{2,1,0:T(8,128)(2,1)S(1)} %copy-done.1, bf16[2,512,1024]{2,1,0:T(8,128)(2,1)S(1)} %collective-permute-done.18.refs_1_, bf16[2,176,512]{2,1,0:T(8,128)(2,1)S(1)} %collective-permute-done.19.refs_2_.refs_5_, ...), custom_call_target="tpu_custom_call" | custom-call | tf_op jit(solution)/shard_map/pallas_call | solution.py:386
  250.3 1.9 collective-permute-done.38.refs_3_
  252.2 1.6 copy-done.8
  254.4 3.2 %collective-permute-start.39 = (f32[64,512]{1,0:T(8,128)S(1)}, f32[64,512]{1,0:T(8,128)S(1)}, u32[]{:S(2)}, u32[]{:S(2)}) collective-permute-start(f32[64,512]{1,0:T(8,128)S(1)} %get-tuple-element.84), channel_id=1, source_target_pairs={{0,4},{4,0},{1,5},{5,1},{2,6},{6,2},{3,7},{7,3},{8,12},{12,8},{9,1... | collective-permute-start | bytes 393224 | tf_op jit(solution)/shard_map/ppermute | solution.py:400
  (128 shorter events, 42.6 us)
Async XLA Ops:
  0.6 60.6 %collective-permute-start = (bf16[512,2048]{1,0:T(8,128)(2,1)}, bf16[512,2048]{1,0:T(8,128)(2,1)S(1)}, u32[]{:S(2)}, u32[]{:S(2)}) collective-permute-start(bf16[512,2048]{1,0:T(8,128)(2,1)} %a_ref.1), channel_id=1, source_target_pairs={{0,4},{4,0},{1,5},{5,1},{2,6},{6,2},{3,7},{7,3},{8,12},{12,8},{9,1... | collective-permute-start | bytes 6291464 | tf_op jit(solution)/shard_map/ppermute | solution.py:400
  56.5 11.8 %collective-permute-start.5 = (bf16[176,2048]{1,0:T(8,128)(2,1)}, bf16[176,2048]{1,0:T(8,128)(2,1)S(1)}, u32[]{:S(2)}, u32[]{:S(2)}) collective-permute-start(bf16[176,2048]{1,0:T(8,128)(2,1)} %get-tuple-element.46.refs_0_), channel_id=1, source_target_pairs={{8,0},{16,8},{24,16},{32,24},{40,32},{48,40},{56,48},{64,56},{72,6... | collective-permute-start | bytes 2162696 | tf_op jit(solution)/shard_map/ppermute | solution.py:503
  62.9 11.3 %collective-permute-start.4 = (bf16[128,512]{1,0:T(8,128)(2,1)S(1)}, bf16[128,512]{1,0:T(8,128)(2,1)S(1)}, u32[]{:S(2)}, u32[]{:S(2)}) collective-permute-start(bf16[128,512]{1,0:T(8,128)(2,1)S(1)} %shard_map.95.refs_0_), channel_id=1, source_target_pairs={{0,32},{1,33},{2,34},{3,35},{4,12},{5,13},{6,14},{7,15},{8,40},{9,... | collective-permute-start | bytes 393224 | tf_op jit(solution)/shard_map/ppermute | solution.py:467
  64.2 10.0 %collective-permute-start.3 = (bf16[128,512]{1,0:T(8,128)(2,1)S(1)}, bf16[128,512]{1,0:T(8,128)(2,1)S(1)}, u32[]{:S(2)}, u32[]{:S(2)}) collective-permute-start(bf16[128,512]{1,0:T(8,128)(2,1)S(1)} %shard_map.95.refs_0_), channel_id=1, source_target_pairs={{0,64},{1,65},{2,66},{3,67},{4,20},{5,21},{6,22},{7,23},{8,72},{9,... | collective-permute-start | bytes 393224 | tf_op jit(solution)/shard_map/ppermute | solution.py:467
  74.3 14.3 %collective-permute-start.6 = (bf16[4,128,512]{2,1,0:T(8,128)(2,1)S(1)}, bf16[4,128,512]{2,1,0:T(8,128)(2,1)S(1)}, u32[]{:S(2)}, u32[]{:S(2)}) collective-permute-start(bf16[4,128,512]{2,1,0:T(8,128)(2,1)S(1)} %shard_map.96.refs_0_), channel_id=1, source_target_pairs={{0,24},{1,25},{2,26},{3,27},{4,7},{5,4},{6,5},{7,6},{8,0},{9,1},{1... | collective-permute-start | bytes 1572872 | tf_op jit(solution)/shard_map/ppermute | solution.py:467
  76.8 17.3 %collective-permute-start.8 = (bf16[4,128,512]{2,1,0:T(8,128)(2,1)S(1)}, bf16[4,128,512]{2,1,0:T(8,128)(2,1)S(1)}, u32[]{:S(2)}, u32[]{:S(2)}) collective-permute-start(bf16[4,128,512]{2,1,0:T(8,128)(2,1)S(1)} %shard_map.96.refs_0_), channel_id=1, source_target_pairs={{0,8},{1,9},{2,10},{3,11},{4,5},{5,6},{6,7},{7,4},{8,16},{9,17},{1... | collective-permute-start | bytes 1572872 | tf_op jit(solution)/shard_map/ppermute | solution.py:467
  76.8 17.3 %collective-permute-start.7 = (bf16[4,128,512]{2,1,0:T(8,128)(2,1)S(1)}, bf16[4,128,512]{2,1,0:T(8,128)(2,1)S(1)}, u32[]{:S(2)}, u32[]{:S(2)}) collective-permute-start(bf16[4,128,512]{2,1,0:T(8,128)(2,1)S(1)} %shard_map.96.refs_0_), channel_id=1, source_target_pairs={{0,16},{1,17},{2,18},{3,19},{4,6},{5,7},{6,4},{7,5},{8,24},{9,25},... | collective-permute-start | bytes 1572872 | tf_op jit(solution)/shard_map/ppermute | solution.py:467
  94.2 34.5 %collective-permute-start.14 = (bf16[512,2048]{1,0:T(8,128)(2,1)S(1)}, bf16[512,2048]{1,0:T(8,128)(2,1)S(1)}, u32[]{:S(2)}, u32[]{:S(2)}) collective-permute-start(bf16[512,2048]{1,0:T(8,128)(2,1)S(1)} %shard_map.98.refs_4_), channel_id=1, source_target_pairs={{0,4},{4,0},{1,5},{5,1},{2,6},{6,2},{3,7},{7,3},{8,12},{12,8},{9,1... | collective-permute-start | bytes 6291464 | tf_op jit(solution)/shard_map/ppermute | solution.py:400
  94.3 23.0 %collective-permute-start.10 = (bf16[4,4,128,256]{3,2,1,0:T(8,128)(2,1)S(1)}, bf16[4,4,128,256]{3,2,1,0:T(8,128)(2,1)S(1)}, u32[]{:S(2)}, u32[]{:S(2)}) collective-permute-start(bf16[4,4,128,256]{3,2,1,0:T(8,128)(2,1)S(1)} %shard_map.99.refs_0_), channel_id=1, source_target_pairs={{0,1},{1,2},{2,3},{3,0},{4,36},{5,37},{6,38},{7,39},{8,9},{9,10},{... | collective-permute-start | bytes 3145736 | tf_op jit(solution)/shard_map/ppermute | solution.py:467
  97.8 21.8 %collective-permute-start.9 = (bf16[4,4,128,256]{3,2,1,0:T(8,128)(2,1)S(1)}, bf16[4,4,128,256]{3,2,1,0:T(8,128)(2,1)S(1)}, u32[]{:S(2)}, u32[]{:S(2)}) collective-permute-start(bf16[4,4,128,256]{3,2,1,0:T(8,128)(2,1)S(1)} %shard_map.99.refs_0_), channel_id=1, source_target_pairs={{0,3},{1,0},{2,1},{3,2},{4,100},{5,101},{6,102},{7,103},{8,11},{9,... | collective-permute-start | bytes 3145736 | tf_op jit(solution)/shard_map/ppermute | solution.py:467
  98.0 25.3 %collective-permute-start.15 = (bf16[176,2048]{1,0:T(8,128)(2,1)S(1)}, bf16[176,2048]{1,0:T(8,128)(2,1)S(1)}, u32[]{:S(2)}, u32[]{:S(2)}) collective-permute-start(bf16[176,2048]{1,0:T(8,128)(2,1)S(1)} %copy-done.26), channel_id=1, source_target_pairs={{8,4},{16,12},{24,20},{32,28},{40,36},{48,44},{56,52},{64,60},{72,... | collective-permute-start | bytes 2162696 | tf_op jit(solution)/shard_map/ppermute | solution.py:504
  117.3 9.9 %collective-permute-start.16 = (bf16[2,4,128,256]{3,2,1,0:T(8,128)(2,1)S(1)}, bf16[2,4,128,256]{3,2,1,0:T(8,128)(2,1)S(1)}, u32[]{:S(2)}, u32[]{:S(2)}) collective-permute-start(bf16[2,4,128,256]{3,2,1,0:T(8,128)(2,1)S(1)} %slice.16), channel_id=1, source_target_pairs={{0,1},{1,2},{2,3},{3,0},{4,36},{5,37},{6,38},{7,39},{8,9},{9,10},{... | collective-permute-start | bytes 1572872 | tf_op jit(solution)/shard_map/ppermute | solution.py:467
  119.6 9.1 %collective-permute-start.17 = (bf16[2,4,128,256]{3,2,1,0:T(8,128)(2,1)S(1)}, bf16[2,4,128,256]{3,2,1,0:T(8,128)(2,1)S(1)}, u32[]{:S(2)}, u32[]{:S(2)}) collective-permute-start(bf16[2,4,128,256]{3,2,1,0:T(8,128)(2,1)S(1)} %slice.17), channel_id=1, source_target_pairs={{0,3},{1,0},{2,1},{3,2},{4,100},{5,101},{6,102},{7,103},{8,11},{9,... | collective-permute-start | bytes 1572872 | tf_op jit(solution)/shard_map/ppermute | solution.py:467
  120.6 41.2 %collective-permute-start.13 = (bf16[4,4,128,256]{3,2,1,0:T(8,128)(2,1)S(1)}, bf16[4,4,128,256]{3,2,1,0:T(8,128)(2,1)S(1)}, u32[]{:S(2)}, u32[]{:S(2)}) collective-permute-start(bf16[4,4,128,256]{3,2,1,0:T(8,128)(2,1)S(1)} %shard_map.100.refs_0_), channel_id=1, source_target_pairs={{0,2},{1,3},{2,0},{3,1},{4,68},{5,69},{6,70},{7,71},{8,10},{9,11},... | collective-permute-start | bytes 3145736 | tf_op jit(solution)/shard_map/ppermute | solution.py:467
  123.3 46.0 %collective-permute-start.12 = (bf16[4,4,128,256]{3,2,1,0:T(8,128)(2,1)S(1)}, bf16[4,4,128,256]{3,2,1,0:T(8,128)(2,1)S(1)}, u32[]{:S(2)}, u32[]{:S(2)}) collective-permute-start(bf16[4,4,128,256]{3,2,1,0:T(8,128)(2,1)S(1)} %shard_map.100.refs_0_), channel_id=1, source_target_pairs={{0,1},{1,2},{2,3},{3,0},{4,36},{5,37},{6,38},{7,39},{8,9},{9,10},{... | collective-permute-start | bytes 3145736 | tf_op jit(solution)/shard_map/ppermute | solution.py:467
  127.2 43.7 %collective-permute-start.11 = (bf16[4,4,128,256]{3,2,1,0:T(8,128)(2,1)S(1)}, bf16[4,4,128,256]{3,2,1,0:T(8,128)(2,1)S(1)}, u32[]{:S(2)}, u32[]{:S(2)}) collective-permute-start(bf16[4,4,128,256]{3,2,1,0:T(8,128)(2,1)S(1)} %shard_map.100.refs_0_), channel_id=1, source_target_pairs={{0,3},{1,0},{2,1},{3,2},{4,100},{5,101},{6,102},{7,103},{8,11},{9,... | collective-permute-start | bytes 3145736 | tf_op jit(solution)/shard_map/ppermute | solution.py:467
  153.1 46.6 %collective-permute-start.19 = (bf16[2,176,512]{2,1,0:T(8,128)(2,1)S(1)}, bf16[2,176,512]{2,1,0:T(8,128)(2,1)S(1)}, u32[]{:S(2)}, u32[]{:S(2)}) collective-permute-start(bf16[2,176,512]{2,1,0:T(8,128)(2,1)S(1)} %get-tuple-element.54), channel_id=1, source_target_pairs={{0,8},{8,16},{16,24},{24,32},{32,40},{40,48},{48,56},{56,64},{64,7... | collective-permute-start | bytes 1081352 | tf_op jit(solution)/shard_map/ppermute | solution.py:524
  154.4 45.4 %collective-permute-start.20 = (bf16[2,176,512]{2,1,0:T(8,128)(2,1)S(1)}, bf16[2,176,512]{2,1,0:T(8,128)(2,1)S(1)}, u32[]{:S(2)}, u32[]{:S(2)}) collective-permute-start(bf16[2,176,512]{2,1,0:T(8,128)(2,1)S(1)} %get-tuple-element.55), channel_id=1, source_target_pairs={{4,8},{12,16},{20,24},{28,32},{36,40},{44,48},{52,56},{60,64},{68,... | collective-permute-start | bytes 1081352 | tf_op jit(solution)/shard_map/ppermute | solution.py:524
  161.9 38.1 %collective-permute-start.23 = (bf16[4,4,128,256]{3,2,1,0:T(8,128)(2,1)}, bf16[4,4,128,256]{3,2,1,0:T(8,128)(2,1)S(1)}, u32[]{:S(2)}, u32[]{:S(2)}) collective-permute-start(bf16[4,4,128,256]{3,2,1,0:T(8,128)(2,1)} %get-tuple-element.61), channel_id=1, source_target_pairs={{0,1},{1,2},{2,3},{3,0},{4,36},{5,37},{6,38},{7,39},{8,9},{9,10},{... | collective-permute-start | bytes 3145736 | tf_op jit(solution)/shard_map/ppermute | solution.py:425
  170.3 32.3 %collective-permute-start.24 = (bf16[4,4,128,256]{3,2,1,0:T(8,128)(2,1)}, bf16[4,4,128,256]{3,2,1,0:T(8,128)(2,1)S(1)}, u32[]{:S(2)}, u32[]{:S(2)}) collective-permute-start(bf16[4,4,128,256]{3,2,1,0:T(8,128)(2,1)} %get-tuple-element.62), channel_id=1, source_target_pairs={{0,3},{1,0},{2,1},{3,2},{4,100},{5,101},{6,102},{7,103},{8,11},{9,... | collective-permute-start | bytes 3145736 | tf_op jit(solution)/shard_map/ppermute | solution.py:425
  170.9 31.7 %collective-permute-start.25 = (bf16[4,4,128,256]{3,2,1,0:T(8,128)(2,1)}, bf16[4,4,128,256]{3,2,1,0:T(8,128)(2,1)S(1)}, u32[]{:S(2)}, u32[]{:S(2)}) collective-permute-start(bf16[4,4,128,256]{3,2,1,0:T(8,128)(2,1)} %get-tuple-element.63), channel_id=1, source_target_pairs={{0,2},{1,3},{2,0},{3,1},{4,68},{5,69},{6,70},{7,71},{8,10},{9,11},... | collective-permute-start | bytes 3145736 | tf_op jit(solution)/shard_map/ppermute | solution.py:425
  199.7 47.2 %collective-permute-start.18 = (bf16[2,512,1024]{2,1,0:T(8,128)(2,1)}, bf16[2,512,1024]{2,1,0:T(8,128)(2,1)S(1)}, u32[]{:S(2)}, u32[]{:S(2)}) collective-permute-start(bf16[2,512,1024]{2,1,0:T(8,128)(2,1)} %get-tuple-element.53), channel_id=1, source_target_pairs={{0,4},{4,0},{1,5},{5,1},{2,6},{6,2},{3,7},{7,3},{8,12},{12,8},{9,1... | collective-permute-start | bytes 6291464 | tf_op jit(solution)/shard_map/ppermute | solution.py:400
  199.9 9.6 %collective-permute-start.29 = (bf16[2,4,128,256]{3,2,1,0:T(8,128)(2,1)S(1)}, bf16[2,4,128,256]{3,2,1,0:T(8,128)(2,1)S(1)}, u32[]{:S(2)}, u32[]{:S(2)}) collective-permute-start(bf16[2,4,128,256]{3,2,1,0:T(8,128)(2,1)S(1)} %get-tuple-element.71), channel_id=1, source_target_pairs={{0,1},{1,2},{2,3},{3,0},{4,36},{5,37},{6,38},{7,39},{8,9},{9,10},{... | collective-permute-start | bytes 1572872 | tf_op jit(solution)/shard_map/ppermute | solution.py:492
  199.9 10.6 %collective-permute-start.30 = (bf16[2,4,128,256]{3,2,1,0:T(8,128)(2,1)S(1)}, bf16[2,4,128,256]{3,2,1,0:T(8,128)(2,1)S(1)}, u32[]{:S(2)}, u32[]{:S(2)}) collective-permute-start(bf16[2,4,128,256]{3,2,1,0:T(8,128)(2,1)S(1)} %get-tuple-element.72), channel_id=1, source_target_pairs={{0,3},{1,0},{2,1},{3,2},{4,100},{5,101},{6,102},{7,103},{8,11},{9,... | collective-permute-start | bytes 1572872 | tf_op jit(solution)/shard_map/ppermute | solution.py:493
  210.8 20.7 %collective-permute-start.31 = (bf16[4,4,128,256]{3,2,1,0:T(8,128)(2,1)S(1)}, bf16[4,4,128,256]{3,2,1,0:T(8,128)(2,1)S(1)}, u32[]{:S(2)}, u32[]{:S(2)}) collective-permute-start(bf16[4,4,128,256]{3,2,1,0:T(8,128)(2,1)S(1)} %get-tuple-element.73), channel_id=1, source_target_pairs={{0,1},{1,2},{2,3},{3,0},{4,36},{5,37},{6,38},{7,39},{8,9},{9,10},{... | collective-permute-start | bytes 3145736 | tf_op jit(solution)/shard_map/ppermute | solution.py:495
  212.1 20.9 %collective-permute-start.32 = (bf16[4,4,128,256]{3,2,1,0:T(8,128)(2,1)S(1)}, bf16[4,4,128,256]{3,2,1,0:T(8,128)(2,1)S(1)}, u32[]{:S(2)}, u32[]{:S(2)}) collective-permute-start(bf16[4,4,128,256]{3,2,1,0:T(8,128)(2,1)S(1)} %get-tuple-element.74), channel_id=1, source_target_pairs={{0,3},{1,0},{2,1},{3,2},{4,100},{5,101},{6,102},{7,103},{8,11},{9,... | collective-permute-start | bytes 3145736 | tf_op jit(solution)/shard_map/ppermute | solution.py:495
  213.6 10.4 %collective-permute-start.21 = (bf16[2,176,512]{2,1,0:T(8,128)(2,1)S(1)}, bf16[2,176,512]{2,1,0:T(8,128)(2,1)S(1)}, u32[]{:S(2)}, u32[]{:S(2)}) collective-permute-start(bf16[2,176,512]{2,1,0:T(8,128)(2,1)S(1)} %get-tuple-element.56), channel_id=1, source_target_pairs={{0,8},{8,16},{16,24},{24,32},{32,40},{40,48},{48,56},{56,64},{64,7... | collective-permute-start | bytes 1081352 | tf_op jit(solution)/shard_map/ppermute | solution.py:528
  214.9 11.0 %collective-permute-start.22 = (bf16[2,176,512]{2,1,0:T(8,128)(2,1)S(1)}, bf16[2,176,512]{2,1,0:T(8,128)(2,1)S(1)}, u32[]{:S(2)}, u32[]{:S(2)}) collective-permute-start(bf16[2,176,512]{2,1,0:T(8,128)(2,1)S(1)} %get-tuple-element.57), channel_id=1, source_target_pairs={{4,8},{12,16},{20,24},{28,32},{36,40},{44,48},{52,56},{60,64},{68,... | collective-permute-start | bytes 1081352 | tf_op jit(solution)/shard_map/ppermute | solution.py:528
  224.0 10.1 %collective-permute-start.26 = (bf16[4,128,256]{2,1,0:T(8,128)(2,1)S(1)}, bf16[4,128,256]{2,1,0:T(8,128)(2,1)S(1)}, u32[]{:S(2)}, u32[]{:S(2)}) collective-permute-start(bf16[4,128,256]{2,1,0:T(8,128)(2,1)S(1)} %get-tuple-element.65), channel_id=1, source_target_pairs={{0,8},{1,9},{2,10},{3,11},{4,5},{5,6},{6,7},{7,4},{8,16},{9,17},{1... | collective-permute-start | bytes 786440 | tf_op jit(solution)/shard_map/ppermute | solution.py:425
  225.9 10.5 %collective-permute-start.27 = (bf16[4,128,256]{2,1,0:T(8,128)(2,1)S(1)}, bf16[4,128,256]{2,1,0:T(8,128)(2,1)S(1)}, u32[]{:S(2)}, u32[]{:S(2)}) collective-permute-start(bf16[4,128,256]{2,1,0:T(8,128)(2,1)S(1)} %get-tuple-element.66), channel_id=1, source_target_pairs={{0,24},{1,25},{2,26},{3,27},{4,7},{5,4},{6,5},{7,6},{8,0},{9,1},{1... | collective-permute-start | bytes 786440 | tf_op jit(solution)/shard_map/ppermute | solution.py:425
  234.1 8.5 %collective-permute-start.34 = (bf16[4,128,256]{2,1,0:T(8,128)(2,1)S(1)}, bf16[4,128,256]{2,1,0:T(8,128)(2,1)S(1)}, u32[]{:S(2)}, u32[]{:S(2)}) collective-permute-start(bf16[4,128,256]{2,1,0:T(8,128)(2,1)S(1)} %get-tuple-element.77), channel_id=1, source_target_pairs={{0,24},{1,25},{2,26},{3,27},{4,7},{5,4},{6,5},{7,6},{8,0},{9,1},{1... | collective-permute-start | bytes 786440 | tf_op jit(solution)/shard_map/ppermute | solution.py:425
  236.4 7.5 %collective-permute-start.35 = (bf16[4,128,256]{2,1,0:T(8,128)(2,1)S(1)}, bf16[4,128,256]{2,1,0:T(8,128)(2,1)S(1)}, u32[]{:S(2)}, u32[]{:S(2)}) collective-permute-start(bf16[4,128,256]{2,1,0:T(8,128)(2,1)S(1)} %get-tuple-element.78), channel_id=1, source_target_pairs={{0,16},{1,17},{2,18},{3,19},{4,6},{5,7},{6,4},{7,5},{8,24},{9,25},... | collective-permute-start | bytes 786440 | tf_op jit(solution)/shard_map/ppermute | solution.py:425
  (36 other events, 445.9 us)

commit v7 on v6

--- a/solution.py
+++ b/solution.py
@@ -87,28 +87,33 @@
 
 
 def main_kernel(weights, extra, meta, me, x_ref, xt_ref, *refs):
-    w0, w1, w3, *w2 = refs[:weights]
     qm, qo, qa, qb, cm, co, ca, cb = refs[weights : weights + 8]
     om, oo, oa, ob, d0, d1, d3, *d2 = refs[weights + 8 + extra : -10]
     k_s, v_s, gk_s, gv_s, q_s, ct_s, ctx_s, gq_s, dw_s, w_s = refs[-10:]
     step = pl.program_id(0)
     block = places(me)
 
-    @pl.when(step == 0)
-    def _():
-        def take(rc, carry):
-            for rb in range(4):
-                far = w2[rb * len(w2) // 4][rb % (4 // len(w2)), rc]
-                for ra, value in enumerate((w0[rb, rc], w1[rb, rc], far, w3[rb, rc])):
-                    bx, bzy = block(ra, rb, rc)
-                    w_s[bx, pl.ds(pl.multiple_of(bzy * 128, 128), 128), :] = value
-            return carry
-
-        lax.fori_loop(0, 4, take, 0)
-
+    if weights == 2:
+        wk, wv = (ref[...].reshape(D, HEAD_DIM) for ref in refs[:2])
+    else:
+        w0, w1, w3, *w2 = refs[:weights]
+
+        @pl.when(step == 0)
+        def _():
+            def take(rc, carry):
+                for rb in range(4):
+                    far = w2[rb // 2][rb % 2, rc]
+                    for ra, value in enumerate((w0[rb, rc], w1[rb, rc], far, w3[rb, rc])):
+                        bx, bzy = block(ra, rb, rc)
+                        w_s[bx, pl.ds(pl.multiple_of(bzy * 128, 128), 128), :] = value
+                return carry
+
+            lax.fori_loop(0, 4, take, 0)
+
+        wk, wv = w_s[step], w_s[2 + step]
     x = x_ref[...]
-    k_s[...] = jnp.dot(x, w_s[step], preferred_element_type=jnp.float32).astype(BF)
-    v_s[...] = jnp.dot(x, w_s[2 + step], preferred_element_type=jnp.float32).astype(BF)
+    k_s[...] = jnp.dot(x, wk, preferred_element_type=jnp.float32).astype(BF)
+    v_s[...] = jnp.dot(x, wv, preferred_element_type=jnp.float32).astype(BF)
     for pool, parts in ((q_s, (qm, qo, qa, qb)), (ct_s, (cm, co, ca, cb))):
         pool[0:TOK, :] = parts[0][...]
         pool[TOK:PAIR, :] = parts[1][...]
@@ -147,6 +152,9 @@
     def narrow(rows, kind):
         return pl.BlockSpec((rows, HEAD_DIM), lambda i, m, e: (0, kind * 4 + i * 2 + chunk))
 
+    def gathered(kind):
+        return pl.BlockSpec((32, 1, 64, HEAD_DIM), lambda i, m, e: (0, kind * 2 + i, 0, e[2]))
+
     def handed(kind):
         return pl.BlockSpec((TOK, HEAD_DIM), lambda i, m, e: (0, i * 4 + kind * 2 + chunk))
 
@@ -161,6 +169,11 @@
 
     parts = [(4, 4, 128, HEAD_DIM)] * 4 if chunk == 0 else [(4, 4, 128, HEAD_DIM)] * 3 + [(2, 4, 128, HEAD_DIM)] * 2
     anywhere = pl.BlockSpec(memory_space=pl.ANY)
+    if len(weights) == 1:
+        weights = [*weights, *weights]
+        weight_specs = [gathered(0), gathered(1)]
+    else:
+        weight_specs = [fixed(*w.shape) for w in weights]
     pair = pltpu.VMEM((PAIR, HEAD_DIM), BF)
     pool = pltpu.VMEM((POOL, HEAD_DIM), BF)
     return pl.pallas_call(
@@ -168,7 +181,7 @@
         grid_spec=pltpu.PrefetchScalarGridSpec(
             num_scalar_prefetch=2,
             grid=(2,),
-            in_specs=[fixed(PAIR, D), fixed(D, PAIR), *[fixed(*w.shape) for w in weights],
+            in_specs=[fixed(PAIR, D), fixed(D, PAIR), *weight_specs,
                       wide(), handed(0), narrow(WIN, 0), narrow(WIN, 0),
                       wide(), handed(1), narrow(WIN, 1), narrow(WIN, 1)]
             + [anywhere] * len(before),
@@ -180,7 +193,7 @@
         + [jax.ShapeDtypeStruct((2, WIN, HALF), BF)] * 2
         + [jax.ShapeDtypeStruct(shape, BF) for shape in parts],
         input_output_aliases={12 + len(weights) + n: n for n in range(len(before))},
-        compiler_params=pltpu.CompilerParams(vmem_limit_bytes=52 * MIB),
+        compiler_params=pltpu.CompilerParams(vmem_limit_bytes=44 * MIB),
         cost_estimate=pl.CostEstimate(flops=12_000_000_000, bytes_accessed=24_000_000, transcendentals=500_000),
     )(meta, me, x, xt, *weights, q, given, sent_a, sent_b, ct, given, sent_a, sent_b, *before)
 
@@ -252,9 +265,9 @@
     device = (t * 2 + core) * 4 + x
     start = jnp.int32(0)
     for slot in range(SEGS):
-        begin, length = start, dec_len[device, slot]
-
-        @pl.when((partner[device, slot] >> 5) != t)
+        begin, length = start, dec_len[slot, device]
+
+        @pl.when((partner[slot, device] >> 5) != t)
         def _():
             info[0] = align(begin, TOK)
             info[2] = begin
@@ -278,8 +291,8 @@
         start = jnp.int32(side * TOK)
         for slot in range(SEGS):
             meta[side * SEGS + slot, 0] = start
-            meta[side * SEGS + slot, 1] = enc_len[device, slot]
-            start = start + enc_len[device, slot]
+            meta[side * SEGS + slot, 1] = enc_len[slot, device]
+            start = start + enc_len[slot, device]
     for near in range(4):
         dp = t * 2 - 1 + near
         device = jnp.clip(dp, 0, 31) * 4 + x
@@ -287,8 +300,8 @@
         same = (dp & 1) == core
         start = jnp.int32(0)
         for slot in range(SEGS):
-            begin, length = start, dec_len[device, slot]
-            owner = partner[device, slot] >> 4
+            begin, length = start, dec_len[slot, device]
+            owner = partner[slot, device] >> 4
             if near in (1, 2):
                 at = begin + jnp.where(same, 0, TOK)
             else:
@@ -296,7 +309,7 @@
 
             @pl.when(real & ((owner >> 1) == t))
             def _():
-                entry = jnp.where((owner & 1) == core, 0, SEGS) + (partner[device, slot] & 3)
+                entry = jnp.where((owner & 1) == core, 0, SEGS) + (partner[slot, device] & 3)
                 meta[entry, 2] = at
                 meta[entry, 3] = length
 
@@ -311,12 +324,12 @@
     return pl.pallas_call(
         depart_kernel,
         in_specs=[scalar, scalar, scalar, scalar, whole, whole],
-        out_specs=[scalar, scalar, whole, whole],
+        out_specs=[scalar, scalar, pl.BlockSpec(memory_space=pltpu.VMEM), pl.BlockSpec(memory_space=pltpu.VMEM)],
         scratch_shapes=[pltpu.SemaphoreType.DMA((8,))],
         out_shape=[jax.ShapeDtypeStruct((2 * SEGS, 4), jnp.int32), jax.ShapeDtypeStruct((4,), jnp.int32)]
         + [jax.ShapeDtypeStruct((WIN, 2048), BF)] * 2,
-        compiler_params=pltpu.CompilerParams(vmem_limit_bytes=60 * MIB),
-    )(me, enc_lengths, dec_lengths, dec_partner, q, ct)
+        compiler_params=pltpu.CompilerParams(vmem_limit_bytes=59 * MIB),
+    )(me, enc_lengths.T, dec_lengths.T, dec_partner.T, q, ct)
 
 
 def hand_kernel(me, q_ref, ct_ref, *refs):
@@ -425,42 +438,41 @@
     return [parts[0]] + [lax.ppermute(parts[r], ALL, shift(phase, r)) for r in (1, 3, 2)]
 
 
-def join_kernel(cols, *refs):
+def join_kernel(*refs):
     for n in range(4):
-        refs[-1][n] = refs[n][..., cols]
-
-
-def join(parts, after, cols):
+        refs[-1][n] = refs[n][...]
+
+
+def join(parts, after):
     whole = pl.BlockSpec(memory_space=pltpu.VMEM)
     return pl.pallas_call(
-        functools.partial(join_kernel, cols),
+        join_kernel,
         in_specs=[whole] * 4 + [pl.BlockSpec(memory_space=pl.ANY)] * len(after),
         out_specs=whole,
-        out_shape=jax.ShapeDtypeStruct((4,) + parts[0].shape[:-1] + (cols.stop - cols.start,), BF),
+        out_shape=jax.ShapeDtypeStruct((4,) + parts[0].shape, BF),
         compiler_params=pltpu.CompilerParams(vmem_limit_bytes=16 * MIB),
     )(*parts, *after)
 
 
-def pick_kernel(me, w_ref, got_ref, *refs):
-    mine = w_ref[:, pl.ds(pl.multiple_of(me[2] * HALF, HALF), HALF)]
+def pick_kernel(me, w_ref, got_ref, out_ref):
+    mine = w_ref[:, pl.ds(pl.multiple_of(me[2] * HALF, HALF), HEAD_DIM)]
     for core in range(2):
 
         @pl.when(me[2] == core)
         def _():
-            refs[-1][core * 64 : core * 64 + 64, :] = mine
-            refs[-1][64 - core * 64 : 128 - core * 64, :] = got_ref[...]
-
-
-def pick(me, weights, got, after):
+            out_ref[core * 64 : core * 64 + 64, :] = mine
+            out_ref[64 - core * 64 : 128 - core * 64, :] = got_ref[...]
+
+
+def pick(me, weights, got):
     whole = pl.BlockSpec(memory_space=pltpu.VMEM)
     return pl.pallas_call(
         pick_kernel,
-        in_specs=[pl.BlockSpec(memory_space=pltpu.SMEM), whole, whole]
-        + [pl.BlockSpec(memory_space=pl.ANY)] * len(after),
+        in_specs=[pl.BlockSpec(memory_space=pltpu.SMEM), whole, whole],
         out_specs=whole,
-        out_shape=jax.ShapeDtypeStruct((128, HALF), BF),
-        compiler_params=pltpu.CompilerParams(vmem_limit_bytes=16 * MIB),
-    )(me, weights, got, *after)
+        out_shape=jax.ShapeDtypeStruct((128, HEAD_DIM), BF),
+        compiler_params=pltpu.CompilerParams(vmem_limit_bytes=16 * MIB),
+    )(me, weights, got)
 
 
 def ring(value, phase, amount):
@@ -498,23 +510,22 @@
 def body(enc_hidden, kv_weights, queries, cotangent, enc_lengths, dec_lengths, dec_partner):
     z, y, c, x = (lax.axis_index(a) for a in ALL)
     me = jnp.stack([z, y, c, x]).astype(jnp.int32)
-    swapped = swap(enc_hidden)
+    cols = [kv_weights[:, n * HEAD_DIM : (n + 1) * HEAD_DIM] for n in range(4)]
+    later = lax.all_gather(jnp.concatenate([cols[1], cols[3]], axis=1), ALL, axis=0).reshape(32, 4, 64, HALF)
+
+    got = swap(jnp.where(c == 0, cols[2], cols[0]))
+    own = pick(me, kv_weights, got)
+    first = [own] + [ring(own, 2, n) for n in (1, 2, 3)]
     meta, info, leave_a, leave_b = depart(me, enc_lengths, dec_lengths, dec_partner, queries, cotangent)
     sent_a = lax.ppermute(leave_a, DP, SEND_A)
     sent_b = lax.ppermute(leave_b, DP, SEND_B)
-
-    got = swap(jnp.where(c == 0, kv_weights[:, HALF:], kv_weights[:, :HALF]))
-    own = pick(me, kv_weights, got, [leave_a, swapped])
-    first = [own] + [ring(own, 2, n) for n in (1, 2, 3)]
-    part = join(first, [sent_a], slice(0, HALF))
+    given = hand(me, queries, cotangent, [leave_a])
+    part = join(first, [given])
     second = [part] + [ring(part, 1, n) for n in (1, 2, 3)]
-    tokens, tokens_t = turn(enc_hidden, swapped, [second[1]])
-    given = hand(me, queries, cotangent, [tokens_t])
-    part = join(second, [given], slice(0, HEAD_DIM))
+    part = join(second, [])
+    tokens, tokens_t = turn(enc_hidden, swap(enc_hidden), [part, sent_a])
     ahead, behind = ring(part, 0, 1), ring(part, 0, -1)
-    weights = [[part, ahead, behind, ring(behind[:2], 0, -1), ring(ahead[2:], 0, 1)]]
-    part = join(second, [ahead, behind], slice(HEAD_DIM, HALF))
-    weights.append([part, ring(part, 0, 1), ring(part, 0, -1), ring(part, 0, 2)])
+    weights = [[part, ahead, behind, ring(behind[:2], 0, -1), ring(ahead[2:], 0, 1)], [later]]
 
     shared = (meta, me, tokens, tokens_t)
     inputs = (queries, cotangent, swap(given), sent_a, sent_b)

time: 260 us -> 214 us (0.82)
  Pallas kernels: 106 us -> 59.8 us
  waiting for transfers between devices: 67.3 us -> 50.8 us
  between operations: 1.11 us -> 14.4 us
    pallas_call x1, Pallas kernels: 49.5 us -> 3.62 us  [depart(): pl.pallas_call(depart_kernel, in_specs=[scalar, scalar, scalar, scalar, w...]
    ppermute x13 -> x10, waiting for transfers between devices: 37.1 us -> 24.3 us  [ring(): return lax.ppermute(value, ALL, shift(phase, -amount))]
    ppermute x12, starting transfers between devices: 22.9 us -> 28.3 us  [exchange(): lax.ppermute(parts[r], ALL, shift(phase, r))]
    ppermute x13 -> x10, starting transfers between devices: 20.1 us -> 16.4 us  [ring(): return lax.ppermute(value, ALL, shift(phase, -amount))]
    pallas_call x2, Pallas kernels: 46.3 us -> 43 us  [run_main(): pl.pallas_call(functools.partial(main_kernel, len(weights), len(before)),...]
    unnamed x59 -> x40, local copies, waits for them, and re-layouts: 13.2 us -> 13.9 us
  transfers between devices with their start and end apart: 40 -> 38, of which waited for: 17 -> 15; matrix products, arithmetic and copies ran while one was open for 2% -> 0% of each run, Pallas kernels for 41% -> 28%
where the time goes in v7:
time: 214 us; the launch traced here: 213 us
  starting transfers between devices  72.2 us (34%)
  Pallas kernels  59.8 us (28%)
  waiting for transfers between devices  50.8 us (24%)
  between operations  14.4 us (7%)
  local copies, waits for them, and re-layouts  13.9 us (6%)
  other arithmetic  2.27 us (1%)
    pallas_call x2, Pallas kernels, run_main(): pl.pallas_call(functools.partial(main_kernel, len(weights), len(before)),...  43 us
    ppermute x12, starting transfers between devices, exchange(): lax.ppermute(parts[r], ALL, shift(phase, r))  28.3 us
    ppermute x10, waiting for transfers between devices, ring(): return lax.ppermute(value, ALL, shift(phase, -amount))  24.3 us
    ppermute x10, starting transfers between devices, ring(): return lax.ppermute(value, ALL, shift(phase, -amount))  16.4 us
    unnamed x40, local copies, waits for them, and re-layouts  13.9 us
    ppermute x4, starting transfers between devices, body(): lax.ppermute(part, DP, pairs)  9.69 us
    ppermute x12, waiting for transfers between devices, exchange(): lax.ppermute(parts[r], ALL, shift(phase, r))  8.96 us
    ppermute x4, waiting for transfers between devices, body(): lax.ppermute(part, DP, pairs)  7.61 us
  transfers between devices with their start and end apart: 38, of which 15 were waited for; matrix products, arithmetic and copies ran while one was open for 0% of the time, Pallas kernels for 28%

profile of v7, /device:TPU:1, one launch (start us, length us, event | category | flops | bytes accessed | tf_op | source)
XLA Modules:
  0.0 213.4 jit_solution(8128169122840070624)
XLA Ops:
  14.0 2.6 %collective-permute-start.3 = (bf16[128,256]{1,0:T(8,128)(2,1)S(1)}, bf16[128,256]{1,0:T(8,128)(2,1)S(1)}, u32[]{:S(2)}, u32[]{:S(2)}) collective-permute-start(bf16[128,256]{1,0:T(8,128)(2,1)S(1)} %shard_map.95.refs_0_), channel_id=1, source_target_pairs={{0,64},{1,65},{2,66},{3,67},{4,20},{5,21},{6,22},{7,23},{8,72},{9,... | collective-permute-start | bytes 196616 | tf_op jit(solution)/shard_map/ppermute | solution.py:479
  17.7 3.6 %shard_map.94 = (s32[8,4]{1,0:T(8,128)}, s32[4]{0:T(128)}, bf16[176,2048]{1,0:T(8,128)(2,1)}, bf16[176,2048]{1,0:T(8,128)(2,1)}) custom-call(s32[4]{0:T(128)} %copy-done.8, s32[4,128]{1,0:T(4,128)} %bitcast.8, s32[4,128]{1,0:T(4,128)} %bitcast.9, s32[4,128]{1,0:T(4,128)} %bitcast.10, bf16[512,2048]{1,0:T(8,128)(2,1)} %refs_2_.1, bf16[512,2048]{1,0:T(8,128)(2,1)} %refs_6_.1), custom_call_target="tpu_custom_call" | custom-call | tf_op jit(solution)/shard_map/pallas_call | solution.py:324
  25.7 2.0 collective-permute-start.9
  29.0 2.5 %collective-permute-start.6 = (bf16[4,128,256]{2,1,0:T(8,128)(2,1)S(1)}, bf16[4,128,256]{2,1,0:T(8,128)(2,1)S(1)}, u32[]{:S(2)}, u32[]{:S(2)}) collective-permute-start(bf16[4,128,256]{2,1,0:T(8,128)(2,1)S(1)} %shard_map.97.refs_0_), channel_id=1, source_target_pairs={{0,16},{1,17},{2,18},{3,19},{4,6},{5,7},{6,4},{7,5},{8,24},{9,25},... | collective-permute-start | bytes 786440 | tf_op jit(solution)/shard_map/ppermute | solution.py:479
  32.6 2.1 collective-permute-done.7.refs_3_
  34.8 3.9 %collective-permute-done.6.refs_2_ = bf16[4,128,256]{2,1,0:T(8,128)(2,1)S(1)} collective-permute-done((bf16[4,128,256]{2,1,0:T(8,128)(2,1)S(1)}, bf16[4,128,256]{2,1,0:T(8,128)(2,1)S(1)}, u32[]{:S(2)}, u32[]{:S(2)}) %collective-permute-start.6) | collective-permute-done | bytes 262176 | tf_op jit(solution)/shard_map/ppermute | solution.py:479
  41.5 3.0 %collective-permute-start.8 = (bf16[176,2048]{1,0:T(8,128)(2,1)S(1)}, bf16[176,2048]{1,0:T(8,128)(2,1)S(1)}, u32[]{:S(2)}, u32[]{:S(2)}) collective-permute-start(bf16[176,2048]{1,0:T(8,128)(2,1)S(1)} %copy-done.6), channel_id=1, source_target_pairs={{8,0},{16,8},{24,16},{32,24},{40,32},{48,40},{56,48},{64,56},{72,6... | collective-permute-start | bytes 2162696 | tf_op jit(solution)/shard_map/ppermute | solution.py:520
  44.6 17.2 %collective-permute-done.12.refs_2_ = bf16[4,4,128,256]{3,2,1,0:T(8,128)(2,1)S(1)} collective-permute-done((bf16[4,4,128,256]{3,2,1,0:T(8,128)(2,1)S(1)}, bf16[4,4,128,256]{3,2,1,0:T(8,128)(2,1)S(1)}, u32[]{:S(2)}, u32[]{:S(2)}) %collective-permute-start.12) | collective-permute-done | bytes 1048608 | tf_op jit(solution)/shard_map/ppermute | solution.py:479
  63.7 2.4 %collective-permute-start.13 = (bf16[2,4,128,256]{3,2,1,0:T(8,128)(2,1)S(1)}, bf16[2,4,128,256]{3,2,1,0:T(8,128)(2,1)S(1)}, u32[]{:S(2)}, u32[]{:S(2)}) collective-permute-start(bf16[2,4,128,256]{3,2,1,0:T(8,128)(2,1)S(1)} %slice.24), channel_id=1, source_target_pairs={{0,1},{1,2},{2,3},{3,0},{4,36},{5,37},{6,38},{7,39},{8,9},{9,10},{... | collective-permute-start | bytes 1572872 | tf_op jit(solution)/shard_map/ppermute | solution.py:479
  67.3 3.6 %shard_map.99 = (bf16[1024,2048]{1,0:T(8,128)(2,1)S(1)}, bf16[2048,1024]{1,0:T(8,128)(2,1)S(1)}) custom-call(bf16[512,2048]{1,0:T(8,128)(2,1)S(1)} %copy-done.3, bf16[512,2048]{1,0:T(8,128)(2,1)} %collective-permute-done.b_ref, bf16[4,4,128,256]{3,2,1,0:T(8,128)(2,1)S(1)} %shard_map.98.refs_0_, ...), custom_call_target="tpu_custom_call" | custom-call | tf_op jit(solution)/shard_map/pallas_call | solution.py:368
  71.0 2.1 copy-done.12
  73.0 1.9 copy-done.13
  77.4 22.0 %shard_map.100 = (bf16[2,512,1024]{2,1,0:T(8,128)(2,1)}, bf16[2,512,1024]{2,1,0:T(8,128)(2,1)}, bf16[2,176,512]{2,1,0:T(8,128)(2,1)}, bf16[2,176,512]{2,1,0:T(8,...) custom-call(s32[8,4]{1,0:T(8,128)S(1)} %copy-done.16, ...), custom_call_target="tpu_custom_call" | custom-call | flops 12000000000 | bytes 24000000 | tf_op jit(solution)/shard_map/pallas_call | solution.py:179
  100.7 3.7 %collective-permute-start.17 = (bf16[2,176,512]{2,1,0:T(8,128)(2,1)}, bf16[2,176,512]{2,1,0:T(8,128)(2,1)S(1)}, u32[]{:S(2)}, u32[]{:S(2)}) collective-permute-start(bf16[2,176,512]{2,1,0:T(8,128)(2,1)} %get-tuple-element.55), channel_id=1, source_target_pairs={{4,8},{12,16},{20,24},{28,32},{36,40},{44,48},{52,56},{60,64},{68,... | collective-permute-start | bytes 1081352 | tf_op jit(solution)/shard_map/ppermute | solution.py:535
  104.5 13.4 %collective-permute-start.20 = (bf16[4,4,128,256]{3,2,1,0:T(8,128)(2,1)}, bf16[4,4,128,256]{3,2,1,0:T(8,128)(2,1)S(1)}, u32[]{:S(2)}, u32[]{:S(2)}) collective-permute-start(bf16[4,4,128,256]{3,2,1,0:T(8,128)(2,1)} %get-tuple-element.61), channel_id=1, source_target_pairs={{0,1},{1,2},{2,3},{3,0},{4,36},{5,37},{6,38},{7,39},{8,9},{9,10},{... | collective-permute-start | bytes 3145736 | tf_op jit(solution)/shard_map/ppermute | solution.py:438
  117.9 5.6 %collective-permute-start.22 = (bf16[4,4,128,256]{3,2,1,0:T(8,128)(2,1)}, bf16[4,4,128,256]{3,2,1,0:T(8,128)(2,1)}, u32[]{:S(2)}, u32[]{:S(2)}) collective-permute-start(bf16[4,4,128,256]{3,2,1,0:T(8,128)(2,1)} %get-tuple-element.63), channel_id=1, source_target_pairs={{0,2},{1,3},{2,0},{3,1},{4,68},{5,69},{6,70},{7,71},{8,10},{9,11},... | collective-permute-start | bytes 3145736 | tf_op jit(solution)/shard_map/ppermute | solution.py:438
  126.1 21.0 %shard_map.101 = (bf16[2,512,1024]{2,1,0:T(8,128)(2,1)S(1)}, bf16[2,512,1024]{2,1,0:T(8,128)(2,1)}, bf16[2,176,512]{2,1,0:T(8,128)(2,1)S(1)}, bf16[2,176,512]{2,...) custom-call(s32[8,4]{1,0:T(8,128)S(1)} %copy-done.16, ...), custom_call_target="tpu_custom_call", output_to_operand_aliasing={{0}: (14, {}), {1}: (15, {})} | custom-call | flops 12000000000 | bytes 24000000 | tf_op jit(solution)/shard_map/pallas_call | solution.py:179
  147.3 2.7 %collective-permute-start.27 = (bf16[2,4,128,256]{3,2,1,0:T(8,128)(2,1)S(1)}, bf16[2,4,128,256]{3,2,1,0:T(8,128)(2,1)S(1)}, u32[]{:S(2)}, u32[]{:S(2)}) collective-permute-start(bf16[2,4,128,256]{3,2,1,0:T(8,128)(2,1)S(1)} %get-tuple-element.72), channel_id=1, source_target_pairs={{0,3},{1,0},{2,1},{3,2},{4,100},{5,101},{6,102},{7,103},{8,11},{9,... | collective-permute-start | bytes 1572872 | tf_op jit(solution)/shard_map/ppermute | solution.py:505
  150.0 2.7 %shard_map.103 = (bf16[4,128,256]{2,1,0:T(8,128)(2,1)S(1)}, bf16[4,128,256]{2,1,0:T(8,128)(2,1)S(1)}, bf16[4,128,256]{2,1,0:T(8,128)(2,1)S(1)}, bf16[4,128,256]{2,1,0:T(8,128)(2,1)S(1)}) custom-call(bf16[4,4,128,256]{3,2,1,0:T(8,128)(2,1)S(1)} %get-tuple-element.60.refs_0_, bf16[4,4,128,256]{3,2,1,0:T(8,128)(2,1)S(1)} %collective-permute-done.20.refs_1_, ...), custom_call_target="tpu_custom_call" | custom-call | tf_op jit(solution)/shard_map/pallas_call | solution.py:212
  152.6 4.2 %collective-permute-done.26.got_a = bf16[2,4,128,256]{3,2,1,0:T(8,128)(2,1)S(1)} collective-permute-done((bf16[2,4,128,256]{3,2,1,0:T(8,128)(2,1)S(1)}, bf16[2,4,128,256]{3,2,1,0:T(8,128)(2,1)S(1)}, u32[]{:S(2)}, u32[]{:S(2)}) %collective-permute-start.26) | collective-permute-done | bytes 524320 | tf_op jit(solution)/shard_map/ppermute | solution.py:504
  157.5 2.3 %collective-permute-start.29 = (bf16[4,4,128,256]{3,2,1,0:T(8,128)(2,1)S(1)}, bf16[4,4,128,256]{3,2,1,0:T(8,128)(2,1)S(1)}, u32[]{:S(2)}, u32[]{:S(2)}) collective-permute-start(bf16[4,4,128,256]{3,2,1,0:T(8,128)(2,1)S(1)} %get-tuple-element.74), channel_id=1, source_target_pairs={{0,3},{1,0},{2,1},{3,2},{4,100},{5,101},{6,102},{7,103},{8,11},{9,... | collective-permute-start | bytes 3145736 | tf_op jit(solution)/shard_map/ppermute | solution.py:507
  161.1 3.4 %collective-permute-start.19 = (bf16[2,176,512]{2,1,0:T(8,128)(2,1)S(1)}, bf16[2,176,512]{2,1,0:T(8,128)(2,1)S(1)}, u32[]{:S(2)}, u32[]{:S(2)}) collective-permute-start(bf16[2,176,512]{2,1,0:T(8,128)(2,1)S(1)} %get-tuple-element.57), channel_id=1, source_target_pairs={{4,8},{12,16},{20,24},{28,32},{36,40},{44,48},{52,56},{60,64},{68,... | collective-permute-start | bytes 1081352 | tf_op jit(solution)/shard_map/ppermute | solution.py:539
  164.6 5.7 %collective-permute-done.18.refs_4_.refs_3_ = bf16[2,176,512]{2,1,0:T(8,128)(2,1)S(1)} collective-permute-done((bf16[2,176,512]{2,1,0:T(8,128)(2,1)S(1)}, bf16[2,176,512]{2,1,0:T(8,128)(2,1)S(1)}, u32[]{:S(2)}, u32[]{:S(2)}) %collective-permute-start.18) | collective-permute-done | bytes 360480 | tf_op jit(solution)/shard_map/ppermute | solution.py:539
  170.2 1.9 collective-permute-done.19.refs_5_.refs_4_
  172.9 4.1 %collective-permute-done.28.refs_1_ = bf16[4,4,128,256]{3,2,1,0:T(8,128)(2,1)S(1)} collective-permute-done((bf16[4,4,128,256]{3,2,1,0:T(8,128)(2,1)S(1)}, bf16[4,4,128,256]{3,2,1,0:T(8,128)(2,1)S(1)}, u32[]{:S(2)}, u32[]{:S(2)}) %collective-permute-start.28) | collective-permute-done | bytes 1048608 | tf_op jit(solution)/shard_map/ppermute | solution.py:507
  177.0 3.2 %collective-permute-start.25 = (bf16[4,128,256]{2,1,0:T(8,128)(2,1)S(1)}, bf16[4,128,256]{2,1,0:T(8,128)(2,1)S(1)}, u32[]{:S(2)}, u32[]{:S(2)}) collective-permute-start(bf16[4,128,256]{2,1,0:T(8,128)(2,1)S(1)} %get-tuple-element.67), channel_id=1, source_target_pairs={{0,16},{1,17},{2,18},{3,19},{4,6},{5,7},{6,4},{7,5},{8,24},{9,25},... | collective-permute-start | bytes 786440 | tf_op jit(solution)/shard_map/ppermute | solution.py:438
  181.0 2.7 %collective-permute-start.31 = (bf16[4,128,256]{2,1,0:T(8,128)(2,1)S(1)}, bf16[4,128,256]{2,1,0:T(8,128)(2,1)S(1)}, u32[]{:S(2)}, u32[]{:S(2)}) collective-permute-start(bf16[4,128,256]{2,1,0:T(8,128)(2,1)S(1)} %get-tuple-element.77), channel_id=1, source_target_pairs={{0,24},{1,25},{2,26},{3,27},{4,7},{5,4},{6,5},{7,6},{8,0},{9,1},{1... | collective-permute-start | bytes 786440 | tf_op jit(solution)/shard_map/ppermute | solution.py:438
  184.2 3.4 %collective-permute-done.30.refs_5_ = bf16[4,128,256]{2,1,0:T(8,128)(2,1)S(1)} collective-permute-done((bf16[4,128,256]{2,1,0:T(8,128)(2,1)S(1)}, bf16[4,128,256]{2,1,0:T(8,128)(2,1)S(1)}, u32[]{:S(2)}, u32[]{:S(2)}) %collective-permute-start.30) | collective-permute-done | bytes 262176 | tf_op jit(solution)/shard_map/ppermute | solution.py:438
  187.7 2.1 collective-permute-done.31.refs_6_
  191.0 2.7 %collective-permute-start.34 = (bf16[128,512]{1,0:T(8,128)(2,1)S(1)}, bf16[128,512]{1,0:T(8,128)(2,1)S(1)}, u32[]{:S(2)}, u32[]{:S(2)}) collective-permute-start(bf16[128,512]{1,0:T(8,128)(2,1)S(1)} %get-tuple-element.81), channel_id=1, source_target_pairs={{0,96},{1,97},{2,98},{3,99},{4,28},{5,29},{6,30},{7,31},{8,104},{9... | collective-permute-start | bytes 393224 | tf_op jit(solution)/shard_map/ppermute | solution.py:438
  193.7 3.4 %shard_map.102 = (bf16[512,2048]{1,0:T(8,128)(2,1)}, bf16[512,2048]{1,0:T(8,128)(2,1)}) custom-call(s32[4]{0:T(128)S(1)} %copy-done.11, bf16[2,512,1024]{2,1,0:T(8,128)(2,1)S(1)} %get-tuple-element.52.refs_0_.refs_4_, bf16[2,512,1024]{2,1,0:T(8,128)(2,1)S(1)} %collective-permute-done.15.refs_1_, ...), custom_call_target="tpu_custom_call" | custom-call | tf_op jit(solution)/shard_map/pallas_call | solution.py:399
  201.2 3.7 %collective-permute-start.36 = (f32[64,512]{1,0:T(8,128)S(1)}, f32[64,512]{1,0:T(8,128)S(1)}, u32[]{:S(2)}, u32[]{:S(2)}) collective-permute-start(f32[64,512]{1,0:T(8,128)S(1)} %get-tuple-element.84), channel_id=1, source_target_pairs={{0,4},{4,0},{1,5},{5,1},{2,6},{6,2},{3,7},{7,3},{8,12},{12,8},{9,1... | collective-permute-start | bytes 393224 | tf_op jit(solution)/shard_map/ppermute | solution.py:413
  (106 shorter events, 38.5 us)
Async XLA Ops:
  7.2 116.3 %all-gather.3.cloned.1.call-start = ((), (), s32[]{:S(2)}) async-start(), calls=%async_computation | async-start | bytes 8454144 | tf_op jit(solution)/shard_map/all_gather | solution.py:514
  10.2 57.1 %collective-permute-start = (bf16[512,2048]{1,0:T(8,128)(2,1)}, bf16[512,2048]{1,0:T(8,128)(2,1)}, u32[]{:S(2)}, u32[]{:S(2)}) collective-permute-start(bf16[512,2048]{1,0:T(8,128)(2,1)} %a_ref.1), channel_id=1, source_target_pairs={{0,4},{4,0},{1,5},{5,1},{2,6},{6,2},{3,7},{7,3},{8,12},{12,8},{9,1... | collective-permute-start | bytes 6291464 | tf_op jit(solution)/shard_map/ppermute | solution.py:413
  12.5 15.2 %collective-permute-start.4 = (bf16[128,256]{1,0:T(8,128)(2,1)S(1)}, bf16[128,256]{1,0:T(8,128)(2,1)S(1)}, u32[]{:S(2)}, u32[]{:S(2)}) collective-permute-start(bf16[128,256]{1,0:T(8,128)(2,1)S(1)} %shard_map.95.refs_0_), channel_id=1, source_target_pairs={{0,32},{1,33},{2,34},{3,35},{4,12},{5,13},{6,14},{7,15},{8,40},{9,... | collective-permute-start | bytes 196616 | tf_op jit(solution)/shard_map/ppermute | solution.py:479
  14.0 13.7 %collective-permute-start.3 = (bf16[128,256]{1,0:T(8,128)(2,1)S(1)}, bf16[128,256]{1,0:T(8,128)(2,1)S(1)}, u32[]{:S(2)}, u32[]{:S(2)}) collective-permute-start(bf16[128,256]{1,0:T(8,128)(2,1)S(1)} %shard_map.95.refs_0_), channel_id=1, source_target_pairs={{0,64},{1,65},{2,66},{3,67},{4,20},{5,21},{6,22},{7,23},{8,72},{9,... | collective-permute-start | bytes 196616 | tf_op jit(solution)/shard_map/ppermute | solution.py:479
  16.6 11.1 %collective-permute-start.2 = (bf16[128,256]{1,0:T(8,128)(2,1)S(1)}, bf16[128,256]{1,0:T(8,128)(2,1)S(1)}, u32[]{:S(2)}, u32[]{:S(2)}) collective-permute-start(bf16[128,256]{1,0:T(8,128)(2,1)S(1)} %shard_map.95.refs_0_), channel_id=1, source_target_pairs={{0,96},{1,97},{2,98},{3,99},{4,28},{5,29},{6,30},{7,31},{8,104},{9... | collective-permute-start | bytes 196616 | tf_op jit(solution)/shard_map/ppermute | solution.py:479
  25.7 50.3 %collective-permute-start.9 = (bf16[512,2048]{1,0:T(8,128)(2,1)S(1)}, bf16[512,2048]{1,0:T(8,128)(2,1)S(1)}, u32[]{:S(2)}, u32[]{:S(2)}) collective-permute-start(bf16[512,2048]{1,0:T(8,128)(2,1)S(1)} %shard_map.96.refs_4_), channel_id=1, source_target_pairs={{0,4},{4,0},{1,5},{5,1},{2,6},{6,2},{3,7},{7,3},{8,12},{12,8},{9,1... | collective-permute-start | bytes 6291464 | tf_op jit(solution)/shard_map/ppermute | solution.py:413
  27.8 7.0 %collective-permute-start.7 = (bf16[4,128,256]{2,1,0:T(8,128)(2,1)S(1)}, bf16[4,128,256]{2,1,0:T(8,128)(2,1)S(1)}, u32[]{:S(2)}, u32[]{:S(2)}) collective-permute-start(bf16[4,128,256]{2,1,0:T(8,128)(2,1)S(1)} %shard_map.97.refs_0_), channel_id=1, source_target_pairs={{0,8},{1,9},{2,10},{3,11},{4,5},{5,6},{6,7},{7,4},{8,16},{9,17},{1... | collective-permute-start | bytes 786440 | tf_op jit(solution)/shard_map/ppermute | solution.py:479
  29.0 9.6 %collective-permute-start.6 = (bf16[4,128,256]{2,1,0:T(8,128)(2,1)S(1)}, bf16[4,128,256]{2,1,0:T(8,128)(2,1)S(1)}, u32[]{:S(2)}, u32[]{:S(2)}) collective-permute-start(bf16[4,128,256]{2,1,0:T(8,128)(2,1)S(1)} %shard_map.97.refs_0_), channel_id=1, source_target_pairs={{0,16},{1,17},{2,18},{3,19},{4,6},{5,7},{6,4},{7,5},{8,24},{9,25},... | collective-permute-start | bytes 786440 | tf_op jit(solution)/shard_map/ppermute | solution.py:479
  31.5 7.2 %collective-permute-start.5 = (bf16[4,128,256]{2,1,0:T(8,128)(2,1)S(1)}, bf16[4,128,256]{2,1,0:T(8,128)(2,1)S(1)}, u32[]{:S(2)}, u32[]{:S(2)}) collective-permute-start(bf16[4,128,256]{2,1,0:T(8,128)(2,1)S(1)} %shard_map.97.refs_0_), channel_id=1, source_target_pairs={{0,24},{1,25},{2,26},{3,27},{4,7},{5,4},{6,5},{7,6},{8,0},{9,1},{1... | collective-permute-start | bytes 786440 | tf_op jit(solution)/shard_map/ppermute | solution.py:479
  38.7 23.0 %collective-permute-start.12 = (bf16[4,4,128,256]{3,2,1,0:T(8,128)(2,1)S(1)}, bf16[4,4,128,256]{3,2,1,0:T(8,128)(2,1)S(1)}, u32[]{:S(2)}, u32[]{:S(2)}) collective-permute-start(bf16[4,4,128,256]{3,2,1,0:T(8,128)(2,1)S(1)} %shard_map.98.refs_0_), channel_id=1, source_target_pairs={{0,1},{1,2},{2,3},{3,0},{4,36},{5,37},{6,38},{7,39},{8,9},{9,10},{... | collective-permute-start | bytes 3145736 | tf_op jit(solution)/shard_map/ppermute | solution.py:479
  39.6 24.1 %collective-permute-start.11 = (bf16[4,4,128,256]{3,2,1,0:T(8,128)(2,1)S(1)}, bf16[4,4,128,256]{3,2,1,0:T(8,128)(2,1)S(1)}, u32[]{:S(2)}, u32[]{:S(2)}) collective-permute-start(bf16[4,4,128,256]{3,2,1,0:T(8,128)(2,1)S(1)} %shard_map.98.refs_0_), channel_id=1, source_target_pairs={{0,3},{1,0},{2,1},{3,2},{4,100},{5,101},{6,102},{7,103},{8,11},{9,... | collective-permute-start | bytes 3145736 | tf_op jit(solution)/shard_map/ppermute | solution.py:479
  41.5 24.6 %collective-permute-start.8 = (bf16[176,2048]{1,0:T(8,128)(2,1)S(1)}, bf16[176,2048]{1,0:T(8,128)(2,1)S(1)}, u32[]{:S(2)}, u32[]{:S(2)}) collective-permute-start(bf16[176,2048]{1,0:T(8,128)(2,1)S(1)} %copy-done.6), channel_id=1, source_target_pairs={{8,0},{16,8},{24,16},{32,24},{40,32},{48,40},{56,48},{64,56},{72,6... | collective-permute-start | bytes 2162696 | tf_op jit(solution)/shard_map/ppermute | solution.py:520
  61.7 13.3 %collective-permute-start.10 = (bf16[176,2048]{1,0:T(8,128)(2,1)S(1)}, bf16[176,2048]{1,0:T(8,128)(2,1)S(1)}, u32[]{:S(2)}, u32[]{:S(2)}) collective-permute-start(bf16[176,2048]{1,0:T(8,128)(2,1)S(1)} %copy-done.19), channel_id=1, source_target_pairs={{8,4},{16,12},{24,20},{32,28},{40,36},{48,44},{56,52},{64,60},{72,... | collective-permute-start | bytes 2162696 | tf_op jit(solution)/shard_map/ppermute | solution.py:521
  63.7 12.4 %collective-permute-start.13 = (bf16[2,4,128,256]{3,2,1,0:T(8,128)(2,1)S(1)}, bf16[2,4,128,256]{3,2,1,0:T(8,128)(2,1)S(1)}, u32[]{:S(2)}, u32[]{:S(2)}) collective-permute-start(bf16[2,4,128,256]{3,2,1,0:T(8,128)(2,1)S(1)} %slice.24), channel_id=1, source_target_pairs={{0,1},{1,2},{2,3},{3,0},{4,36},{5,37},{6,38},{7,39},{8,9},{9,10},{... | collective-permute-start | bytes 1572872 | tf_op jit(solution)/shard_map/ppermute | solution.py:479
  66.1 9.9 %collective-permute-start.14 = (bf16[2,4,128,256]{3,2,1,0:T(8,128)(2,1)S(1)}, bf16[2,4,128,256]{3,2,1,0:T(8,128)(2,1)S(1)}, u32[]{:S(2)}, u32[]{:S(2)}) collective-permute-start(bf16[2,4,128,256]{3,2,1,0:T(8,128)(2,1)S(1)} %slice.25), channel_id=1, source_target_pairs={{0,3},{1,0},{2,1},{3,2},{4,100},{5,101},{6,102},{7,103},{8,11},{9,... | collective-permute-start | bytes 1572872 | tf_op jit(solution)/shard_map/ppermute | solution.py:479
  99.4 47.7 %collective-permute-start.16 = (bf16[2,176,512]{2,1,0:T(8,128)(2,1)}, bf16[2,176,512]{2,1,0:T(8,128)(2,1)S(1)}, u32[]{:S(2)}, u32[]{:S(2)}) collective-permute-start(bf16[2,176,512]{2,1,0:T(8,128)(2,1)} %get-tuple-element.54), channel_id=1, source_target_pairs={{0,8},{8,16},{16,24},{24,32},{32,40},{40,48},{48,56},{56,64},{64,7... | collective-permute-start | bytes 1081352 | tf_op jit(solution)/shard_map/ppermute | solution.py:535
  100.7 46.5 %collective-permute-start.17 = (bf16[2,176,512]{2,1,0:T(8,128)(2,1)}, bf16[2,176,512]{2,1,0:T(8,128)(2,1)S(1)}, u32[]{:S(2)}, u32[]{:S(2)}) collective-permute-start(bf16[2,176,512]{2,1,0:T(8,128)(2,1)} %get-tuple-element.55), channel_id=1, source_target_pairs={{4,8},{12,16},{20,24},{28,32},{36,40},{44,48},{52,56},{60,64},{68,... | collective-permute-start | bytes 1081352 | tf_op jit(solution)/shard_map/ppermute | solution.py:535
  104.5 42.8 %collective-permute-start.20 = (bf16[4,4,128,256]{3,2,1,0:T(8,128)(2,1)}, bf16[4,4,128,256]{3,2,1,0:T(8,128)(2,1)S(1)}, u32[]{:S(2)}, u32[]{:S(2)}) collective-permute-start(bf16[4,4,128,256]{3,2,1,0:T(8,128)(2,1)} %get-tuple-element.61), channel_id=1, source_target_pairs={{0,1},{1,2},{2,3},{3,0},{4,36},{5,37},{6,38},{7,39},{8,9},{9,10},{... | collective-permute-start | bytes 3145736 | tf_op jit(solution)/shard_map/ppermute | solution.py:438
  117.9 32.1 %collective-permute-start.21 = (bf16[4,4,128,256]{3,2,1,0:T(8,128)(2,1)}, bf16[4,4,128,256]{3,2,1,0:T(8,128)(2,1)}, u32[]{:S(2)}, u32[]{:S(2)}) collective-permute-start(bf16[4,4,128,256]{3,2,1,0:T(8,128)(2,1)} %get-tuple-element.62), channel_id=1, source_target_pairs={{0,3},{1,0},{2,1},{3,2},{4,100},{5,101},{6,102},{7,103},{8,11},{9,... | collective-permute-start | bytes 3145736 | tf_op jit(solution)/shard_map/ppermute | solution.py:438
  117.9 32.1 %collective-permute-start.22 = (bf16[4,4,128,256]{3,2,1,0:T(8,128)(2,1)}, bf16[4,4,128,256]{3,2,1,0:T(8,128)(2,1)}, u32[]{:S(2)}, u32[]{:S(2)}) collective-permute-start(bf16[4,4,128,256]{3,2,1,0:T(8,128)(2,1)} %get-tuple-element.63), channel_id=1, source_target_pairs={{0,2},{1,3},{2,0},{3,1},{4,68},{5,69},{6,70},{7,71},{8,10},{9,11},... | collective-permute-start | bytes 3145736 | tf_op jit(solution)/shard_map/ppermute | solution.py:438
  147.1 46.6 %collective-permute-start.15 = (bf16[2,512,1024]{2,1,0:T(8,128)(2,1)}, bf16[2,512,1024]{2,1,0:T(8,128)(2,1)S(1)}, u32[]{:S(2)}, u32[]{:S(2)}) collective-permute-start(bf16[2,512,1024]{2,1,0:T(8,128)(2,1)} %get-tuple-element.53), channel_id=1, source_target_pairs={{0,4},{4,0},{1,5},{5,1},{2,6},{6,2},{3,7},{7,3},{8,12},{12,8},{9,1... | collective-permute-start | bytes 6291464 | tf_op jit(solution)/shard_map/ppermute | solution.py:413
  147.2 9.6 %collective-permute-start.26 = (bf16[2,4,128,256]{3,2,1,0:T(8,128)(2,1)S(1)}, bf16[2,4,128,256]{3,2,1,0:T(8,128)(2,1)S(1)}, u32[]{:S(2)}, u32[]{:S(2)}) collective-permute-start(bf16[2,4,128,256]{3,2,1,0:T(8,128)(2,1)S(1)} %get-tuple-element.71), channel_id=1, source_target_pairs={{0,1},{1,2},{2,3},{3,0},{4,36},{5,37},{6,38},{7,39},{8,9},{9,10},{... | collective-permute-start | bytes 1572872 | tf_op jit(solution)/shard_map/ppermute | solution.py:504
  147.3 9.5 %collective-permute-start.27 = (bf16[2,4,128,256]{3,2,1,0:T(8,128)(2,1)S(1)}, bf16[2,4,128,256]{3,2,1,0:T(8,128)(2,1)S(1)}, u32[]{:S(2)}, u32[]{:S(2)}) collective-permute-start(bf16[2,4,128,256]{3,2,1,0:T(8,128)(2,1)S(1)} %get-tuple-element.72), channel_id=1, source_target_pairs={{0,3},{1,0},{2,1},{3,2},{4,100},{5,101},{6,102},{7,103},{8,11},{9,... | collective-permute-start | bytes 1572872 | tf_op jit(solution)/shard_map/ppermute | solution.py:505
  157.1 19.9 %collective-permute-start.28 = (bf16[4,4,128,256]{3,2,1,0:T(8,128)(2,1)S(1)}, bf16[4,4,128,256]{3,2,1,0:T(8,128)(2,1)S(1)}, u32[]{:S(2)}, u32[]{:S(2)}) collective-permute-start(bf16[4,4,128,256]{3,2,1,0:T(8,128)(2,1)S(1)} %get-tuple-element.73), channel_id=1, source_target_pairs={{0,1},{1,2},{2,3},{3,0},{4,36},{5,37},{6,38},{7,39},{8,9},{9,10},{... | collective-permute-start | bytes 3145736 | tf_op jit(solution)/shard_map/ppermute | solution.py:507
  157.5 22.6 %collective-permute-start.29 = (bf16[4,4,128,256]{3,2,1,0:T(8,128)(2,1)S(1)}, bf16[4,4,128,256]{3,2,1,0:T(8,128)(2,1)S(1)}, u32[]{:S(2)}, u32[]{:S(2)}) collective-permute-start(bf16[4,4,128,256]{3,2,1,0:T(8,128)(2,1)S(1)} %get-tuple-element.74), channel_id=1, source_target_pairs={{0,3},{1,0},{2,1},{3,2},{4,100},{5,101},{6,102},{7,103},{8,11},{9,... | collective-permute-start | bytes 3145736 | tf_op jit(solution)/shard_map/ppermute | solution.py:507
  159.9 10.4 %collective-permute-start.18 = (bf16[2,176,512]{2,1,0:T(8,128)(2,1)S(1)}, bf16[2,176,512]{2,1,0:T(8,128)(2,1)S(1)}, u32[]{:S(2)}, u32[]{:S(2)}) collective-permute-start(bf16[2,176,512]{2,1,0:T(8,128)(2,1)S(1)} %get-tuple-element.56), channel_id=1, source_target_pairs={{0,8},{8,16},{16,24},{24,32},{32,40},{40,48},{48,56},{56,64},{64,7... | collective-permute-start | bytes 1081352 | tf_op jit(solution)/shard_map/ppermute | solution.py:539
  161.1 11.0 %collective-permute-start.19 = (bf16[2,176,512]{2,1,0:T(8,128)(2,1)S(1)}, bf16[2,176,512]{2,1,0:T(8,128)(2,1)S(1)}, u32[]{:S(2)}, u32[]{:S(2)}) collective-permute-start(bf16[2,176,512]{2,1,0:T(8,128)(2,1)S(1)} %get-tuple-element.57), channel_id=1, source_target_pairs={{4,8},{12,16},{20,24},{28,32},{36,40},{44,48},{52,56},{60,64},{68,... | collective-permute-start | bytes 1081352 | tf_op jit(solution)/shard_map/ppermute | solution.py:539
  170.2 10.7 %collective-permute-start.23 = (bf16[4,128,256]{2,1,0:T(8,128)(2,1)S(1)}, bf16[4,128,256]{2,1,0:T(8,128)(2,1)S(1)}, u32[]{:S(2)}, u32[]{:S(2)}) collective-permute-start(bf16[4,128,256]{2,1,0:T(8,128)(2,1)S(1)} %get-tuple-element.65), channel_id=1, source_target_pairs={{0,8},{1,9},{2,10},{3,11},{4,5},{5,6},{6,7},{7,4},{8,16},{9,17},{1... | collective-permute-start | bytes 786440 | tf_op jit(solution)/shard_map/ppermute | solution.py:438
  172.2 11.4 %collective-permute-start.24 = (bf16[4,128,256]{2,1,0:T(8,128)(2,1)S(1)}, bf16[4,128,256]{2,1,0:T(8,128)(2,1)S(1)}, u32[]{:S(2)}, u32[]{:S(2)}) collective-permute-start(bf16[4,128,256]{2,1,0:T(8,128)(2,1)S(1)} %get-tuple-element.66), channel_id=1, source_target_pairs={{0,24},{1,25},{2,26},{3,27},{4,7},{5,4},{6,5},{7,6},{8,0},{9,1},{1... | collective-permute-start | bytes 786440 | tf_op jit(solution)/shard_map/ppermute | solution.py:438
  177.0 7.2 %collective-permute-start.25 = (bf16[4,128,256]{2,1,0:T(8,128)(2,1)S(1)}, bf16[4,128,256]{2,1,0:T(8,128)(2,1)S(1)}, u32[]{:S(2)}, u32[]{:S(2)}) collective-permute-start(bf16[4,128,256]{2,1,0:T(8,128)(2,1)S(1)} %get-tuple-element.67), channel_id=1, source_target_pairs={{0,16},{1,17},{2,18},{3,19},{4,6},{5,7},{6,4},{7,5},{8,24},{9,25},... | collective-permute-start | bytes 786440 | tf_op jit(solution)/shard_map/ppermute | solution.py:438
  181.0 8.8 %collective-permute-start.31 = (bf16[4,128,256]{2,1,0:T(8,128)(2,1)S(1)}, bf16[4,128,256]{2,1,0:T(8,128)(2,1)S(1)}, u32[]{:S(2)}, u32[]{:S(2)}) collective-permute-start(bf16[4,128,256]{2,1,0:T(8,128)(2,1)S(1)} %get-tuple-element.77), channel_id=1, source_target_pairs={{0,24},{1,25},{2,26},{3,27},{4,7},{5,4},{6,5},{7,6},{8,0},{9,1},{1... | collective-permute-start | bytes 786440 | tf_op jit(solution)/shard_map/ppermute | solution.py:438
  183.6 7.0 %collective-permute-start.32 = (bf16[4,128,256]{2,1,0:T(8,128)(2,1)S(1)}, bf16[4,128,256]{2,1,0:T(8,128)(2,1)S(1)}, u32[]{:S(2)}, u32[]{:S(2)}) collective-permute-start(bf16[4,128,256]{2,1,0:T(8,128)(2,1)S(1)} %get-tuple-element.78), channel_id=1, source_target_pairs={{0,16},{1,17},{2,18},{3,19},{4,6},{5,7},{6,4},{7,5},{8,24},{9,25},... | collective-permute-start | bytes 786440 | tf_op jit(solution)/shard_map/ppermute | solution.py:438
  (26 other events, 217.3 us)
Sparse Core Ops, SparseCore 0:
  11.7 85.7 all-gather.2

commit v8 on v7

--- a/solution.py
+++ b/solution.py
@@ -156,7 +156,7 @@
         return pl.BlockSpec((32, 1, 64, HEAD_DIM), lambda i, m, e: (0, kind * 2 + i, 0, e[2]))
 
     def handed(kind):
-        return pl.BlockSpec((TOK, HEAD_DIM), lambda i, m, e: (0, i * 4 + kind * 2 + chunk))
+        return pl.BlockSpec((TOK, HEAD_DIM), lambda i, m, e: (0, i * 8 + kind * 2 + chunk))
 
     def out(rows):
         return pl.BlockSpec((2, rows, HEAD_DIM), lambda i, m, e: (0, 0, i * 2 + chunk))
@@ -332,12 +332,13 @@
     )(me, enc_lengths.T, dec_lengths.T, dec_partner.T, q, ct)
 
 
-def hand_kernel(me, q_ref, ct_ref, *refs):
+def hand_kernel(me, q_ref, ct_ref, x_ref, *refs):
     refs[-1][:, :HALF] = q_ref[...]
-    refs[-1][:, HALF:] = ct_ref[...]
-
-
-def hand(me, q, ct, after):
+    refs[-1][:, HALF : 2 * HALF] = ct_ref[...]
+    refs[-1][:, 2 * HALF :] = x_ref[...]
+
+
+def hand(me, q, ct, x, after):
     def half(i, me):
         return (0, i * 2 + 1 - me[2])
 
@@ -347,12 +348,13 @@
         grid_spec=pltpu.PrefetchScalarGridSpec(
             num_scalar_prefetch=1,
             grid=(2,),
-            in_specs=[part, part] + [pl.BlockSpec(memory_space=pl.ANY)] * len(after),
-            out_specs=pl.BlockSpec((TOK, 2 * HALF), lambda i, me: (0, i)),
+            in_specs=[part, part, pl.BlockSpec((TOK, 2 * HALF), lambda i, me: (0, i))]
+            + [pl.BlockSpec(memory_space=pl.ANY)] * len(after),
+            out_specs=pl.BlockSpec((TOK, 4 * HALF), lambda i, me: (0, i)),
         ),
-        out_shape=jax.ShapeDtypeStruct((TOK, 2048), BF),
-        compiler_params=pltpu.CompilerParams(vmem_limit_bytes=16 * MIB),
-    )(me, q, ct, *after)
+        out_shape=jax.ShapeDtypeStruct((TOK, 4096), BF),
+        compiler_params=pltpu.CompilerParams(vmem_limit_bytes=24 * MIB),
+    )(me, q, ct, x, *after)
 
 
 def turn_kernel(a_ref, b_ref, *refs):
@@ -368,7 +370,8 @@
     return pl.pallas_call(
         turn_kernel,
         grid=(D // 512,),
-        in_specs=[part, part] + [pl.BlockSpec(memory_space=pl.ANY)] * len(after),
+        in_specs=[part, pl.BlockSpec((TOK, 512), lambda i: (0, i + 2 + 2 * (i // 2)))]
+        + [pl.BlockSpec(memory_space=pl.ANY)] * len(after),
         out_specs=[pl.BlockSpec((PAIR, 512), lambda i: (0, i)), pl.BlockSpec((512, PAIR), lambda i: (i, 0))],
         out_shape=[jax.ShapeDtypeStruct((PAIR, D), BF), jax.ShapeDtypeStruct((D, PAIR), BF)],
         compiler_params=pltpu.CompilerParams(vmem_limit_bytes=16 * MIB),
@@ -454,7 +457,7 @@
     )(*parts, *after)
 
 
-def pick_kernel(me, w_ref, got_ref, out_ref):
+def pick_kernel(me, w_ref, got_ref, after, out_ref):
     mine = w_ref[:, pl.ds(pl.multiple_of(me[2] * HALF, HALF), HEAD_DIM)]
     for core in range(2):
 
@@ -464,15 +467,15 @@
             out_ref[64 - core * 64 : 128 - core * 64, :] = got_ref[...]
 
 
-def pick(me, weights, got):
+def pick(me, weights, got, after):
     whole = pl.BlockSpec(memory_space=pltpu.VMEM)
     return pl.pallas_call(
         pick_kernel,
-        in_specs=[pl.BlockSpec(memory_space=pltpu.SMEM), whole, whole],
+        in_specs=[pl.BlockSpec(memory_space=pltpu.SMEM), whole, whole, pl.BlockSpec(memory_space=pl.ANY)],
         out_specs=whole,
         out_shape=jax.ShapeDtypeStruct((128, HEAD_DIM), BF),
         compiler_params=pltpu.CompilerParams(vmem_limit_bytes=16 * MIB),
-    )(me, weights, got)
+    )(me, weights, got, after)
 
 
 def ring(value, phase, amount):
@@ -513,22 +516,23 @@
     cols = [kv_weights[:, n * HEAD_DIM : (n + 1) * HEAD_DIM] for n in range(4)]
     later = lax.all_gather(jnp.concatenate([cols[1], cols[3]], axis=1), ALL, axis=0).reshape(32, 4, 64, HALF)
 
-    got = swap(jnp.where(c == 0, cols[2], cols[0]))
-    own = pick(me, kv_weights, got)
-    first = [own] + [ring(own, 2, n) for n in (1, 2, 3)]
     meta, info, leave_a, leave_b = depart(me, enc_lengths, dec_lengths, dec_partner, queries, cotangent)
     sent_a = lax.ppermute(leave_a, DP, SEND_A)
     sent_b = lax.ppermute(leave_b, DP, SEND_B)
-    given = hand(me, queries, cotangent, [leave_a])
-    part = join(first, [given])
-    second = [part] + [ring(part, 1, n) for n in (1, 2, 3)]
-    part = join(second, [])
-    tokens, tokens_t = turn(enc_hidden, swap(enc_hidden), [part, sent_a])
+
+    got = swap(jnp.where(c == 0, cols[2], cols[0]))
+    own = pick(me, kv_weights, got, leave_a)
+    first = [own] + [ring(own, 2, n) for n in (1, 2, 3)]
+    handed = hand(me, queries, cotangent, enc_hidden, first[1:])
+    given = swap(handed)
+    part = join(first, [handed, sent_a, sent_b])
+    part = join([part] + [ring(part, 1, n) for n in (1, 2, 3)], [])
+    tokens, tokens_t = turn(enc_hidden, given, [part])
     ahead, behind = ring(part, 0, 1), ring(part, 0, -1)
     weights = [[part, ahead, behind, ring(behind[:2], 0, -1), ring(ahead[2:], 0, 1)], [later]]
 
     shared = (meta, me, tokens, tokens_t)
-    inputs = (queries, cotangent, swap(given), sent_a, sent_b)
+    inputs = (queries, cotangent, given, sent_a, sent_b)
     home = [back(SEND_A), back(SEND_B)]
 
     *results, d0, d1, d3, d2 = run_main(0, *shared, weights[0], *inputs)

time: 214 us -> 226 us (1.056)
  waiting for transfers between devices: 50.8 us -> 69.1 us
  starting transfers between devices: 72.2 us -> 68.2 us
  local copies, waits for them, and re-layouts: 13.9 us -> 11.6 us
    ppermute x12, starting transfers between devices: 28.3 us -> 15.2 us  [exchange(): lax.ppermute(parts[r], ALL, shift(phase, r))]
    ppermute x10, waiting for transfers between devices: 24.3 us -> 33 us  [ring(): return lax.ppermute(value, ALL, shift(phase, -amount))]
    ppermute x1, waiting for transfers between devices: 0.01 us -> 8.37 us  [body(): sent_a = lax.ppermute(leave_a, DP, SEND_A)]
    ppermute x4, starting transfers between devices: 9.69 us -> 16.2 us  [body(): lax.ppermute(part, DP, pairs)]
    ppermute x1, waiting for transfers between devices: 0.01 us -> 6.41 us  [body(): sent_b = lax.ppermute(leave_b, DP, SEND_B)]
    ppermute x4, waiting for transfers between devices: 7.61 us -> 3.92 us  [body(): lax.ppermute(part, DP, pairs)]
    ppermute x12, waiting for transfers between devices: 8.96 us -> 11.7 us  [exchange(): lax.ppermute(parts[r], ALL, shift(phase, r))]
    unnamed x40 -> x34, local copies, waits for them, and re-layouts: 13.9 us -> 11.5 us
  transfers between devices with their start and end apart: 38 -> 37, of which waited for: 15 -> 19; matrix products, arithmetic and copies ran while one was open for 0% -> 0% of each run, Pallas kernels for 28% -> 26%
where the time goes in v8:
time: 226 us; the launch traced here: 225 us
  waiting for transfers between devices  69.1 us (31%)
  starting transfers between devices  68.2 us (30%)
  Pallas kernels  58.9 us (26%)
  between operations  14.3 us (6%)
  local copies, waits for them, and re-layouts  11.6 us (5%)
  other arithmetic  2.82 us (1%)
    pallas_call x2, Pallas kernels, run_main(): pl.pallas_call(functools.partial(main_kernel, len(weights), len(before)),...  42.9 us
    ppermute x10, waiting for transfers between devices, ring(): return lax.ppermute(value, ALL, shift(phase, -amount))  33 us
    ppermute x10, starting transfers between devices, ring(): return lax.ppermute(value, ALL, shift(phase, -amount))  17 us
    ppermute x4, starting transfers between devices, body(): lax.ppermute(part, DP, pairs)  16.2 us
    ppermute x12, starting transfers between devices, exchange(): lax.ppermute(parts[r], ALL, shift(phase, r))  15.2 us
    ppermute x12, waiting for transfers between devices, exchange(): lax.ppermute(parts[r], ALL, shift(phase, r))  11.7 us
    unnamed x34, local copies, waits for them, and re-layouts  11.5 us
    ppermute x1, waiting for transfers between devices, body(): sent_a = lax.ppermute(leave_a, DP, SEND_A)  8.37 us
  transfers between devices with their start and end apart: 37, of which 19 were waited for; matrix products, arithmetic and copies ran while one was open for 0% of the time, Pallas kernels for 26%

profile of v8, /device:TPU:1, one launch (start us, length us, event | category | flops | bytes accessed | tf_op | source)
XLA Modules:
  0.0 225.0 jit_solution(1058782271483899434)
XLA Ops:
  10.8 3.6 %shard_map.94 = (s32[8,4]{1,0:T(8,128)}, s32[4]{0:T(128)}, bf16[176,2048]{1,0:T(8,128)(2,1)}, bf16[176,2048]{1,0:T(8,128)(2,1)}) custom-call(s32[4]{0:T(128)} %pad_add_fusion.me, s32[4,128]{1,0:T(4,128)} %bitcast.10, s32[4,128]{1,0:T(4,128)} %bitcast.11, s32[4,128]{1,0:T(4,128)} %bitcast.12, bf16[512,2048]{1,0:T(8,128)(2,1)} %refs_2_.1, ...), custom_call_target="tpu_custom_call" | custom-call | tf_op jit(solution)/shard_map/pallas_call | solution.py:324
  17.6 2.6 %collective-permute-start.2 = (bf16[128,256]{1,0:T(8,128)(2,1)S(1)}, bf16[128,256]{1,0:T(8,128)(2,1)S(1)}, u32[]{:S(2)}, u32[]{:S(2)}) collective-permute-start(bf16[128,256]{1,0:T(8,128)(2,1)S(1)} %shard_map.95.refs_0_), channel_id=1, source_target_pairs={{0,64},{1,65},{2,66},{3,67},{4,20},{5,21},{6,22},{7,23},{8,72},{9,... | collective-permute-start | bytes 196616 | tf_op jit(solution)/shard_map/ppermute | solution.py:482
  28.4 2.5 %collective-permute-start.4 = (bf16[512,4096]{1,0:T(8,128)(2,1)S(1)}, bf16[512,4096]{1,0:T(8,128)(2,1)S(1)}, u32[]{:S(2)}, u32[]{:S(2)}) collective-permute-start(bf16[512,4096]{1,0:T(8,128)(2,1)S(1)} %shard_map.96.refs_4_), channel_id=1, source_target_pairs={{0,4},{4,0},{1,5},{5,1},{2,6},{6,2},{3,7},{7,3},{8,12},{12,8},{9,1... | collective-permute-start | bytes 12582920 | tf_op jit(solution)/shard_map/ppermute | solution.py:416
  30.9 3.1 %collective-permute-start.6 = (bf16[176,2048]{1,0:T(8,128)(2,1)S(1)}, bf16[176,2048]{1,0:T(8,128)(2,1)S(1)}, u32[]{:S(2)}, u32[]{:S(2)}) collective-permute-start(bf16[176,2048]{1,0:T(8,128)(2,1)S(1)} %copy-done.16), channel_id=1, source_target_pairs={{8,4},{16,12},{24,20},{32,28},{40,36},{48,44},{56,52},{64,60},{72,... | collective-permute-start | bytes 2162696 | tf_op jit(solution)/shard_map/ppermute | solution.py:521
  34.0 3.2 %collective-permute-start.5 = (bf16[176,2048]{1,0:T(8,128)(2,1)S(1)}, bf16[176,2048]{1,0:T(8,128)(2,1)S(1)}, u32[]{:S(2)}, u32[]{:S(2)}) collective-permute-start(bf16[176,2048]{1,0:T(8,128)(2,1)S(1)} %copy-done.10), channel_id=1, source_target_pairs={{8,0},{16,8},{24,16},{32,24},{40,32},{48,40},{56,48},{64,56},{72,6... | collective-permute-start | bytes 2162696 | tf_op jit(solution)/shard_map/ppermute | solution.py:520
  37.3 6.4 %collective-permute-done.6.refs_6_.refs_8_.refs_12_.refs_5_.refs_9_ = bf16[176,2048]{1,0:T(8,128)(2,1)S(1)} collective-permute-done((bf16[176,2048]{1,0:T(8,128)(2,1)S(1)}, bf16[176,2048]{1,0:T(8,128)(2,1)S(1)}, u32[]{:S(2)}, u32[]{:S(2)}) %collective-permute-start.6) | collective-permute-done | bytes 720928 | tf_op jit(solution)/shard_map/ppermute | solution.py:521
  43.7 8.4 %collective-permute-done.5.refs_5_.refs_7_.refs_11_.refs_4_.refs_8_ = bf16[176,2048]{1,0:T(8,128)(2,1)S(1)} collective-permute-done((bf16[176,2048]{1,0:T(8,128)(2,1)S(1)}, bf16[176,2048]{1,0:T(8,128)(2,1)S(1)}, u32[]{:S(2)}, u32[]{:S(2)}) %collective-permute-start.5) | collective-permute-done | bytes 720928 | tf_op jit(solution)/shard_map/ppermute | solution.py:520
  53.3 2.4 %collective-permute-start.8 = (bf16[4,128,256]{2,1,0:T(8,128)(2,1)S(1)}, bf16[4,128,256]{2,1,0:T(8,128)(2,1)S(1)}, u32[]{:S(2)}, u32[]{:S(2)}) collective-permute-start(bf16[4,128,256]{2,1,0:T(8,128)(2,1)S(1)} %shard_map.97.refs_0_), channel_id=1, source_target_pairs={{0,16},{1,17},{2,18},{3,19},{4,6},{5,7},{6,4},{7,5},{8,24},{9,25},... | collective-permute-start | bytes 786440 | tf_op jit(solution)/shard_map/ppermute | solution.py:482
  56.8 2.6 %collective-permute-done.9.refs_3_ = bf16[4,128,256]{2,1,0:T(8,128)(2,1)S(1)} collective-permute-done((bf16[4,128,256]{2,1,0:T(8,128)(2,1)S(1)}, bf16[4,128,256]{2,1,0:T(8,128)(2,1)S(1)}, u32[]{:S(2)}, u32[]{:S(2)}) %collective-permute-start.9) | collective-permute-done | bytes 262176 | tf_op jit(solution)/shard_map/ppermute | solution.py:482
  59.4 3.8 %collective-permute-done.8.refs_2_ = bf16[4,128,256]{2,1,0:T(8,128)(2,1)S(1)} collective-permute-done((bf16[4,128,256]{2,1,0:T(8,128)(2,1)S(1)}, bf16[4,128,256]{2,1,0:T(8,128)(2,1)S(1)}, u32[]{:S(2)}, u32[]{:S(2)}) %collective-permute-start.8) | collective-permute-done | bytes 262176 | tf_op jit(solution)/shard_map/ppermute | solution.py:482
  63.3 2.7 %collective-permute-start.11 = (bf16[4,4,128,256]{3,2,1,0:T(8,128)(2,1)S(1)}, bf16[4,4,128,256]{3,2,1,0:T(8,128)(2,1)S(1)}, u32[]{:S(2)}, u32[]{:S(2)}) collective-permute-start(bf16[4,4,128,256]{3,2,1,0:T(8,128)(2,1)S(1)} %shard_map.98.refs_0_), channel_id=1, source_target_pairs={{0,1},{1,2},{2,3},{3,0},{4,36},{5,37},{6,38},{7,39},{8,9},{9,10},{... | collective-permute-start | bytes 3145736 | tf_op jit(solution)/shard_map/ppermute | solution.py:482
  67.3 24.0 %collective-permute-done.11.refs_2_ = bf16[4,4,128,256]{3,2,1,0:T(8,128)(2,1)S(1)} collective-permute-done((bf16[4,4,128,256]{3,2,1,0:T(8,128)(2,1)S(1)}, bf16[4,4,128,256]{3,2,1,0:T(8,128)(2,1)S(1)}, u32[]{:S(2)}, u32[]{:S(2)}) %collective-permute-start.11) | collective-permute-done | bytes 1048608 | tf_op jit(solution)/shard_map/ppermute | solution.py:482
  91.6 2.8 %collective-permute-start.13 = (bf16[2,4,128,256]{3,2,1,0:T(8,128)(2,1)S(1)}, bf16[2,4,128,256]{3,2,1,0:T(8,128)(2,1)S(1)}, u32[]{:S(2)}, u32[]{:S(2)}) collective-permute-start(bf16[2,4,128,256]{3,2,1,0:T(8,128)(2,1)S(1)} %slice.25), channel_id=1, source_target_pairs={{0,3},{1,0},{2,1},{3,2},{4,100},{5,101},{6,102},{7,103},{8,11},{9,... | collective-permute-start | bytes 1572872 | tf_op jit(solution)/shard_map/ppermute | solution.py:482
  94.4 2.2 shard_map.99
  96.7 2.1 copy-done.6
  101.0 22.0 %shard_map.100 = (bf16[2,512,1024]{2,1,0:T(8,128)(2,1)}, bf16[2,512,1024]{2,1,0:T(8,128)(2,1)}, bf16[2,176,512]{2,1,0:T(8,128)(2,1)}, bf16[2,176,512]{2,1,0:T(8,...) custom-call(s32[8,4]{1,0:T(8,128)S(1)} %copy-done.13, ...), custom_call_target="tpu_custom_call" | custom-call | flops 12000000000 | bytes 24000000 | tf_op jit(solution)/shard_map/pallas_call | solution.py:179
  124.3 7.4 %collective-permute-start.16 = (bf16[2,176,512]{2,1,0:T(8,128)(2,1)}, bf16[2,176,512]{2,1,0:T(8,128)(2,1)S(1)}, u32[]{:S(2)}, u32[]{:S(2)}) collective-permute-start(bf16[2,176,512]{2,1,0:T(8,128)(2,1)} %get-tuple-element.55), channel_id=1, source_target_pairs={{4,8},{12,16},{20,24},{28,32},{36,40},{44,48},{52,56},{60,64},{68,... | collective-permute-start | bytes 1081352 | tf_op jit(solution)/shard_map/ppermute | solution.py:539
  131.8 2.7 %collective-permute-start.20 = (bf16[4,4,128,256]{3,2,1,0:T(8,128)(2,1)}, bf16[4,4,128,256]{3,2,1,0:T(8,128)(2,1)}, u32[]{:S(2)}, u32[]{:S(2)}) collective-permute-start(bf16[4,4,128,256]{3,2,1,0:T(8,128)(2,1)} %get-tuple-element.62), channel_id=1, source_target_pairs={{0,3},{1,0},{2,1},{3,2},{4,100},{5,101},{6,102},{7,103},{8,11},{9,... | collective-permute-start | bytes 3145736 | tf_op jit(solution)/shard_map/ppermute | solution.py:441
  136.2 20.9 %shard_map.101 = (bf16[2,512,1024]{2,1,0:T(8,128)(2,1)S(1)}, bf16[2,512,1024]{2,1,0:T(8,128)(2,1)}, bf16[2,176,512]{2,1,0:T(8,128)(2,1)S(1)}, bf16[2,176,512]{2,...) custom-call(s32[8,4]{1,0:T(8,128)S(1)} %copy-done.13, ...), custom_call_target="tpu_custom_call", output_to_operand_aliasing={{0}: (14, {}), {1}: (15, {})} | custom-call | flops 12000000000 | bytes 24000000 | tf_op jit(solution)/shard_map/pallas_call | solution.py:179
  160.6 3.6 %collective-permute-done.21.refs_3_ = bf16[4,4,128,256]{3,2,1,0:T(8,128)(2,1)} collective-permute-done((bf16[4,4,128,256]{3,2,1,0:T(8,128)(2,1)}, bf16[4,4,128,256]{3,2,1,0:T(8,128)(2,1)}, u32[]{:S(2)}, u32[]{:S(2)}) %collective-permute-start.21) | collective-permute-done | bytes 1048608 | tf_op jit(solution)/shard_map/ppermute | solution.py:441
  164.2 2.9 %shard_map.103 = (bf16[4,128,256]{2,1,0:T(8,128)(2,1)S(1)}, bf16[4,128,256]{2,1,0:T(8,128)(2,1)S(1)}, bf16[4,128,256]{2,1,0:T(8,128)(2,1)S(1)}, bf16[4,128,256]{2,1,0:T(8,128)(2,1)S(1)}) custom-call(bf16[4,4,128,256]{3,2,1,0:T(8,128)(2,1)S(1)} %get-tuple-element.60.refs_0_, bf16[4,4,128,256]{3,2,1,0:T(8,128)(2,1)} %collective-permute-done.19.refs_1_, ...), custom_call_target="tpu_custom_call" | custom-call | tf_op jit(solution)/shard_map/pallas_call | solution.py:212
  167.0 2.5 %collective-permute-done.25.got_a = bf16[2,4,128,256]{3,2,1,0:T(8,128)(2,1)S(1)} collective-permute-done((bf16[2,4,128,256]{3,2,1,0:T(8,128)(2,1)S(1)}, bf16[2,4,128,256]{3,2,1,0:T(8,128)(2,1)S(1)}, u32[]{:S(2)}, u32[]{:S(2)}) %collective-permute-start.25) | collective-permute-done | bytes 524320 | tf_op jit(solution)/shard_map/ppermute | solution.py:507
  173.9 6.2 %collective-permute-start.18 = (bf16[2,176,512]{2,1,0:T(8,128)(2,1)S(1)}, bf16[2,176,512]{2,1,0:T(8,128)(2,1)S(1)}, u32[]{:S(2)}, u32[]{:S(2)}) collective-permute-start(bf16[2,176,512]{2,1,0:T(8,128)(2,1)S(1)} %get-tuple-element.57), channel_id=1, source_target_pairs={{4,8},{12,16},{20,24},{28,32},{36,40},{44,48},{52,56},{60,64},{68,... | collective-permute-start | bytes 1081352 | tf_op jit(solution)/shard_map/ppermute | solution.py:543
  182.3 3.0 %collective-permute-done.18.refs_5_.refs_4_ = bf16[2,176,512]{2,1,0:T(8,128)(2,1)S(1)} collective-permute-done((bf16[2,176,512]{2,1,0:T(8,128)(2,1)S(1)}, bf16[2,176,512]{2,1,0:T(8,128)(2,1)S(1)}, u32[]{:S(2)}, u32[]{:S(2)}) %collective-permute-start.18) | collective-permute-done | bytes 360480 | tf_op jit(solution)/shard_map/ppermute | solution.py:543
  185.3 2.6 %collective-permute-start.23 = (bf16[4,128,256]{2,1,0:T(8,128)(2,1)S(1)}, bf16[4,128,256]{2,1,0:T(8,128)(2,1)S(1)}, u32[]{:S(2)}, u32[]{:S(2)}) collective-permute-start(bf16[4,128,256]{2,1,0:T(8,128)(2,1)S(1)} %get-tuple-element.66), channel_id=1, source_target_pairs={{0,24},{1,25},{2,26},{3,27},{4,7},{5,4},{6,5},{7,6},{8,0},{9,1},{1... | collective-permute-start | bytes 786440 | tf_op jit(solution)/shard_map/ppermute | solution.py:441
  187.9 2.2 collective-permute-done.27.refs_1_
  192.7 2.0 collective-permute-start.29
  197.0 2.8 %collective-permute-done.29.refs_5_ = bf16[4,128,256]{2,1,0:T(8,128)(2,1)S(1)} collective-permute-done((bf16[4,128,256]{2,1,0:T(8,128)(2,1)S(1)}, bf16[4,128,256]{2,1,0:T(8,128)(2,1)S(1)}, u32[]{:S(2)}, u32[]{:S(2)}) %collective-permute-start.29) | collective-permute-done | bytes 262176 | tf_op jit(solution)/shard_map/ppermute | solution.py:441
  200.5 2.2 collective-permute-done.31.refs_7_
  203.1 2.7 %collective-permute-start.33 = (bf16[128,512]{1,0:T(8,128)(2,1)S(1)}, bf16[128,512]{1,0:T(8,128)(2,1)S(1)}, u32[]{:S(2)}, u32[]{:S(2)}) collective-permute-start(bf16[128,512]{1,0:T(8,128)(2,1)S(1)} %get-tuple-element.81), channel_id=1, source_target_pairs={{0,96},{1,97},{2,98},{3,99},{4,28},{5,29},{6,30},{7,31},{8,104},{9... | collective-permute-start | bytes 393224 | tf_op jit(solution)/shard_map/ppermute | solution.py:441
  205.8 3.4 %shard_map.102 = (bf16[512,2048]{1,0:T(8,128)(2,1)}, bf16[512,2048]{1,0:T(8,128)(2,1)}) custom-call(s32[4]{0:T(128)S(1)} %copy-done.14, bf16[2,512,1024]{2,1,0:T(8,128)(2,1)S(1)} %get-tuple-element.52.refs_0_.refs_4_, bf16[2,512,1024]{2,1,0:T(8,128)(2,1)S(1)} %collective-permute-done.14.refs_1_, ...), custom_call_target="tpu_custom_call" | custom-call | tf_op jit(solution)/shard_map/pallas_call | solution.py:402
  213.3 3.1 %collective-permute-start.35 = (f32[64,512]{1,0:T(8,128)S(1)}, f32[64,512]{1,0:T(8,128)S(1)}, u32[]{:S(2)}, u32[]{:S(2)}) collective-permute-start(f32[64,512]{1,0:T(8,128)S(1)} %get-tuple-element.84), channel_id=1, source_target_pairs={{0,4},{4,0},{1,5},{5,1},{2,6},{6,2},{3,7},{7,3},{8,12},{12,8},{9,1... | collective-permute-start | bytes 393224 | tf_op jit(solution)/shard_map/ppermute | solution.py:416
  (98 shorter events, 46.0 us)
Async XLA Ops:
  7.2 127.4 %all-gather.3.cloned.1.call-start = ((), (), s32[]{:S(2)}) async-start(), calls=%async_computation | async-start | bytes 8454144 | tf_op jit(solution)/shard_map/all_gather | solution.py:517
  8.7 5.8 %collective-permute-start = (bf16[64,256]{1,0:T(8,128)(2,1)S(1)}, bf16[64,256]{1,0:T(8,128)(2,1)S(1)}, u32[]{:S(2)}, u32[]{:S(2)}) collective-permute-start(bf16[64,256]{1,0:T(8,128)(2,1)S(1)} %get-tuple-element.88), channel_id=1, source_target_pairs={{0,4},{4,0},{1,5},{5,1},{2,6},{6,2},{3,7},{7,3},{8,12},{12,8},{9,1... | collective-permute-start | bytes 98312 | tf_op jit(solution)/shard_map/ppermute | solution.py:416
  28.4 66.1 %collective-permute-start.4 = (bf16[512,4096]{1,0:T(8,128)(2,1)S(1)}, bf16[512,4096]{1,0:T(8,128)(2,1)S(1)}, u32[]{:S(2)}, u32[]{:S(2)}) collective-permute-start(bf16[512,4096]{1,0:T(8,128)(2,1)S(1)} %shard_map.96.refs_4_), channel_id=1, source_target_pairs={{0,4},{4,0},{1,5},{5,1},{2,6},{6,2},{3,7},{7,3},{8,12},{12,8},{9,1... | collective-permute-start | bytes 12582920 | tf_op jit(solution)/shard_map/ppermute | solution.py:416
  30.9 12.8 %collective-permute-start.6 = (bf16[176,2048]{1,0:T(8,128)(2,1)S(1)}, bf16[176,2048]{1,0:T(8,128)(2,1)S(1)}, u32[]{:S(2)}, u32[]{:S(2)}) collective-permute-start(bf16[176,2048]{1,0:T(8,128)(2,1)S(1)} %copy-done.16), channel_id=1, source_target_pairs={{8,4},{16,12},{24,20},{32,28},{40,36},{48,44},{56,52},{64,60},{72,... | collective-permute-start | bytes 2162696 | tf_op jit(solution)/shard_map/ppermute | solution.py:521
  34.0 18.0 %collective-permute-start.5 = (bf16[176,2048]{1,0:T(8,128)(2,1)S(1)}, bf16[176,2048]{1,0:T(8,128)(2,1)S(1)}, u32[]{:S(2)}, u32[]{:S(2)}) collective-permute-start(bf16[176,2048]{1,0:T(8,128)(2,1)S(1)} %copy-done.10), channel_id=1, source_target_pairs={{8,0},{16,8},{24,16},{32,24},{40,32},{48,40},{56,48},{64,56},{72,6... | collective-permute-start | bytes 2162696 | tf_op jit(solution)/shard_map/ppermute | solution.py:520
  52.1 7.3 %collective-permute-start.9 = (bf16[4,128,256]{2,1,0:T(8,128)(2,1)S(1)}, bf16[4,128,256]{2,1,0:T(8,128)(2,1)S(1)}, u32[]{:S(2)}, u32[]{:S(2)}) collective-permute-start(bf16[4,128,256]{2,1,0:T(8,128)(2,1)S(1)} %shard_map.97.refs_0_), channel_id=1, source_target_pairs={{0,8},{1,9},{2,10},{3,11},{4,5},{5,6},{6,7},{7,4},{8,16},{9,17},{1... | collective-permute-start | bytes 786440 | tf_op jit(solution)/shard_map/ppermute | solution.py:482
  53.3 9.9 %collective-permute-start.8 = (bf16[4,128,256]{2,1,0:T(8,128)(2,1)S(1)}, bf16[4,128,256]{2,1,0:T(8,128)(2,1)S(1)}, u32[]{:S(2)}, u32[]{:S(2)}) collective-permute-start(bf16[4,128,256]{2,1,0:T(8,128)(2,1)S(1)} %shard_map.97.refs_0_), channel_id=1, source_target_pairs={{0,16},{1,17},{2,18},{3,19},{4,6},{5,7},{6,4},{7,5},{8,24},{9,25},... | collective-permute-start | bytes 786440 | tf_op jit(solution)/shard_map/ppermute | solution.py:482
  55.7 7.5 %collective-permute-start.7 = (bf16[4,128,256]{2,1,0:T(8,128)(2,1)S(1)}, bf16[4,128,256]{2,1,0:T(8,128)(2,1)S(1)}, u32[]{:S(2)}, u32[]{:S(2)}) collective-permute-start(bf16[4,128,256]{2,1,0:T(8,128)(2,1)S(1)} %shard_map.97.refs_0_), channel_id=1, source_target_pairs={{0,24},{1,25},{2,26},{3,27},{4,7},{5,4},{6,5},{7,6},{8,0},{9,1},{1... | collective-permute-start | bytes 786440 | tf_op jit(solution)/shard_map/ppermute | solution.py:482
  63.3 28.1 %collective-permute-start.11 = (bf16[4,4,128,256]{3,2,1,0:T(8,128)(2,1)S(1)}, bf16[4,4,128,256]{3,2,1,0:T(8,128)(2,1)S(1)}, u32[]{:S(2)}, u32[]{:S(2)}) collective-permute-start(bf16[4,4,128,256]{3,2,1,0:T(8,128)(2,1)S(1)} %shard_map.98.refs_0_), channel_id=1, source_target_pairs={{0,1},{1,2},{2,3},{3,0},{4,36},{5,37},{6,38},{7,39},{8,9},{9,10},{... | collective-permute-start | bytes 3145736 | tf_op jit(solution)/shard_map/ppermute | solution.py:482
  65.9 25.6 %collective-permute-start.10 = (bf16[4,4,128,256]{3,2,1,0:T(8,128)(2,1)S(1)}, bf16[4,4,128,256]{3,2,1,0:T(8,128)(2,1)S(1)}, u32[]{:S(2)}, u32[]{:S(2)}) collective-permute-start(bf16[4,4,128,256]{3,2,1,0:T(8,128)(2,1)S(1)} %shard_map.98.refs_0_), channel_id=1, source_target_pairs={{0,3},{1,0},{2,1},{3,2},{4,100},{5,101},{6,102},{7,103},{8,11},{9,... | collective-permute-start | bytes 3145736 | tf_op jit(solution)/shard_map/ppermute | solution.py:482
  91.4 9.6 %collective-permute-start.12 = (bf16[2,4,128,256]{3,2,1,0:T(8,128)(2,1)S(1)}, bf16[2,4,128,256]{3,2,1,0:T(8,128)(2,1)S(1)}, u32[]{:S(2)}, u32[]{:S(2)}) collective-permute-start(bf16[2,4,128,256]{3,2,1,0:T(8,128)(2,1)S(1)} %slice.24), channel_id=1, source_target_pairs={{0,1},{1,2},{2,3},{3,0},{4,36},{5,37},{6,38},{7,39},{8,9},{9,10},{... | collective-permute-start | bytes 1572872 | tf_op jit(solution)/shard_map/ppermute | solution.py:482
  91.6 9.3 %collective-permute-start.13 = (bf16[2,4,128,256]{3,2,1,0:T(8,128)(2,1)S(1)}, bf16[2,4,128,256]{3,2,1,0:T(8,128)(2,1)S(1)}, u32[]{:S(2)}, u32[]{:S(2)}) collective-permute-start(bf16[2,4,128,256]{3,2,1,0:T(8,128)(2,1)S(1)} %slice.25), channel_id=1, source_target_pairs={{0,3},{1,0},{2,1},{3,2},{4,100},{5,101},{6,102},{7,103},{8,11},{9,... | collective-permute-start | bytes 1572872 | tf_op jit(solution)/shard_map/ppermute | solution.py:482
  123.0 34.0 %collective-permute-start.15 = (bf16[2,176,512]{2,1,0:T(8,128)(2,1)}, bf16[2,176,512]{2,1,0:T(8,128)(2,1)S(1)}, u32[]{:S(2)}, u32[]{:S(2)}) collective-permute-start(bf16[2,176,512]{2,1,0:T(8,128)(2,1)} %get-tuple-element.54), channel_id=1, source_target_pairs={{0,8},{8,16},{16,24},{24,32},{32,40},{40,48},{48,56},{56,64},{64,7... | collective-permute-start | bytes 1081352 | tf_op jit(solution)/shard_map/ppermute | solution.py:539
  124.3 33.6 %collective-permute-start.16 = (bf16[2,176,512]{2,1,0:T(8,128)(2,1)}, bf16[2,176,512]{2,1,0:T(8,128)(2,1)S(1)}, u32[]{:S(2)}, u32[]{:S(2)}) collective-permute-start(bf16[2,176,512]{2,1,0:T(8,128)(2,1)} %get-tuple-element.55), channel_id=1, source_target_pairs={{4,8},{12,16},{20,24},{28,32},{36,40},{44,48},{52,56},{60,64},{68,... | collective-permute-start | bytes 1081352 | tf_op jit(solution)/shard_map/ppermute | solution.py:539
  131.7 27.4 %collective-permute-start.19 = (bf16[4,4,128,256]{3,2,1,0:T(8,128)(2,1)}, bf16[4,4,128,256]{3,2,1,0:T(8,128)(2,1)}, u32[]{:S(2)}, u32[]{:S(2)}) collective-permute-start(bf16[4,4,128,256]{3,2,1,0:T(8,128)(2,1)} %get-tuple-element.61), channel_id=1, source_target_pairs={{0,1},{1,2},{2,3},{3,0},{4,36},{5,37},{6,38},{7,39},{8,9},{9,10},{... | collective-permute-start | bytes 3145736 | tf_op jit(solution)/shard_map/ppermute | solution.py:441
  131.8 28.8 %collective-permute-start.20 = (bf16[4,4,128,256]{3,2,1,0:T(8,128)(2,1)}, bf16[4,4,128,256]{3,2,1,0:T(8,128)(2,1)}, u32[]{:S(2)}, u32[]{:S(2)}) collective-permute-start(bf16[4,4,128,256]{3,2,1,0:T(8,128)(2,1)} %get-tuple-element.62), channel_id=1, source_target_pairs={{0,3},{1,0},{2,1},{3,2},{4,100},{5,101},{6,102},{7,103},{8,11},{9,... | collective-permute-start | bytes 3145736 | tf_op jit(solution)/shard_map/ppermute | solution.py:441
  134.5 29.7 %collective-permute-start.21 = (bf16[4,4,128,256]{3,2,1,0:T(8,128)(2,1)}, bf16[4,4,128,256]{3,2,1,0:T(8,128)(2,1)}, u32[]{:S(2)}, u32[]{:S(2)}) collective-permute-start(bf16[4,4,128,256]{3,2,1,0:T(8,128)(2,1)} %get-tuple-element.63), channel_id=1, source_target_pairs={{0,2},{1,3},{2,0},{3,1},{4,68},{5,69},{6,70},{7,71},{8,10},{9,11},... | collective-permute-start | bytes 3145736 | tf_op jit(solution)/shard_map/ppermute | solution.py:441
  157.0 48.7 %collective-permute-start.14 = (bf16[2,512,1024]{2,1,0:T(8,128)(2,1)}, bf16[2,512,1024]{2,1,0:T(8,128)(2,1)S(1)}, u32[]{:S(2)}, u32[]{:S(2)}) collective-permute-start(bf16[2,512,1024]{2,1,0:T(8,128)(2,1)} %get-tuple-element.53), channel_id=1, source_target_pairs={{0,4},{4,0},{1,5},{5,1},{2,6},{6,2},{3,7},{7,3},{8,12},{12,8},{9,1... | collective-permute-start | bytes 6291464 | tf_op jit(solution)/shard_map/ppermute | solution.py:416
  157.9 11.7 %collective-permute-start.25 = (bf16[2,4,128,256]{3,2,1,0:T(8,128)(2,1)S(1)}, bf16[2,4,128,256]{3,2,1,0:T(8,128)(2,1)S(1)}, u32[]{:S(2)}, u32[]{:S(2)}) collective-permute-start(bf16[2,4,128,256]{3,2,1,0:T(8,128)(2,1)S(1)} %get-tuple-element.71), channel_id=1, source_target_pairs={{0,1},{1,2},{2,3},{3,0},{4,36},{5,37},{6,38},{7,39},{8,9},{9,10},{... | collective-permute-start | bytes 1572872 | tf_op jit(solution)/shard_map/ppermute | solution.py:507
  159.1 10.5 %collective-permute-start.26 = (bf16[2,4,128,256]{3,2,1,0:T(8,128)(2,1)S(1)}, bf16[2,4,128,256]{3,2,1,0:T(8,128)(2,1)S(1)}, u32[]{:S(2)}, u32[]{:S(2)}) collective-permute-start(bf16[2,4,128,256]{3,2,1,0:T(8,128)(2,1)S(1)} %get-tuple-element.72), channel_id=1, source_target_pairs={{0,3},{1,0},{2,1},{3,2},{4,100},{5,101},{6,102},{7,103},{8,11},{9,... | collective-permute-start | bytes 1572872 | tf_op jit(solution)/shard_map/ppermute | solution.py:508
  169.9 20.2 %collective-permute-start.27 = (bf16[4,4,128,256]{3,2,1,0:T(8,128)(2,1)S(1)}, bf16[4,4,128,256]{3,2,1,0:T(8,128)(2,1)S(1)}, u32[]{:S(2)}, u32[]{:S(2)}) collective-permute-start(bf16[4,4,128,256]{3,2,1,0:T(8,128)(2,1)S(1)} %get-tuple-element.73), channel_id=1, source_target_pairs={{0,1},{1,2},{2,3},{3,0},{4,36},{5,37},{6,38},{7,39},{8,9},{9,10},{... | collective-permute-start | bytes 3145736 | tf_op jit(solution)/shard_map/ppermute | solution.py:510
  170.7 21.4 %collective-permute-start.28 = (bf16[4,4,128,256]{3,2,1,0:T(8,128)(2,1)S(1)}, bf16[4,4,128,256]{3,2,1,0:T(8,128)(2,1)S(1)}, u32[]{:S(2)}, u32[]{:S(2)}) collective-permute-start(bf16[4,4,128,256]{3,2,1,0:T(8,128)(2,1)S(1)} %get-tuple-element.74), channel_id=1, source_target_pairs={{0,3},{1,0},{2,1},{3,2},{4,100},{5,101},{6,102},{7,103},{8,11},{9,... | collective-permute-start | bytes 3145736 | tf_op jit(solution)/shard_map/ppermute | solution.py:510
  172.6 8.5 %collective-permute-start.17 = (bf16[2,176,512]{2,1,0:T(8,128)(2,1)S(1)}, bf16[2,176,512]{2,1,0:T(8,128)(2,1)S(1)}, u32[]{:S(2)}, u32[]{:S(2)}) collective-permute-start(bf16[2,176,512]{2,1,0:T(8,128)(2,1)S(1)} %get-tuple-element.56), channel_id=1, source_target_pairs={{0,8},{8,16},{16,24},{24,32},{32,40},{40,48},{48,56},{56,64},{64,7... | collective-permute-start | bytes 1081352 | tf_op jit(solution)/shard_map/ppermute | solution.py:543
  173.9 11.4 %collective-permute-start.18 = (bf16[2,176,512]{2,1,0:T(8,128)(2,1)S(1)}, bf16[2,176,512]{2,1,0:T(8,128)(2,1)S(1)}, u32[]{:S(2)}, u32[]{:S(2)}) collective-permute-start(bf16[2,176,512]{2,1,0:T(8,128)(2,1)S(1)} %get-tuple-element.57), channel_id=1, source_target_pairs={{4,8},{12,16},{20,24},{28,32},{36,40},{44,48},{52,56},{60,64},{68,... | collective-permute-start | bytes 1081352 | tf_op jit(solution)/shard_map/ppermute | solution.py:543
  181.1 13.7 %collective-permute-start.22 = (bf16[4,128,256]{2,1,0:T(8,128)(2,1)S(1)}, bf16[4,128,256]{2,1,0:T(8,128)(2,1)S(1)}, u32[]{:S(2)}, u32[]{:S(2)}) collective-permute-start(bf16[4,128,256]{2,1,0:T(8,128)(2,1)S(1)} %get-tuple-element.65), channel_id=1, source_target_pairs={{0,8},{1,9},{2,10},{3,11},{4,5},{5,6},{6,7},{7,4},{8,16},{9,17},{1... | collective-permute-start | bytes 786440 | tf_op jit(solution)/shard_map/ppermute | solution.py:441
  185.3 10.2 %collective-permute-start.23 = (bf16[4,128,256]{2,1,0:T(8,128)(2,1)S(1)}, bf16[4,128,256]{2,1,0:T(8,128)(2,1)S(1)}, u32[]{:S(2)}, u32[]{:S(2)}) collective-permute-start(bf16[4,128,256]{2,1,0:T(8,128)(2,1)S(1)} %get-tuple-element.66), channel_id=1, source_target_pairs={{0,24},{1,25},{2,26},{3,27},{4,7},{5,4},{6,5},{7,6},{8,0},{9,1},{1... | collective-permute-start | bytes 786440 | tf_op jit(solution)/shard_map/ppermute | solution.py:441
  190.1 6.9 %collective-permute-start.24 = (bf16[4,128,256]{2,1,0:T(8,128)(2,1)S(1)}, bf16[4,128,256]{2,1,0:T(8,128)(2,1)S(1)}, u32[]{:S(2)}, u32[]{:S(2)}) collective-permute-start(bf16[4,128,256]{2,1,0:T(8,128)(2,1)S(1)} %get-tuple-element.67), channel_id=1, source_target_pairs={{0,16},{1,17},{2,18},{3,19},{4,6},{5,7},{6,4},{7,5},{8,24},{9,25},... | collective-permute-start | bytes 786440 | tf_op jit(solution)/shard_map/ppermute | solution.py:441
  192.7 7.1 %collective-permute-start.29 = (bf16[4,128,256]{2,1,0:T(8,128)(2,1)S(1)}, bf16[4,128,256]{2,1,0:T(8,128)(2,1)S(1)}, u32[]{:S(2)}, u32[]{:S(2)}) collective-permute-start(bf16[4,128,256]{2,1,0:T(8,128)(2,1)S(1)} %get-tuple-element.76), channel_id=1, source_target_pairs={{0,8},{1,9},{2,10},{3,11},{4,5},{5,6},{6,7},{7,4},{8,16},{9,17},{1... | collective-permute-start | bytes 786440 | tf_op jit(solution)/shard_map/ppermute | solution.py:441
  194.7 5.8 %collective-permute-start.30 = (bf16[4,128,256]{2,1,0:T(8,128)(2,1)S(1)}, bf16[4,128,256]{2,1,0:T(8,128)(2,1)S(1)}, u32[]{:S(2)}, u32[]{:S(2)}) collective-permute-start(bf16[4,128,256]{2,1,0:T(8,128)(2,1)S(1)} %get-tuple-element.77), channel_id=1, source_target_pairs={{0,24},{1,25},{2,26},{3,27},{4,7},{5,4},{6,5},{7,6},{8,0},{9,1},{1... | collective-permute-start | bytes 786440 | tf_op jit(solution)/shard_map/ppermute | solution.py:441
  195.5 7.3 %collective-permute-start.31 = (bf16[4,128,256]{2,1,0:T(8,128)(2,1)S(1)}, bf16[4,128,256]{2,1,0:T(8,128)(2,1)S(1)}, u32[]{:S(2)}, u32[]{:S(2)}) collective-permute-start(bf16[4,128,256]{2,1,0:T(8,128)(2,1)S(1)} %get-tuple-element.78), channel_id=1, source_target_pairs={{0,16},{1,17},{2,18},{3,19},{4,6},{5,7},{6,4},{7,5},{8,24},{9,25},... | collective-permute-start | bytes 786440 | tf_op jit(solution)/shard_map/ppermute | solution.py:441
  203.0 6.1 %collective-permute-start.32 = (bf16[128,512]{1,0:T(8,128)(2,1)S(1)}, bf16[128,512]{1,0:T(8,128)(2,1)S(1)}, u32[]{:S(2)}, u32[]{:S(2)}) collective-permute-start(bf16[128,512]{1,0:T(8,128)(2,1)S(1)} %get-tuple-element.80), channel_id=1, source_target_pairs={{0,32},{1,33},{2,34},{3,35},{4,12},{5,13},{6,14},{7,15},{8,40},{9,... | collective-permute-start | bytes 393224 | tf_op jit(solution)/shard_map/ppermute | solution.py:441
  203.1 6.1 %collective-permute-start.33 = (bf16[128,512]{1,0:T(8,128)(2,1)S(1)}, bf16[128,512]{1,0:T(8,128)(2,1)S(1)}, u32[]{:S(2)}, u32[]{:S(2)}) collective-permute-start(bf16[128,512]{1,0:T(8,128)(2,1)S(1)} %get-tuple-element.81), channel_id=1, source_target_pairs={{0,96},{1,97},{2,98},{3,99},{4,28},{5,29},{6,30},{7,31},{8,104},{9... | collective-permute-start | bytes 393224 | tf_op jit(solution)/shard_map/ppermute | solution.py:441
  (22 other events, 150.1 us)
Sparse Core Ops, SparseCore 0:
  11.7 79.5 all-gather.2

commit v9 on v8

--- a/solution.py
+++ b/solution.py
@@ -93,27 +93,23 @@
     step = pl.program_id(0)
     block = places(me)
 
-    if weights == 2:
-        wk, wv = (ref[...].reshape(D, HEAD_DIM) for ref in refs[:2])
-    else:
-        w0, w1, w3, *w2 = refs[:weights]
-
-        @pl.when(step == 0)
-        def _():
-            def take(rc, carry):
-                for rb in range(4):
-                    far = w2[rb // 2][rb % 2, rc]
-                    for ra, value in enumerate((w0[rb, rc], w1[rb, rc], far, w3[rb, rc])):
-                        bx, bzy = block(ra, rb, rc)
-                        w_s[bx, pl.ds(pl.multiple_of(bzy * 128, 128), 128), :] = value
-                return carry
-
-            lax.fori_loop(0, 4, take, 0)
-
-        wk, wv = w_s[step], w_s[2 + step]
+    w0, w1, w3, *w2 = refs[:weights]
+
+    @pl.when(step == 0)
+    def _():
+        def take(rc, carry):
+            for rb in range(4):
+                far = w2[rb * len(w2) // 4][rb % (4 // len(w2)), rc]
+                for ra, value in enumerate((w0[rb, rc], w1[rb, rc], far, w3[rb, rc])):
+                    bx, bzy = block(ra, rb, rc)
+                    w_s[bx, pl.ds(pl.multiple_of(bzy * 128, 128), 128), :] = value
+            return carry
+
+        lax.fori_loop(0, 4, take, 0)
+
     x = x_ref[...]
-    k_s[...] = jnp.dot(x, wk, preferred_element_type=jnp.float32).astype(BF)
-    v_s[...] = jnp.dot(x, wv, preferred_element_type=jnp.float32).astype(BF)
+    k_s[...] = jnp.dot(x, w_s[step], preferred_element_type=jnp.float32).astype(BF)
+    v_s[...] = jnp.dot(x, w_s[2 + step], preferred_element_type=jnp.float32).astype(BF)
     for pool, parts in ((q_s, (qm, qo, qa, qb)), (ct_s, (cm, co, ca, cb))):
         pool[0:TOK, :] = parts[0][...]
         pool[TOK:PAIR, :] = parts[1][...]
@@ -152,9 +148,6 @@
     def narrow(rows, kind):
         return pl.BlockSpec((rows, HEAD_DIM), lambda i, m, e: (0, kind * 4 + i * 2 + chunk))
 
-    def gathered(kind):
-        return pl.BlockSpec((32, 1, 64, HEAD_DIM), lambda i, m, e: (0, kind * 2 + i, 0, e[2]))
-
     def handed(kind):
         return pl.BlockSpec((TOK, HEAD_DIM), lambda i, m, e: (0, i * 8 + kind * 2 + chunk))
 
@@ -169,11 +162,6 @@
 
     parts = [(4, 4, 128, HEAD_DIM)] * 4 if chunk == 0 else [(4, 4, 128, HEAD_DIM)] * 3 + [(2, 4, 128, HEAD_DIM)] * 2
     anywhere = pl.BlockSpec(memory_space=pl.ANY)
-    if len(weights) == 1:
-        weights = [*weights, *weights]
-        weight_specs = [gathered(0), gathered(1)]
-    else:
-        weight_specs = [fixed(*w.shape) for w in weights]
     pair = pltpu.VMEM((PAIR, HEAD_DIM), BF)
     pool = pltpu.VMEM((POOL, HEAD_DIM), BF)
     return pl.pallas_call(
@@ -181,7 +169,7 @@
         grid_spec=pltpu.PrefetchScalarGridSpec(
             num_scalar_prefetch=2,
             grid=(2,),
-            in_specs=[fixed(PAIR, D), fixed(D, PAIR), *weight_specs,
+            in_specs=[fixed(PAIR, D), fixed(D, PAIR), *[fixed(*w.shape) for w in weights],
                       wide(), handed(0), narrow(WIN, 0), narrow(WIN, 0),
                       wide(), handed(1), narrow(WIN, 1), narrow(WIN, 1)]
             + [anywhere] * len(before),
@@ -441,24 +429,24 @@
     return [parts[0]] + [lax.ppermute(parts[r], ALL, shift(phase, r)) for r in (1, 3, 2)]
 
 
-def join_kernel(*refs):
+def join_kernel(cols, *refs):
     for n in range(4):
-        refs[-1][n] = refs[n][...]
-
-
-def join(parts, after):
+        refs[-1][n] = refs[n][..., cols]
+
+
+def join(parts, after, cols=slice(0, HEAD_DIM)):
     whole = pl.BlockSpec(memory_space=pltpu.VMEM)
     return pl.pallas_call(
-        join_kernel,
+        functools.partial(join_kernel, cols),
         in_specs=[whole] * 4 + [pl.BlockSpec(memory_space=pl.ANY)] * len(after),
         out_specs=whole,
-        out_shape=jax.ShapeDtypeStruct((4,) + parts[0].shape, BF),
+        out_shape=jax.ShapeDtypeStruct((4,) + parts[0].shape[:-1] + (HEAD_DIM,), BF),
         compiler_params=pltpu.CompilerParams(vmem_limit_bytes=16 * MIB),
     )(*parts, *after)
 
 
 def pick_kernel(me, w_ref, got_ref, after, out_ref):
-    mine = w_ref[:, pl.ds(pl.multiple_of(me[2] * HALF, HALF), HEAD_DIM)]
+    mine = w_ref[:, pl.ds(pl.multiple_of(me[2] * HALF, HALF), HALF)]
     for core in range(2):
 
         @pl.when(me[2] == core)
@@ -473,7 +461,7 @@
         pick_kernel,
         in_specs=[pl.BlockSpec(memory_space=pltpu.SMEM), whole, whole, pl.BlockSpec(memory_space=pl.ANY)],
         out_specs=whole,
-        out_shape=jax.ShapeDtypeStruct((128, HEAD_DIM), BF),
+        out_shape=jax.ShapeDtypeStruct((128, HALF), BF),
         compiler_params=pltpu.CompilerParams(vmem_limit_bytes=16 * MIB),
     )(me, weights, got, after)
 
@@ -513,23 +501,22 @@
 def body(enc_hidden, kv_weights, queries, cotangent, enc_lengths, dec_lengths, dec_partner):
     z, y, c, x = (lax.axis_index(a) for a in ALL)
     me = jnp.stack([z, y, c, x]).astype(jnp.int32)
-    cols = [kv_weights[:, n * HEAD_DIM : (n + 1) * HEAD_DIM] for n in range(4)]
-    later = lax.all_gather(jnp.concatenate([cols[1], cols[3]], axis=1), ALL, axis=0).reshape(32, 4, 64, HALF)
-
     meta, info, leave_a, leave_b = depart(me, enc_lengths, dec_lengths, dec_partner, queries, cotangent)
     sent_a = lax.ppermute(leave_a, DP, SEND_A)
     sent_b = lax.ppermute(leave_b, DP, SEND_B)
 
-    got = swap(jnp.where(c == 0, cols[2], cols[0]))
+    got = swap(jnp.where(c == 0, kv_weights[:, HALF:], kv_weights[:, :HALF]))
     own = pick(me, kv_weights, got, leave_a)
     first = [own] + [ring(own, 2, n) for n in (1, 2, 3)]
-    handed = hand(me, queries, cotangent, enc_hidden, first[1:])
-    given = swap(handed)
-    part = join(first, [handed, sent_a, sent_b])
+    part = join(first, [sent_a, sent_b])
+    given = swap(hand(me, queries, cotangent, enc_hidden, [part]))
     part = join([part] + [ring(part, 1, n) for n in (1, 2, 3)], [])
     tokens, tokens_t = turn(enc_hidden, given, [part])
     ahead, behind = ring(part, 0, 1), ring(part, 0, -1)
-    weights = [[part, ahead, behind, ring(behind[:2], 0, -1), ring(ahead[2:], 0, 1)], [later]]
+    weights = [[part, ahead, behind, ring(behind[:2], 0, -1), ring(ahead[2:], 0, 1)]]
+    part = join(first, [tokens_t], slice(HEAD_DIM, HALF))
+    part = join([part] + [ring(part, 1, n) for n in (1, 2, 3)], weights[0][3:])
+    weights.append([part, ring(part, 0, 1), ring(part, 0, -1), ring(part, 0, 2)])
 
     shared = (meta, me, tokens, tokens_t)
     inputs = (queries, cotangent, given, sent_a, sent_b)

time: 226 us -> 203 us (0.90)
  between operations: 14.3 us -> 1 us
  waiting for transfers between devices: 69.1 us -> 64.7 us
  Pallas kernels: 58.9 us -> 55.6 us
    ppermute x1, waiting for transfers between devices: 8.37 us -> 0.01 us  [body(): sent_a = lax.ppermute(leave_a, DP, SEND_A)]
    ppermute x1, waiting for transfers between devices: 6.41 us -> 0.01 us  [body(): sent_b = lax.ppermute(leave_b, DP, SEND_B)]
    ppermute x10 -> x16, starting transfers between devices: 17 us -> 21.2 us  [ring(): return lax.ppermute(value, ALL, shift(phase, -amount))]
    ppermute x12, waiting for transfers between devices: 11.7 us -> 15.7 us  [exchange(): lax.ppermute(parts[r], ALL, shift(phase, r))]
    ppermute x4, starting transfers between devices: 8.01 us -> 5.44 us  [swap(): return lax.ppermute(value, 'c', [(0, 1), (1, 0)])]
    ppermute x12, starting transfers between devices: 15.2 us -> 12.6 us  [exchange(): lax.ppermute(parts[r], ALL, shift(phase, r))]
    ppermute x10 -> x16, waiting for transfers between devices: 33 us -> 34.9 us  [ring(): return lax.ppermute(value, ALL, shift(phase, -amount))]
    unnamed x34 -> x32, local copies, waits for them, and re-layouts: 11.5 us -> 12.4 us
  transfers between devices with their start and end apart: 37 -> 42, of which waited for: 19 -> 17; matrix products, arithmetic and copies ran while one was open for 0% -> 0% of each run, Pallas kernels for 26% -> 25%
where the time goes in v9:
time: 203 us
  starting transfers between devices  66.8 us (33%)
  waiting for transfers between devices  64.7 us (32%)
  Pallas kernels  55.6 us (27%)
  local copies, waits for them, and re-layouts  12.4 us (6%)
  other arithmetic  2.28 us (1%)
    pallas_call x2, Pallas kernels, run_main(): pl.pallas_call(functools.partial(main_kernel, len(weights), len(before)),...  41.6 us
    ppermute x16, waiting for transfers between devices, ring(): return lax.ppermute(value, ALL, shift(phase, -amount))  34.9 us
    ppermute x16, starting transfers between devices, ring(): return lax.ppermute(value, ALL, shift(phase, -amount))  21.2 us
    ppermute x12, waiting for transfers between devices, exchange(): lax.ppermute(parts[r], ALL, shift(phase, r))  15.7 us
    ppermute x4, starting transfers between devices, body(): lax.ppermute(part, DP, pairs)  14.1 us
    ppermute x12, starting transfers between devices, exchange(): lax.ppermute(parts[r], ALL, shift(phase, r))  12.6 us
    unnamed x32, local copies, waits for them, and re-layouts  12.4 us
    ppermute x4, starting transfers between devices, swap(): return lax.ppermute(value, 'c', [(0, 1), (1, 0)])  5.44 us
  transfers between devices with their start and end apart: 42, of which 17 were waited for; matrix products, arithmetic and copies ran while one was open for 0% of the time, Pallas kernels for 25%

profile of v9, /device:TPU:1, one launch (start us, length us, event | category | flops | bytes accessed | tf_op | source)
XLA Modules:
  0.0 202.9 jit_solution(6293888656407381772)
XLA Ops:
  1.3 3.5 %shard_map.94 = (s32[8,4]{1,0:T(8,128)}, s32[4]{0:T(128)}, bf16[176,2048]{1,0:T(8,128)(2,1)}, bf16[176,2048]{1,0:T(8,128)(2,1)}) custom-call(s32[4]{0:T(128)} %pad_add_fusion.me, s32[4,128]{1,0:T(4,128)} %bitcast.7, s32[4,128]{1,0:T(4,128)} %bitcast.8, s32[4,128]{1,0:T(4,128)} %bitcast.9, bf16[512,2048]{1,0:T(8,128)(2,1)} %refs_4_.1, bf16[512,2048]{1,0:T(8,128)(2,1)} %refs_8_.1), custom_call_target="tpu_custom_call" | custom-call | tf_op jit(solution)/shard_map/pallas_call | solution.py:312
  4.8 4.7 %collective-permute-start.5 = (bf16[176,2048]{1,0:T(8,128)(2,1)}, bf16[176,2048]{1,0:T(8,128)(2,1)S(1)}, u32[]{:S(2)}, u32[]{:S(2)}) collective-permute-start(bf16[176,2048]{1,0:T(8,128)(2,1)} %get-tuple-element.47), channel_id=1, source_target_pairs={{8,4},{16,12},{24,20},{32,28},{40,36},{48,44},{56,52},{64,60},{72,... | collective-permute-start | bytes 2162696 | tf_op jit(solution)/shard_map/ppermute | solution.py:506
  9.5 3.2 %collective-permute-start.4 = (bf16[176,2048]{1,0:T(8,128)(2,1)}, bf16[176,2048]{1,0:T(8,128)(2,1)S(1)}, u32[]{:S(2)}, u32[]{:S(2)}) collective-permute-start(bf16[176,2048]{1,0:T(8,128)(2,1)} %get-tuple-element.46.after), channel_id=1, source_target_pairs={{8,0},{16,8},{24,16},{32,24},{40,32},{48,40},{56,48},{64,56},{72,6... | collective-permute-start | bytes 2162696 | tf_op jit(solution)/shard_map/ppermute | solution.py:505
  18.6 2.9 %collective-permute-start.2 = (bf16[128,512]{1,0:T(8,128)(2,1)S(1)}, bf16[128,512]{1,0:T(8,128)(2,1)S(1)}, u32[]{:S(2)}, u32[]{:S(2)}) collective-permute-start(bf16[128,512]{1,0:T(8,128)(2,1)S(1)} %shard_map.95.refs_0_), channel_id=1, source_target_pairs={{0,64},{1,65},{2,66},{3,67},{4,20},{5,21},{6,22},{7,23},{8,72},{9,... | collective-permute-start | bytes 393224 | tf_op jit(solution)/shard_map/ppermute | solution.py:470
  22.3 9.4 %collective-permute-done.3.refs_3_ = bf16[128,512]{1,0:T(8,128)(2,1)S(1)} collective-permute-done((bf16[128,512]{1,0:T(8,128)(2,1)S(1)}, bf16[128,512]{1,0:T(8,128)(2,1)S(1)}, u32[]{:S(2)}, u32[]{:S(2)}) %collective-permute-start.3) | collective-permute-done | bytes 131104 | tf_op jit(solution)/shard_map/ppermute | solution.py:470
  36.4 3.7 %collective-permute-start.6 = (bf16[512,4096]{1,0:T(8,128)(2,1)S(1)}, bf16[512,4096]{1,0:T(8,128)(2,1)S(1)}, u32[]{:S(2)}, u32[]{:S(2)}) collective-permute-start(bf16[512,4096]{1,0:T(8,128)(2,1)S(1)} %shard_map.97), channel_id=1, source_target_pairs={{0,4},{4,0},{1,5},{5,1},{2,6},{6,2},{3,7},{7,3},{8,12},{12,8},{9,1... | collective-permute-start | bytes 12582920 | tf_op jit(solution)/shard_map/ppermute | solution.py:404
  41.4 2.5 %collective-permute-start.8 = (bf16[4,128,256]{2,1,0:T(8,128)(2,1)S(1)}, bf16[4,128,256]{2,1,0:T(8,128)(2,1)S(1)}, u32[]{:S(2)}, u32[]{:S(2)}) collective-permute-start(bf16[4,128,256]{2,1,0:T(8,128)(2,1)S(1)} %shard_map.96.refs_0_), channel_id=1, source_target_pairs={{0,16},{1,17},{2,18},{3,19},{4,6},{5,7},{6,4},{7,5},{8,24},{9,25},... | collective-permute-start | bytes 786440 | tf_op jit(solution)/shard_map/ppermute | solution.py:470
  45.0 1.9 collective-permute-done.9.refs_3_
  46.9 3.5 %collective-permute-done.8.refs_2_ = bf16[4,128,256]{2,1,0:T(8,128)(2,1)S(1)} collective-permute-done((bf16[4,128,256]{2,1,0:T(8,128)(2,1)S(1)}, bf16[4,128,256]{2,1,0:T(8,128)(2,1)S(1)}, u32[]{:S(2)}, u32[]{:S(2)}) %collective-permute-start.8) | collective-permute-done | bytes 262176 | tf_op jit(solution)/shard_map/ppermute | solution.py:470
  52.0 12.5 %collective-permute-done.15.refs_1_ = bf16[4,4,128,256]{3,2,1,0:T(8,128)(2,1)S(1)} collective-permute-done((bf16[4,4,128,256]{3,2,1,0:T(8,128)(2,1)S(1)}, bf16[4,4,128,256]{3,2,1,0:T(8,128)(2,1)S(1)}, u32[]{:S(2)}, u32[]{:S(2)}) %collective-permute-start.15) | collective-permute-done | bytes 1048608 | tf_op jit(solution)/shard_map/ppermute | solution.py:470
  66.2 2.2 %shard_map.99 = (bf16[1024,2048]{1,0:T(8,128)(2,1)S(1)}, bf16[2048,1024]{1,0:T(8,128)(2,1)S(1)}) custom-call(bf16[512,2048]{1,0:T(8,128)(2,1)S(1)} %copy-done.2, bf16[512,4096]{1,0:T(8,128)(2,1)S(1)} %collective-permute-done.6.b_ref.refs_6_.refs_10_.refs_5_.refs_9_, bf16[4,4,128,256]{3,2,1,0:T(8,128)(2,1)S(1)} %shard_map.98.refs_0_), custom_call_target="tpu_custom_call" | custom-call | tf_op jit(solution)/shard_map/pallas_call | solution.py:358
  68.4 2.0 copy-done.12
  70.4 2.0 copy-done.6
  73.8 2.1 %collective-permute-start.11 = (bf16[4,128,256]{2,1,0:T(8,128)(2,1)S(1)}, bf16[4,128,256]{2,1,0:T(8,128)(2,1)S(1)}, u32[]{:S(2)}, u32[]{:S(2)}) collective-permute-start(bf16[4,128,256]{2,1,0:T(8,128)(2,1)S(1)} %shard_map.100.refs_0_), channel_id=1, source_target_pairs={{0,16},{1,17},{2,18},{3,19},{4,6},{5,7},{6,4},{7,5},{8,24},{9,25},... | collective-permute-start | bytes 786440 | tf_op jit(solution)/shard_map/ppermute | solution.py:470
  77.2 7.6 %collective-permute-done.12.refs_3_ = bf16[4,128,256]{2,1,0:T(8,128)(2,1)S(1)} collective-permute-done((bf16[4,128,256]{2,1,0:T(8,128)(2,1)S(1)}, bf16[4,128,256]{2,1,0:T(8,128)(2,1)S(1)}, u32[]{:S(2)}, u32[]{:S(2)}) %collective-permute-start.12) | collective-permute-done | bytes 262176 | tf_op jit(solution)/shard_map/ppermute | solution.py:470
  88.6 20.8 %shard_map.102 = (bf16[2,512,1024]{2,1,0:T(8,128)(2,1)}, bf16[2,512,1024]{2,1,0:T(8,128)(2,1)}, bf16[2,176,512]{2,1,0:T(8,128)(2,1)S(1)}, bf16[2,176,512]{2,1,0:...) custom-call(s32[8,4]{1,0:T(8,128)S(1)} %copy-done.13, ...), custom_call_target="tpu_custom_call" | custom-call | flops 12000000000 | bytes 24000000 | tf_op jit(solution)/shard_map/pallas_call | solution.py:167
  110.7 7.2 %collective-permute-start.22 = (bf16[2,176,512]{2,1,0:T(8,128)(2,1)S(1)}, bf16[2,176,512]{2,1,0:T(8,128)(2,1)S(1)}, u32[]{:S(2)}, u32[]{:S(2)}) collective-permute-start(bf16[2,176,512]{2,1,0:T(8,128)(2,1)S(1)} %get-tuple-element.55), channel_id=1, source_target_pairs={{4,8},{12,16},{20,24},{28,32},{36,40},{44,48},{52,56},{60,64},{68,... | collective-permute-start | bytes 1081352 | tf_op jit(solution)/shard_map/ppermute | solution.py:526
  118.0 2.7 %collective-permute-start.26 = (bf16[4,4,128,256]{3,2,1,0:T(8,128)(2,1)S(1)}, bf16[4,4,128,256]{3,2,1,0:T(8,128)(2,1)S(1)}, u32[]{:S(2)}, u32[]{:S(2)}) collective-permute-start(bf16[4,4,128,256]{3,2,1,0:T(8,128)(2,1)S(1)} %get-tuple-element.62), channel_id=1, source_target_pairs={{0,3},{1,0},{2,1},{3,2},{4,100},{5,101},{6,102},{7,103},{8,11},{9,... | collective-permute-start | bytes 3145736 | tf_op jit(solution)/shard_map/ppermute | solution.py:429
  120.7 20.8 %shard_map.103 = (bf16[2,512,1024]{2,1,0:T(8,128)(2,1)}, bf16[2,512,1024]{2,1,0:T(8,128)(2,1)}, bf16[2,176,512]{2,1,0:T(8,128)(2,1)S(1)}, bf16[2,176,512]{2,1,0:...) custom-call(s32[8,4]{1,0:T(8,128)S(1)} %copy-done.13, ...), custom_call_target="tpu_custom_call", output_to_operand_aliasing={{0}: (16, {}), {1}: (17, {})} | custom-call | flops 12000000000 | bytes 24000000 | tf_op jit(solution)/shard_map/pallas_call | solution.py:167
  142.6 1.7 collective-permute-start.32
  144.3 6.8 %collective-permute-done.27.refs_3_ = bf16[4,4,128,256]{3,2,1,0:T(8,128)(2,1)S(1)} collective-permute-done((bf16[4,4,128,256]{3,2,1,0:T(8,128)(2,1)S(1)}, bf16[4,4,128,256]{3,2,1,0:T(8,128)(2,1)S(1)}, u32[]{:S(2)}, u32[]{:S(2)}) %collective-permute-start.27) | collective-permute-done | bytes 1048608 | tf_op jit(solution)/shard_map/ppermute | solution.py:429
  153.6 3.0 %collective-permute-done.31.got_a = bf16[2,4,128,256]{3,2,1,0:T(8,128)(2,1)S(1)} collective-permute-done((bf16[2,4,128,256]{3,2,1,0:T(8,128)(2,1)S(1)}, bf16[2,4,128,256]{3,2,1,0:T(8,128)(2,1)S(1)}, u32[]{:S(2)}, u32[]{:S(2)}) %collective-permute-start.31) | collective-permute-done | bytes 524320 | tf_op jit(solution)/shard_map/ppermute | solution.py:495
  157.0 2.7 %collective-permute-start.34 = (bf16[4,4,128,256]{3,2,1,0:T(8,128)(2,1)S(1)}, bf16[4,4,128,256]{3,2,1,0:T(8,128)(2,1)S(1)}, u32[]{:S(2)}, u32[]{:S(2)}) collective-permute-start(bf16[4,4,128,256]{3,2,1,0:T(8,128)(2,1)S(1)} %get-tuple-element.74), channel_id=1, source_target_pairs={{0,3},{1,0},{2,1},{3,2},{4,100},{5,101},{6,102},{7,103},{8,11},{9,... | collective-permute-start | bytes 3145736 | tf_op jit(solution)/shard_map/ppermute | solution.py:498
  160.9 4.4 %collective-permute-start.24 = (bf16[2,176,512]{2,1,0:T(8,128)(2,1)S(1)}, bf16[2,176,512]{2,1,0:T(8,128)(2,1)S(1)}, u32[]{:S(2)}, u32[]{:S(2)}) collective-permute-start(bf16[2,176,512]{2,1,0:T(8,128)(2,1)S(1)} %get-tuple-element.57), channel_id=1, source_target_pairs={{4,8},{12,16},{20,24},{28,32},{36,40},{44,48},{52,56},{60,64},{68,... | collective-permute-start | bytes 1081352 | tf_op jit(solution)/shard_map/ppermute | solution.py:530
  165.3 3.6 %collective-permute-done.23.refs_4_.refs_3_ = bf16[2,176,512]{2,1,0:T(8,128)(2,1)S(1)} collective-permute-done((bf16[2,176,512]{2,1,0:T(8,128)(2,1)S(1)}, bf16[2,176,512]{2,1,0:T(8,128)(2,1)S(1)}, u32[]{:S(2)}, u32[]{:S(2)}) %collective-permute-start.23) | collective-permute-done | bytes 360480 | tf_op jit(solution)/shard_map/ppermute | solution.py:530
  169.0 1.9 collective-permute-start.28
  172.0 4.4 %collective-permute-done.33.refs_1_ = bf16[4,4,128,256]{3,2,1,0:T(8,128)(2,1)S(1)} collective-permute-done((bf16[4,4,128,256]{3,2,1,0:T(8,128)(2,1)S(1)}, bf16[4,4,128,256]{3,2,1,0:T(8,128)(2,1)S(1)}, u32[]{:S(2)}, u32[]{:S(2)}) %collective-permute-start.33) | collective-permute-done | bytes 1048608 | tf_op jit(solution)/shard_map/ppermute | solution.py:498
  178.5 2.7 %collective-permute-start.36 = (bf16[4,128,256]{2,1,0:T(8,128)(2,1)S(1)}, bf16[4,128,256]{2,1,0:T(8,128)(2,1)S(1)}, u32[]{:S(2)}, u32[]{:S(2)}) collective-permute-start(bf16[4,128,256]{2,1,0:T(8,128)(2,1)S(1)} %get-tuple-element.77), channel_id=1, source_target_pairs={{0,24},{1,25},{2,26},{3,27},{4,7},{5,4},{6,5},{7,6},{8,0},{9,1},{1... | collective-permute-start | bytes 786440 | tf_op jit(solution)/shard_map/ppermute | solution.py:429
  183.3 3.0 %collective-permute-done.35.refs_5_ = bf16[4,128,256]{2,1,0:T(8,128)(2,1)S(1)} collective-permute-done((bf16[4,128,256]{2,1,0:T(8,128)(2,1)S(1)}, bf16[4,128,256]{2,1,0:T(8,128)(2,1)S(1)}, u32[]{:S(2)}, u32[]{:S(2)}) %collective-permute-start.35) | collective-permute-done | bytes 262176 | tf_op jit(solution)/shard_map/ppermute | solution.py:429
  189.1 2.7 %collective-permute-start.39 = (bf16[128,512]{1,0:T(8,128)(2,1)S(1)}, bf16[128,512]{1,0:T(8,128)(2,1)S(1)}, u32[]{:S(2)}, u32[]{:S(2)}) collective-permute-start(bf16[128,512]{1,0:T(8,128)(2,1)S(1)} %get-tuple-element.81), channel_id=1, source_target_pairs={{0,96},{1,97},{2,98},{3,99},{4,28},{5,29},{6,30},{7,31},{8,104},{9... | collective-permute-start | bytes 393224 | tf_op jit(solution)/shard_map/ppermute | solution.py:429
  191.8 3.4 %shard_map.104 = (bf16[512,2048]{1,0:T(8,128)(2,1)}, bf16[512,2048]{1,0:T(8,128)(2,1)}) custom-call(s32[4]{0:T(128)S(1)} %copy-done.11, bf16[2,512,1024]{2,1,0:T(8,128)(2,1)S(1)} %copy-done.1, bf16[2,512,1024]{2,1,0:T(8,128)(2,1)S(1)} %collective-permute-done.20.refs_1_, bf16[2,176,512]{2,1,0:T(8,128)(2,1)S(1)} %collective-permute-done.21.refs_2_.refs_5_, ...), custom_call_target="tpu_custom_call" | custom-call | tf_op jit(solution)/shard_map/pallas_call | solution.py:390
  195.2 2.2 %collective-permute-done.40.refs_3_ = bf16[128,512]{1,0:T(8,128)(2,1)S(1)} collective-permute-done((bf16[128,512]{1,0:T(8,128)(2,1)S(1)}, bf16[128,512]{1,0:T(8,128)(2,1)S(1)}, u32[]{:S(2)}, u32[]{:S(2)}) %collective-permute-start.40) | collective-permute-done | bytes 131104 | tf_op jit(solution)/shard_map/ppermute | solution.py:429
  (106 shorter events, 44.3 us)
Async XLA Ops:
  4.8 26.9 %collective-permute-start.5 = (bf16[176,2048]{1,0:T(8,128)(2,1)}, bf16[176,2048]{1,0:T(8,128)(2,1)S(1)}, u32[]{:S(2)}, u32[]{:S(2)}) collective-permute-start(bf16[176,2048]{1,0:T(8,128)(2,1)} %get-tuple-element.47), channel_id=1, source_target_pairs={{8,4},{16,12},{24,20},{32,28},{40,36},{48,44},{56,52},{64,60},{72,... | collective-permute-start | bytes 2162696 | tf_op jit(solution)/shard_map/ppermute | solution.py:506
  9.5 22.2 %collective-permute-start.4 = (bf16[176,2048]{1,0:T(8,128)(2,1)}, bf16[176,2048]{1,0:T(8,128)(2,1)S(1)}, u32[]{:S(2)}, u32[]{:S(2)}) collective-permute-start(bf16[176,2048]{1,0:T(8,128)(2,1)} %get-tuple-element.46.after), channel_id=1, source_target_pairs={{8,0},{16,8},{24,16},{32,24},{40,32},{48,40},{56,48},{64,56},{72,6... | collective-permute-start | bytes 2162696 | tf_op jit(solution)/shard_map/ppermute | solution.py:505
  17.6 14.1 %collective-permute-start.3 = (bf16[128,512]{1,0:T(8,128)(2,1)S(1)}, bf16[128,512]{1,0:T(8,128)(2,1)S(1)}, u32[]{:S(2)}, u32[]{:S(2)}) collective-permute-start(bf16[128,512]{1,0:T(8,128)(2,1)S(1)} %shard_map.95.refs_0_), channel_id=1, source_target_pairs={{0,32},{1,33},{2,34},{3,35},{4,12},{5,13},{6,14},{7,15},{8,40},{9,... | collective-permute-start | bytes 393224 | tf_op jit(solution)/shard_map/ppermute | solution.py:470
  18.6 13.1 %collective-permute-start.2 = (bf16[128,512]{1,0:T(8,128)(2,1)S(1)}, bf16[128,512]{1,0:T(8,128)(2,1)S(1)}, u32[]{:S(2)}, u32[]{:S(2)}) collective-permute-start(bf16[128,512]{1,0:T(8,128)(2,1)S(1)} %shard_map.95.refs_0_), channel_id=1, source_target_pairs={{0,64},{1,65},{2,66},{3,67},{4,20},{5,21},{6,22},{7,23},{8,72},{9,... | collective-permute-start | bytes 393224 | tf_op jit(solution)/shard_map/ppermute | solution.py:470
  21.5 10.2 %collective-permute-start.1 = (bf16[128,512]{1,0:T(8,128)(2,1)S(1)}, bf16[128,512]{1,0:T(8,128)(2,1)S(1)}, u32[]{:S(2)}, u32[]{:S(2)}) collective-permute-start(bf16[128,512]{1,0:T(8,128)(2,1)S(1)} %shard_map.95.refs_0_), channel_id=1, source_target_pairs={{0,96},{1,97},{2,98},{3,99},{4,28},{5,29},{6,30},{7,31},{8,104},{9... | collective-permute-start | bytes 393224 | tf_op jit(solution)/shard_map/ppermute | solution.py:470
  36.4 29.7 %collective-permute-start.6 = (bf16[512,4096]{1,0:T(8,128)(2,1)S(1)}, bf16[512,4096]{1,0:T(8,128)(2,1)S(1)}, u32[]{:S(2)}, u32[]{:S(2)}) collective-permute-start(bf16[512,4096]{1,0:T(8,128)(2,1)S(1)} %shard_map.97), channel_id=1, source_target_pairs={{0,4},{4,0},{1,5},{5,1},{2,6},{6,2},{3,7},{7,3},{8,12},{12,8},{9,1... | collective-permute-start | bytes 12582920 | tf_op jit(solution)/shard_map/ppermute | solution.py:404
  41.4 9.0 %collective-permute-start.8 = (bf16[4,128,256]{2,1,0:T(8,128)(2,1)S(1)}, bf16[4,128,256]{2,1,0:T(8,128)(2,1)S(1)}, u32[]{:S(2)}, u32[]{:S(2)}) collective-permute-start(bf16[4,128,256]{2,1,0:T(8,128)(2,1)S(1)} %shard_map.96.refs_0_), channel_id=1, source_target_pairs={{0,16},{1,17},{2,18},{3,19},{4,6},{5,7},{6,4},{7,5},{8,24},{9,25},... | collective-permute-start | bytes 786440 | tf_op jit(solution)/shard_map/ppermute | solution.py:470
  50.5 14.0 %collective-permute-start.15 = (bf16[4,4,128,256]{3,2,1,0:T(8,128)(2,1)S(1)}, bf16[4,4,128,256]{3,2,1,0:T(8,128)(2,1)S(1)}, u32[]{:S(2)}, u32[]{:S(2)}) collective-permute-start(bf16[4,4,128,256]{3,2,1,0:T(8,128)(2,1)S(1)} %shard_map.98.refs_0_), channel_id=1, source_target_pairs={{0,3},{1,0},{2,1},{3,2},{4,100},{5,101},{6,102},{7,103},{8,11},{9,... | collective-permute-start | bytes 3145736 | tf_op jit(solution)/shard_map/ppermute | solution.py:470
  50.6 15.3 %collective-permute-start.13 = (bf16[4,4,128,256]{3,2,1,0:T(8,128)(2,1)S(1)}, bf16[4,4,128,256]{3,2,1,0:T(8,128)(2,1)S(1)}, u32[]{:S(2)}, u32[]{:S(2)}) collective-permute-start(bf16[4,4,128,256]{3,2,1,0:T(8,128)(2,1)S(1)} %shard_map.98.refs_0_), channel_id=1, source_target_pairs={{0,1},{1,2},{2,3},{3,0},{4,36},{5,37},{6,38},{7,39},{8,9},{9,10},{... | collective-permute-start | bytes 3145736 | tf_op jit(solution)/shard_map/ppermute | solution.py:470
  64.5 12.6 %collective-permute-start.16 = (bf16[2,4,128,256]{3,2,1,0:T(8,128)(2,1)S(1)}, bf16[2,4,128,256]{3,2,1,0:T(8,128)(2,1)S(1)}, u32[]{:S(2)}, u32[]{:S(2)}) collective-permute-start(bf16[2,4,128,256]{3,2,1,0:T(8,128)(2,1)S(1)} %slice.17), channel_id=1, source_target_pairs={{0,3},{1,0},{2,1},{3,2},{4,100},{5,101},{6,102},{7,103},{8,11},{9,... | collective-permute-start | bytes 1572872 | tf_op jit(solution)/shard_map/ppermute | solution.py:470
  65.9 11.3 %collective-permute-start.14 = (bf16[2,4,128,256]{3,2,1,0:T(8,128)(2,1)S(1)}, bf16[2,4,128,256]{3,2,1,0:T(8,128)(2,1)S(1)}, u32[]{:S(2)}, u32[]{:S(2)}) collective-permute-start(bf16[2,4,128,256]{3,2,1,0:T(8,128)(2,1)S(1)} %slice.16), channel_id=1, source_target_pairs={{0,1},{1,2},{2,3},{3,0},{4,36},{5,37},{6,38},{7,39},{8,9},{9,10},{... | collective-permute-start | bytes 1572872 | tf_op jit(solution)/shard_map/ppermute | solution.py:470
  72.4 12.4 %collective-permute-start.12 = (bf16[4,128,256]{2,1,0:T(8,128)(2,1)S(1)}, bf16[4,128,256]{2,1,0:T(8,128)(2,1)S(1)}, u32[]{:S(2)}, u32[]{:S(2)}) collective-permute-start(bf16[4,128,256]{2,1,0:T(8,128)(2,1)S(1)} %shard_map.100.refs_0_), channel_id=1, source_target_pairs={{0,8},{1,9},{2,10},{3,11},{4,5},{5,6},{6,7},{7,4},{8,16},{9,17},{1... | collective-permute-start | bytes 786440 | tf_op jit(solution)/shard_map/ppermute | solution.py:470
  73.8 11.0 %collective-permute-start.11 = (bf16[4,128,256]{2,1,0:T(8,128)(2,1)S(1)}, bf16[4,128,256]{2,1,0:T(8,128)(2,1)S(1)}, u32[]{:S(2)}, u32[]{:S(2)}) collective-permute-start(bf16[4,128,256]{2,1,0:T(8,128)(2,1)S(1)} %shard_map.100.refs_0_), channel_id=1, source_target_pairs={{0,16},{1,17},{2,18},{3,19},{4,6},{5,7},{6,4},{7,5},{8,24},{9,25},... | collective-permute-start | bytes 786440 | tf_op jit(solution)/shard_map/ppermute | solution.py:470
  75.9 8.9 %collective-permute-start.10 = (bf16[4,128,256]{2,1,0:T(8,128)(2,1)S(1)}, bf16[4,128,256]{2,1,0:T(8,128)(2,1)S(1)}, u32[]{:S(2)}, u32[]{:S(2)}) collective-permute-start(bf16[4,128,256]{2,1,0:T(8,128)(2,1)S(1)} %shard_map.100.refs_0_), channel_id=1, source_target_pairs={{0,24},{1,25},{2,26},{3,27},{4,7},{5,4},{6,5},{7,6},{8,0},{9,1},{1... | collective-permute-start | bytes 786440 | tf_op jit(solution)/shard_map/ppermute | solution.py:470
  84.9 33.0 %collective-permute-start.19 = (bf16[4,4,128,256]{3,2,1,0:T(8,128)(2,1)S(1)}, bf16[4,4,128,256]{3,2,1,0:T(8,128)(2,1)S(1)}, u32[]{:S(2)}, u32[]{:S(2)}) collective-permute-start(bf16[4,4,128,256]{3,2,1,0:T(8,128)(2,1)S(1)} %shard_map.101.refs_0_), channel_id=1, source_target_pairs={{0,2},{1,3},{2,0},{3,1},{4,68},{5,69},{6,70},{7,71},{8,10},{9,11},... | collective-permute-start | bytes 3145736 | tf_op jit(solution)/shard_map/ppermute | solution.py:470
  86.0 32.0 %collective-permute-start.18 = (bf16[4,4,128,256]{3,2,1,0:T(8,128)(2,1)S(1)}, bf16[4,4,128,256]{3,2,1,0:T(8,128)(2,1)S(1)}, u32[]{:S(2)}, u32[]{:S(2)}) collective-permute-start(bf16[4,4,128,256]{3,2,1,0:T(8,128)(2,1)S(1)} %shard_map.101.refs_0_), channel_id=1, source_target_pairs={{0,1},{1,2},{2,3},{3,0},{4,36},{5,37},{6,38},{7,39},{8,9},{9,10},{... | collective-permute-start | bytes 3145736 | tf_op jit(solution)/shard_map/ppermute | solution.py:470
  87.4 33.2 %collective-permute-start.17 = (bf16[4,4,128,256]{3,2,1,0:T(8,128)(2,1)S(1)}, bf16[4,4,128,256]{3,2,1,0:T(8,128)(2,1)S(1)}, u32[]{:S(2)}, u32[]{:S(2)}) collective-permute-start(bf16[4,4,128,256]{3,2,1,0:T(8,128)(2,1)S(1)} %shard_map.101.refs_0_), channel_id=1, source_target_pairs={{0,3},{1,0},{2,1},{3,2},{4,100},{5,101},{6,102},{7,103},{8,11},{9,... | collective-permute-start | bytes 3145736 | tf_op jit(solution)/shard_map/ppermute | solution.py:470
  109.4 32.0 %collective-permute-start.21 = (bf16[2,176,512]{2,1,0:T(8,128)(2,1)S(1)}, bf16[2,176,512]{2,1,0:T(8,128)(2,1)S(1)}, u32[]{:S(2)}, u32[]{:S(2)}) collective-permute-start(bf16[2,176,512]{2,1,0:T(8,128)(2,1)S(1)} %get-tuple-element.54), channel_id=1, source_target_pairs={{0,8},{8,16},{16,24},{24,32},{32,40},{40,48},{48,56},{56,64},{64,7... | collective-permute-start | bytes 1081352 | tf_op jit(solution)/shard_map/ppermute | solution.py:526
  110.7 30.9 %collective-permute-start.22 = (bf16[2,176,512]{2,1,0:T(8,128)(2,1)S(1)}, bf16[2,176,512]{2,1,0:T(8,128)(2,1)S(1)}, u32[]{:S(2)}, u32[]{:S(2)}) collective-permute-start(bf16[2,176,512]{2,1,0:T(8,128)(2,1)S(1)} %get-tuple-element.55), channel_id=1, source_target_pairs={{4,8},{12,16},{20,24},{28,32},{36,40},{44,48},{52,56},{60,64},{68,... | collective-permute-start | bytes 1081352 | tf_op jit(solution)/shard_map/ppermute | solution.py:526
  117.9 24.7 %collective-permute-start.25 = (bf16[4,4,128,256]{3,2,1,0:T(8,128)(2,1)S(1)}, bf16[4,4,128,256]{3,2,1,0:T(8,128)(2,1)S(1)}, u32[]{:S(2)}, u32[]{:S(2)}) collective-permute-start(bf16[4,4,128,256]{3,2,1,0:T(8,128)(2,1)S(1)} %get-tuple-element.61), channel_id=1, source_target_pairs={{0,1},{1,2},{2,3},{3,0},{4,36},{5,37},{6,38},{7,39},{8,9},{9,10},{... | collective-permute-start | bytes 3145736 | tf_op jit(solution)/shard_map/ppermute | solution.py:429
  118.0 26.3 %collective-permute-start.26 = (bf16[4,4,128,256]{3,2,1,0:T(8,128)(2,1)S(1)}, bf16[4,4,128,256]{3,2,1,0:T(8,128)(2,1)S(1)}, u32[]{:S(2)}, u32[]{:S(2)}) collective-permute-start(bf16[4,4,128,256]{3,2,1,0:T(8,128)(2,1)S(1)} %get-tuple-element.62), channel_id=1, source_target_pairs={{0,3},{1,0},{2,1},{3,2},{4,100},{5,101},{6,102},{7,103},{8,11},{9,... | collective-permute-start | bytes 3145736 | tf_op jit(solution)/shard_map/ppermute | solution.py:429
  120.7 30.4 %collective-permute-start.27 = (bf16[4,4,128,256]{3,2,1,0:T(8,128)(2,1)S(1)}, bf16[4,4,128,256]{3,2,1,0:T(8,128)(2,1)S(1)}, u32[]{:S(2)}, u32[]{:S(2)}) collective-permute-start(bf16[4,4,128,256]{3,2,1,0:T(8,128)(2,1)S(1)} %get-tuple-element.63), channel_id=1, source_target_pairs={{0,2},{1,3},{2,0},{3,1},{4,68},{5,69},{6,70},{7,71},{8,10},{9,11},... | collective-permute-start | bytes 3145736 | tf_op jit(solution)/shard_map/ppermute | solution.py:429
  141.5 50.3 %collective-permute-start.20 = (bf16[2,512,1024]{2,1,0:T(8,128)(2,1)}, bf16[2,512,1024]{2,1,0:T(8,128)(2,1)S(1)}, u32[]{:S(2)}, u32[]{:S(2)}) collective-permute-start(bf16[2,512,1024]{2,1,0:T(8,128)(2,1)} %get-tuple-element.53), channel_id=1, source_target_pairs={{0,4},{4,0},{1,5},{5,1},{2,6},{6,2},{3,7},{7,3},{8,12},{12,8},{9,1... | collective-permute-start | bytes 6291464 | tf_op jit(solution)/shard_map/ppermute | solution.py:404
  141.6 15.0 %collective-permute-start.31 = (bf16[2,4,128,256]{3,2,1,0:T(8,128)(2,1)S(1)}, bf16[2,4,128,256]{3,2,1,0:T(8,128)(2,1)S(1)}, u32[]{:S(2)}, u32[]{:S(2)}) collective-permute-start(bf16[2,4,128,256]{3,2,1,0:T(8,128)(2,1)S(1)} %get-tuple-element.71), channel_id=1, source_target_pairs={{0,1},{1,2},{2,3},{3,0},{4,36},{5,37},{6,38},{7,39},{8,9},{9,10},{... | collective-permute-start | bytes 1572872 | tf_op jit(solution)/shard_map/ppermute | solution.py:495
  142.6 14.0 %collective-permute-start.32 = (bf16[2,4,128,256]{3,2,1,0:T(8,128)(2,1)S(1)}, bf16[2,4,128,256]{3,2,1,0:T(8,128)(2,1)S(1)}, u32[]{:S(2)}, u32[]{:S(2)}) collective-permute-start(bf16[2,4,128,256]{3,2,1,0:T(8,128)(2,1)S(1)} %get-tuple-element.72), channel_id=1, source_target_pairs={{0,3},{1,0},{2,1},{3,2},{4,100},{5,101},{6,102},{7,103},{8,11},{9,... | collective-permute-start | bytes 1572872 | tf_op jit(solution)/shard_map/ppermute | solution.py:496
  156.9 19.5 %collective-permute-start.33 = (bf16[4,4,128,256]{3,2,1,0:T(8,128)(2,1)S(1)}, bf16[4,4,128,256]{3,2,1,0:T(8,128)(2,1)S(1)}, u32[]{:S(2)}, u32[]{:S(2)}) collective-permute-start(bf16[4,4,128,256]{3,2,1,0:T(8,128)(2,1)S(1)} %get-tuple-element.73), channel_id=1, source_target_pairs={{0,1},{1,2},{2,3},{3,0},{4,36},{5,37},{6,38},{7,39},{8,9},{9,10},{... | collective-permute-start | bytes 3145736 | tf_op jit(solution)/shard_map/ppermute | solution.py:498
  157.0 20.7 %collective-permute-start.34 = (bf16[4,4,128,256]{3,2,1,0:T(8,128)(2,1)S(1)}, bf16[4,4,128,256]{3,2,1,0:T(8,128)(2,1)S(1)}, u32[]{:S(2)}, u32[]{:S(2)}) collective-permute-start(bf16[4,4,128,256]{3,2,1,0:T(8,128)(2,1)S(1)} %get-tuple-element.74), channel_id=1, source_target_pairs={{0,3},{1,0},{2,1},{3,2},{4,100},{5,101},{6,102},{7,103},{8,11},{9,... | collective-permute-start | bytes 3145736 | tf_op jit(solution)/shard_map/ppermute | solution.py:498
  159.6 9.3 %collective-permute-start.23 = (bf16[2,176,512]{2,1,0:T(8,128)(2,1)S(1)}, bf16[2,176,512]{2,1,0:T(8,128)(2,1)S(1)}, u32[]{:S(2)}, u32[]{:S(2)}) collective-permute-start(bf16[2,176,512]{2,1,0:T(8,128)(2,1)S(1)} %get-tuple-element.56), channel_id=1, source_target_pairs={{0,8},{8,16},{16,24},{24,32},{32,40},{40,48},{48,56},{56,64},{64,7... | collective-permute-start | bytes 1081352 | tf_op jit(solution)/shard_map/ppermute | solution.py:530
  160.9 10.7 %collective-permute-start.24 = (bf16[2,176,512]{2,1,0:T(8,128)(2,1)S(1)}, bf16[2,176,512]{2,1,0:T(8,128)(2,1)S(1)}, u32[]{:S(2)}, u32[]{:S(2)}) collective-permute-start(bf16[2,176,512]{2,1,0:T(8,128)(2,1)S(1)} %get-tuple-element.57), channel_id=1, source_target_pairs={{4,8},{12,16},{20,24},{28,32},{36,40},{44,48},{52,56},{60,64},{68,... | collective-permute-start | bytes 1081352 | tf_op jit(solution)/shard_map/ppermute | solution.py:530
  169.0 9.5 %collective-permute-start.28 = (bf16[4,128,256]{2,1,0:T(8,128)(2,1)S(1)}, bf16[4,128,256]{2,1,0:T(8,128)(2,1)S(1)}, u32[]{:S(2)}, u32[]{:S(2)}) collective-permute-start(bf16[4,128,256]{2,1,0:T(8,128)(2,1)S(1)} %get-tuple-element.65), channel_id=1, source_target_pairs={{0,8},{1,9},{2,10},{3,11},{4,5},{5,6},{6,7},{7,4},{8,16},{9,17},{1... | collective-permute-start | bytes 786440 | tf_op jit(solution)/shard_map/ppermute | solution.py:429
  171.7 9.5 %collective-permute-start.29 = (bf16[4,128,256]{2,1,0:T(8,128)(2,1)S(1)}, bf16[4,128,256]{2,1,0:T(8,128)(2,1)S(1)}, u32[]{:S(2)}, u32[]{:S(2)}) collective-permute-start(bf16[4,128,256]{2,1,0:T(8,128)(2,1)S(1)} %get-tuple-element.66), channel_id=1, source_target_pairs={{0,24},{1,25},{2,26},{3,27},{4,7},{5,4},{6,5},{7,6},{8,0},{9,1},{1... | collective-permute-start | bytes 786440 | tf_op jit(solution)/shard_map/ppermute | solution.py:429
  178.5 8.8 %collective-permute-start.36 = (bf16[4,128,256]{2,1,0:T(8,128)(2,1)S(1)}, bf16[4,128,256]{2,1,0:T(8,128)(2,1)S(1)}, u32[]{:S(2)}, u32[]{:S(2)}) collective-permute-start(bf16[4,128,256]{2,1,0:T(8,128)(2,1)S(1)} %get-tuple-element.77), channel_id=1, source_target_pairs={{0,24},{1,25},{2,26},{3,27},{4,7},{5,4},{6,5},{7,6},{8,0},{9,1},{1... | collective-permute-start | bytes 786440 | tf_op jit(solution)/shard_map/ppermute | solution.py:429
  (26 other events, 162.5 us)

commit v10 on v9

--- a/solution.py
+++ b/solution.py
@@ -149,7 +149,7 @@
         return pl.BlockSpec((rows, HEAD_DIM), lambda i, m, e: (0, kind * 4 + i * 2 + chunk))
 
     def handed(kind):
-        return pl.BlockSpec((TOK, HEAD_DIM), lambda i, m, e: (0, i * 8 + kind * 2 + chunk))
+        return pl.BlockSpec((TOK, HEAD_DIM), lambda i, m, e: (0, i * 4 + kind * 2 + chunk))
 
     def out(rows):
         return pl.BlockSpec((2, rows, HEAD_DIM), lambda i, m, e: (0, 0, i * 2 + chunk))
@@ -211,19 +211,19 @@
 def add_both_kernel(*refs):
     for chunk in range(2):
         total = add(refs[chunk * 4 : chunk * 4 + 4]).astype(BF)
-        for n, out in enumerate(refs[8:]):
+        for n, out in enumerate(refs[-4:]):
             out[:, chunk * HEAD_DIM : (chunk + 1) * HEAD_DIM] = total[n]
 
 
-def add_both(first, second):
+def add_both(first, second, after):
     whole = pl.BlockSpec(memory_space=pltpu.VMEM)
     return pl.pallas_call(
         add_both_kernel,
-        in_specs=[whole] * 8,
+        in_specs=[whole] * 8 + [pl.BlockSpec(memory_space=pl.ANY)] * len(after),
         out_specs=[whole] * 4,
         out_shape=[jax.ShapeDtypeStruct((128, HALF), BF)] * 4,
         compiler_params=pltpu.CompilerParams(vmem_limit_bytes=16 * MIB),
-    )(*first, *second)
+    )(*first, *second, *after)
 
 
 def add_last_kernel(me, *refs):
@@ -320,13 +320,12 @@
     )(me, enc_lengths.T, dec_lengths.T, dec_partner.T, q, ct)
 
 
-def hand_kernel(me, q_ref, ct_ref, x_ref, *refs):
+def hand_kernel(me, q_ref, ct_ref, *refs):
     refs[-1][:, :HALF] = q_ref[...]
-    refs[-1][:, HALF : 2 * HALF] = ct_ref[...]
-    refs[-1][:, 2 * HALF :] = x_ref[...]
-
-
-def hand(me, q, ct, x, after):
+    refs[-1][:, HALF:] = ct_ref[...]
+
+
+def hand(me, q, ct, after):
     def half(i, me):
         return (0, i * 2 + 1 - me[2])
 
@@ -336,17 +335,17 @@
         grid_spec=pltpu.PrefetchScalarGridSpec(
             num_scalar_prefetch=1,
             grid=(2,),
-            in_specs=[part, part, pl.BlockSpec((TOK, 2 * HALF), lambda i, me: (0, i))]
-            + [pl.BlockSpec(memory_space=pl.ANY)] * len(after),
-            out_specs=pl.BlockSpec((TOK, 4 * HALF), lambda i, me: (0, i)),
+            in_specs=[part, part] + [pl.BlockSpec(memory_space=pl.ANY)] * len(after),
+            out_specs=pl.BlockSpec((TOK, 2 * HALF), lambda i, me: (0, i)),
         ),
-        out_shape=jax.ShapeDtypeStruct((TOK, 4096), BF),
-        compiler_params=pltpu.CompilerParams(vmem_limit_bytes=24 * MIB),
-    )(me, q, ct, x, *after)
+        out_shape=jax.ShapeDtypeStruct((TOK, 2048), BF),
+        compiler_params=pltpu.CompilerParams(vmem_limit_bytes=57 * MIB),
+    )(me, q, ct, *after)
 
 
 def turn_kernel(a_ref, b_ref, *refs):
-    x_ref, xt_ref = refs[-2:]
+    x_ref, xt_ref, mark = refs[-3:]
+    mark[...] = jnp.zeros_like(mark)
     for n, ref in enumerate((a_ref, b_ref)):
         value = ref[...]
         x_ref[n * TOK : (n + 1) * TOK, :] = value
@@ -358,16 +357,19 @@
     return pl.pallas_call(
         turn_kernel,
         grid=(D // 512,),
-        in_specs=[part, pl.BlockSpec((TOK, 512), lambda i: (0, i + 2 + 2 * (i // 2)))]
+        in_specs=[part, part]
         + [pl.BlockSpec(memory_space=pl.ANY)] * len(after),
-        out_specs=[pl.BlockSpec((PAIR, 512), lambda i: (0, i)), pl.BlockSpec((512, PAIR), lambda i: (i, 0))],
-        out_shape=[jax.ShapeDtypeStruct((PAIR, D), BF), jax.ShapeDtypeStruct((D, PAIR), BF)],
-        compiler_params=pltpu.CompilerParams(vmem_limit_bytes=16 * MIB),
+        out_specs=[pl.BlockSpec((PAIR, 512), lambda i: (0, i)), pl.BlockSpec((512, PAIR), lambda i: (i, 0)),
+                   pl.BlockSpec((8, 128), lambda i: (0, 0))],
+        out_shape=[jax.ShapeDtypeStruct((PAIR, D), BF), jax.ShapeDtypeStruct((D, PAIR), BF),
+                   jax.ShapeDtypeStruct((8, 128), jnp.float32)],
+        compiler_params=pltpu.CompilerParams(vmem_limit_bytes=57 * MIB),
     )(a, b, *after)
 
 
 def finish_kernel(info, *refs):
-    ins, outs = refs[:6], refs[6:]
+    ins, outs, mark = refs[:6], refs[6:8], refs[8]
+    mark[...] = jnp.zeros_like(mark)
     win = pl.multiple_of(info[0], 16)
     core, start, length = info[1], info[2] - info[0], info[3]
     rows = pl.ds(win, WIN)
@@ -393,10 +395,10 @@
             num_scalar_prefetch=1,
             grid=(2,),
             in_specs=[source(TOK, HALF)] * 2 + [source(WIN, HEAD_DIM)] * 4,
-            out_specs=[out, out],
+            out_specs=[out, out, pl.BlockSpec((8, 128), lambda i, e: (0, 0))],
         ),
-        out_shape=[jax.ShapeDtypeStruct((TOK, 2048), BF)] * 2,
-        compiler_params=pltpu.CompilerParams(vmem_limit_bytes=32 * MIB),
+        out_shape=[jax.ShapeDtypeStruct((TOK, 2048), BF)] * 2 + [jax.ShapeDtypeStruct((8, 128), jnp.float32)],
+        compiler_params=pltpu.CompilerParams(vmem_limit_bytes=59 * MIB),
     )(info, *pieces)
 
 
@@ -445,7 +447,8 @@
     )(*parts, *after)
 
 
-def pick_kernel(me, w_ref, got_ref, after, out_ref):
+def pick_kernel(me, w_ref, got_ref, *refs):
+    out_ref = refs[-1]
     mine = w_ref[:, pl.ds(pl.multiple_of(me[2] * HALF, HALF), HALF)]
     for core in range(2):
 
@@ -459,11 +462,12 @@
     whole = pl.BlockSpec(memory_space=pltpu.VMEM)
     return pl.pallas_call(
         pick_kernel,
-        in_specs=[pl.BlockSpec(memory_space=pltpu.SMEM), whole, whole, pl.BlockSpec(memory_space=pl.ANY)],
+        in_specs=[pl.BlockSpec(memory_space=pltpu.SMEM), whole, whole]
+        + [pl.BlockSpec(memory_space=pl.ANY)] * len(after),
         out_specs=whole,
         out_shape=jax.ShapeDtypeStruct((128, HALF), BF),
         compiler_params=pltpu.CompilerParams(vmem_limit_bytes=16 * MIB),
-    )(me, weights, got, after)
+    )(me, weights, got, *after)
 
 
 def ring(value, phase, amount):
@@ -501,21 +505,22 @@
 def body(enc_hidden, kv_weights, queries, cotangent, enc_lengths, dec_lengths, dec_partner):
     z, y, c, x = (lax.axis_index(a) for a in ALL)
     me = jnp.stack([z, y, c, x]).astype(jnp.int32)
+    swapped = swap(enc_hidden)
     meta, info, leave_a, leave_b = depart(me, enc_lengths, dec_lengths, dec_partner, queries, cotangent)
     sent_a = lax.ppermute(leave_a, DP, SEND_A)
     sent_b = lax.ppermute(leave_b, DP, SEND_B)
 
     got = swap(jnp.where(c == 0, kv_weights[:, HALF:], kv_weights[:, :HALF]))
-    own = pick(me, kv_weights, got, leave_a)
+    own = pick(me, kv_weights, got, [info, swapped])
     first = [own] + [ring(own, 2, n) for n in (1, 2, 3)]
     part = join(first, [sent_a, sent_b])
-    given = swap(hand(me, queries, cotangent, enc_hidden, [part]))
+    given = swap(hand(me, queries, cotangent, [part]))
     part = join([part] + [ring(part, 1, n) for n in (1, 2, 3)], [])
-    tokens, tokens_t = turn(enc_hidden, given, [part])
+    tokens, tokens_t, turned = turn(enc_hidden, swapped, [part])
     ahead, behind = ring(part, 0, 1), ring(part, 0, -1)
     weights = [[part, ahead, behind, ring(behind[:2], 0, -1), ring(ahead[2:], 0, 1)]]
-    part = join(first, [tokens_t], slice(HEAD_DIM, HALF))
-    part = join([part] + [ring(part, 1, n) for n in (1, 2, 3)], weights[0][3:])
+    part = join(first, [turned], slice(HEAD_DIM, HALF))
+    part = join([part] + [ring(part, 1, n) for n in (1, 2, 3)], [ahead, behind])
     weights.append([part, ring(part, 0, 1), ring(part, 0, -1), ring(part, 0, 2)])
 
     shared = (meta, me, tokens, tokens_t)
@@ -529,12 +534,12 @@
     mine, other = results[:2]
     late = [lax.ppermute(part, DP, pairs) for part, pairs in zip(results[2:], home)]
 
-    first = add_parts(parts, [mine, *returned])
+    first = add_parts(parts, [far_a, *returned])
     parts = scatter_ring(d0, d1, d3, far_a, far_b, first[0])
     first = exchange(first, 1)
-    second = exchange(add_parts(parts, late), 1)
-    context, grad_queries = finish(info, [mine, swap(other), *returned, *late])
-    kept, given = add_last(me, exchange(add_both(first, second), 2), [context])
+    second = exchange(add_parts(parts, first[1:]), 1)
+    context, grad_queries, finished = finish(info, [mine, swap(other), *returned, *late])
+    kept, given = add_last(me, exchange(add_both(first, second, late), 2), [finished])
     got = swap(given)
     grad = jnp.concatenate([jnp.where(c == 0, kept, got), jnp.where(c == 0, got, kept)], axis=1)
     return context, grad_queries, grad

time: 203 us -> 202 us (level)
  Pallas kernels: 55.6 us -> 63 us
  local copies, waits for them, and re-layouts: 12.4 us -> 6.25 us
  waiting for transfers between devices: 64.7 us -> 62.2 us
    ppermute x16, waiting for transfers between devices: 34.9 us -> 22 us  [ring(): return lax.ppermute(value, ALL, shift(phase, -amount))]
    ppermute x1, waiting for transfers between devices: 0.01 us -> 7.05 us  [body(): sent_b = lax.ppermute(leave_b, DP, SEND_B)]
    ppermute x12, waiting for transfers between devices: 15.7 us -> 22.7 us  [exchange(): lax.ppermute(parts[r], ALL, shift(phase, r))]
    unnamed x32 -> x50, local copies, waits for them, and re-layouts: 12.4 us -> 6.17 us
    ppermute x1, waiting for transfers between devices: 4.41 us -> 0.01 us  [scatter_ring(): lax.ppermute(ahead, ALL, shift(0, 1))]
    pallas_call x2, Pallas kernels: 2.46 us -> 6.43 us  [the longest x1 6.18 us: turn(): pl.pallas_call(turn_kernel, grid=(D // 512,), in_specs=[part, part] + [pl...]
    ppermute x16, starting transfers between devices: 21.2 us -> 24.5 us  [ring(): return lax.ppermute(value, ALL, shift(phase, -amount))]
    ppermute x4 -> x5, starting transfers between devices: 5.44 us -> 8.65 us  [swap(): return lax.ppermute(value, 'c', [(0, 1), (1, 0)])]
  transfers between devices with their start and end apart: 42 -> 43, of which waited for: 17 -> 17; matrix products, arithmetic and copies ran while one was open for 0% -> 1% of each run, Pallas kernels for 25% -> 29%
where the time goes in v10:
time: 202 us; the launch traced here: 201 us
  starting transfers between devices  66.5 us (33%)
  Pallas kernels  63 us (31%)
  waiting for transfers between devices  62.2 us (31%)
  local copies, waits for them, and re-layouts  6.25 us (3%)
  other arithmetic  2.2 us (1%)
    pallas_call x2, Pallas kernels, run_main(): pl.pallas_call(functools.partial(main_kernel, len(weights), len(before)),...  41.6 us
    ppermute x16, starting transfers between devices, ring(): return lax.ppermute(value, ALL, shift(phase, -amount))  24.5 us
    ppermute x12, waiting for transfers between devices, exchange(): lax.ppermute(parts[r], ALL, shift(phase, r))  22.7 us
    ppermute x16, waiting for transfers between devices, ring(): return lax.ppermute(value, ALL, shift(phase, -amount))  22 us
    ppermute x12, starting transfers between devices, exchange(): lax.ppermute(parts[r], ALL, shift(phase, r))  12.3 us
    ppermute x4, starting transfers between devices, body(): lax.ppermute(part, DP, pairs)  11.1 us
    ppermute x5, starting transfers between devices, swap(): return lax.ppermute(value, 'c', [(0, 1), (1, 0)])  8.65 us
    ppermute x1, waiting for transfers between devices, body(): sent_b = lax.ppermute(leave_b, DP, SEND_B)  7.05 us
  transfers between devices with their start and end apart: 43, of which 17 were waited for; matrix products, arithmetic and copies ran while one was open for 1% of the time, Pallas kernels for 29%

profile of v10, /device:TPU:1, one launch (start us, length us, event | category | flops | bytes accessed | tf_op | source)
XLA Modules:
  0.0 201.4 jit_solution(14166819660137885986)
XLA Ops:
  2.7 3.5 %shard_map.94 = (s32[8,4]{1,0:T(8,128)}, s32[4]{0:T(128)}, bf16[176,2048]{1,0:T(8,128)(2,1)}, bf16[176,2048]{1,0:T(8,128)(2,1)}) custom-call(s32[4]{0:T(128)} %pad_add_fusion.me, s32[4,128]{1,0:T(4,128)} %bitcast.7, s32[4,128]{1,0:T(4,128)} %bitcast.8, s32[4,128]{1,0:T(4,128)} %bitcast.9, bf16[512,2048]{1,0:T(8,128)(2,1)} %refs_4_.1, bf16[512,2048]{1,0:T(8,128)(2,1)} %refs_8_.1), custom_call_target="tpu_custom_call" | custom-call | tf_op jit(solution)/shard_map/pallas_call | solution.py:312
  6.3 3.3 %collective-permute-start.5 = (bf16[176,2048]{1,0:T(8,128)(2,1)}, bf16[176,2048]{1,0:T(8,128)(2,1)S(1)}, u32[]{:S(2)}, u32[]{:S(2)}) collective-permute-start(bf16[176,2048]{1,0:T(8,128)(2,1)} %get-tuple-element.48), channel_id=1, source_target_pairs={{8,0},{16,8},{24,16},{32,24},{40,32},{48,40},{56,48},{64,56},{72,6... | collective-permute-start | bytes 2162696 | tf_op jit(solution)/shard_map/ppermute | solution.py:510
  17.7 4.7 %collective-permute-start.3 = (bf16[128,512]{1,0:T(8,128)(2,1)S(1)}, bf16[128,512]{1,0:T(8,128)(2,1)S(1)}, u32[]{:S(2)}, u32[]{:S(2)}) collective-permute-start(bf16[128,512]{1,0:T(8,128)(2,1)S(1)} %shard_map.95.refs_0_), channel_id=1, source_target_pairs={{0,64},{1,65},{2,66},{3,67},{4,20},{5,21},{6,22},{7,23},{8,72},{9,... | collective-permute-start | bytes 393224 | tf_op jit(solution)/shard_map/ppermute | solution.py:474
  22.5 7.1 %collective-permute-done.6.refs_5_.refs_8_.refs_12_.refs_7_.refs_11_ = bf16[176,2048]{1,0:T(8,128)(2,1)S(1)} collective-permute-done((bf16[176,2048]{1,0:T(8,128)(2,1)}, bf16[176,2048]{1,0:T(8,128)(2,1)S(1)}, u32[]{:S(2)}, u32[]{:S(2)}) %collective-permute-start.6) | collective-permute-done | bytes 720928 | tf_op jit(solution)/shard_map/ppermute | solution.py:511
  29.5 2.2 %collective-permute-done.4.refs_3_ = bf16[128,512]{1,0:T(8,128)(2,1)S(1)} collective-permute-done((bf16[128,512]{1,0:T(8,128)(2,1)S(1)}, bf16[128,512]{1,0:T(8,128)(2,1)S(1)}, u32[]{:S(2)}, u32[]{:S(2)}) %collective-permute-start.4) | collective-permute-done | bytes 131104 | tf_op jit(solution)/shard_map/ppermute | solution.py:474
  32.6 3.3 %shard_map.101 = bf16[512,2048]{1,0:T(8,128)(2,1)} custom-call(s32[4]{0:T(128)} %pad_add_fusion.me, bf16[512,2048]{1,0:T(8,128)(2,1)} %refs_4_.1, bf16[512,2048]{1,0:T(8,128)(2,1)} %refs_8_.1, bf16[4,128,256]{2,1,0:T(8,128)(2,1)} %copy-done.4), custom_call_target="tpu_custom_call" | custom-call | tf_op jit(solution)/shard_map/pallas_call | solution.py:333
  35.8 3.7 %collective-permute-start.18 = (bf16[512,2048]{1,0:T(8,128)(2,1)}, bf16[512,2048]{1,0:T(8,128)(2,1)}, u32[]{:S(2)}, u32[]{:S(2)}) collective-permute-start(bf16[512,2048]{1,0:T(8,128)(2,1)} %shard_map.101), channel_id=1, source_target_pairs={{0,4},{4,0},{1,5},{5,1},{2,6},{6,2},{3,7},{7,3},{8,12},{12,8},{9,1... | collective-permute-start | bytes 6291464 | tf_op jit(solution)/shard_map/ppermute | solution.py:406
  40.8 2.5 %collective-permute-start.8 = (bf16[4,128,256]{2,1,0:T(8,128)(2,1)}, bf16[4,128,256]{2,1,0:T(8,128)(2,1)S(1)}, u32[]{:S(2)}, u32[]{:S(2)}) collective-permute-start(bf16[4,128,256]{2,1,0:T(8,128)(2,1)} %copy-done.4), channel_id=1, source_target_pairs={{0,16},{1,17},{2,18},{3,19},{4,6},{5,7},{6,4},{7,5},{8,24},{9,25},... | collective-permute-start | bytes 786440 | tf_op jit(solution)/shard_map/ppermute | solution.py:474
  46.5 3.5 %collective-permute-done.8.refs_2_ = bf16[4,128,256]{2,1,0:T(8,128)(2,1)S(1)} collective-permute-done((bf16[4,128,256]{2,1,0:T(8,128)(2,1)}, bf16[4,128,256]{2,1,0:T(8,128)(2,1)S(1)}, u32[]{:S(2)}, u32[]{:S(2)}) %collective-permute-start.8) | collective-permute-done | bytes 262176 | tf_op jit(solution)/shard_map/ppermute | solution.py:474
  51.1 2.7 %collective-permute-start.13 = (bf16[4,4,128,256]{3,2,1,0:T(8,128)(2,1)S(1)}, bf16[4,4,128,256]{3,2,1,0:T(8,128)(2,1)S(1)}, u32[]{:S(2)}, u32[]{:S(2)}) collective-permute-start(bf16[4,4,128,256]{3,2,1,0:T(8,128)(2,1)S(1)} %shard_map.97.refs_0_), channel_id=1, source_target_pairs={{0,3},{1,0},{2,1},{3,2},{4,100},{5,101},{6,102},{7,103},{8,11},{9,... | collective-permute-start | bytes 3145736 | tf_op jit(solution)/shard_map/ppermute | solution.py:474
  53.8 6.2 %shard_map.98 = (bf16[1024,2048]{1,0:T(8,128)(2,1)}, bf16[2048,1024]{1,0:T(8,128)(2,1)}, f32[8,128]{1,0:T(8,128)}) custom-call(bf16[512,2048]{1,0:T(8,128)(2,1)} %a_ref.1, bf16[512,2048]{1,0:T(8,128)(2,1)} %copy-done, bf16[4,4,128,256]{3,2,1,0:T(8,128)(2,1)} %copy-done.1), custom_call_target="tpu_custom_call" | custom-call | tf_op jit(solution)/shard_map/pallas_call | solution.py:357
  62.1 4.1 %collective-permute-done.14.refs_5_.refs_2_ = bf16[4,4,128,256]{3,2,1,0:T(8,128)(2,1)S(1)} collective-permute-done((bf16[4,4,128,256]{3,2,1,0:T(8,128)(2,1)S(1)}, bf16[4,4,128,256]{3,2,1,0:T(8,128)(2,1)S(1)}, u32[]{:S(2)}, u32[]{:S(2)}) %collective-permute-start.14) | collective-permute-done | bytes 1048608 | tf_op jit(solution)/shard_map/ppermute | solution.py:474
  66.5 2.7 %collective-permute-start.20 = (bf16[2,4,128,256]{3,2,1,0:T(8,128)(2,1)S(1)}, bf16[2,4,128,256]{3,2,1,0:T(8,128)(2,1)S(1)}, u32[]{:S(2)}, u32[]{:S(2)}) collective-permute-start(bf16[2,4,128,256]{3,2,1,0:T(8,128)(2,1)S(1)} %slice.17), channel_id=1, source_target_pairs={{0,3},{1,0},{2,1},{3,2},{4,100},{5,101},{6,102},{7,103},{8,11},{9,... | collective-permute-start | bytes 1572872 | tf_op jit(solution)/shard_map/ppermute | solution.py:474
  69.2 2.7 %collective-permute-start.11 = (bf16[4,128,256]{2,1,0:T(8,128)(2,1)S(1)}, bf16[4,128,256]{2,1,0:T(8,128)(2,1)S(1)}, u32[]{:S(2)}, u32[]{:S(2)}) collective-permute-start(bf16[4,128,256]{2,1,0:T(8,128)(2,1)S(1)} %shard_map.99.refs_0_), channel_id=1, source_target_pairs={{0,16},{1,17},{2,18},{3,19},{4,6},{5,7},{6,4},{7,5},{8,24},{9,25},... | collective-permute-start | bytes 786440 | tf_op jit(solution)/shard_map/ppermute | solution.py:474
  73.0 5.0 %collective-permute-done.11.refs_2_ = bf16[4,128,256]{2,1,0:T(8,128)(2,1)S(1)} collective-permute-done((bf16[4,128,256]{2,1,0:T(8,128)(2,1)S(1)}, bf16[4,128,256]{2,1,0:T(8,128)(2,1)S(1)}, u32[]{:S(2)}, u32[]{:S(2)}) %collective-permute-start.11) | collective-permute-done | bytes 262176 | tf_op jit(solution)/shard_map/ppermute | solution.py:474
  78.0 5.0 %collective-permute-done.10.refs_1_ = bf16[4,128,256]{2,1,0:T(8,128)(2,1)S(1)} collective-permute-done((bf16[4,128,256]{2,1,0:T(8,128)(2,1)S(1)}, bf16[4,128,256]{2,1,0:T(8,128)(2,1)S(1)}, u32[]{:S(2)}, u32[]{:S(2)}) %collective-permute-start.10) | collective-permute-done | bytes 262176 | tf_op jit(solution)/shard_map/ppermute | solution.py:474
  83.6 2.4 %collective-permute-start.15 = (bf16[4,4,128,256]{3,2,1,0:T(8,128)(2,1)S(1)}, bf16[4,4,128,256]{3,2,1,0:T(8,128)(2,1)S(1)}, u32[]{:S(2)}, u32[]{:S(2)}) collective-permute-start(bf16[4,4,128,256]{3,2,1,0:T(8,128)(2,1)S(1)} %shard_map.100.refs_0_), channel_id=1, source_target_pairs={{0,3},{1,0},{2,1},{3,2},{4,100},{5,101},{6,102},{7,103},{8,11},{9,... | collective-permute-start | bytes 3145736 | tf_op jit(solution)/shard_map/ppermute | solution.py:474
  85.9 20.8 %shard_map.102 = (bf16[2,512,1024]{2,1,0:T(8,128)(2,1)}, bf16[2,512,1024]{2,1,0:T(8,128)(2,1)}, bf16[2,176,512]{2,1,0:T(8,128)(2,1)S(1)}, bf16[2,176,512]{2,1,0:...) custom-call(s32[8,4]{1,0:T(8,128)S(1)} %copy-done.22, ...), custom_call_target="tpu_custom_call" | custom-call | flops 12000000000 | bytes 24000000 | tf_op jit(solution)/shard_map/pallas_call | solution.py:167
  108.0 6.6 %collective-permute-start.23 = (bf16[2,176,512]{2,1,0:T(8,128)(2,1)S(1)}, bf16[2,176,512]{2,1,0:T(8,128)(2,1)S(1)}, u32[]{:S(2)}, u32[]{:S(2)}) collective-permute-start(bf16[2,176,512]{2,1,0:T(8,128)(2,1)S(1)} %get-tuple-element.58), channel_id=1, source_target_pairs={{4,8},{12,16},{20,24},{28,32},{36,40},{44,48},{52,56},{60,64},{68,... | collective-permute-start | bytes 1081352 | tf_op jit(solution)/shard_map/ppermute | solution.py:531
  114.7 2.7 %collective-permute-start.27 = (bf16[4,4,128,256]{3,2,1,0:T(8,128)(2,1)S(1)}, bf16[4,4,128,256]{3,2,1,0:T(8,128)(2,1)S(1)}, u32[]{:S(2)}, u32[]{:S(2)}) collective-permute-start(bf16[4,4,128,256]{3,2,1,0:T(8,128)(2,1)S(1)} %get-tuple-element.65), channel_id=1, source_target_pairs={{0,3},{1,0},{2,1},{3,2},{4,100},{5,101},{6,102},{7,103},{8,11},{9,... | collective-permute-start | bytes 3145736 | tf_op jit(solution)/shard_map/ppermute | solution.py:431
  117.9 20.8 %shard_map.103 = (bf16[2,512,1024]{2,1,0:T(8,128)(2,1)}, bf16[2,512,1024]{2,1,0:T(8,128)(2,1)}, bf16[2,176,512]{2,1,0:T(8,128)(2,1)S(1)}, bf16[2,176,512]{2,1,0:...) custom-call(s32[8,4]{1,0:T(8,128)S(1)} %copy-done.22, ...), custom_call_target="tpu_custom_call", output_to_operand_aliasing={{0}: (16, {}), {1}: (17, {})} | custom-call | flops 12000000000 | bytes 24000000 | tf_op jit(solution)/shard_map/pallas_call | solution.py:167
  140.7 6.9 %collective-permute-done.28.refs_3_ = bf16[4,4,128,256]{3,2,1,0:T(8,128)(2,1)S(1)} collective-permute-done((bf16[4,4,128,256]{3,2,1,0:T(8,128)(2,1)S(1)}, bf16[4,4,128,256]{3,2,1,0:T(8,128)(2,1)S(1)}, u32[]{:S(2)}, u32[]{:S(2)}) %collective-permute-start.28) | collective-permute-done | bytes 1048608 | tf_op jit(solution)/shard_map/ppermute | solution.py:431
  148.6 4.6 %collective-permute-done.32.got_a = bf16[2,4,128,256]{3,2,1,0:T(8,128)(2,1)S(1)} collective-permute-done((bf16[2,4,128,256]{3,2,1,0:T(8,128)(2,1)S(1)}, bf16[2,4,128,256]{3,2,1,0:T(8,128)(2,1)S(1)}, u32[]{:S(2)}, u32[]{:S(2)}) %collective-permute-start.32) | collective-permute-done | bytes 524320 | tf_op jit(solution)/shard_map/ppermute | solution.py:499
  153.5 2.7 %collective-permute-start.35 = (bf16[4,4,128,256]{3,2,1,0:T(8,128)(2,1)S(1)}, bf16[4,4,128,256]{3,2,1,0:T(8,128)(2,1)S(1)}, u32[]{:S(2)}, u32[]{:S(2)}) collective-permute-start(bf16[4,4,128,256]{3,2,1,0:T(8,128)(2,1)S(1)} %get-tuple-element.77), channel_id=1, source_target_pairs={{0,3},{1,0},{2,1},{3,2},{4,100},{5,101},{6,102},{7,103},{8,11},{9,... | collective-permute-start | bytes 3145736 | tf_op jit(solution)/shard_map/ppermute | solution.py:502
  156.2 2.7 %collective-permute-start.30 = (bf16[4,128,256]{2,1,0:T(8,128)(2,1)S(1)}, bf16[4,128,256]{2,1,0:T(8,128)(2,1)S(1)}, u32[]{:S(2)}, u32[]{:S(2)}) collective-permute-start(bf16[4,128,256]{2,1,0:T(8,128)(2,1)S(1)} %get-tuple-element.70), channel_id=1, source_target_pairs={{0,24},{1,25},{2,26},{3,27},{4,7},{5,4},{6,5},{7,6},{8,0},{9,1},{1... | collective-permute-start | bytes 786440 | tf_op jit(solution)/shard_map/ppermute | solution.py:431
  158.9 6.9 %collective-permute-done.29.refs_3_.refs_1_ = bf16[4,128,256]{2,1,0:T(8,128)(2,1)S(1)} collective-permute-done((bf16[4,128,256]{2,1,0:T(8,128)(2,1)S(1)}, bf16[4,128,256]{2,1,0:T(8,128)(2,1)S(1)}, u32[]{:S(2)}, u32[]{:S(2)}) %collective-permute-start.29) | collective-permute-done | bytes 262176 | tf_op jit(solution)/shard_map/ppermute | solution.py:431
  167.1 5.4 %collective-permute-done.31.refs_5_.refs_3_ = bf16[4,128,256]{2,1,0:T(8,128)(2,1)S(1)} collective-permute-done((bf16[4,128,256]{2,1,0:T(8,128)(2,1)S(1)}, bf16[4,128,256]{2,1,0:T(8,128)(2,1)S(1)}, u32[]{:S(2)}, u32[]{:S(2)}) %collective-permute-start.31) | collective-permute-done | bytes 262176 | tf_op jit(solution)/shard_map/ppermute | solution.py:431
  175.5 2.4 %collective-permute-start.37 = (bf16[4,128,256]{2,1,0:T(8,128)(2,1)S(1)}, bf16[4,128,256]{2,1,0:T(8,128)(2,1)S(1)}, u32[]{:S(2)}, u32[]{:S(2)}) collective-permute-start(bf16[4,128,256]{2,1,0:T(8,128)(2,1)S(1)} %get-tuple-element.80), channel_id=1, source_target_pairs={{0,24},{1,25},{2,26},{3,27},{4,7},{5,4},{6,5},{7,6},{8,0},{9,1},{1... | collective-permute-start | bytes 786440 | tf_op jit(solution)/shard_map/ppermute | solution.py:431
  177.9 3.6 %collective-permute-done.25.refs_5_.refs_9_ = bf16[2,176,512]{2,1,0:T(8,128)(2,1)S(1)} collective-permute-done((bf16[2,176,512]{2,1,0:T(8,128)(2,1)S(1)}, bf16[2,176,512]{2,1,0:T(8,128)(2,1)S(1)}, u32[]{:S(2)}, u32[]{:S(2)}) %collective-permute-start.25) | collective-permute-done | bytes 360480 | tf_op jit(solution)/shard_map/ppermute | solution.py:535
  185.3 2.7 %collective-permute-start.40 = (bf16[128,512]{1,0:T(8,128)(2,1)S(1)}, bf16[128,512]{1,0:T(8,128)(2,1)S(1)}, u32[]{:S(2)}, u32[]{:S(2)}) collective-permute-start(bf16[128,512]{1,0:T(8,128)(2,1)S(1)} %get-tuple-element.84), channel_id=1, source_target_pairs={{0,96},{1,97},{2,98},{3,99},{4,28},{5,29},{6,30},{7,31},{8,104},{9... | collective-permute-start | bytes 393224 | tf_op jit(solution)/shard_map/ppermute | solution.py:431
  190.1 5.0 %shard_map.104 = (bf16[512,2048]{1,0:T(8,128)(2,1)}, bf16[512,2048]{1,0:T(8,128)(2,1)}, f32[8,128]{1,0:T(8,128)}) custom-call(s32[4]{0:T(128)} %get-tuple-element.46.refs_0_.info, bf16[2,512,1024]{2,1,0:T(8,128)(2,1)} %get-tuple-element.55.refs_0_, bf16[2,512,1024]{2,1,0:T(8,128)(2,1)} %copy-done.23, bf16[2,176,512]{2,1,0:T(8,128)(2,1)} %copy-done.8, ...), custom_call_target="tpu_custom_call" | custom-call | tf_op jit(solution)/shard_map/pallas_call | solution.py:392
  196.4 3.3 %collective-permute-start.42 = (f32[64,512]{1,0:T(8,128)S(1)}, f32[64,512]{1,0:T(8,128)S(1)}, u32[]{:S(2)}, u32[]{:S(2)}) collective-permute-start(f32[64,512]{1,0:T(8,128)S(1)} %get-tuple-element.88), channel_id=1, source_target_pairs={{0,4},{4,0},{1,5},{5,1},{2,6},{6,2},{3,7},{7,3},{8,12},{12,8},{9,1... | collective-permute-start | bytes 393224 | tf_op jit(solution)/shard_map/ppermute | solution.py:406
  (126 shorter events, 38.7 us)
Async XLA Ops:
  0.6 13.3 %collective-permute-start = (bf16[512,2048]{1,0:T(8,128)(2,1)}, bf16[512,2048]{1,0:T(8,128)(2,1)S(1)}, u32[]{:S(2)}, u32[]{:S(2)}) collective-permute-start(bf16[512,2048]{1,0:T(8,128)(2,1)} %a_ref.1), channel_id=1, source_target_pairs={{0,4},{4,0},{1,5},{5,1},{2,6},{6,2},{3,7},{7,3},{8,12},{12,8},{9,1... | collective-permute-start | bytes 6291464 | tf_op jit(solution)/shard_map/ppermute | solution.py:406
  6.3 16.2 %collective-permute-start.5 = (bf16[176,2048]{1,0:T(8,128)(2,1)}, bf16[176,2048]{1,0:T(8,128)(2,1)S(1)}, u32[]{:S(2)}, u32[]{:S(2)}) collective-permute-start(bf16[176,2048]{1,0:T(8,128)(2,1)} %get-tuple-element.48), channel_id=1, source_target_pairs={{8,0},{16,8},{24,16},{32,24},{40,32},{48,40},{56,48},{64,56},{72,6... | collective-permute-start | bytes 2162696 | tf_op jit(solution)/shard_map/ppermute | solution.py:510
  9.6 19.9 %collective-permute-start.6 = (bf16[176,2048]{1,0:T(8,128)(2,1)}, bf16[176,2048]{1,0:T(8,128)(2,1)S(1)}, u32[]{:S(2)}, u32[]{:S(2)}) collective-permute-start(bf16[176,2048]{1,0:T(8,128)(2,1)} %get-tuple-element.49), channel_id=1, source_target_pairs={{8,4},{16,12},{24,20},{32,28},{40,36},{48,44},{56,52},{64,60},{72,... | collective-permute-start | bytes 2162696 | tf_op jit(solution)/shard_map/ppermute | solution.py:511
  16.3 15.4 %collective-permute-start.4 = (bf16[128,512]{1,0:T(8,128)(2,1)S(1)}, bf16[128,512]{1,0:T(8,128)(2,1)S(1)}, u32[]{:S(2)}, u32[]{:S(2)}) collective-permute-start(bf16[128,512]{1,0:T(8,128)(2,1)S(1)} %shard_map.95.refs_0_), channel_id=1, source_target_pairs={{0,32},{1,33},{2,34},{3,35},{4,12},{5,13},{6,14},{7,15},{8,40},{9,... | collective-permute-start | bytes 393224 | tf_op jit(solution)/shard_map/ppermute | solution.py:474
  17.7 14.0 %collective-permute-start.3 = (bf16[128,512]{1,0:T(8,128)(2,1)S(1)}, bf16[128,512]{1,0:T(8,128)(2,1)S(1)}, u32[]{:S(2)}, u32[]{:S(2)}) collective-permute-start(bf16[128,512]{1,0:T(8,128)(2,1)S(1)} %shard_map.95.refs_0_), channel_id=1, source_target_pairs={{0,64},{1,65},{2,66},{3,67},{4,20},{5,21},{6,22},{7,23},{8,72},{9,... | collective-permute-start | bytes 393224 | tf_op jit(solution)/shard_map/ppermute | solution.py:474
  22.5 9.3 %collective-permute-start.2 = (bf16[128,512]{1,0:T(8,128)(2,1)S(1)}, bf16[128,512]{1,0:T(8,128)(2,1)S(1)}, u32[]{:S(2)}, u32[]{:S(2)}) collective-permute-start(bf16[128,512]{1,0:T(8,128)(2,1)S(1)} %shard_map.95.refs_0_), channel_id=1, source_target_pairs={{0,96},{1,97},{2,98},{3,99},{4,28},{5,29},{6,30},{7,31},{8,104},{9... | collective-permute-start | bytes 393224 | tf_op jit(solution)/shard_map/ppermute | solution.py:474
  35.8 50.1 %collective-permute-start.18 = (bf16[512,2048]{1,0:T(8,128)(2,1)}, bf16[512,2048]{1,0:T(8,128)(2,1)}, u32[]{:S(2)}, u32[]{:S(2)}) collective-permute-start(bf16[512,2048]{1,0:T(8,128)(2,1)} %shard_map.101), channel_id=1, source_target_pairs={{0,4},{4,0},{1,5},{5,1},{2,6},{6,2},{3,7},{7,3},{8,12},{12,8},{9,1... | collective-permute-start | bytes 6291464 | tf_op jit(solution)/shard_map/ppermute | solution.py:406
  40.8 9.2 %collective-permute-start.8 = (bf16[4,128,256]{2,1,0:T(8,128)(2,1)}, bf16[4,128,256]{2,1,0:T(8,128)(2,1)S(1)}, u32[]{:S(2)}, u32[]{:S(2)}) collective-permute-start(bf16[4,128,256]{2,1,0:T(8,128)(2,1)} %copy-done.4), channel_id=1, source_target_pairs={{0,16},{1,17},{2,18},{3,19},{4,6},{5,7},{6,4},{7,5},{8,24},{9,25},... | collective-permute-start | bytes 786440 | tf_op jit(solution)/shard_map/ppermute | solution.py:474
  51.1 15.2 %collective-permute-start.14 = (bf16[4,4,128,256]{3,2,1,0:T(8,128)(2,1)S(1)}, bf16[4,4,128,256]{3,2,1,0:T(8,128)(2,1)S(1)}, u32[]{:S(2)}, u32[]{:S(2)}) collective-permute-start(bf16[4,4,128,256]{3,2,1,0:T(8,128)(2,1)S(1)} %shard_map.97.refs_0_), channel_id=1, source_target_pairs={{0,1},{1,2},{2,3},{3,0},{4,36},{5,37},{6,38},{7,39},{8,9},{9,10},{... | collective-permute-start | bytes 3145736 | tf_op jit(solution)/shard_map/ppermute | solution.py:474
  51.1 15.3 %collective-permute-start.13 = (bf16[4,4,128,256]{3,2,1,0:T(8,128)(2,1)S(1)}, bf16[4,4,128,256]{3,2,1,0:T(8,128)(2,1)S(1)}, u32[]{:S(2)}, u32[]{:S(2)}) collective-permute-start(bf16[4,4,128,256]{3,2,1,0:T(8,128)(2,1)S(1)} %shard_map.97.refs_0_), channel_id=1, source_target_pairs={{0,3},{1,0},{2,1},{3,2},{4,100},{5,101},{6,102},{7,103},{8,11},{9,... | collective-permute-start | bytes 3145736 | tf_op jit(solution)/shard_map/ppermute | solution.py:474
  60.7 11.2 %collective-permute-start.12 = (bf16[4,128,256]{2,1,0:T(8,128)(2,1)S(1)}, bf16[4,128,256]{2,1,0:T(8,128)(2,1)S(1)}, u32[]{:S(2)}, u32[]{:S(2)}) collective-permute-start(bf16[4,128,256]{2,1,0:T(8,128)(2,1)S(1)} %shard_map.99.refs_0_), channel_id=1, source_target_pairs={{0,8},{1,9},{2,10},{3,11},{4,5},{5,6},{6,7},{7,4},{8,16},{9,17},{1... | collective-permute-start | bytes 786440 | tf_op jit(solution)/shard_map/ppermute | solution.py:474
  66.3 17.2 %collective-permute-start.19 = (bf16[2,4,128,256]{3,2,1,0:T(8,128)(2,1)S(1)}, bf16[2,4,128,256]{3,2,1,0:T(8,128)(2,1)S(1)}, u32[]{:S(2)}, u32[]{:S(2)}) collective-permute-start(bf16[2,4,128,256]{3,2,1,0:T(8,128)(2,1)S(1)} %slice.16), channel_id=1, source_target_pairs={{0,1},{1,2},{2,3},{3,0},{4,36},{5,37},{6,38},{7,39},{8,9},{9,10},{... | collective-permute-start | bytes 1572872 | tf_op jit(solution)/shard_map/ppermute | solution.py:474
  66.5 19.4 %collective-permute-start.20 = (bf16[2,4,128,256]{3,2,1,0:T(8,128)(2,1)S(1)}, bf16[2,4,128,256]{3,2,1,0:T(8,128)(2,1)S(1)}, u32[]{:S(2)}, u32[]{:S(2)}) collective-permute-start(bf16[2,4,128,256]{3,2,1,0:T(8,128)(2,1)S(1)} %slice.17), channel_id=1, source_target_pairs={{0,3},{1,0},{2,1},{3,2},{4,100},{5,101},{6,102},{7,103},{8,11},{9,... | collective-permute-start | bytes 1572872 | tf_op jit(solution)/shard_map/ppermute | solution.py:474
  71.9 11.1 %collective-permute-start.10 = (bf16[4,128,256]{2,1,0:T(8,128)(2,1)S(1)}, bf16[4,128,256]{2,1,0:T(8,128)(2,1)S(1)}, u32[]{:S(2)}, u32[]{:S(2)}) collective-permute-start(bf16[4,128,256]{2,1,0:T(8,128)(2,1)S(1)} %shard_map.99.refs_0_), channel_id=1, source_target_pairs={{0,24},{1,25},{2,26},{3,27},{4,7},{5,4},{6,5},{7,6},{8,0},{9,1},{1... | collective-permute-start | bytes 786440 | tf_op jit(solution)/shard_map/ppermute | solution.py:474
  83.1 31.5 %collective-permute-start.17 = (bf16[4,4,128,256]{3,2,1,0:T(8,128)(2,1)S(1)}, bf16[4,4,128,256]{3,2,1,0:T(8,128)(2,1)S(1)}, u32[]{:S(2)}, u32[]{:S(2)}) collective-permute-start(bf16[4,4,128,256]{3,2,1,0:T(8,128)(2,1)S(1)} %shard_map.100.refs_0_), channel_id=1, source_target_pairs={{0,2},{1,3},{2,0},{3,1},{4,68},{5,69},{6,70},{7,71},{8,10},{9,11},... | collective-permute-start | bytes 3145736 | tf_op jit(solution)/shard_map/ppermute | solution.py:474
  83.2 31.5 %collective-permute-start.16 = (bf16[4,4,128,256]{3,2,1,0:T(8,128)(2,1)S(1)}, bf16[4,4,128,256]{3,2,1,0:T(8,128)(2,1)S(1)}, u32[]{:S(2)}, u32[]{:S(2)}) collective-permute-start(bf16[4,4,128,256]{3,2,1,0:T(8,128)(2,1)S(1)} %shard_map.100.refs_0_), channel_id=1, source_target_pairs={{0,1},{1,2},{2,3},{3,0},{4,36},{5,37},{6,38},{7,39},{8,9},{9,10},{... | collective-permute-start | bytes 3145736 | tf_op jit(solution)/shard_map/ppermute | solution.py:474
  83.6 33.8 %collective-permute-start.15 = (bf16[4,4,128,256]{3,2,1,0:T(8,128)(2,1)S(1)}, bf16[4,4,128,256]{3,2,1,0:T(8,128)(2,1)S(1)}, u32[]{:S(2)}, u32[]{:S(2)}) collective-permute-start(bf16[4,4,128,256]{3,2,1,0:T(8,128)(2,1)S(1)} %shard_map.100.refs_0_), channel_id=1, source_target_pairs={{0,3},{1,0},{2,1},{3,2},{4,100},{5,101},{6,102},{7,103},{8,11},{9,... | collective-permute-start | bytes 3145736 | tf_op jit(solution)/shard_map/ppermute | solution.py:474
  106.7 32.1 %collective-permute-start.22 = (bf16[2,176,512]{2,1,0:T(8,128)(2,1)S(1)}, bf16[2,176,512]{2,1,0:T(8,128)(2,1)S(1)}, u32[]{:S(2)}, u32[]{:S(2)}) collective-permute-start(bf16[2,176,512]{2,1,0:T(8,128)(2,1)S(1)} %get-tuple-element.57), channel_id=1, source_target_pairs={{0,8},{8,16},{16,24},{24,32},{32,40},{40,48},{48,56},{56,64},{64,7... | collective-permute-start | bytes 1081352 | tf_op jit(solution)/shard_map/ppermute | solution.py:531
  108.0 30.9 %collective-permute-start.23 = (bf16[2,176,512]{2,1,0:T(8,128)(2,1)S(1)}, bf16[2,176,512]{2,1,0:T(8,128)(2,1)S(1)}, u32[]{:S(2)}, u32[]{:S(2)}) collective-permute-start(bf16[2,176,512]{2,1,0:T(8,128)(2,1)S(1)} %get-tuple-element.58), channel_id=1, source_target_pairs={{4,8},{12,16},{20,24},{28,32},{36,40},{44,48},{52,56},{60,64},{68,... | collective-permute-start | bytes 1081352 | tf_op jit(solution)/shard_map/ppermute | solution.py:531
  114.6 26.1 %collective-permute-start.26 = (bf16[4,4,128,256]{3,2,1,0:T(8,128)(2,1)S(1)}, bf16[4,4,128,256]{3,2,1,0:T(8,128)(2,1)S(1)}, u32[]{:S(2)}, u32[]{:S(2)}) collective-permute-start(bf16[4,4,128,256]{3,2,1,0:T(8,128)(2,1)S(1)} %get-tuple-element.64), channel_id=1, source_target_pairs={{0,1},{1,2},{2,3},{3,0},{4,36},{5,37},{6,38},{7,39},{8,9},{9,10},{... | collective-permute-start | bytes 3145736 | tf_op jit(solution)/shard_map/ppermute | solution.py:431
  114.7 26.0 %collective-permute-start.27 = (bf16[4,4,128,256]{3,2,1,0:T(8,128)(2,1)S(1)}, bf16[4,4,128,256]{3,2,1,0:T(8,128)(2,1)S(1)}, u32[]{:S(2)}, u32[]{:S(2)}) collective-permute-start(bf16[4,4,128,256]{3,2,1,0:T(8,128)(2,1)S(1)} %get-tuple-element.65), channel_id=1, source_target_pairs={{0,3},{1,0},{2,1},{3,2},{4,100},{5,101},{6,102},{7,103},{8,11},{9,... | collective-permute-start | bytes 3145736 | tf_op jit(solution)/shard_map/ppermute | solution.py:431
  117.4 30.3 %collective-permute-start.28 = (bf16[4,4,128,256]{3,2,1,0:T(8,128)(2,1)S(1)}, bf16[4,4,128,256]{3,2,1,0:T(8,128)(2,1)S(1)}, u32[]{:S(2)}, u32[]{:S(2)}) collective-permute-start(bf16[4,4,128,256]{3,2,1,0:T(8,128)(2,1)S(1)} %get-tuple-element.66), channel_id=1, source_target_pairs={{0,2},{1,3},{2,0},{3,1},{4,68},{5,69},{6,70},{7,71},{8,10},{9,11},... | collective-permute-start | bytes 3145736 | tf_op jit(solution)/shard_map/ppermute | solution.py:431
  138.8 50.0 %collective-permute-start.21 = (bf16[2,512,1024]{2,1,0:T(8,128)(2,1)}, bf16[2,512,1024]{2,1,0:T(8,128)(2,1)S(1)}, u32[]{:S(2)}, u32[]{:S(2)}) collective-permute-start(bf16[2,512,1024]{2,1,0:T(8,128)(2,1)} %get-tuple-element.56), channel_id=1, source_target_pairs={{0,4},{4,0},{1,5},{5,1},{2,6},{6,2},{3,7},{7,3},{8,12},{12,8},{9,1... | collective-permute-start | bytes 6291464 | tf_op jit(solution)/shard_map/ppermute | solution.py:406
  138.9 9.6 %collective-permute-start.33 = (bf16[2,4,128,256]{3,2,1,0:T(8,128)(2,1)S(1)}, bf16[2,4,128,256]{3,2,1,0:T(8,128)(2,1)S(1)}, u32[]{:S(2)}, u32[]{:S(2)}) collective-permute-start(bf16[2,4,128,256]{3,2,1,0:T(8,128)(2,1)S(1)} %get-tuple-element.75), channel_id=1, source_target_pairs={{0,3},{1,0},{2,1},{3,2},{4,100},{5,101},{6,102},{7,103},{8,11},{9,... | collective-permute-start | bytes 1572872 | tf_op jit(solution)/shard_map/ppermute | solution.py:500
  140.7 12.4 %collective-permute-start.32 = (bf16[2,4,128,256]{3,2,1,0:T(8,128)(2,1)S(1)}, bf16[2,4,128,256]{3,2,1,0:T(8,128)(2,1)S(1)}, u32[]{:S(2)}, u32[]{:S(2)}) collective-permute-start(bf16[2,4,128,256]{3,2,1,0:T(8,128)(2,1)S(1)} %get-tuple-element.67.refs_4_), channel_id=1, source_target_pairs={{0,1},{1,2},{2,3},{3,0},{4,36},{5,37},{6,38},{7,39},{8,9},{9,10},{... | collective-permute-start | bytes 1572872 | tf_op jit(solution)/shard_map/ppermute | solution.py:499
  153.4 21.0 %collective-permute-start.34 = (bf16[4,4,128,256]{3,2,1,0:T(8,128)(2,1)S(1)}, bf16[4,4,128,256]{3,2,1,0:T(8,128)(2,1)S(1)}, u32[]{:S(2)}, u32[]{:S(2)}) collective-permute-start(bf16[4,4,128,256]{3,2,1,0:T(8,128)(2,1)S(1)} %get-tuple-element.76), channel_id=1, source_target_pairs={{0,1},{1,2},{2,3},{3,0},{4,36},{5,37},{6,38},{7,39},{8,9},{9,10},{... | collective-permute-start | bytes 3145736 | tf_op jit(solution)/shard_map/ppermute | solution.py:502
  153.5 20.9 %collective-permute-start.35 = (bf16[4,4,128,256]{3,2,1,0:T(8,128)(2,1)S(1)}, bf16[4,4,128,256]{3,2,1,0:T(8,128)(2,1)S(1)}, u32[]{:S(2)}, u32[]{:S(2)}) collective-permute-start(bf16[4,4,128,256]{3,2,1,0:T(8,128)(2,1)S(1)} %get-tuple-element.77), channel_id=1, source_target_pairs={{0,3},{1,0},{2,1},{3,2},{4,100},{5,101},{6,102},{7,103},{8,11},{9,... | collective-permute-start | bytes 3145736 | tf_op jit(solution)/shard_map/ppermute | solution.py:502
  156.2 9.6 %collective-permute-start.29 = (bf16[4,128,256]{2,1,0:T(8,128)(2,1)S(1)}, bf16[4,128,256]{2,1,0:T(8,128)(2,1)S(1)}, u32[]{:S(2)}, u32[]{:S(2)}) collective-permute-start(bf16[4,128,256]{2,1,0:T(8,128)(2,1)S(1)} %get-tuple-element.69), channel_id=1, source_target_pairs={{0,8},{1,9},{2,10},{3,11},{4,5},{5,6},{6,7},{7,4},{8,16},{9,17},{1... | collective-permute-start | bytes 786440 | tf_op jit(solution)/shard_map/ppermute | solution.py:431
  156.2 9.6 %collective-permute-start.30 = (bf16[4,128,256]{2,1,0:T(8,128)(2,1)S(1)}, bf16[4,128,256]{2,1,0:T(8,128)(2,1)S(1)}, u32[]{:S(2)}, u32[]{:S(2)}) collective-permute-start(bf16[4,128,256]{2,1,0:T(8,128)(2,1)S(1)} %get-tuple-element.70), channel_id=1, source_target_pairs={{0,24},{1,25},{2,26},{3,27},{4,7},{5,4},{6,5},{7,6},{8,0},{9,1},{1... | collective-permute-start | bytes 786440 | tf_op jit(solution)/shard_map/ppermute | solution.py:431
  165.8 12.1 %collective-permute-start.24 = (bf16[2,176,512]{2,1,0:T(8,128)(2,1)S(1)}, bf16[2,176,512]{2,1,0:T(8,128)(2,1)S(1)}, u32[]{:S(2)}, u32[]{:S(2)}) collective-permute-start(bf16[2,176,512]{2,1,0:T(8,128)(2,1)S(1)} %get-tuple-element.59), channel_id=1, source_target_pairs={{0,8},{8,16},{16,24},{24,32},{32,40},{40,48},{48,56},{56,64},{64,7... | collective-permute-start | bytes 1081352 | tf_op jit(solution)/shard_map/ppermute | solution.py:535
  185.2 9.9 %collective-permute-start.39 = (bf16[128,512]{1,0:T(8,128)(2,1)S(1)}, bf16[128,512]{1,0:T(8,128)(2,1)S(1)}, u32[]{:S(2)}, u32[]{:S(2)}) collective-permute-start(bf16[128,512]{1,0:T(8,128)(2,1)S(1)} %get-tuple-element.83), channel_id=1, source_target_pairs={{0,32},{1,33},{2,34},{3,35},{4,12},{5,13},{6,14},{7,15},{8,40},{9,... | collective-permute-start | bytes 393224 | tf_op jit(solution)/shard_map/ppermute | solution.py:431
  185.3 9.8 %collective-permute-start.40 = (bf16[128,512]{1,0:T(8,128)(2,1)S(1)}, bf16[128,512]{1,0:T(8,128)(2,1)S(1)}, u32[]{:S(2)}, u32[]{:S(2)}) collective-permute-start(bf16[128,512]{1,0:T(8,128)(2,1)S(1)} %get-tuple-element.84), channel_id=1, source_target_pairs={{0,96},{1,97},{2,98},{3,99},{4,28},{5,29},{6,30},{7,31},{8,104},{9... | collective-permute-start | bytes 393224 | tf_op jit(solution)/shard_map/ppermute | solution.py:431
  (36 other events, 266.6 us)

commit v11 on v10

--- a/solution.py
+++ b/solution.py
@@ -139,8 +139,7 @@
 
 
 def run_main(chunk, meta, me, x, xt, weights, q, ct, given, sent_a, sent_b, before=()):
-    def fixed(*shape):
-        return pl.BlockSpec(shape, lambda i, m, e: (0,) * len(shape), pipeline_mode=pl.Buffered(1))
+    whole = pl.BlockSpec(memory_space=pltpu.VMEM)
 
     def wide():
         return pl.BlockSpec((TOK, HEAD_DIM), lambda i, m, e: (0, i * 4 + e[2] * 2 + chunk))
@@ -156,9 +155,6 @@
 
     def out_far():
         return pl.BlockSpec((2, WIN, HEAD_DIM), lambda i, m, e: (0, 0, i))
-
-    def part(shape):
-        return pl.BlockSpec(shape, lambda i, m, e: (0, 0, 0, 0))
 
     parts = [(4, 4, 128, HEAD_DIM)] * 4 if chunk == 0 else [(4, 4, 128, HEAD_DIM)] * 3 + [(2, 4, 128, HEAD_DIM)] * 2
     anywhere = pl.BlockSpec(memory_space=pl.ANY)
@@ -169,11 +165,11 @@
         grid_spec=pltpu.PrefetchScalarGridSpec(
             num_scalar_prefetch=2,
             grid=(2,),
-            in_specs=[fixed(PAIR, D), fixed(D, PAIR), *[fixed(*w.shape) for w in weights],
+            in_specs=[whole, whole, *[whole for w in weights],
                       wide(), handed(0), narrow(WIN, 0), narrow(WIN, 0),
                       wide(), handed(1), narrow(WIN, 1), narrow(WIN, 1)]
             + [anywhere] * len(before),
-            out_specs=[out(TOK), out(TOK), out_far(), out_far(), *[part(shape) for shape in parts]],
+            out_specs=[out(TOK), out(TOK), out_far(), out_far(), *[whole for shape in parts]],
             scratch_shapes=[pair, pair, pair, pair, pool, pool, pool, pool,
                             pltpu.VMEM((4, D, HEAD_DIM), BF), pltpu.VMEM((4, D, HEAD_DIM), BF)],
         ),
@@ -181,7 +177,7 @@
         + [jax.ShapeDtypeStruct((2, WIN, HALF), BF)] * 2
         + [jax.ShapeDtypeStruct(shape, BF) for shape in parts],
         input_output_aliases={12 + len(weights) + n: n for n in range(len(before))},
-        compiler_params=pltpu.CompilerParams(vmem_limit_bytes=44 * MIB),
+        compiler_params=pltpu.CompilerParams(vmem_limit_bytes=28 * MIB),
         cost_estimate=pl.CostEstimate(flops=12_000_000_000, bytes_accessed=24_000_000, transcendentals=500_000),
     )(meta, me, x, xt, *weights, q, given, sent_a, sent_b, ct, given, sent_a, sent_b, *before)
 
@@ -539,7 +535,7 @@
     first = exchange(first, 1)
     second = exchange(add_parts(parts, first[1:]), 1)
     context, grad_queries, finished = finish(info, [mine, swap(other), *returned, *late])
-    kept, given = add_last(me, exchange(add_both(first, second, late), 2), [finished])
+    kept, given = add_last(me, exchange(add_both(first, second, [finished]), 2), [])
     got = swap(given)
     grad = jnp.concatenate([jnp.where(c == 0, kept, got), jnp.where(c == 0, got, kept)], axis=1)
     return context, grad_queries, grad

time: 202 us -> 203 us (level)
  Pallas kernels: 63 us -> 58.5 us
  local copies, waits for them, and re-layouts: 6.25 us -> 10.7 us
    pallas_call x2, Pallas kernels: 41.6 us -> 37.1 us  [run_main(): pl.pallas_call(functools.partial(main_kernel, len(weights), len(before)),...]
    unnamed x50 -> x56, local copies, waits for them, and re-layouts: 6.17 us -> 10.6 us
  transfers between devices with their start and end apart: 43 -> 43, of which waited for: 17 -> 16; matrix products, arithmetic and copies ran while one was open for 1% -> 1% of each run, Pallas kernels for 29% -> 27%
where the time goes in v11:
time: 203 us; the launch traced here: 202 us
  starting transfers between devices  66.2 us (33%)
  waiting for transfers between devices  63.3 us (31%)
  Pallas kernels  58.5 us (29%)
  local copies, waits for them, and re-layouts  10.7 us (5%)
  other arithmetic  2.24 us (1%)
    pallas_call x2, Pallas kernels, run_main(): pl.pallas_call(functools.partial(main_kernel, len(weights), len(before)),...  37.1 us
    ppermute x16, starting transfers between devices, ring(): return lax.ppermute(value, ALL, shift(phase, -amount))  24.5 us
    ppermute x12, waiting for transfers between devices, exchange(): lax.ppermute(parts[r], ALL, shift(phase, r))  23.6 us
    ppermute x16, waiting for transfers between devices, ring(): return lax.ppermute(value, ALL, shift(phase, -amount))  22.1 us
    ppermute x12, starting transfers between devices, exchange(): lax.ppermute(parts[r], ALL, shift(phase, r))  12.7 us
    ppermute x4, starting transfers between devices, body(): lax.ppermute(part, DP, pairs)  10.9 us
    unnamed x56, local copies, waits for them, and re-layouts  10.6 us
    ppermute x5, starting transfers between devices, swap(): return lax.ppermute(value, 'c', [(0, 1), (1, 0)])  7.98 us
  transfers between devices with their start and end apart: 43, of which 16 were waited for; matrix products, arithmetic and copies ran while one was open for 1% of the time, Pallas kernels for 27%

profile of v11, /device:TPU:1, one launch (start us, length us, event | category | flops | bytes accessed | tf_op | source)
XLA Modules:
  0.0 202.1 jit_solution(17756410581962563063)
XLA Ops:
  2.7 3.5 %shard_map.94 = (s32[8,4]{1,0:T(8,128)}, s32[4]{0:T(128)}, bf16[176,2048]{1,0:T(8,128)(2,1)}, bf16[176,2048]{1,0:T(8,128)(2,1)}) custom-call(s32[4]{0:T(128)} %pad_add_fusion.me, s32[4,128]{1,0:T(4,128)} %bitcast.7, s32[4,128]{1,0:T(4,128)} %bitcast.8, s32[4,128]{1,0:T(4,128)} %bitcast.9, bf16[512,2048]{1,0:T(8,128)(2,1)} %refs_4_.1, bf16[512,2048]{1,0:T(8,128)(2,1)} %refs_8_.1), custom_call_target="tpu_custom_call" | custom-call | tf_op jit(solution)/shard_map/pallas_call | solution.py:308
  6.3 3.3 %collective-permute-start.5 = (bf16[176,2048]{1,0:T(8,128)(2,1)}, bf16[176,2048]{1,0:T(8,128)(2,1)S(1)}, u32[]{:S(2)}, u32[]{:S(2)}) collective-permute-start(bf16[176,2048]{1,0:T(8,128)(2,1)} %get-tuple-element.48), channel_id=1, source_target_pairs={{8,0},{16,8},{24,16},{32,24},{40,32},{48,40},{56,48},{64,56},{72,6... | collective-permute-start | bytes 2162696 | tf_op jit(solution)/shard_map/ppermute | solution.py:506
  17.7 4.7 %collective-permute-start.3 = (bf16[128,512]{1,0:T(8,128)(2,1)S(1)}, bf16[128,512]{1,0:T(8,128)(2,1)S(1)}, u32[]{:S(2)}, u32[]{:S(2)}) collective-permute-start(bf16[128,512]{1,0:T(8,128)(2,1)S(1)} %shard_map.95.refs_0_), channel_id=1, source_target_pairs={{0,64},{1,65},{2,66},{3,67},{4,20},{5,21},{6,22},{7,23},{8,72},{9,... | collective-permute-start | bytes 393224 | tf_op jit(solution)/shard_map/ppermute | solution.py:470
  22.4 7.1 %collective-permute-done.6.refs_5_.refs_8_.refs_12_.refs_7_.refs_11_ = bf16[176,2048]{1,0:T(8,128)(2,1)S(1)} collective-permute-done((bf16[176,2048]{1,0:T(8,128)(2,1)}, bf16[176,2048]{1,0:T(8,128)(2,1)S(1)}, u32[]{:S(2)}, u32[]{:S(2)}) %collective-permute-start.6) | collective-permute-done | bytes 720928 | tf_op jit(solution)/shard_map/ppermute | solution.py:507
  32.6 3.3 %shard_map.101 = bf16[512,2048]{1,0:T(8,128)(2,1)} custom-call(s32[4]{0:T(128)} %pad_add_fusion.me, bf16[512,2048]{1,0:T(8,128)(2,1)} %refs_4_.1, bf16[512,2048]{1,0:T(8,128)(2,1)} %refs_8_.1, bf16[4,128,256]{2,1,0:T(8,128)(2,1)} %copy-done.5), custom_call_target="tpu_custom_call" | custom-call | tf_op jit(solution)/shard_map/pallas_call | solution.py:329
  35.9 3.7 %collective-permute-start.18 = (bf16[512,2048]{1,0:T(8,128)(2,1)}, bf16[512,2048]{1,0:T(8,128)(2,1)}, u32[]{:S(2)}, u32[]{:S(2)}) collective-permute-start(bf16[512,2048]{1,0:T(8,128)(2,1)} %shard_map.101), channel_id=1, source_target_pairs={{0,4},{4,0},{1,5},{5,1},{2,6},{6,2},{3,7},{7,3},{8,12},{12,8},{9,1... | collective-permute-start | bytes 6291464 | tf_op jit(solution)/shard_map/ppermute | solution.py:402
  40.8 2.5 %collective-permute-start.8 = (bf16[4,128,256]{2,1,0:T(8,128)(2,1)}, bf16[4,128,256]{2,1,0:T(8,128)(2,1)S(1)}, u32[]{:S(2)}, u32[]{:S(2)}) collective-permute-start(bf16[4,128,256]{2,1,0:T(8,128)(2,1)} %copy-done.5), channel_id=1, source_target_pairs={{0,16},{1,17},{2,18},{3,19},{4,6},{5,7},{6,4},{7,5},{8,24},{9,25},... | collective-permute-start | bytes 786440 | tf_op jit(solution)/shard_map/ppermute | solution.py:470
  46.5 3.5 %collective-permute-done.8.refs_2_ = bf16[4,128,256]{2,1,0:T(8,128)(2,1)S(1)} collective-permute-done((bf16[4,128,256]{2,1,0:T(8,128)(2,1)}, bf16[4,128,256]{2,1,0:T(8,128)(2,1)S(1)}, u32[]{:S(2)}, u32[]{:S(2)}) %collective-permute-start.8) | collective-permute-done | bytes 262176 | tf_op jit(solution)/shard_map/ppermute | solution.py:470
  51.2 2.7 %collective-permute-start.13 = (bf16[4,4,128,256]{3,2,1,0:T(8,128)(2,1)S(1)}, bf16[4,4,128,256]{3,2,1,0:T(8,128)(2,1)S(1)}, u32[]{:S(2)}, u32[]{:S(2)}) collective-permute-start(bf16[4,4,128,256]{3,2,1,0:T(8,128)(2,1)S(1)} %shard_map.97.refs_0_), channel_id=1, source_target_pairs={{0,3},{1,0},{2,1},{3,2},{4,100},{5,101},{6,102},{7,103},{8,11},{9,... | collective-permute-start | bytes 3145736 | tf_op jit(solution)/shard_map/ppermute | solution.py:470
  53.8 6.1 %shard_map.98 = (bf16[1024,2048]{1,0:T(8,128)(2,1)}, bf16[2048,1024]{1,0:T(8,128)(2,1)}, f32[8,128]{1,0:T(8,128)}) custom-call(bf16[512,2048]{1,0:T(8,128)(2,1)} %a_ref.1, bf16[512,2048]{1,0:T(8,128)(2,1)} %copy-done.2, bf16[4,4,128,256]{3,2,1,0:T(8,128)(2,1)} %copy-done.3), custom_call_target="tpu_custom_call" | custom-call | tf_op jit(solution)/shard_map/pallas_call | solution.py:353
  62.1 4.2 %collective-permute-done.14.refs_5_.refs_2_ = bf16[4,4,128,256]{3,2,1,0:T(8,128)(2,1)S(1)} collective-permute-done((bf16[4,4,128,256]{3,2,1,0:T(8,128)(2,1)S(1)}, bf16[4,4,128,256]{3,2,1,0:T(8,128)(2,1)S(1)}, u32[]{:S(2)}, u32[]{:S(2)}) %collective-permute-start.14) | collective-permute-done | bytes 1048608 | tf_op jit(solution)/shard_map/ppermute | solution.py:470
  66.5 2.7 %collective-permute-start.20 = (bf16[2,4,128,256]{3,2,1,0:T(8,128)(2,1)S(1)}, bf16[2,4,128,256]{3,2,1,0:T(8,128)(2,1)S(1)}, u32[]{:S(2)}, u32[]{:S(2)}) collective-permute-start(bf16[2,4,128,256]{3,2,1,0:T(8,128)(2,1)S(1)} %slice.17), channel_id=1, source_target_pairs={{0,3},{1,0},{2,1},{3,2},{4,100},{5,101},{6,102},{7,103},{8,11},{9,... | collective-permute-start | bytes 1572872 | tf_op jit(solution)/shard_map/ppermute | solution.py:470
  69.3 2.7 %collective-permute-start.11 = (bf16[4,128,256]{2,1,0:T(8,128)(2,1)S(1)}, bf16[4,128,256]{2,1,0:T(8,128)(2,1)S(1)}, u32[]{:S(2)}, u32[]{:S(2)}) collective-permute-start(bf16[4,128,256]{2,1,0:T(8,128)(2,1)S(1)} %shard_map.99.refs_0_), channel_id=1, source_target_pairs={{0,16},{1,17},{2,18},{3,19},{4,6},{5,7},{6,4},{7,5},{8,24},{9,25},... | collective-permute-start | bytes 786440 | tf_op jit(solution)/shard_map/ppermute | solution.py:470
  73.0 5.0 %collective-permute-done.11.refs_2_ = bf16[4,128,256]{2,1,0:T(8,128)(2,1)S(1)} collective-permute-done((bf16[4,128,256]{2,1,0:T(8,128)(2,1)S(1)}, bf16[4,128,256]{2,1,0:T(8,128)(2,1)S(1)}, u32[]{:S(2)}, u32[]{:S(2)}) %collective-permute-start.11) | collective-permute-done | bytes 262176 | tf_op jit(solution)/shard_map/ppermute | solution.py:470
  78.1 5.0 %collective-permute-done.10.refs_1_ = bf16[4,128,256]{2,1,0:T(8,128)(2,1)S(1)} collective-permute-done((bf16[4,128,256]{2,1,0:T(8,128)(2,1)S(1)}, bf16[4,128,256]{2,1,0:T(8,128)(2,1)S(1)}, u32[]{:S(2)}, u32[]{:S(2)}) %collective-permute-start.10) | collective-permute-done | bytes 262176 | tf_op jit(solution)/shard_map/ppermute | solution.py:470
  83.6 2.4 %collective-permute-start.15 = (bf16[4,4,128,256]{3,2,1,0:T(8,128)(2,1)S(1)}, bf16[4,4,128,256]{3,2,1,0:T(8,128)(2,1)S(1)}, u32[]{:S(2)}, u32[]{:S(2)}) collective-permute-start(bf16[4,4,128,256]{3,2,1,0:T(8,128)(2,1)S(1)} %shard_map.100.refs_0_), channel_id=1, source_target_pairs={{0,3},{1,0},{2,1},{3,2},{4,100},{5,101},{6,102},{7,103},{8,11},{9,... | collective-permute-start | bytes 3145736 | tf_op jit(solution)/shard_map/ppermute | solution.py:470
  88.2 18.6 %shard_map.102 = (bf16[2,512,1024]{2,1,0:T(8,128)(2,1)S(1)}, bf16[2,512,1024]{2,1,0:T(8,128)(2,1)S(1)}, bf16[2,176,512]{2,1,0:T(8,128)(2,1)S(1)}, bf16[2,176,512...) custom-call(s32[8,4]{1,0:T(8,128)S(1)} %copy-done.24, ...), custom_call_target="tpu_custom_call" | custom-call | flops 12000000000 | bytes 24000000 | tf_op jit(solution)/shard_map/pallas_call | solution.py:163
  108.1 6.5 %collective-permute-start.23 = (bf16[2,176,512]{2,1,0:T(8,128)(2,1)S(1)}, bf16[2,176,512]{2,1,0:T(8,128)(2,1)S(1)}, u32[]{:S(2)}, u32[]{:S(2)}) collective-permute-start(bf16[2,176,512]{2,1,0:T(8,128)(2,1)S(1)} %get-tuple-element.58), channel_id=1, source_target_pairs={{4,8},{12,16},{20,24},{28,32},{36,40},{44,48},{52,56},{60,64},{68,... | collective-permute-start | bytes 1081352 | tf_op jit(solution)/shard_map/ppermute | solution.py:527
  114.6 2.7 %collective-permute-start.27 = (bf16[4,4,128,256]{3,2,1,0:T(8,128)(2,1)S(1)}, bf16[4,4,128,256]{3,2,1,0:T(8,128)(2,1)S(1)}, u32[]{:S(2)}, u32[]{:S(2)}) collective-permute-start(bf16[4,4,128,256]{3,2,1,0:T(8,128)(2,1)S(1)} %get-tuple-element.65), channel_id=1, source_target_pairs={{0,3},{1,0},{2,1},{3,2},{4,100},{5,101},{6,102},{7,103},{8,11},{9,... | collective-permute-start | bytes 3145736 | tf_op jit(solution)/shard_map/ppermute | solution.py:427
  120.1 18.5 %shard_map.103 = (bf16[2,512,1024]{2,1,0:T(8,128)(2,1)S(1)}, bf16[2,512,1024]{2,1,0:T(8,128)(2,1)S(1)}, bf16[2,176,512]{2,1,0:T(8,128)(2,1)S(1)}, bf16[2,176,512...) custom-call(s32[8,4]{1,0:T(8,128)S(1)} %copy-done.24, ...), custom_call_target="tpu_custom_call", output_to_operand_aliasing={{0}: (16, {}), {1}: (17, {})} | custom-call | flops 12000000000 | bytes 24000000 | tf_op jit(solution)/shard_map/pallas_call | solution.py:163
  140.6 7.0 %collective-permute-done.28.refs_3_ = bf16[4,4,128,256]{3,2,1,0:T(8,128)(2,1)S(1)} collective-permute-done((bf16[4,4,128,256]{3,2,1,0:T(8,128)(2,1)S(1)}, bf16[4,4,128,256]{3,2,1,0:T(8,128)(2,1)S(1)}, u32[]{:S(2)}, u32[]{:S(2)}) %collective-permute-start.28) | collective-permute-done | bytes 1048608 | tf_op jit(solution)/shard_map/ppermute | solution.py:427
  148.6 4.6 %collective-permute-done.32.got_a = bf16[2,4,128,256]{3,2,1,0:T(8,128)(2,1)S(1)} collective-permute-done((bf16[2,4,128,256]{3,2,1,0:T(8,128)(2,1)S(1)}, bf16[2,4,128,256]{3,2,1,0:T(8,128)(2,1)S(1)}, u32[]{:S(2)}, u32[]{:S(2)}) %collective-permute-start.32) | collective-permute-done | bytes 524320 | tf_op jit(solution)/shard_map/ppermute | solution.py:495
  153.5 2.7 %collective-permute-start.35 = (bf16[4,4,128,256]{3,2,1,0:T(8,128)(2,1)S(1)}, bf16[4,4,128,256]{3,2,1,0:T(8,128)(2,1)S(1)}, u32[]{:S(2)}, u32[]{:S(2)}) collective-permute-start(bf16[4,4,128,256]{3,2,1,0:T(8,128)(2,1)S(1)} %get-tuple-element.77), channel_id=1, source_target_pairs={{0,3},{1,0},{2,1},{3,2},{4,100},{5,101},{6,102},{7,103},{8,11},{9,... | collective-permute-start | bytes 3145736 | tf_op jit(solution)/shard_map/ppermute | solution.py:498
  156.2 2.7 %collective-permute-start.30 = (bf16[4,128,256]{2,1,0:T(8,128)(2,1)S(1)}, bf16[4,128,256]{2,1,0:T(8,128)(2,1)S(1)}, u32[]{:S(2)}, u32[]{:S(2)}) collective-permute-start(bf16[4,128,256]{2,1,0:T(8,128)(2,1)S(1)} %get-tuple-element.70), channel_id=1, source_target_pairs={{0,24},{1,25},{2,26},{3,27},{4,7},{5,4},{6,5},{7,6},{8,0},{9,1},{1... | collective-permute-start | bytes 786440 | tf_op jit(solution)/shard_map/ppermute | solution.py:427
  158.9 6.9 %collective-permute-done.29.refs_3_.refs_1_ = bf16[4,128,256]{2,1,0:T(8,128)(2,1)S(1)} collective-permute-done((bf16[4,128,256]{2,1,0:T(8,128)(2,1)S(1)}, bf16[4,128,256]{2,1,0:T(8,128)(2,1)S(1)}, u32[]{:S(2)}, u32[]{:S(2)}) %collective-permute-start.29) | collective-permute-done | bytes 262176 | tf_op jit(solution)/shard_map/ppermute | solution.py:427
  167.1 5.4 %collective-permute-done.31.refs_5_.refs_3_ = bf16[4,128,256]{2,1,0:T(8,128)(2,1)S(1)} collective-permute-done((bf16[4,128,256]{2,1,0:T(8,128)(2,1)S(1)}, bf16[4,128,256]{2,1,0:T(8,128)(2,1)S(1)}, u32[]{:S(2)}, u32[]{:S(2)}) %collective-permute-start.31) | collective-permute-done | bytes 262176 | tf_op jit(solution)/shard_map/ppermute | solution.py:427
  175.5 2.4 %collective-permute-start.37 = (bf16[4,128,256]{2,1,0:T(8,128)(2,1)S(1)}, bf16[4,128,256]{2,1,0:T(8,128)(2,1)S(1)}, u32[]{:S(2)}, u32[]{:S(2)}) collective-permute-start(bf16[4,128,256]{2,1,0:T(8,128)(2,1)S(1)} %get-tuple-element.80), channel_id=1, source_target_pairs={{0,24},{1,25},{2,26},{3,27},{4,7},{5,4},{6,5},{7,6},{8,0},{9,1},{1... | collective-permute-start | bytes 786440 | tf_op jit(solution)/shard_map/ppermute | solution.py:427
  177.9 3.6 %collective-permute-done.25.refs_5_ = bf16[2,176,512]{2,1,0:T(8,128)(2,1)S(1)} collective-permute-done((bf16[2,176,512]{2,1,0:T(8,128)(2,1)S(1)}, bf16[2,176,512]{2,1,0:T(8,128)(2,1)S(1)}, u32[]{:S(2)}, u32[]{:S(2)}) %collective-permute-start.25) | collective-permute-done | bytes 360480 | tf_op jit(solution)/shard_map/ppermute | solution.py:531
  183.0 5.0 %shard_map.104 = (bf16[512,2048]{1,0:T(8,128)(2,1)}, bf16[512,2048]{1,0:T(8,128)(2,1)}, f32[8,128]{1,0:T(8,128)}) custom-call(s32[4]{0:T(128)} %get-tuple-element.46.refs_0_.info, bf16[2,512,1024]{2,1,0:T(8,128)(2,1)} %copy-done.7, bf16[2,512,1024]{2,1,0:T(8,128)(2,1)} %copy-done.25, bf16[2,176,512]{2,1,0:T(8,128)(2,1)} %copy-done.8, ...), custom_call_target="tpu_custom_call" | custom-call | tf_op jit(solution)/shard_map/pallas_call | solution.py:388
  189.1 2.7 %collective-permute-start.40 = (bf16[128,512]{1,0:T(8,128)(2,1)S(1)}, bf16[128,512]{1,0:T(8,128)(2,1)S(1)}, u32[]{:S(2)}, u32[]{:S(2)}) collective-permute-start(bf16[128,512]{1,0:T(8,128)(2,1)S(1)} %get-tuple-element.85), channel_id=1, source_target_pairs={{0,96},{1,97},{2,98},{3,99},{4,28},{5,29},{6,30},{7,31},{8,104},{9... | collective-permute-start | bytes 393224 | tf_op jit(solution)/shard_map/ppermute | solution.py:427
  194.4 2.7 %collective-permute-done.41.refs_3_ = bf16[128,512]{1,0:T(8,128)(2,1)S(1)} collective-permute-done((bf16[128,512]{1,0:T(8,128)(2,1)S(1)}, bf16[128,512]{1,0:T(8,128)(2,1)S(1)}, u32[]{:S(2)}, u32[]{:S(2)}) %collective-permute-start.41) | collective-permute-done | bytes 131104 | tf_op jit(solution)/shard_map/ppermute | solution.py:427
  197.7 2.6 %collective-permute-start.42 = (f32[64,512]{1,0:T(8,128)S(1)}, f32[64,512]{1,0:T(8,128)S(1)}, u32[]{:S(2)}, u32[]{:S(2)}) collective-permute-start(f32[64,512]{1,0:T(8,128)S(1)} %get-tuple-element.88), channel_id=1, source_target_pairs={{0,4},{4,0},{1,5},{5,1},{2,6},{6,2},{3,7},{7,3},{8,12},{12,8},{9,1... | collective-permute-start | bytes 393224 | tf_op jit(solution)/shard_map/ppermute | solution.py:402
  (132 shorter events, 43.8 us)
Async XLA Ops:
  0.6 13.4 %collective-permute-start = (bf16[512,2048]{1,0:T(8,128)(2,1)}, bf16[512,2048]{1,0:T(8,128)(2,1)S(1)}, u32[]{:S(2)}, u32[]{:S(2)}) collective-permute-start(bf16[512,2048]{1,0:T(8,128)(2,1)} %a_ref.1), channel_id=1, source_target_pairs={{0,4},{4,0},{1,5},{5,1},{2,6},{6,2},{3,7},{7,3},{8,12},{12,8},{9,1... | collective-permute-start | bytes 6291464 | tf_op jit(solution)/shard_map/ppermute | solution.py:402
  6.3 16.1 %collective-permute-start.5 = (bf16[176,2048]{1,0:T(8,128)(2,1)}, bf16[176,2048]{1,0:T(8,128)(2,1)S(1)}, u32[]{:S(2)}, u32[]{:S(2)}) collective-permute-start(bf16[176,2048]{1,0:T(8,128)(2,1)} %get-tuple-element.48), channel_id=1, source_target_pairs={{8,0},{16,8},{24,16},{32,24},{40,32},{48,40},{56,48},{64,56},{72,6... | collective-permute-start | bytes 2162696 | tf_op jit(solution)/shard_map/ppermute | solution.py:506
  9.6 19.9 %collective-permute-start.6 = (bf16[176,2048]{1,0:T(8,128)(2,1)}, bf16[176,2048]{1,0:T(8,128)(2,1)S(1)}, u32[]{:S(2)}, u32[]{:S(2)}) collective-permute-start(bf16[176,2048]{1,0:T(8,128)(2,1)} %get-tuple-element.49), channel_id=1, source_target_pairs={{8,4},{16,12},{24,20},{32,28},{40,36},{48,44},{56,52},{64,60},{72,... | collective-permute-start | bytes 2162696 | tf_op jit(solution)/shard_map/ppermute | solution.py:507
  16.2 15.5 %collective-permute-start.4 = (bf16[128,512]{1,0:T(8,128)(2,1)S(1)}, bf16[128,512]{1,0:T(8,128)(2,1)S(1)}, u32[]{:S(2)}, u32[]{:S(2)}) collective-permute-start(bf16[128,512]{1,0:T(8,128)(2,1)S(1)} %shard_map.95.refs_0_), channel_id=1, source_target_pairs={{0,32},{1,33},{2,34},{3,35},{4,12},{5,13},{6,14},{7,15},{8,40},{9,... | collective-permute-start | bytes 393224 | tf_op jit(solution)/shard_map/ppermute | solution.py:470
  17.7 14.1 %collective-permute-start.3 = (bf16[128,512]{1,0:T(8,128)(2,1)S(1)}, bf16[128,512]{1,0:T(8,128)(2,1)S(1)}, u32[]{:S(2)}, u32[]{:S(2)}) collective-permute-start(bf16[128,512]{1,0:T(8,128)(2,1)S(1)} %shard_map.95.refs_0_), channel_id=1, source_target_pairs={{0,64},{1,65},{2,66},{3,67},{4,20},{5,21},{6,22},{7,23},{8,72},{9,... | collective-permute-start | bytes 393224 | tf_op jit(solution)/shard_map/ppermute | solution.py:470
  22.4 9.3 %collective-permute-start.2 = (bf16[128,512]{1,0:T(8,128)(2,1)S(1)}, bf16[128,512]{1,0:T(8,128)(2,1)S(1)}, u32[]{:S(2)}, u32[]{:S(2)}) collective-permute-start(bf16[128,512]{1,0:T(8,128)(2,1)S(1)} %shard_map.95.refs_0_), channel_id=1, source_target_pairs={{0,96},{1,97},{2,98},{3,99},{4,28},{5,29},{6,30},{7,31},{8,104},{9... | collective-permute-start | bytes 393224 | tf_op jit(solution)/shard_map/ppermute | solution.py:470
  35.9 50.1 %collective-permute-start.18 = (bf16[512,2048]{1,0:T(8,128)(2,1)}, bf16[512,2048]{1,0:T(8,128)(2,1)}, u32[]{:S(2)}, u32[]{:S(2)}) collective-permute-start(bf16[512,2048]{1,0:T(8,128)(2,1)} %shard_map.101), channel_id=1, source_target_pairs={{0,4},{4,0},{1,5},{5,1},{2,6},{6,2},{3,7},{7,3},{8,12},{12,8},{9,1... | collective-permute-start | bytes 6291464 | tf_op jit(solution)/shard_map/ppermute | solution.py:402
  51.1 15.2 %collective-permute-start.14 = (bf16[4,4,128,256]{3,2,1,0:T(8,128)(2,1)S(1)}, bf16[4,4,128,256]{3,2,1,0:T(8,128)(2,1)S(1)}, u32[]{:S(2)}, u32[]{:S(2)}) collective-permute-start(bf16[4,4,128,256]{3,2,1,0:T(8,128)(2,1)S(1)} %shard_map.97.refs_0_), channel_id=1, source_target_pairs={{0,1},{1,2},{2,3},{3,0},{4,36},{5,37},{6,38},{7,39},{8,9},{9,10},{... | collective-permute-start | bytes 3145736 | tf_op jit(solution)/shard_map/ppermute | solution.py:470
  51.2 15.3 %collective-permute-start.13 = (bf16[4,4,128,256]{3,2,1,0:T(8,128)(2,1)S(1)}, bf16[4,4,128,256]{3,2,1,0:T(8,128)(2,1)S(1)}, u32[]{:S(2)}, u32[]{:S(2)}) collective-permute-start(bf16[4,4,128,256]{3,2,1,0:T(8,128)(2,1)S(1)} %shard_map.97.refs_0_), channel_id=1, source_target_pairs={{0,3},{1,0},{2,1},{3,2},{4,100},{5,101},{6,102},{7,103},{8,11},{9,... | collective-permute-start | bytes 3145736 | tf_op jit(solution)/shard_map/ppermute | solution.py:470
  60.7 11.3 %collective-permute-start.12 = (bf16[4,128,256]{2,1,0:T(8,128)(2,1)S(1)}, bf16[4,128,256]{2,1,0:T(8,128)(2,1)S(1)}, u32[]{:S(2)}, u32[]{:S(2)}) collective-permute-start(bf16[4,128,256]{2,1,0:T(8,128)(2,1)S(1)} %shard_map.99.refs_0_), channel_id=1, source_target_pairs={{0,8},{1,9},{2,10},{3,11},{4,5},{5,6},{6,7},{7,4},{8,16},{9,17},{1... | collective-permute-start | bytes 786440 | tf_op jit(solution)/shard_map/ppermute | solution.py:470
  66.4 17.2 %collective-permute-start.19 = (bf16[2,4,128,256]{3,2,1,0:T(8,128)(2,1)S(1)}, bf16[2,4,128,256]{3,2,1,0:T(8,128)(2,1)S(1)}, u32[]{:S(2)}, u32[]{:S(2)}) collective-permute-start(bf16[2,4,128,256]{3,2,1,0:T(8,128)(2,1)S(1)} %slice.16), channel_id=1, source_target_pairs={{0,1},{1,2},{2,3},{3,0},{4,36},{5,37},{6,38},{7,39},{8,9},{9,10},{... | collective-permute-start | bytes 1572872 | tf_op jit(solution)/shard_map/ppermute | solution.py:470
  66.5 19.4 %collective-permute-start.20 = (bf16[2,4,128,256]{3,2,1,0:T(8,128)(2,1)S(1)}, bf16[2,4,128,256]{3,2,1,0:T(8,128)(2,1)S(1)}, u32[]{:S(2)}, u32[]{:S(2)}) collective-permute-start(bf16[2,4,128,256]{3,2,1,0:T(8,128)(2,1)S(1)} %slice.17), channel_id=1, source_target_pairs={{0,3},{1,0},{2,1},{3,2},{4,100},{5,101},{6,102},{7,103},{8,11},{9,... | collective-permute-start | bytes 1572872 | tf_op jit(solution)/shard_map/ppermute | solution.py:470
  71.9 11.1 %collective-permute-start.10 = (bf16[4,128,256]{2,1,0:T(8,128)(2,1)S(1)}, bf16[4,128,256]{2,1,0:T(8,128)(2,1)S(1)}, u32[]{:S(2)}, u32[]{:S(2)}) collective-permute-start(bf16[4,128,256]{2,1,0:T(8,128)(2,1)S(1)} %shard_map.99.refs_0_), channel_id=1, source_target_pairs={{0,24},{1,25},{2,26},{3,27},{4,7},{5,4},{6,5},{7,6},{8,0},{9,1},{1... | collective-permute-start | bytes 786440 | tf_op jit(solution)/shard_map/ppermute | solution.py:470
  83.1 31.4 %collective-permute-start.17 = (bf16[4,4,128,256]{3,2,1,0:T(8,128)(2,1)S(1)}, bf16[4,4,128,256]{3,2,1,0:T(8,128)(2,1)S(1)}, u32[]{:S(2)}, u32[]{:S(2)}) collective-permute-start(bf16[4,4,128,256]{3,2,1,0:T(8,128)(2,1)S(1)} %shard_map.100.refs_0_), channel_id=1, source_target_pairs={{0,2},{1,3},{2,0},{3,1},{4,68},{5,69},{6,70},{7,71},{8,10},{9,11},... | collective-permute-start | bytes 3145736 | tf_op jit(solution)/shard_map/ppermute | solution.py:470
  83.2 31.4 %collective-permute-start.16 = (bf16[4,4,128,256]{3,2,1,0:T(8,128)(2,1)S(1)}, bf16[4,4,128,256]{3,2,1,0:T(8,128)(2,1)S(1)}, u32[]{:S(2)}, u32[]{:S(2)}) collective-permute-start(bf16[4,4,128,256]{3,2,1,0:T(8,128)(2,1)S(1)} %shard_map.100.refs_0_), channel_id=1, source_target_pairs={{0,1},{1,2},{2,3},{3,0},{4,36},{5,37},{6,38},{7,39},{8,9},{9,10},{... | collective-permute-start | bytes 3145736 | tf_op jit(solution)/shard_map/ppermute | solution.py:470
  83.6 33.7 %collective-permute-start.15 = (bf16[4,4,128,256]{3,2,1,0:T(8,128)(2,1)S(1)}, bf16[4,4,128,256]{3,2,1,0:T(8,128)(2,1)S(1)}, u32[]{:S(2)}, u32[]{:S(2)}) collective-permute-start(bf16[4,4,128,256]{3,2,1,0:T(8,128)(2,1)S(1)} %shard_map.100.refs_0_), channel_id=1, source_target_pairs={{0,3},{1,0},{2,1},{3,2},{4,100},{5,101},{6,102},{7,103},{8,11},{9,... | collective-permute-start | bytes 3145736 | tf_op jit(solution)/shard_map/ppermute | solution.py:470
  106.8 31.9 %collective-permute-start.22 = (bf16[2,176,512]{2,1,0:T(8,128)(2,1)S(1)}, bf16[2,176,512]{2,1,0:T(8,128)(2,1)S(1)}, u32[]{:S(2)}, u32[]{:S(2)}) collective-permute-start(bf16[2,176,512]{2,1,0:T(8,128)(2,1)S(1)} %get-tuple-element.57), channel_id=1, source_target_pairs={{0,8},{8,16},{16,24},{24,32},{32,40},{40,48},{48,56},{56,64},{64,7... | collective-permute-start | bytes 1081352 | tf_op jit(solution)/shard_map/ppermute | solution.py:527
  108.1 30.7 %collective-permute-start.23 = (bf16[2,176,512]{2,1,0:T(8,128)(2,1)S(1)}, bf16[2,176,512]{2,1,0:T(8,128)(2,1)S(1)}, u32[]{:S(2)}, u32[]{:S(2)}) collective-permute-start(bf16[2,176,512]{2,1,0:T(8,128)(2,1)S(1)} %get-tuple-element.58), channel_id=1, source_target_pairs={{4,8},{12,16},{20,24},{28,32},{36,40},{44,48},{52,56},{60,64},{68,... | collective-permute-start | bytes 1081352 | tf_op jit(solution)/shard_map/ppermute | solution.py:527
  114.5 26.1 %collective-permute-start.26 = (bf16[4,4,128,256]{3,2,1,0:T(8,128)(2,1)S(1)}, bf16[4,4,128,256]{3,2,1,0:T(8,128)(2,1)S(1)}, u32[]{:S(2)}, u32[]{:S(2)}) collective-permute-start(bf16[4,4,128,256]{3,2,1,0:T(8,128)(2,1)S(1)} %get-tuple-element.64), channel_id=1, source_target_pairs={{0,1},{1,2},{2,3},{3,0},{4,36},{5,37},{6,38},{7,39},{8,9},{9,10},{... | collective-permute-start | bytes 3145736 | tf_op jit(solution)/shard_map/ppermute | solution.py:427
  114.6 26.0 %collective-permute-start.27 = (bf16[4,4,128,256]{3,2,1,0:T(8,128)(2,1)S(1)}, bf16[4,4,128,256]{3,2,1,0:T(8,128)(2,1)S(1)}, u32[]{:S(2)}, u32[]{:S(2)}) collective-permute-start(bf16[4,4,128,256]{3,2,1,0:T(8,128)(2,1)S(1)} %get-tuple-element.65), channel_id=1, source_target_pairs={{0,3},{1,0},{2,1},{3,2},{4,100},{5,101},{6,102},{7,103},{8,11},{9,... | collective-permute-start | bytes 3145736 | tf_op jit(solution)/shard_map/ppermute | solution.py:427
  117.3 30.3 %collective-permute-start.28 = (bf16[4,4,128,256]{3,2,1,0:T(8,128)(2,1)S(1)}, bf16[4,4,128,256]{3,2,1,0:T(8,128)(2,1)S(1)}, u32[]{:S(2)}, u32[]{:S(2)}) collective-permute-start(bf16[4,4,128,256]{3,2,1,0:T(8,128)(2,1)S(1)} %get-tuple-element.66), channel_id=1, source_target_pairs={{0,2},{1,3},{2,0},{3,1},{4,68},{5,69},{6,70},{7,71},{8,10},{9,11},... | collective-permute-start | bytes 3145736 | tf_op jit(solution)/shard_map/ppermute | solution.py:427
  138.7 42.8 %collective-permute-start.21 = (bf16[2,512,1024]{2,1,0:T(8,128)(2,1)S(1)}, bf16[2,512,1024]{2,1,0:T(8,128)(2,1)S(1)}, u32[]{:S(2)}, u32[]{:S(2)}) collective-permute-start(bf16[2,512,1024]{2,1,0:T(8,128)(2,1)S(1)} %get-tuple-element.56), channel_id=1, source_target_pairs={{0,4},{4,0},{1,5},{5,1},{2,6},{6,2},{3,7},{7,3},{8,12},{12,8},{9,1... | collective-permute-start | bytes 6291464 | tf_op jit(solution)/shard_map/ppermute | solution.py:402
  138.8 9.7 %collective-permute-start.33 = (bf16[2,4,128,256]{3,2,1,0:T(8,128)(2,1)S(1)}, bf16[2,4,128,256]{3,2,1,0:T(8,128)(2,1)S(1)}, u32[]{:S(2)}, u32[]{:S(2)}) collective-permute-start(bf16[2,4,128,256]{3,2,1,0:T(8,128)(2,1)S(1)} %get-tuple-element.75), channel_id=1, source_target_pairs={{0,3},{1,0},{2,1},{3,2},{4,100},{5,101},{6,102},{7,103},{8,11},{9,... | collective-permute-start | bytes 1572872 | tf_op jit(solution)/shard_map/ppermute | solution.py:496
  140.6 12.5 %collective-permute-start.32 = (bf16[2,4,128,256]{3,2,1,0:T(8,128)(2,1)S(1)}, bf16[2,4,128,256]{3,2,1,0:T(8,128)(2,1)S(1)}, u32[]{:S(2)}, u32[]{:S(2)}) collective-permute-start(bf16[2,4,128,256]{3,2,1,0:T(8,128)(2,1)S(1)} %get-tuple-element.67.refs_4_), channel_id=1, source_target_pairs={{0,1},{1,2},{2,3},{3,0},{4,36},{5,37},{6,38},{7,39},{8,9},{9,10},{... | collective-permute-start | bytes 1572872 | tf_op jit(solution)/shard_map/ppermute | solution.py:495
  153.5 21.0 %collective-permute-start.34 = (bf16[4,4,128,256]{3,2,1,0:T(8,128)(2,1)S(1)}, bf16[4,4,128,256]{3,2,1,0:T(8,128)(2,1)S(1)}, u32[]{:S(2)}, u32[]{:S(2)}) collective-permute-start(bf16[4,4,128,256]{3,2,1,0:T(8,128)(2,1)S(1)} %get-tuple-element.76), channel_id=1, source_target_pairs={{0,1},{1,2},{2,3},{3,0},{4,36},{5,37},{6,38},{7,39},{8,9},{9,10},{... | collective-permute-start | bytes 3145736 | tf_op jit(solution)/shard_map/ppermute | solution.py:498
  153.5 20.9 %collective-permute-start.35 = (bf16[4,4,128,256]{3,2,1,0:T(8,128)(2,1)S(1)}, bf16[4,4,128,256]{3,2,1,0:T(8,128)(2,1)S(1)}, u32[]{:S(2)}, u32[]{:S(2)}) collective-permute-start(bf16[4,4,128,256]{3,2,1,0:T(8,128)(2,1)S(1)} %get-tuple-element.77), channel_id=1, source_target_pairs={{0,3},{1,0},{2,1},{3,2},{4,100},{5,101},{6,102},{7,103},{8,11},{9,... | collective-permute-start | bytes 3145736 | tf_op jit(solution)/shard_map/ppermute | solution.py:498
  156.2 9.6 %collective-permute-start.29 = (bf16[4,128,256]{2,1,0:T(8,128)(2,1)S(1)}, bf16[4,128,256]{2,1,0:T(8,128)(2,1)S(1)}, u32[]{:S(2)}, u32[]{:S(2)}) collective-permute-start(bf16[4,128,256]{2,1,0:T(8,128)(2,1)S(1)} %get-tuple-element.69), channel_id=1, source_target_pairs={{0,8},{1,9},{2,10},{3,11},{4,5},{5,6},{6,7},{7,4},{8,16},{9,17},{1... | collective-permute-start | bytes 786440 | tf_op jit(solution)/shard_map/ppermute | solution.py:427
  156.2 9.6 %collective-permute-start.30 = (bf16[4,128,256]{2,1,0:T(8,128)(2,1)S(1)}, bf16[4,128,256]{2,1,0:T(8,128)(2,1)S(1)}, u32[]{:S(2)}, u32[]{:S(2)}) collective-permute-start(bf16[4,128,256]{2,1,0:T(8,128)(2,1)S(1)} %get-tuple-element.70), channel_id=1, source_target_pairs={{0,24},{1,25},{2,26},{3,27},{4,7},{5,4},{6,5},{7,6},{8,0},{9,1},{1... | collective-permute-start | bytes 786440 | tf_op jit(solution)/shard_map/ppermute | solution.py:427
  165.8 12.1 %collective-permute-start.24 = (bf16[2,176,512]{2,1,0:T(8,128)(2,1)S(1)}, bf16[2,176,512]{2,1,0:T(8,128)(2,1)S(1)}, u32[]{:S(2)}, u32[]{:S(2)}) collective-permute-start(bf16[2,176,512]{2,1,0:T(8,128)(2,1)S(1)} %get-tuple-element.59), channel_id=1, source_target_pairs={{0,8},{8,16},{16,24},{24,32},{32,40},{40,48},{48,56},{56,64},{64,7... | collective-permute-start | bytes 1081352 | tf_op jit(solution)/shard_map/ppermute | solution.py:531
  175.2 12.8 %collective-permute-start.36 = (bf16[4,128,256]{2,1,0:T(8,128)(2,1)S(1)}, bf16[4,128,256]{2,1,0:T(8,128)(2,1)S(1)}, u32[]{:S(2)}, u32[]{:S(2)}) collective-permute-start(bf16[4,128,256]{2,1,0:T(8,128)(2,1)S(1)} %get-tuple-element.79), channel_id=1, source_target_pairs={{0,8},{1,9},{2,10},{3,11},{4,5},{5,6},{6,7},{7,4},{8,16},{9,17},{1... | collective-permute-start | bytes 786440 | tf_op jit(solution)/shard_map/ppermute | solution.py:427
  175.5 12.5 %collective-permute-start.37 = (bf16[4,128,256]{2,1,0:T(8,128)(2,1)S(1)}, bf16[4,128,256]{2,1,0:T(8,128)(2,1)S(1)}, u32[]{:S(2)}, u32[]{:S(2)}) collective-permute-start(bf16[4,128,256]{2,1,0:T(8,128)(2,1)S(1)} %get-tuple-element.80), channel_id=1, source_target_pairs={{0,24},{1,25},{2,26},{3,27},{4,7},{5,4},{6,5},{7,6},{8,0},{9,1},{1... | collective-permute-start | bytes 786440 | tf_op jit(solution)/shard_map/ppermute | solution.py:427
  177.9 10.1 %collective-permute-start.38 = (bf16[4,128,256]{2,1,0:T(8,128)(2,1)S(1)}, bf16[4,128,256]{2,1,0:T(8,128)(2,1)S(1)}, u32[]{:S(2)}, u32[]{:S(2)}) collective-permute-start(bf16[4,128,256]{2,1,0:T(8,128)(2,1)S(1)} %get-tuple-element.81), channel_id=1, source_target_pairs={{0,16},{1,17},{2,18},{3,19},{4,6},{5,7},{6,4},{7,5},{8,24},{9,25},... | collective-permute-start | bytes 786440 | tf_op jit(solution)/shard_map/ppermute | solution.py:427
  (39 other events, 283.1 us)

commit v12 on v11

--- a/solution.py
+++ b/solution.py
@@ -138,7 +138,7 @@
         lax.fori_loop(0, 4, put, 0)
 
 
-def run_main(chunk, meta, me, x, xt, weights, q, ct, given, sent_a, sent_b, before=()):
+def run_main(chunk, meta, me, x, xt, weights, q, ct, q_other, ct_other, sent_a, sent_b, before=()):
     whole = pl.BlockSpec(memory_space=pltpu.VMEM)
 
     def wide():
@@ -146,9 +146,6 @@
 
     def narrow(rows, kind):
         return pl.BlockSpec((rows, HEAD_DIM), lambda i, m, e: (0, kind * 4 + i * 2 + chunk))
-
-    def handed(kind):
-        return pl.BlockSpec((TOK, HEAD_DIM), lambda i, m, e: (0, i * 4 + kind * 2 + chunk))
 
     def out(rows):
         return pl.BlockSpec((2, rows, HEAD_DIM), lambda i, m, e: (0, 0, i * 2 + chunk))
@@ -166,8 +163,8 @@
             num_scalar_prefetch=2,
             grid=(2,),
             in_specs=[whole, whole, *[whole for w in weights],
-                      wide(), handed(0), narrow(WIN, 0), narrow(WIN, 0),
-                      wide(), handed(1), narrow(WIN, 1), narrow(WIN, 1)]
+                      wide(), wide(), narrow(WIN, 0), narrow(WIN, 0),
+                      wide(), wide(), narrow(WIN, 1), narrow(WIN, 1)]
             + [anywhere] * len(before),
             out_specs=[out(TOK), out(TOK), out_far(), out_far(), *[whole for shape in parts]],
             scratch_shapes=[pair, pair, pair, pair, pool, pool, pool, pool,
@@ -177,9 +174,9 @@
         + [jax.ShapeDtypeStruct((2, WIN, HALF), BF)] * 2
         + [jax.ShapeDtypeStruct(shape, BF) for shape in parts],
         input_output_aliases={12 + len(weights) + n: n for n in range(len(before))},
-        compiler_params=pltpu.CompilerParams(vmem_limit_bytes=28 * MIB),
+        compiler_params=pltpu.CompilerParams(vmem_limit_bytes=34 * MIB),
         cost_estimate=pl.CostEstimate(flops=12_000_000_000, bytes_accessed=24_000_000, transcendentals=500_000),
-    )(meta, me, x, xt, *weights, q, given, sent_a, sent_b, ct, given, sent_a, sent_b, *before)
+    )(meta, me, x, xt, *weights, q, q_other, sent_a, sent_b, ct, ct_other, sent_a, sent_b, *before)
 
 
 def add(refs):
@@ -316,29 +313,6 @@
     )(me, enc_lengths.T, dec_lengths.T, dec_partner.T, q, ct)
 
 
-def hand_kernel(me, q_ref, ct_ref, *refs):
-    refs[-1][:, :HALF] = q_ref[...]
-    refs[-1][:, HALF:] = ct_ref[...]
-
-
-def hand(me, q, ct, after):
-    def half(i, me):
-        return (0, i * 2 + 1 - me[2])
-
-    part = pl.BlockSpec((TOK, HALF), half)
-    return pl.pallas_call(
-        hand_kernel,
-        grid_spec=pltpu.PrefetchScalarGridSpec(
-            num_scalar_prefetch=1,
-            grid=(2,),
-            in_specs=[part, part] + [pl.BlockSpec(memory_space=pl.ANY)] * len(after),
-            out_specs=pl.BlockSpec((TOK, 2 * HALF), lambda i, me: (0, i)),
-        ),
-        out_shape=jax.ShapeDtypeStruct((TOK, 2048), BF),
-        compiler_params=pltpu.CompilerParams(vmem_limit_bytes=57 * MIB),
-    )(me, q, ct, *after)
-
-
 def turn_kernel(a_ref, b_ref, *refs):
     x_ref, xt_ref, mark = refs[-3:]
     mark[...] = jnp.zeros_like(mark)
@@ -359,7 +333,7 @@
                    pl.BlockSpec((8, 128), lambda i: (0, 0))],
         out_shape=[jax.ShapeDtypeStruct((PAIR, D), BF), jax.ShapeDtypeStruct((D, PAIR), BF),
                    jax.ShapeDtypeStruct((8, 128), jnp.float32)],
-        compiler_params=pltpu.CompilerParams(vmem_limit_bytes=57 * MIB),
+        compiler_params=pltpu.CompilerParams(vmem_limit_bytes=16 * MIB),
     )(a, b, *after)
 
 
@@ -501,26 +475,25 @@
 def body(enc_hidden, kv_weights, queries, cotangent, enc_lengths, dec_lengths, dec_partner):
     z, y, c, x = (lax.axis_index(a) for a in ALL)
     me = jnp.stack([z, y, c, x]).astype(jnp.int32)
-    swapped = swap(enc_hidden)
+    swapped = [swap(value) for value in (enc_hidden, queries, cotangent)]
     meta, info, leave_a, leave_b = depart(me, enc_lengths, dec_lengths, dec_partner, queries, cotangent)
     sent_a = lax.ppermute(leave_a, DP, SEND_A)
     sent_b = lax.ppermute(leave_b, DP, SEND_B)
 
     got = swap(jnp.where(c == 0, kv_weights[:, HALF:], kv_weights[:, :HALF]))
-    own = pick(me, kv_weights, got, [info, swapped])
+    own = pick(me, kv_weights, got, [info, *swapped])
     first = [own] + [ring(own, 2, n) for n in (1, 2, 3)]
-    part = join(first, [sent_a, sent_b])
-    given = swap(hand(me, queries, cotangent, [part]))
+    tokens, tokens_t, turned = turn(enc_hidden, swapped[0], [first[1]])
+    part = join(first, [turned, sent_a, sent_b])
     part = join([part] + [ring(part, 1, n) for n in (1, 2, 3)], [])
-    tokens, tokens_t, turned = turn(enc_hidden, swapped, [part])
     ahead, behind = ring(part, 0, 1), ring(part, 0, -1)
     weights = [[part, ahead, behind, ring(behind[:2], 0, -1), ring(ahead[2:], 0, 1)]]
-    part = join(first, [turned], slice(HEAD_DIM, HALF))
+    part = join(first, [part], slice(HEAD_DIM, HALF))
     part = join([part] + [ring(part, 1, n) for n in (1, 2, 3)], [ahead, behind])
     weights.append([part, ring(part, 0, 1), ring(part, 0, -1), ring(part, 0, 2)])
 
     shared = (meta, me, tokens, tokens_t)
-    inputs = (queries, cotangent, given, sent_a, sent_b)
+    inputs = (queries, cotangent, *swapped[1:], sent_a, sent_b)
     home = [back(SEND_A), back(SEND_B)]
 
     *results, d0, d1, d3, d2 = run_main(0, *shared, weights[0], *inputs)

time: 203 us -> 198 us (0.975)
  Pallas kernels: 58.5 us -> 54.8 us
  local copies, waits for them, and re-layouts: 10.7 us -> 7.02 us
  waiting for transfers between devices: 63.3 us -> 65.4 us
    ppermute x16, waiting for transfers between devices: 22.1 us -> 31.1 us  [ring(): return lax.ppermute(value, ALL, shift(phase, -amount))]
    pallas_call x1, Pallas kernels: 6.09 us -> 2.12 us  [turn(): pl.pallas_call(turn_kernel, grid=(D // 512,), in_specs=[part, part] + [pl...]
    ppermute x12, waiting for transfers between devices: 23.6 us -> 19.7 us  [exchange(): lax.ppermute(parts[r], ALL, shift(phase, r))]
    unnamed x56 -> x34, local copies, waits for them, and re-layouts: 10.6 us -> 6.95 us
    ppermute x12, starting transfers between devices: 12.7 us -> 16.3 us  [exchange(): lax.ppermute(parts[r], ALL, shift(phase, r))]
    pallas_call x2, Pallas kernels: 37.1 us -> 40.6 us  [run_main(): pl.pallas_call(functools.partial(main_kernel, len(weights), len(before)),...]
    pallas_call x1 -> x0, Pallas kernels: 3.28 us -> none  [hand(): pl.pallas_call(hand_kernel, grid_spec=pltpu.PrefetchScalarGridSpec(num_sc...]
    ppermute x5 -> x6, starting transfers between devices: 7.98 us -> 4.97 us  [swap(): return lax.ppermute(value, 'c', [(0, 1), (1, 0)])]
  transfers between devices with their start and end apart: 43 -> 44, of which waited for: 16 -> 18; matrix products, arithmetic and copies ran while one was open for 1% -> 1% of each run, Pallas kernels for 27% -> 27%
where the time goes in v12:
time: 198 us
  starting transfers between devices  67.2 us (34%)
  waiting for transfers between devices  65.4 us (33%)
  Pallas kernels  54.8 us (28%)
  local copies, waits for them, and re-layouts  7.02 us (4%)
  other arithmetic  2.27 us (1%)
    pallas_call x2, Pallas kernels, run_main(): pl.pallas_call(functools.partial(main_kernel, len(weights), len(before)),...  40.6 us
    ppermute x16, waiting for transfers between devices, ring(): return lax.ppermute(value, ALL, shift(phase, -amount))  31.1 us
    ppermute x16, starting transfers between devices, ring(): return lax.ppermute(value, ALL, shift(phase, -amount))  24.8 us
    ppermute x12, waiting for transfers between devices, exchange(): lax.ppermute(parts[r], ALL, shift(phase, r))  19.7 us
    ppermute x12, starting transfers between devices, exchange(): lax.ppermute(parts[r], ALL, shift(phase, r))  16.3 us
    ppermute x4, starting transfers between devices, body(): lax.ppermute(part, DP, pairs)  9.7 us
    unnamed x34, local copies, waits for them, and re-layouts  6.95 us
    ppermute x1, waiting for transfers between devices, body(): sent_b = lax.ppermute(leave_b, DP, SEND_B)  5.43 us
  transfers between devices with their start and end apart: 44, of which 18 were waited for; matrix products, arithmetic and copies ran while one was open for 1% of the time, Pallas kernels for 27%

profile of v12, /device:TPU:1, one launch (start us, length us, event | category | flops | bytes accessed | tf_op | source)
XLA Modules:
  0.0 197.7 jit_solution(14442616719571723408)
XLA Ops:
  4.4 3.6 %shard_map.94 = (s32[8,4]{1,0:T(8,128)}, s32[4]{0:T(128)}, bf16[176,2048]{1,0:T(8,128)(2,1)}, bf16[176,2048]{1,0:T(8,128)(2,1)}) custom-call(s32[4]{0:T(128)} %pad_add_fusion.me, s32[4,128]{1,0:T(4,128)} %bitcast.7, s32[4,128]{1,0:T(4,128)} %bitcast.8, s32[4,128]{1,0:T(4,128)} %bitcast.9, bf16[512,2048]{1,0:T(8,128)(2,1)} %refs_4_.1, bf16[512,2048]{1,0:T(8,128)(2,1)} %refs_8_.1), custom_call_target="tpu_custom_call" | custom-call | tf_op jit(solution)/shard_map/pallas_call | solution.py:305
  8.0 3.3 %collective-permute-start.7 = (bf16[176,2048]{1,0:T(8,128)(2,1)}, bf16[176,2048]{1,0:T(8,128)(2,1)S(1)}, u32[]{:S(2)}, u32[]{:S(2)}) collective-permute-start(bf16[176,2048]{1,0:T(8,128)(2,1)} %get-tuple-element.51), channel_id=1, source_target_pairs={{8,0},{16,8},{24,16},{32,24},{40,32},{48,40},{56,48},{64,56},{72,6... | collective-permute-start | bytes 2162696 | tf_op jit(solution)/shard_map/ppermute | solution.py:480
  11.3 2.5 %collective-permute-start.8 = (bf16[176,2048]{1,0:T(8,128)(2,1)}, bf16[176,2048]{1,0:T(8,128)(2,1)S(1)}, u32[]{:S(2)}, u32[]{:S(2)}) collective-permute-start(bf16[176,2048]{1,0:T(8,128)(2,1)} %get-tuple-element.52), channel_id=1, source_target_pairs={{8,4},{16,12},{24,20},{32,28},{40,36},{48,44},{56,52},{64,60},{72,... | collective-permute-start | bytes 2162696 | tf_op jit(solution)/shard_map/ppermute | solution.py:481
  15.1 5.0 %collective-permute-start.4 = (bf16[128,512]{1,0:T(8,128)(2,1)S(1)}, bf16[128,512]{1,0:T(8,128)(2,1)S(1)}, u32[]{:S(2)}, u32[]{:S(2)}) collective-permute-start(bf16[128,512]{1,0:T(8,128)(2,1)S(1)} %shard_map.95.refs_0_), channel_id=1, source_target_pairs={{0,96},{1,97},{2,98},{3,99},{4,28},{5,29},{6,30},{7,31},{8,104},{9... | collective-permute-start | bytes 393224 | tf_op jit(solution)/shard_map/ppermute | solution.py:444
  22.1 2.1 %shard_map.96 = (bf16[1024,2048]{1,0:T(8,128)(2,1)S(1)}, bf16[2048,1024]{1,0:T(8,128)(2,1)S(1)}, f32[8,128]{1,0:T(8,128)S(1)}) custom-call(bf16[512,2048]{1,0:T(8,128)(2,1)S(1)} %copy-done.2, bf16[512,2048]{1,0:T(8,128)(2,1)S(1)} %collective-permute-done.refs_1_.b_ref, bf16[128,512]{1,0:T(8,128)(2,1)S(1)} %collective-permute-done.4.refs_0_.refs_1_), custom_call_target="tpu_custom_call" | custom-call | tf_op jit(solution)/shard_map/pallas_call | solution.py:327
  24.2 2.0 %copy-done.10 = bf16[2048,1024]{1,0:T(8,128)(2,1)} copy-done((bf16[2048,1024]{1,0:T(8,128)(2,1)}, bf16[2048,1024]{1,0:T(8,128)(2,1)S(1)}, u32[]{:S(2)}) %copy-start.10) | copy-done | bytes 4194328
  26.2 5.4 %collective-permute-done.8.refs_6_.refs_8_.refs_12_.refs_7_.refs_11_ = bf16[176,2048]{1,0:T(8,128)(2,1)S(1)} collective-permute-done((bf16[176,2048]{1,0:T(8,128)(2,1)}, bf16[176,2048]{1,0:T(8,128)(2,1)S(1)}, u32[]{:S(2)}, u32[]{:S(2)}) %collective-permute-start.8) | collective-permute-done | bytes 720928 | tf_op jit(solution)/shard_map/ppermute | solution.py:481
  34.8 2.5 %collective-permute-start.10 = (bf16[4,128,256]{2,1,0:T(8,128)(2,1)S(1)}, bf16[4,128,256]{2,1,0:T(8,128)(2,1)S(1)}, u32[]{:S(2)}, u32[]{:S(2)}) collective-permute-start(bf16[4,128,256]{2,1,0:T(8,128)(2,1)S(1)} %shard_map.97.refs_0_), channel_id=1, source_target_pairs={{0,16},{1,17},{2,18},{3,19},{4,6},{5,7},{6,4},{7,5},{8,24},{9,25},... | collective-permute-start | bytes 786440 | tf_op jit(solution)/shard_map/ppermute | solution.py:444
  40.0 4.1 %collective-permute-done.10.refs_2_ = bf16[4,128,256]{2,1,0:T(8,128)(2,1)S(1)} collective-permute-done((bf16[4,128,256]{2,1,0:T(8,128)(2,1)S(1)}, bf16[4,128,256]{2,1,0:T(8,128)(2,1)S(1)}, u32[]{:S(2)}, u32[]{:S(2)}) %collective-permute-start.10) | collective-permute-done | bytes 262176 | tf_op jit(solution)/shard_map/ppermute | solution.py:444
  47.6 12.4 %collective-permute-done.16.refs_5_.refs_2_ = bf16[4,4,128,256]{3,2,1,0:T(8,128)(2,1)S(1)} collective-permute-done((bf16[4,4,128,256]{3,2,1,0:T(8,128)(2,1)S(1)}, bf16[4,4,128,256]{3,2,1,0:T(8,128)(2,1)S(1)}, u32[]{:S(2)}, u32[]{:S(2)}) %collective-permute-start.16) | collective-permute-done | bytes 1048608 | tf_op jit(solution)/shard_map/ppermute | solution.py:444
  60.2 2.7 %collective-permute-start.21 = (bf16[2,4,128,256]{3,2,1,0:T(8,128)(2,1)S(1)}, bf16[2,4,128,256]{3,2,1,0:T(8,128)(2,1)S(1)}, u32[]{:S(2)}, u32[]{:S(2)}) collective-permute-start(bf16[2,4,128,256]{3,2,1,0:T(8,128)(2,1)S(1)} %slice.17), channel_id=1, source_target_pairs={{0,3},{1,0},{2,1},{3,2},{4,100},{5,101},{6,102},{7,103},{8,11},{9,... | collective-permute-start | bytes 1572872 | tf_op jit(solution)/shard_map/ppermute | solution.py:444
  64.1 2.1 %collective-permute-start.13 = (bf16[4,128,256]{2,1,0:T(8,128)(2,1)S(1)}, bf16[4,128,256]{2,1,0:T(8,128)(2,1)S(1)}, u32[]{:S(2)}, u32[]{:S(2)}) collective-permute-start(bf16[4,128,256]{2,1,0:T(8,128)(2,1)S(1)} %shard_map.99.refs_0_), channel_id=1, source_target_pairs={{0,16},{1,17},{2,18},{3,19},{4,6},{5,7},{6,4},{7,5},{8,24},{9,25},... | collective-permute-start | bytes 786440 | tf_op jit(solution)/shard_map/ppermute | solution.py:444
  67.5 2.8 %collective-permute-done.14.refs_3_ = bf16[4,128,256]{2,1,0:T(8,128)(2,1)S(1)} collective-permute-done((bf16[4,128,256]{2,1,0:T(8,128)(2,1)S(1)}, bf16[4,128,256]{2,1,0:T(8,128)(2,1)S(1)}, u32[]{:S(2)}, u32[]{:S(2)}) %collective-permute-start.14) | collective-permute-done | bytes 262176 | tf_op jit(solution)/shard_map/ppermute | solution.py:444
  70.3 6.8 %collective-permute-done.13.refs_2_ = bf16[4,128,256]{2,1,0:T(8,128)(2,1)S(1)} collective-permute-done((bf16[4,128,256]{2,1,0:T(8,128)(2,1)S(1)}, bf16[4,128,256]{2,1,0:T(8,128)(2,1)S(1)}, u32[]{:S(2)}, u32[]{:S(2)}) %collective-permute-start.13) | collective-permute-done | bytes 262176 | tf_op jit(solution)/shard_map/ppermute | solution.py:444
  80.9 20.6 %shard_map.101 = (bf16[2,512,1024]{2,1,0:T(8,128)(2,1)S(1)}, bf16[2,512,1024]{2,1,0:T(8,128)(2,1)S(1)}, bf16[2,176,512]{2,1,0:T(8,128)(2,1)}, bf16[2,176,512]{2,...) custom-call(s32[8,4]{1,0:T(8,128)S(1)} %copy-done.13, ...), custom_call_target="tpu_custom_call" | custom-call | flops 12000000000 | bytes 24000000 | tf_op jit(solution)/shard_map/pallas_call | solution.py:160
  102.8 5.2 %collective-permute-start.24 = (bf16[2,176,512]{2,1,0:T(8,128)(2,1)S(1)}, bf16[2,176,512]{2,1,0:T(8,128)(2,1)S(1)}, u32[]{:S(2)}, u32[]{:S(2)}) collective-permute-start(bf16[2,176,512]{2,1,0:T(8,128)(2,1)S(1)} %get-tuple-element.58), channel_id=1, source_target_pairs={{4,8},{12,16},{20,24},{28,32},{36,40},{44,48},{52,56},{60,64},{68,... | collective-permute-start | bytes 1081352 | tf_op jit(solution)/shard_map/ppermute | solution.py:500
  108.0 2.5 %collective-permute-start.27 = (bf16[4,4,128,256]{3,2,1,0:T(8,128)(2,1)S(1)}, bf16[4,4,128,256]{3,2,1,0:T(8,128)(2,1)S(1)}, u32[]{:S(2)}, u32[]{:S(2)}) collective-permute-start(bf16[4,4,128,256]{3,2,1,0:T(8,128)(2,1)S(1)} %get-tuple-element.64), channel_id=1, source_target_pairs={{0,1},{1,2},{2,3},{3,0},{4,36},{5,37},{6,38},{7,39},{8,9},{9,10},{... | collective-permute-start | bytes 3145736 | tf_op jit(solution)/shard_map/ppermute | solution.py:401
  114.5 20.0 %shard_map.102 = (bf16[2,512,1024]{2,1,0:T(8,128)(2,1)S(1)}, bf16[2,512,1024]{2,1,0:T(8,128)(2,1)S(1)}, bf16[2,176,512]{2,1,0:T(8,128)(2,1)S(1)}, bf16[2,176,512...) custom-call(s32[8,4]{1,0:T(8,128)S(1)} %copy-done.13, ...), custom_call_target="tpu_custom_call", output_to_operand_aliasing={{0}: (16, {}), {1}: (17, {})} | custom-call | flops 12000000000 | bytes 24000000 | tf_op jit(solution)/shard_map/pallas_call | solution.py:160
  134.7 2.0 %collective-permute-start.34 = (bf16[2,4,128,256]{3,2,1,0:T(8,128)(2,1)S(1)}, bf16[2,4,128,256]{3,2,1,0:T(8,128)(2,1)S(1)}, u32[]{:S(2)}, u32[]{:S(2)}) collective-permute-start(bf16[2,4,128,256]{3,2,1,0:T(8,128)(2,1)S(1)} %get-tuple-element.75), channel_id=1, source_target_pairs={{0,3},{1,0},{2,1},{3,2},{4,100},{5,101},{6,102},{7,103},{8,11},{9,... | collective-permute-start | bytes 1572872 | tf_op jit(solution)/shard_map/ppermute | solution.py:470
  137.5 3.1 %collective-permute-done.29.refs_3_ = bf16[4,4,128,256]{3,2,1,0:T(8,128)(2,1)S(1)} collective-permute-done((bf16[4,4,128,256]{3,2,1,0:T(8,128)(2,1)S(1)}, bf16[4,4,128,256]{3,2,1,0:T(8,128)(2,1)S(1)}, u32[]{:S(2)}, u32[]{:S(2)}) %collective-permute-start.29) | collective-permute-done | bytes 1048608 | tf_op jit(solution)/shard_map/ppermute | solution.py:401
  141.5 2.7 %collective-permute-done.34.got_b = bf16[2,4,128,256]{3,2,1,0:T(8,128)(2,1)S(1)} collective-permute-done((bf16[2,4,128,256]{3,2,1,0:T(8,128)(2,1)S(1)}, bf16[2,4,128,256]{3,2,1,0:T(8,128)(2,1)S(1)}, u32[]{:S(2)}, u32[]{:S(2)}) %collective-permute-start.34) | collective-permute-done | bytes 524320 | tf_op jit(solution)/shard_map/ppermute | solution.py:470
  144.3 1.9 collective-permute-done.33.got_a
  149.2 2.7 %collective-permute-start.31 = (bf16[4,128,256]{2,1,0:T(8,128)(2,1)S(1)}, bf16[4,128,256]{2,1,0:T(8,128)(2,1)S(1)}, u32[]{:S(2)}, u32[]{:S(2)}) collective-permute-start(bf16[4,128,256]{2,1,0:T(8,128)(2,1)S(1)} %get-tuple-element.70), channel_id=1, source_target_pairs={{0,24},{1,25},{2,26},{3,27},{4,7},{5,4},{6,5},{7,6},{8,0},{9,1},{1... | collective-permute-start | bytes 786440 | tf_op jit(solution)/shard_map/ppermute | solution.py:401
  151.9 6.9 %collective-permute-done.30.refs_3_.refs_1_ = bf16[4,128,256]{2,1,0:T(8,128)(2,1)S(1)} collective-permute-done((bf16[4,128,256]{2,1,0:T(8,128)(2,1)S(1)}, bf16[4,128,256]{2,1,0:T(8,128)(2,1)S(1)}, u32[]{:S(2)}, u32[]{:S(2)}) %collective-permute-start.30) | collective-permute-done | bytes 262176 | tf_op jit(solution)/shard_map/ppermute | solution.py:401
  161.2 5.5 %collective-permute-done.32.refs_5_.refs_3_ = bf16[4,128,256]{2,1,0:T(8,128)(2,1)S(1)} collective-permute-done((bf16[4,128,256]{2,1,0:T(8,128)(2,1)S(1)}, bf16[4,128,256]{2,1,0:T(8,128)(2,1)S(1)}, u32[]{:S(2)}, u32[]{:S(2)}) %collective-permute-start.32) | collective-permute-done | bytes 262176 | tf_op jit(solution)/shard_map/ppermute | solution.py:401
  166.7 1.9 collective-permute-start.26
  169.9 2.2 %collective-permute-start.38 = (bf16[4,128,256]{2,1,0:T(8,128)(2,1)S(1)}, bf16[4,128,256]{2,1,0:T(8,128)(2,1)S(1)}, u32[]{:S(2)}, u32[]{:S(2)}) collective-permute-start(bf16[4,128,256]{2,1,0:T(8,128)(2,1)S(1)} %get-tuple-element.80), channel_id=1, source_target_pairs={{0,24},{1,25},{2,26},{3,27},{4,7},{5,4},{6,5},{7,6},{8,0},{9,1},{1... | collective-permute-start | bytes 786440 | tf_op jit(solution)/shard_map/ppermute | solution.py:401
  172.3 3.4 %collective-permute-done.26.refs_5_ = bf16[2,176,512]{2,1,0:T(8,128)(2,1)S(1)} collective-permute-done((bf16[2,176,512]{2,1,0:T(8,128)(2,1)S(1)}, bf16[2,176,512]{2,1,0:T(8,128)(2,1)S(1)}, u32[]{:S(2)}, u32[]{:S(2)}) %collective-permute-start.26) | collective-permute-done | bytes 360480 | tf_op jit(solution)/shard_map/ppermute | solution.py:504
  177.2 5.0 %shard_map.103 = (bf16[512,2048]{1,0:T(8,128)(2,1)}, bf16[512,2048]{1,0:T(8,128)(2,1)}, f32[8,128]{1,0:T(8,128)}) custom-call(s32[4]{0:T(128)} %get-tuple-element.46.refs_0_.info, bf16[2,512,1024]{2,1,0:T(8,128)(2,1)} %copy-done, bf16[2,512,1024]{2,1,0:T(8,128)(2,1)} %copy-done.14, bf16[2,176,512]{2,1,0:T(8,128)(2,1)} %copy-done.3, ...), custom_call_target="tpu_custom_call" | custom-call | tf_op jit(solution)/shard_map/pallas_call | solution.py:362
  184.5 2.8 %collective-permute-start.41 = (bf16[128,512]{1,0:T(8,128)(2,1)S(1)}, bf16[128,512]{1,0:T(8,128)(2,1)S(1)}, u32[]{:S(2)}, u32[]{:S(2)}) collective-permute-start(bf16[128,512]{1,0:T(8,128)(2,1)S(1)} %get-tuple-element.85), channel_id=1, source_target_pairs={{0,96},{1,97},{2,98},{3,99},{4,28},{5,29},{6,30},{7,31},{8,104},{9... | collective-permute-start | bytes 393224 | tf_op jit(solution)/shard_map/ppermute | solution.py:401
  189.8 2.8 %collective-permute-done.42.refs_3_ = bf16[128,512]{1,0:T(8,128)(2,1)S(1)} collective-permute-done((bf16[128,512]{1,0:T(8,128)(2,1)S(1)}, bf16[128,512]{1,0:T(8,128)(2,1)S(1)}, u32[]{:S(2)}, u32[]{:S(2)}) %collective-permute-start.42) | collective-permute-done | bytes 131104 | tf_op jit(solution)/shard_map/ppermute | solution.py:401
  193.2 2.7 %collective-permute-start.43 = (f32[64,512]{1,0:T(8,128)S(1)}, f32[64,512]{1,0:T(8,128)S(1)}, u32[]{:S(2)}, u32[]{:S(2)}) collective-permute-start(f32[64,512]{1,0:T(8,128)S(1)} %get-tuple-element.88), channel_id=1, source_target_pairs={{0,4},{4,0},{1,5},{5,1},{2,6},{6,2},{3,7},{7,3},{8,12},{12,8},{9,1... | collective-permute-start | bytes 393224 | tf_op jit(solution)/shard_map/ppermute | solution.py:376
  (111 shorter events, 45.2 us)
Async XLA Ops:
  0.6 13.2 %collective-permute-start = (bf16[512,2048]{1,0:T(8,128)(2,1)}, bf16[512,2048]{1,0:T(8,128)(2,1)S(1)}, u32[]{:S(2)}, u32[]{:S(2)}) collective-permute-start(bf16[512,2048]{1,0:T(8,128)(2,1)} %a_ref.1), channel_id=1, source_target_pairs={{0,4},{4,0},{1,5},{5,1},{2,6},{6,2},{3,7},{7,3},{8,12},{12,8},{9,1... | collective-permute-start | bytes 6291464 | tf_op jit(solution)/shard_map/ppermute | solution.py:376
  2.1 11.8 %collective-permute-start.2 = (bf16[512,2048]{1,0:T(8,128)(2,1)}, bf16[512,2048]{1,0:T(8,128)(2,1)}, u32[]{:S(2)}, u32[]{:S(2)}) collective-permute-start(bf16[512,2048]{1,0:T(8,128)(2,1)} %refs_4_.1), channel_id=1, source_target_pairs={{0,4},{4,0},{1,5},{5,1},{2,6},{6,2},{3,7},{7,3},{8,12},{12,8},{9,1... | collective-permute-start | bytes 6291464 | tf_op jit(solution)/shard_map/ppermute | solution.py:376
  2.2 11.7 %collective-permute-start.3 = (bf16[512,2048]{1,0:T(8,128)(2,1)}, bf16[512,2048]{1,0:T(8,128)(2,1)}, u32[]{:S(2)}, u32[]{:S(2)}) collective-permute-start(bf16[512,2048]{1,0:T(8,128)(2,1)} %refs_8_.1), channel_id=1, source_target_pairs={{0,4},{4,0},{1,5},{5,1},{2,6},{6,2},{3,7},{7,3},{8,12},{12,8},{9,1... | collective-permute-start | bytes 6291464 | tf_op jit(solution)/shard_map/ppermute | solution.py:376
  8.0 18.2 %collective-permute-start.7 = (bf16[176,2048]{1,0:T(8,128)(2,1)}, bf16[176,2048]{1,0:T(8,128)(2,1)S(1)}, u32[]{:S(2)}, u32[]{:S(2)}) collective-permute-start(bf16[176,2048]{1,0:T(8,128)(2,1)} %get-tuple-element.51), channel_id=1, source_target_pairs={{8,0},{16,8},{24,16},{32,24},{40,32},{48,40},{56,48},{64,56},{72,6... | collective-permute-start | bytes 2162696 | tf_op jit(solution)/shard_map/ppermute | solution.py:480
  11.3 20.3 %collective-permute-start.8 = (bf16[176,2048]{1,0:T(8,128)(2,1)}, bf16[176,2048]{1,0:T(8,128)(2,1)S(1)}, u32[]{:S(2)}, u32[]{:S(2)}) collective-permute-start(bf16[176,2048]{1,0:T(8,128)(2,1)} %get-tuple-element.52), channel_id=1, source_target_pairs={{8,4},{16,12},{24,20},{32,28},{40,36},{48,44},{56,52},{64,60},{72,... | collective-permute-start | bytes 2162696 | tf_op jit(solution)/shard_map/ppermute | solution.py:481
  20.1 13.3 %collective-permute-start.6 = (bf16[128,512]{1,0:T(8,128)(2,1)S(1)}, bf16[128,512]{1,0:T(8,128)(2,1)S(1)}, u32[]{:S(2)}, u32[]{:S(2)}) collective-permute-start(bf16[128,512]{1,0:T(8,128)(2,1)S(1)} %shard_map.95.refs_0_), channel_id=1, source_target_pairs={{0,32},{1,33},{2,34},{3,35},{4,12},{5,13},{6,14},{7,15},{8,40},{9,... | collective-permute-start | bytes 393224 | tf_op jit(solution)/shard_map/ppermute | solution.py:444
  20.1 13.3 %collective-permute-start.5 = (bf16[128,512]{1,0:T(8,128)(2,1)S(1)}, bf16[128,512]{1,0:T(8,128)(2,1)S(1)}, u32[]{:S(2)}, u32[]{:S(2)}) collective-permute-start(bf16[128,512]{1,0:T(8,128)(2,1)S(1)} %shard_map.95.refs_0_), channel_id=1, source_target_pairs={{0,64},{1,65},{2,66},{3,67},{4,20},{5,21},{6,22},{7,23},{8,72},{9,... | collective-permute-start | bytes 393224 | tf_op jit(solution)/shard_map/ppermute | solution.py:444
  44.2 15.9 %collective-permute-start.16 = (bf16[4,4,128,256]{3,2,1,0:T(8,128)(2,1)S(1)}, bf16[4,4,128,256]{3,2,1,0:T(8,128)(2,1)S(1)}, u32[]{:S(2)}, u32[]{:S(2)}) collective-permute-start(bf16[4,4,128,256]{3,2,1,0:T(8,128)(2,1)S(1)} %shard_map.98.refs_4_.refs_0_), channel_id=1, source_target_pairs={{0,1},{1,2},{2,3},{3,0},{4,36},{5,37},{6,38},{7,39},{8,9},{9,10},{... | collective-permute-start | bytes 3145736 | tf_op jit(solution)/shard_map/ppermute | solution.py:444
  45.9 14.3 %collective-permute-start.15 = (bf16[4,4,128,256]{3,2,1,0:T(8,128)(2,1)S(1)}, bf16[4,4,128,256]{3,2,1,0:T(8,128)(2,1)S(1)}, u32[]{:S(2)}, u32[]{:S(2)}) collective-permute-start(bf16[4,4,128,256]{3,2,1,0:T(8,128)(2,1)S(1)} %shard_map.98.refs_4_.refs_0_), channel_id=1, source_target_pairs={{0,3},{1,0},{2,1},{3,2},{4,100},{5,101},{6,102},{7,103},{8,11},{9,... | collective-permute-start | bytes 3145736 | tf_op jit(solution)/shard_map/ppermute | solution.py:444
  60.0 20.8 %collective-permute-start.20 = (bf16[2,4,128,256]{3,2,1,0:T(8,128)(2,1)S(1)}, bf16[2,4,128,256]{3,2,1,0:T(8,128)(2,1)S(1)}, u32[]{:S(2)}, u32[]{:S(2)}) collective-permute-start(bf16[2,4,128,256]{3,2,1,0:T(8,128)(2,1)S(1)} %slice.16), channel_id=1, source_target_pairs={{0,1},{1,2},{2,3},{3,0},{4,36},{5,37},{6,38},{7,39},{8,9},{9,10},{... | collective-permute-start | bytes 1572872 | tf_op jit(solution)/shard_map/ppermute | solution.py:444
  60.2 20.7 %collective-permute-start.21 = (bf16[2,4,128,256]{3,2,1,0:T(8,128)(2,1)S(1)}, bf16[2,4,128,256]{3,2,1,0:T(8,128)(2,1)S(1)}, u32[]{:S(2)}, u32[]{:S(2)}) collective-permute-start(bf16[2,4,128,256]{3,2,1,0:T(8,128)(2,1)S(1)} %slice.17), channel_id=1, source_target_pairs={{0,3},{1,0},{2,1},{3,2},{4,100},{5,101},{6,102},{7,103},{8,11},{9,... | collective-permute-start | bytes 1572872 | tf_op jit(solution)/shard_map/ppermute | solution.py:444
  64.1 13.0 %collective-permute-start.13 = (bf16[4,128,256]{2,1,0:T(8,128)(2,1)S(1)}, bf16[4,128,256]{2,1,0:T(8,128)(2,1)S(1)}, u32[]{:S(2)}, u32[]{:S(2)}) collective-permute-start(bf16[4,128,256]{2,1,0:T(8,128)(2,1)S(1)} %shard_map.99.refs_0_), channel_id=1, source_target_pairs={{0,16},{1,17},{2,18},{3,19},{4,6},{5,7},{6,4},{7,5},{8,24},{9,25},... | collective-permute-start | bytes 786440 | tf_op jit(solution)/shard_map/ppermute | solution.py:444
  66.2 11.8 %collective-permute-start.12 = (bf16[4,128,256]{2,1,0:T(8,128)(2,1)S(1)}, bf16[4,128,256]{2,1,0:T(8,128)(2,1)S(1)}, u32[]{:S(2)}, u32[]{:S(2)}) collective-permute-start(bf16[4,128,256]{2,1,0:T(8,128)(2,1)S(1)} %shard_map.99.refs_0_), channel_id=1, source_target_pairs={{0,24},{1,25},{2,26},{3,27},{4,7},{5,4},{6,5},{7,6},{8,0},{9,1},{1... | collective-permute-start | bytes 786440 | tf_op jit(solution)/shard_map/ppermute | solution.py:444
  78.0 30.0 %collective-permute-start.19 = (bf16[4,4,128,256]{3,2,1,0:T(8,128)(2,1)S(1)}, bf16[4,4,128,256]{3,2,1,0:T(8,128)(2,1)S(1)}, u32[]{:S(2)}, u32[]{:S(2)}) collective-permute-start(bf16[4,4,128,256]{3,2,1,0:T(8,128)(2,1)S(1)} %shard_map.100.refs_0_), channel_id=1, source_target_pairs={{0,2},{1,3},{2,0},{3,1},{4,68},{5,69},{6,70},{7,71},{8,10},{9,11},... | collective-permute-start | bytes 3145736 | tf_op jit(solution)/shard_map/ppermute | solution.py:444
  78.2 32.4 %collective-permute-start.18 = (bf16[4,4,128,256]{3,2,1,0:T(8,128)(2,1)S(1)}, bf16[4,4,128,256]{3,2,1,0:T(8,128)(2,1)S(1)}, u32[]{:S(2)}, u32[]{:S(2)}) collective-permute-start(bf16[4,4,128,256]{3,2,1,0:T(8,128)(2,1)S(1)} %shard_map.100.refs_0_), channel_id=1, source_target_pairs={{0,1},{1,2},{2,3},{3,0},{4,36},{5,37},{6,38},{7,39},{8,9},{9,10},{... | collective-permute-start | bytes 3145736 | tf_op jit(solution)/shard_map/ppermute | solution.py:444
  79.6 32.1 %collective-permute-start.17 = (bf16[4,4,128,256]{3,2,1,0:T(8,128)(2,1)S(1)}, bf16[4,4,128,256]{3,2,1,0:T(8,128)(2,1)S(1)}, u32[]{:S(2)}, u32[]{:S(2)}) collective-permute-start(bf16[4,4,128,256]{3,2,1,0:T(8,128)(2,1)S(1)} %shard_map.100.refs_0_), channel_id=1, source_target_pairs={{0,3},{1,0},{2,1},{3,2},{4,100},{5,101},{6,102},{7,103},{8,11},{9,... | collective-permute-start | bytes 3145736 | tf_op jit(solution)/shard_map/ppermute | solution.py:444
  101.5 33.1 %collective-permute-start.23 = (bf16[2,176,512]{2,1,0:T(8,128)(2,1)}, bf16[2,176,512]{2,1,0:T(8,128)(2,1)S(1)}, u32[]{:S(2)}, u32[]{:S(2)}) collective-permute-start(bf16[2,176,512]{2,1,0:T(8,128)(2,1)} %get-tuple-element.57), channel_id=1, source_target_pairs={{0,8},{8,16},{16,24},{24,32},{32,40},{40,48},{48,56},{56,64},{64,7... | collective-permute-start | bytes 1081352 | tf_op jit(solution)/shard_map/ppermute | solution.py:500
  102.8 31.9 %collective-permute-start.24 = (bf16[2,176,512]{2,1,0:T(8,128)(2,1)S(1)}, bf16[2,176,512]{2,1,0:T(8,128)(2,1)S(1)}, u32[]{:S(2)}, u32[]{:S(2)}) collective-permute-start(bf16[2,176,512]{2,1,0:T(8,128)(2,1)S(1)} %get-tuple-element.58), channel_id=1, source_target_pairs={{4,8},{12,16},{20,24},{28,32},{36,40},{44,48},{52,56},{60,64},{68,... | collective-permute-start | bytes 1081352 | tf_op jit(solution)/shard_map/ppermute | solution.py:500
  108.0 28.7 %collective-permute-start.27 = (bf16[4,4,128,256]{3,2,1,0:T(8,128)(2,1)S(1)}, bf16[4,4,128,256]{3,2,1,0:T(8,128)(2,1)S(1)}, u32[]{:S(2)}, u32[]{:S(2)}) collective-permute-start(bf16[4,4,128,256]{3,2,1,0:T(8,128)(2,1)S(1)} %get-tuple-element.64), channel_id=1, source_target_pairs={{0,1},{1,2},{2,3},{3,0},{4,36},{5,37},{6,38},{7,39},{8,9},{9,10},{... | collective-permute-start | bytes 3145736 | tf_op jit(solution)/shard_map/ppermute | solution.py:401
  111.5 26.0 %collective-permute-start.28 = (bf16[4,4,128,256]{3,2,1,0:T(8,128)(2,1)S(1)}, bf16[4,4,128,256]{3,2,1,0:T(8,128)(2,1)S(1)}, u32[]{:S(2)}, u32[]{:S(2)}) collective-permute-start(bf16[4,4,128,256]{3,2,1,0:T(8,128)(2,1)S(1)} %get-tuple-element.65), channel_id=1, source_target_pairs={{0,3},{1,0},{2,1},{3,2},{4,100},{5,101},{6,102},{7,103},{8,11},{9,... | collective-permute-start | bytes 3145736 | tf_op jit(solution)/shard_map/ppermute | solution.py:401
  111.8 28.8 %collective-permute-start.29 = (bf16[4,4,128,256]{3,2,1,0:T(8,128)(2,1)S(1)}, bf16[4,4,128,256]{3,2,1,0:T(8,128)(2,1)S(1)}, u32[]{:S(2)}, u32[]{:S(2)}) collective-permute-start(bf16[4,4,128,256]{3,2,1,0:T(8,128)(2,1)S(1)} %get-tuple-element.66), channel_id=1, source_target_pairs={{0,2},{1,3},{2,0},{3,1},{4,68},{5,69},{6,70},{7,71},{8,10},{9,11},... | collective-permute-start | bytes 3145736 | tf_op jit(solution)/shard_map/ppermute | solution.py:401
  134.6 41.2 %collective-permute-start.22 = (bf16[2,512,1024]{2,1,0:T(8,128)(2,1)S(1)}, bf16[2,512,1024]{2,1,0:T(8,128)(2,1)S(1)}, u32[]{:S(2)}, u32[]{:S(2)}) collective-permute-start(bf16[2,512,1024]{2,1,0:T(8,128)(2,1)S(1)} %get-tuple-element.56), channel_id=1, source_target_pairs={{0,4},{4,0},{1,5},{5,1},{2,6},{6,2},{3,7},{7,3},{8,12},{12,8},{9,1... | collective-permute-start | bytes 6291464 | tf_op jit(solution)/shard_map/ppermute | solution.py:376
  134.7 9.6 %collective-permute-start.34 = (bf16[2,4,128,256]{3,2,1,0:T(8,128)(2,1)S(1)}, bf16[2,4,128,256]{3,2,1,0:T(8,128)(2,1)S(1)}, u32[]{:S(2)}, u32[]{:S(2)}) collective-permute-start(bf16[2,4,128,256]{3,2,1,0:T(8,128)(2,1)S(1)} %get-tuple-element.75), channel_id=1, source_target_pairs={{0,3},{1,0},{2,1},{3,2},{4,100},{5,101},{6,102},{7,103},{8,11},{9,... | collective-permute-start | bytes 1572872 | tf_op jit(solution)/shard_map/ppermute | solution.py:470
  136.7 9.5 %collective-permute-start.33 = (bf16[2,4,128,256]{3,2,1,0:T(8,128)(2,1)S(1)}, bf16[2,4,128,256]{3,2,1,0:T(8,128)(2,1)S(1)}, u32[]{:S(2)}, u32[]{:S(2)}) collective-permute-start(bf16[2,4,128,256]{3,2,1,0:T(8,128)(2,1)S(1)} %get-tuple-element.67.refs_4_), channel_id=1, source_target_pairs={{0,1},{1,2},{2,3},{3,0},{4,36},{5,37},{6,38},{7,39},{8,9},{9,10},{... | collective-permute-start | bytes 1572872 | tf_op jit(solution)/shard_map/ppermute | solution.py:469
  146.5 22.1 %collective-permute-start.35 = (bf16[4,4,128,256]{3,2,1,0:T(8,128)(2,1)S(1)}, bf16[4,4,128,256]{3,2,1,0:T(8,128)(2,1)S(1)}, u32[]{:S(2)}, u32[]{:S(2)}) collective-permute-start(bf16[4,4,128,256]{3,2,1,0:T(8,128)(2,1)S(1)} %get-tuple-element.76), channel_id=1, source_target_pairs={{0,1},{1,2},{2,3},{3,0},{4,36},{5,37},{6,38},{7,39},{8,9},{9,10},{... | collective-permute-start | bytes 3145736 | tf_op jit(solution)/shard_map/ppermute | solution.py:472
  147.4 21.3 %collective-permute-start.36 = (bf16[4,4,128,256]{3,2,1,0:T(8,128)(2,1)S(1)}, bf16[4,4,128,256]{3,2,1,0:T(8,128)(2,1)S(1)}, u32[]{:S(2)}, u32[]{:S(2)}) collective-permute-start(bf16[4,4,128,256]{3,2,1,0:T(8,128)(2,1)S(1)} %get-tuple-element.77), channel_id=1, source_target_pairs={{0,3},{1,0},{2,1},{3,2},{4,100},{5,101},{6,102},{7,103},{8,11},{9,... | collective-permute-start | bytes 3145736 | tf_op jit(solution)/shard_map/ppermute | solution.py:472
  149.2 9.6 %collective-permute-start.30 = (bf16[4,128,256]{2,1,0:T(8,128)(2,1)S(1)}, bf16[4,128,256]{2,1,0:T(8,128)(2,1)S(1)}, u32[]{:S(2)}, u32[]{:S(2)}) collective-permute-start(bf16[4,128,256]{2,1,0:T(8,128)(2,1)S(1)} %get-tuple-element.69), channel_id=1, source_target_pairs={{0,8},{1,9},{2,10},{3,11},{4,5},{5,6},{6,7},{7,4},{8,16},{9,17},{1... | collective-permute-start | bytes 786440 | tf_op jit(solution)/shard_map/ppermute | solution.py:401
  149.2 10.7 %collective-permute-start.31 = (bf16[4,128,256]{2,1,0:T(8,128)(2,1)S(1)}, bf16[4,128,256]{2,1,0:T(8,128)(2,1)S(1)}, u32[]{:S(2)}, u32[]{:S(2)}) collective-permute-start(bf16[4,128,256]{2,1,0:T(8,128)(2,1)S(1)} %get-tuple-element.70), channel_id=1, source_target_pairs={{0,24},{1,25},{2,26},{3,27},{4,7},{5,4},{6,5},{7,6},{8,0},{9,1},{1... | collective-permute-start | bytes 786440 | tf_op jit(solution)/shard_map/ppermute | solution.py:401
  159.9 12.2 %collective-permute-start.25 = (bf16[2,176,512]{2,1,0:T(8,128)(2,1)S(1)}, bf16[2,176,512]{2,1,0:T(8,128)(2,1)S(1)}, u32[]{:S(2)}, u32[]{:S(2)}) collective-permute-start(bf16[2,176,512]{2,1,0:T(8,128)(2,1)S(1)} %get-tuple-element.59), channel_id=1, source_target_pairs={{0,8},{8,16},{16,24},{24,32},{32,40},{40,48},{48,56},{56,64},{64,7... | collective-permute-start | bytes 1081352 | tf_op jit(solution)/shard_map/ppermute | solution.py:504
  169.4 12.8 %collective-permute-start.37 = (bf16[4,128,256]{2,1,0:T(8,128)(2,1)S(1)}, bf16[4,128,256]{2,1,0:T(8,128)(2,1)S(1)}, u32[]{:S(2)}, u32[]{:S(2)}) collective-permute-start(bf16[4,128,256]{2,1,0:T(8,128)(2,1)S(1)} %get-tuple-element.79), channel_id=1, source_target_pairs={{0,8},{1,9},{2,10},{3,11},{4,5},{5,6},{6,7},{7,4},{8,16},{9,17},{1... | collective-permute-start | bytes 786440 | tf_op jit(solution)/shard_map/ppermute | solution.py:401
  169.9 12.2 %collective-permute-start.38 = (bf16[4,128,256]{2,1,0:T(8,128)(2,1)S(1)}, bf16[4,128,256]{2,1,0:T(8,128)(2,1)S(1)}, u32[]{:S(2)}, u32[]{:S(2)}) collective-permute-start(bf16[4,128,256]{2,1,0:T(8,128)(2,1)S(1)} %get-tuple-element.80), channel_id=1, source_target_pairs={{0,24},{1,25},{2,26},{3,27},{4,7},{5,4},{6,5},{7,6},{8,0},{9,1},{1... | collective-permute-start | bytes 786440 | tf_op jit(solution)/shard_map/ppermute | solution.py:401
  172.1 10.0 %collective-permute-start.39 = (bf16[4,128,256]{2,1,0:T(8,128)(2,1)S(1)}, bf16[4,128,256]{2,1,0:T(8,128)(2,1)S(1)}, u32[]{:S(2)}, u32[]{:S(2)}) collective-permute-start(bf16[4,128,256]{2,1,0:T(8,128)(2,1)S(1)} %get-tuple-element.81), channel_id=1, source_target_pairs={{0,16},{1,17},{2,18},{3,19},{4,6},{5,7},{6,4},{7,5},{8,24},{9,25},... | collective-permute-start | bytes 786440 | tf_op jit(solution)/shard_map/ppermute | solution.py:401
  (29 other events, 197.2 us)

commit v13 on v12

--- a/solution.py
+++ b/solution.py
@@ -174,7 +174,7 @@
         + [jax.ShapeDtypeStruct((2, WIN, HALF), BF)] * 2
         + [jax.ShapeDtypeStruct(shape, BF) for shape in parts],
         input_output_aliases={12 + len(weights) + n: n for n in range(len(before))},
-        compiler_params=pltpu.CompilerParams(vmem_limit_bytes=34 * MIB),
+        compiler_params=pltpu.CompilerParams(vmem_limit_bytes=32 * MIB),
         cost_estimate=pl.CostEstimate(flops=12_000_000_000, bytes_accessed=24_000_000, transcendentals=500_000),
     )(meta, me, x, xt, *weights, q, q_other, sent_a, sent_b, ct, ct_other, sent_a, sent_b, *before)
 
@@ -368,7 +368,7 @@
             out_specs=[out, out, pl.BlockSpec((8, 128), lambda i, e: (0, 0))],
         ),
         out_shape=[jax.ShapeDtypeStruct((TOK, 2048), BF)] * 2 + [jax.ShapeDtypeStruct((8, 128), jnp.float32)],
-        compiler_params=pltpu.CompilerParams(vmem_limit_bytes=59 * MIB),
+        compiler_params=pltpu.CompilerParams(vmem_limit_bytes=24 * MIB),
     )(info, *pieces)
 
 
@@ -508,7 +508,7 @@
     first = exchange(first, 1)
     second = exchange(add_parts(parts, first[1:]), 1)
     context, grad_queries, finished = finish(info, [mine, swap(other), *returned, *late])
-    kept, given = add_last(me, exchange(add_both(first, second, [finished]), 2), [])
+    kept, given = add_last(me, exchange(add_both(first, second, late), 2), [finished])
     got = swap(given)
     grad = jnp.concatenate([jnp.where(c == 0, kept, got), jnp.where(c == 0, got, kept)], axis=1)
     return context, grad_queries, grad

time: 198 us -> 194 us (0.980)
  local copies, waits for them, and re-layouts: 7.02 us -> 2.68 us
  Pallas kernels: 54.8 us -> 52.4 us
  waiting for transfers between devices: 65.4 us -> 67.6 us
    unnamed x34 -> x20, local copies, waits for them, and re-layouts: 6.95 us -> 2.61 us
    ppermute x1, waiting for transfers between devices: 2.75 us -> 0.43 us  [scatter_ring(): got_b = lax.ppermute(far_b, ALL, shift(0, -1))]
    ppermute x1, waiting for transfers between devices: 1.92 us -> 4.18 us  [scatter_ring(): got_a = lax.ppermute(far_a, ALL, shift(0, 1))]
    ppermute x12, waiting for transfers between devices: 19.7 us -> 21.7 us  [exchange(): lax.ppermute(parts[r], ALL, shift(phase, r))]
  transfers between devices with their start and end apart: 44 -> 44, of which waited for: 18 -> 20; matrix products, arithmetic and copies ran while one was open for 1% -> 1% of each run, Pallas kernels for 27% -> 27%
where the time goes in v13:
time: 194 us
  starting transfers between devices  68.2 us (35%)
  waiting for transfers between devices  67.6 us (35%)
  Pallas kernels  52.4 us (27%)
  local copies, waits for them, and re-layouts  2.68 us (1%)
  other arithmetic  2.21 us (1%)
    pallas_call x2, Pallas kernels, run_main(): pl.pallas_call(functools.partial(main_kernel, len(weights), len(before)),...  39.8 us
    ppermute x16, waiting for transfers between devices, ring(): return lax.ppermute(value, ALL, shift(phase, -amount))  31.1 us
    ppermute x16, starting transfers between devices, ring(): return lax.ppermute(value, ALL, shift(phase, -amount))  24.8 us
    ppermute x12, waiting for transfers between devices, exchange(): lax.ppermute(parts[r], ALL, shift(phase, r))  21.7 us
    ppermute x12, starting transfers between devices, exchange(): lax.ppermute(parts[r], ALL, shift(phase, r))  15.9 us
    ppermute x4, starting transfers between devices, body(): lax.ppermute(part, DP, pairs)  9.73 us
    ppermute x6, starting transfers between devices, swap(): return lax.ppermute(value, 'c', [(0, 1), (1, 0)])  6.52 us
    ppermute x1, waiting for transfers between devices, body(): sent_b = lax.ppermute(leave_b, DP, SEND_B)  5.47 us
  transfers between devices with their start and end apart: 44, of which 20 were waited for; matrix products, arithmetic and copies ran while one was open for 1% of the time, Pallas kernels for 27%

profile of v13, /device:TPU:1, one launch (start us, length us, event | category | flops | bytes accessed | tf_op | source)
XLA Modules:
  0.0 194.0 jit_solution(3191146574252831120)
XLA Ops:
  4.3 3.6 %shard_map.94 = (s32[8,4]{1,0:T(8,128)}, s32[4]{0:T(128)}, bf16[176,2048]{1,0:T(8,128)(2,1)}, bf16[176,2048]{1,0:T(8,128)(2,1)}) custom-call(s32[4]{0:T(128)} %pad_add_fusion.me, s32[4,128]{1,0:T(4,128)} %bitcast.7, s32[4,128]{1,0:T(4,128)} %bitcast.8, s32[4,128]{1,0:T(4,128)} %bitcast.9, bf16[512,2048]{1,0:T(8,128)(2,1)} %refs_4_.1, bf16[512,2048]{1,0:T(8,128)(2,1)} %refs_8_.1), custom_call_target="tpu_custom_call" | custom-call | tf_op jit(solution)/shard_map/pallas_call | solution.py:305
  7.9 3.3 %collective-permute-start.7 = (bf16[176,2048]{1,0:T(8,128)(2,1)}, bf16[176,2048]{1,0:T(8,128)(2,1)S(1)}, u32[]{:S(2)}, u32[]{:S(2)}) collective-permute-start(bf16[176,2048]{1,0:T(8,128)(2,1)} %get-tuple-element.51), channel_id=1, source_target_pairs={{8,0},{16,8},{24,16},{32,24},{40,32},{48,40},{56,48},{64,56},{72,6... | collective-permute-start | bytes 2162696 | tf_op jit(solution)/shard_map/ppermute | solution.py:480
  11.3 2.5 %collective-permute-start.8 = (bf16[176,2048]{1,0:T(8,128)(2,1)}, bf16[176,2048]{1,0:T(8,128)(2,1)S(1)}, u32[]{:S(2)}, u32[]{:S(2)}) collective-permute-start(bf16[176,2048]{1,0:T(8,128)(2,1)} %get-tuple-element.52), channel_id=1, source_target_pairs={{8,4},{16,12},{24,20},{32,28},{40,36},{48,44},{56,52},{64,60},{72,... | collective-permute-start | bytes 2162696 | tf_op jit(solution)/shard_map/ppermute | solution.py:481
  15.0 5.0 %collective-permute-start.4 = (bf16[128,512]{1,0:T(8,128)(2,1)S(1)}, bf16[128,512]{1,0:T(8,128)(2,1)S(1)}, u32[]{:S(2)}, u32[]{:S(2)}) collective-permute-start(bf16[128,512]{1,0:T(8,128)(2,1)S(1)} %shard_map.95.refs_0_), channel_id=1, source_target_pairs={{0,96},{1,97},{2,98},{3,99},{4,28},{5,29},{6,30},{7,31},{8,104},{9... | collective-permute-start | bytes 393224 | tf_op jit(solution)/shard_map/ppermute | solution.py:444
  22.0 2.1 %shard_map.96 = (bf16[1024,2048]{1,0:T(8,128)(2,1)S(1)}, bf16[2048,1024]{1,0:T(8,128)(2,1)S(1)}, f32[8,128]{1,0:T(8,128)S(1)}) custom-call(bf16[512,2048]{1,0:T(8,128)(2,1)S(1)} %copy-done.2, bf16[512,2048]{1,0:T(8,128)(2,1)S(1)} %collective-permute-done.refs_1_.b_ref, bf16[128,512]{1,0:T(8,128)(2,1)S(1)} %collective-permute-done.4.refs_0_.refs_1_), custom_call_target="tpu_custom_call" | custom-call | tf_op jit(solution)/shard_map/pallas_call | solution.py:327
  24.1 2.0 %copy-done.8 = bf16[2048,1024]{1,0:T(8,128)(2,1)} copy-done((bf16[2048,1024]{1,0:T(8,128)(2,1)}, bf16[2048,1024]{1,0:T(8,128)(2,1)S(1)}, u32[]{:S(2)}) %copy-start.8) | copy-done | bytes 4194328
  26.1 5.5 %collective-permute-done.8.refs_6_.refs_8_.refs_12_.refs_7_.refs_11_ = bf16[176,2048]{1,0:T(8,128)(2,1)S(1)} collective-permute-done((bf16[176,2048]{1,0:T(8,128)(2,1)}, bf16[176,2048]{1,0:T(8,128)(2,1)S(1)}, u32[]{:S(2)}, u32[]{:S(2)}) %collective-permute-start.8) | collective-permute-done | bytes 720928 | tf_op jit(solution)/shard_map/ppermute | solution.py:481
  34.7 2.5 %collective-permute-start.10 = (bf16[4,128,256]{2,1,0:T(8,128)(2,1)S(1)}, bf16[4,128,256]{2,1,0:T(8,128)(2,1)S(1)}, u32[]{:S(2)}, u32[]{:S(2)}) collective-permute-start(bf16[4,128,256]{2,1,0:T(8,128)(2,1)S(1)} %shard_map.97.refs_0_), channel_id=1, source_target_pairs={{0,16},{1,17},{2,18},{3,19},{4,6},{5,7},{6,4},{7,5},{8,24},{9,25},... | collective-permute-start | bytes 786440 | tf_op jit(solution)/shard_map/ppermute | solution.py:444
  39.9 4.1 %collective-permute-done.10.refs_2_ = bf16[4,128,256]{2,1,0:T(8,128)(2,1)S(1)} collective-permute-done((bf16[4,128,256]{2,1,0:T(8,128)(2,1)S(1)}, bf16[4,128,256]{2,1,0:T(8,128)(2,1)S(1)}, u32[]{:S(2)}, u32[]{:S(2)}) %collective-permute-start.10) | collective-permute-done | bytes 262176 | tf_op jit(solution)/shard_map/ppermute | solution.py:444
  47.5 12.4 %collective-permute-done.16.refs_5_.refs_2_ = bf16[4,4,128,256]{3,2,1,0:T(8,128)(2,1)S(1)} collective-permute-done((bf16[4,4,128,256]{3,2,1,0:T(8,128)(2,1)S(1)}, bf16[4,4,128,256]{3,2,1,0:T(8,128)(2,1)S(1)}, u32[]{:S(2)}, u32[]{:S(2)}) %collective-permute-start.16) | collective-permute-done | bytes 1048608 | tf_op jit(solution)/shard_map/ppermute | solution.py:444
  60.1 2.7 %collective-permute-start.21 = (bf16[2,4,128,256]{3,2,1,0:T(8,128)(2,1)S(1)}, bf16[2,4,128,256]{3,2,1,0:T(8,128)(2,1)S(1)}, u32[]{:S(2)}, u32[]{:S(2)}) collective-permute-start(bf16[2,4,128,256]{3,2,1,0:T(8,128)(2,1)S(1)} %slice.17), channel_id=1, source_target_pairs={{0,3},{1,0},{2,1},{3,2},{4,100},{5,101},{6,102},{7,103},{8,11},{9,... | collective-permute-start | bytes 1572872 | tf_op jit(solution)/shard_map/ppermute | solution.py:444
  64.0 2.1 %collective-permute-start.13 = (bf16[4,128,256]{2,1,0:T(8,128)(2,1)S(1)}, bf16[4,128,256]{2,1,0:T(8,128)(2,1)S(1)}, u32[]{:S(2)}, u32[]{:S(2)}) collective-permute-start(bf16[4,128,256]{2,1,0:T(8,128)(2,1)S(1)} %shard_map.99.refs_0_), channel_id=1, source_target_pairs={{0,16},{1,17},{2,18},{3,19},{4,6},{5,7},{6,4},{7,5},{8,24},{9,25},... | collective-permute-start | bytes 786440 | tf_op jit(solution)/shard_map/ppermute | solution.py:444
  67.4 2.8 %collective-permute-done.14.refs_3_ = bf16[4,128,256]{2,1,0:T(8,128)(2,1)S(1)} collective-permute-done((bf16[4,128,256]{2,1,0:T(8,128)(2,1)S(1)}, bf16[4,128,256]{2,1,0:T(8,128)(2,1)S(1)}, u32[]{:S(2)}, u32[]{:S(2)}) %collective-permute-start.14) | collective-permute-done | bytes 262176 | tf_op jit(solution)/shard_map/ppermute | solution.py:444
  70.2 6.8 %collective-permute-done.13.refs_2_ = bf16[4,128,256]{2,1,0:T(8,128)(2,1)S(1)} collective-permute-done((bf16[4,128,256]{2,1,0:T(8,128)(2,1)S(1)}, bf16[4,128,256]{2,1,0:T(8,128)(2,1)S(1)}, u32[]{:S(2)}, u32[]{:S(2)}) %collective-permute-start.13) | collective-permute-done | bytes 262176 | tf_op jit(solution)/shard_map/ppermute | solution.py:444
  80.9 19.9 %shard_map.101 = (bf16[2,512,1024]{2,1,0:T(8,128)(2,1)S(1)}, bf16[2,512,1024]{2,1,0:T(8,128)(2,1)S(1)}, bf16[2,176,512]{2,1,0:T(8,128)(2,1)S(1)}, bf16[2,176,512...) custom-call(s32[8,4]{1,0:T(8,128)S(1)} %copy-done.9, ...), custom_call_target="tpu_custom_call" | custom-call | flops 12000000000 | bytes 24000000 | tf_op jit(solution)/shard_map/pallas_call | solution.py:160
  102.1 5.3 %collective-permute-start.24 = (bf16[2,176,512]{2,1,0:T(8,128)(2,1)S(1)}, bf16[2,176,512]{2,1,0:T(8,128)(2,1)S(1)}, u32[]{:S(2)}, u32[]{:S(2)}) collective-permute-start(bf16[2,176,512]{2,1,0:T(8,128)(2,1)S(1)} %get-tuple-element.58), channel_id=1, source_target_pairs={{4,8},{12,16},{20,24},{28,32},{36,40},{44,48},{52,56},{60,64},{68,... | collective-permute-start | bytes 1081352 | tf_op jit(solution)/shard_map/ppermute | solution.py:500
  107.3 2.5 %collective-permute-start.27 = (bf16[4,4,128,256]{3,2,1,0:T(8,128)(2,1)S(1)}, bf16[4,4,128,256]{3,2,1,0:T(8,128)(2,1)S(1)}, u32[]{:S(2)}, u32[]{:S(2)}) collective-permute-start(bf16[4,4,128,256]{3,2,1,0:T(8,128)(2,1)S(1)} %get-tuple-element.64), channel_id=1, source_target_pairs={{0,1},{1,2},{2,3},{3,0},{4,36},{5,37},{6,38},{7,39},{8,9},{9,10},{... | collective-permute-start | bytes 3145736 | tf_op jit(solution)/shard_map/ppermute | solution.py:401
  111.7 19.9 %shard_map.102 = (bf16[2,512,1024]{2,1,0:T(8,128)(2,1)S(1)}, bf16[2,512,1024]{2,1,0:T(8,128)(2,1)S(1)}, bf16[2,176,512]{2,1,0:T(8,128)(2,1)S(1)}, bf16[2,176,512...) custom-call(s32[8,4]{1,0:T(8,128)S(1)} %copy-done.9, ...), custom_call_target="tpu_custom_call", output_to_operand_aliasing={{0}: (16, {}), {1}: (17, {})} | custom-call | flops 12000000000 | bytes 24000000 | tf_op jit(solution)/shard_map/pallas_call | solution.py:160
  131.7 2.1 %collective-permute-start.34 = (bf16[2,4,128,256]{3,2,1,0:T(8,128)(2,1)S(1)}, bf16[2,4,128,256]{3,2,1,0:T(8,128)(2,1)S(1)}, u32[]{:S(2)}, u32[]{:S(2)}) collective-permute-start(bf16[2,4,128,256]{3,2,1,0:T(8,128)(2,1)S(1)} %get-tuple-element.75), channel_id=1, source_target_pairs={{0,3},{1,0},{2,1},{3,2},{4,100},{5,101},{6,102},{7,103},{8,11},{9,... | collective-permute-start | bytes 1572872 | tf_op jit(solution)/shard_map/ppermute | solution.py:470
  134.4 5.5 %collective-permute-done.29.refs_3_ = bf16[4,4,128,256]{3,2,1,0:T(8,128)(2,1)S(1)} collective-permute-done((bf16[4,4,128,256]{3,2,1,0:T(8,128)(2,1)S(1)}, bf16[4,4,128,256]{3,2,1,0:T(8,128)(2,1)S(1)}, u32[]{:S(2)}, u32[]{:S(2)}) %collective-permute-start.29) | collective-permute-done | bytes 1048608 | tf_op jit(solution)/shard_map/ppermute | solution.py:401
  141.1 4.2 %collective-permute-done.33.got_a = bf16[2,4,128,256]{3,2,1,0:T(8,128)(2,1)S(1)} collective-permute-done((bf16[2,4,128,256]{3,2,1,0:T(8,128)(2,1)S(1)}, bf16[2,4,128,256]{3,2,1,0:T(8,128)(2,1)S(1)}, u32[]{:S(2)}, u32[]{:S(2)}) %collective-permute-start.33) | collective-permute-done | bytes 524320 | tf_op jit(solution)/shard_map/ppermute | solution.py:469
  146.4 1.9 %collective-permute-start.36 = (bf16[4,4,128,256]{3,2,1,0:T(8,128)(2,1)S(1)}, bf16[4,4,128,256]{3,2,1,0:T(8,128)(2,1)S(1)}, u32[]{:S(2)}, u32[]{:S(2)}) collective-permute-start(bf16[4,4,128,256]{3,2,1,0:T(8,128)(2,1)S(1)} %get-tuple-element.77), channel_id=1, source_target_pairs={{0,3},{1,0},{2,1},{3,2},{4,100},{5,101},{6,102},{7,103},{8,11},{9,... | collective-permute-start | bytes 3145736 | tf_op jit(solution)/shard_map/ppermute | solution.py:472
  148.4 2.7 %collective-permute-start.31 = (bf16[4,128,256]{2,1,0:T(8,128)(2,1)S(1)}, bf16[4,128,256]{2,1,0:T(8,128)(2,1)S(1)}, u32[]{:S(2)}, u32[]{:S(2)}) collective-permute-start(bf16[4,128,256]{2,1,0:T(8,128)(2,1)S(1)} %get-tuple-element.70), channel_id=1, source_target_pairs={{0,24},{1,25},{2,26},{3,27},{4,7},{5,4},{6,5},{7,6},{8,0},{9,1},{1... | collective-permute-start | bytes 786440 | tf_op jit(solution)/shard_map/ppermute | solution.py:401
  151.1 6.9 %collective-permute-done.30.refs_3_.refs_1_ = bf16[4,128,256]{2,1,0:T(8,128)(2,1)S(1)} collective-permute-done((bf16[4,128,256]{2,1,0:T(8,128)(2,1)S(1)}, bf16[4,128,256]{2,1,0:T(8,128)(2,1)S(1)}, u32[]{:S(2)}, u32[]{:S(2)}) %collective-permute-start.30) | collective-permute-done | bytes 262176 | tf_op jit(solution)/shard_map/ppermute | solution.py:401
  159.4 5.4 %collective-permute-done.32.refs_5_.refs_3_ = bf16[4,128,256]{2,1,0:T(8,128)(2,1)S(1)} collective-permute-done((bf16[4,128,256]{2,1,0:T(8,128)(2,1)S(1)}, bf16[4,128,256]{2,1,0:T(8,128)(2,1)S(1)}, u32[]{:S(2)}, u32[]{:S(2)}) %collective-permute-start.32) | collective-permute-done | bytes 262176 | tf_op jit(solution)/shard_map/ppermute | solution.py:401
  164.8 1.9 collective-permute-start.26
  168.2 2.0 %collective-permute-start.38 = (bf16[4,128,256]{2,1,0:T(8,128)(2,1)S(1)}, bf16[4,128,256]{2,1,0:T(8,128)(2,1)S(1)}, u32[]{:S(2)}, u32[]{:S(2)}) collective-permute-start(bf16[4,128,256]{2,1,0:T(8,128)(2,1)S(1)} %get-tuple-element.80), channel_id=1, source_target_pairs={{0,24},{1,25},{2,26},{3,27},{4,7},{5,4},{6,5},{7,6},{8,0},{9,1},{1... | collective-permute-start | bytes 786440 | tf_op jit(solution)/shard_map/ppermute | solution.py:401
  170.2 3.6 %collective-permute-done.26.refs_5_.refs_9_ = bf16[2,176,512]{2,1,0:T(8,128)(2,1)S(1)} collective-permute-done((bf16[2,176,512]{2,1,0:T(8,128)(2,1)S(1)}, bf16[2,176,512]{2,1,0:T(8,128)(2,1)S(1)}, u32[]{:S(2)}, u32[]{:S(2)}) %collective-permute-start.26) | collective-permute-done | bytes 360480 | tf_op jit(solution)/shard_map/ppermute | solution.py:504
  174.3 2.1 %collective-permute-done.38.refs_6_ = bf16[4,128,256]{2,1,0:T(8,128)(2,1)S(1)} collective-permute-done((bf16[4,128,256]{2,1,0:T(8,128)(2,1)S(1)}, bf16[4,128,256]{2,1,0:T(8,128)(2,1)S(1)}, u32[]{:S(2)}, u32[]{:S(2)}) %collective-permute-start.38) | collective-permute-done | bytes 262176 | tf_op jit(solution)/shard_map/ppermute | solution.py:401
  178.7 3.4 %collective-permute-start.41 = (bf16[128,512]{1,0:T(8,128)(2,1)S(1)}, bf16[128,512]{1,0:T(8,128)(2,1)S(1)}, u32[]{:S(2)}, u32[]{:S(2)}) collective-permute-start(bf16[128,512]{1,0:T(8,128)(2,1)S(1)} %get-tuple-element.84), channel_id=1, source_target_pairs={{0,96},{1,97},{2,98},{3,99},{4,28},{5,29},{6,30},{7,31},{8,104},{9... | collective-permute-start | bytes 393224 | tf_op jit(solution)/shard_map/ppermute | solution.py:401
  183.2 3.4 %shard_map.103 = (bf16[512,2048]{1,0:T(8,128)(2,1)}, bf16[512,2048]{1,0:T(8,128)(2,1)}, f32[8,128]{1,0:T(8,128)S(1)}) custom-call(s32[4]{0:T(128)S(1)} %copy-done.6, bf16[2,512,1024]{2,1,0:T(8,128)(2,1)S(1)} %get-tuple-element.55.refs_0_, bf16[2,512,1024]{2,1,0:T(8,128)(2,1)S(1)} %collective-permute-done.22.refs_1_, ...), custom_call_target="tpu_custom_call" | custom-call | tf_op jit(solution)/shard_map/pallas_call | solution.py:362
  188.0 4.3 %collective-permute-start.43 = (f32[64,512]{1,0:T(8,128)S(1)}, f32[64,512]{1,0:T(8,128)S(1)}, u32[]{:S(2)}, u32[]{:S(2)}) collective-permute-start(f32[64,512]{1,0:T(8,128)S(1)} %get-tuple-element.88), channel_id=1, source_target_pairs={{0,4},{4,0},{1,5},{5,1},{2,6},{6,2},{3,7},{7,3},{8,12},{12,8},{9,1... | collective-permute-start | bytes 393224 | tf_op jit(solution)/shard_map/ppermute | solution.py:376
  (97 shorter events, 38.7 us)
Async XLA Ops:
  0.6 13.2 %collective-permute-start = (bf16[512,2048]{1,0:T(8,128)(2,1)}, bf16[512,2048]{1,0:T(8,128)(2,1)S(1)}, u32[]{:S(2)}, u32[]{:S(2)}) collective-permute-start(bf16[512,2048]{1,0:T(8,128)(2,1)} %a_ref.1), channel_id=1, source_target_pairs={{0,4},{4,0},{1,5},{5,1},{2,6},{6,2},{3,7},{7,3},{8,12},{12,8},{9,1... | collective-permute-start | bytes 6291464 | tf_op jit(solution)/shard_map/ppermute | solution.py:376
  2.1 11.7 %collective-permute-start.2 = (bf16[512,2048]{1,0:T(8,128)(2,1)}, bf16[512,2048]{1,0:T(8,128)(2,1)}, u32[]{:S(2)}, u32[]{:S(2)}) collective-permute-start(bf16[512,2048]{1,0:T(8,128)(2,1)} %refs_4_.1), channel_id=1, source_target_pairs={{0,4},{4,0},{1,5},{5,1},{2,6},{6,2},{3,7},{7,3},{8,12},{12,8},{9,1... | collective-permute-start | bytes 6291464 | tf_op jit(solution)/shard_map/ppermute | solution.py:376
  2.2 11.6 %collective-permute-start.3 = (bf16[512,2048]{1,0:T(8,128)(2,1)}, bf16[512,2048]{1,0:T(8,128)(2,1)}, u32[]{:S(2)}, u32[]{:S(2)}) collective-permute-start(bf16[512,2048]{1,0:T(8,128)(2,1)} %refs_8_.1), channel_id=1, source_target_pairs={{0,4},{4,0},{1,5},{5,1},{2,6},{6,2},{3,7},{7,3},{8,12},{12,8},{9,1... | collective-permute-start | bytes 6291464 | tf_op jit(solution)/shard_map/ppermute | solution.py:376
  7.9 18.2 %collective-permute-start.7 = (bf16[176,2048]{1,0:T(8,128)(2,1)}, bf16[176,2048]{1,0:T(8,128)(2,1)S(1)}, u32[]{:S(2)}, u32[]{:S(2)}) collective-permute-start(bf16[176,2048]{1,0:T(8,128)(2,1)} %get-tuple-element.51), channel_id=1, source_target_pairs={{8,0},{16,8},{24,16},{32,24},{40,32},{48,40},{56,48},{64,56},{72,6... | collective-permute-start | bytes 2162696 | tf_op jit(solution)/shard_map/ppermute | solution.py:480
  11.3 20.3 %collective-permute-start.8 = (bf16[176,2048]{1,0:T(8,128)(2,1)}, bf16[176,2048]{1,0:T(8,128)(2,1)S(1)}, u32[]{:S(2)}, u32[]{:S(2)}) collective-permute-start(bf16[176,2048]{1,0:T(8,128)(2,1)} %get-tuple-element.52), channel_id=1, source_target_pairs={{8,4},{16,12},{24,20},{32,28},{40,36},{48,44},{56,52},{64,60},{72,... | collective-permute-start | bytes 2162696 | tf_op jit(solution)/shard_map/ppermute | solution.py:481
  20.0 13.4 %collective-permute-start.6 = (bf16[128,512]{1,0:T(8,128)(2,1)S(1)}, bf16[128,512]{1,0:T(8,128)(2,1)S(1)}, u32[]{:S(2)}, u32[]{:S(2)}) collective-permute-start(bf16[128,512]{1,0:T(8,128)(2,1)S(1)} %shard_map.95.refs_0_), channel_id=1, source_target_pairs={{0,32},{1,33},{2,34},{3,35},{4,12},{5,13},{6,14},{7,15},{8,40},{9,... | collective-permute-start | bytes 393224 | tf_op jit(solution)/shard_map/ppermute | solution.py:444
  20.0 13.4 %collective-permute-start.5 = (bf16[128,512]{1,0:T(8,128)(2,1)S(1)}, bf16[128,512]{1,0:T(8,128)(2,1)S(1)}, u32[]{:S(2)}, u32[]{:S(2)}) collective-permute-start(bf16[128,512]{1,0:T(8,128)(2,1)S(1)} %shard_map.95.refs_0_), channel_id=1, source_target_pairs={{0,64},{1,65},{2,66},{3,67},{4,20},{5,21},{6,22},{7,23},{8,72},{9,... | collective-permute-start | bytes 393224 | tf_op jit(solution)/shard_map/ppermute | solution.py:444
  34.7 9.3 %collective-permute-start.10 = (bf16[4,128,256]{2,1,0:T(8,128)(2,1)S(1)}, bf16[4,128,256]{2,1,0:T(8,128)(2,1)S(1)}, u32[]{:S(2)}, u32[]{:S(2)}) collective-permute-start(bf16[4,128,256]{2,1,0:T(8,128)(2,1)S(1)} %shard_map.97.refs_0_), channel_id=1, source_target_pairs={{0,16},{1,17},{2,18},{3,19},{4,6},{5,7},{6,4},{7,5},{8,24},{9,25},... | collective-permute-start | bytes 786440 | tf_op jit(solution)/shard_map/ppermute | solution.py:444
  44.1 15.9 %collective-permute-start.16 = (bf16[4,4,128,256]{3,2,1,0:T(8,128)(2,1)S(1)}, bf16[4,4,128,256]{3,2,1,0:T(8,128)(2,1)S(1)}, u32[]{:S(2)}, u32[]{:S(2)}) collective-permute-start(bf16[4,4,128,256]{3,2,1,0:T(8,128)(2,1)S(1)} %shard_map.98.refs_4_.refs_0_), channel_id=1, source_target_pairs={{0,1},{1,2},{2,3},{3,0},{4,36},{5,37},{6,38},{7,39},{8,9},{9,10},{... | collective-permute-start | bytes 3145736 | tf_op jit(solution)/shard_map/ppermute | solution.py:444
  45.8 14.3 %collective-permute-start.15 = (bf16[4,4,128,256]{3,2,1,0:T(8,128)(2,1)S(1)}, bf16[4,4,128,256]{3,2,1,0:T(8,128)(2,1)S(1)}, u32[]{:S(2)}, u32[]{:S(2)}) collective-permute-start(bf16[4,4,128,256]{3,2,1,0:T(8,128)(2,1)S(1)} %shard_map.98.refs_4_.refs_0_), channel_id=1, source_target_pairs={{0,3},{1,0},{2,1},{3,2},{4,100},{5,101},{6,102},{7,103},{8,11},{9,... | collective-permute-start | bytes 3145736 | tf_op jit(solution)/shard_map/ppermute | solution.py:444
  60.0 20.9 %collective-permute-start.20 = (bf16[2,4,128,256]{3,2,1,0:T(8,128)(2,1)S(1)}, bf16[2,4,128,256]{3,2,1,0:T(8,128)(2,1)S(1)}, u32[]{:S(2)}, u32[]{:S(2)}) collective-permute-start(bf16[2,4,128,256]{3,2,1,0:T(8,128)(2,1)S(1)} %slice.16), channel_id=1, source_target_pairs={{0,1},{1,2},{2,3},{3,0},{4,36},{5,37},{6,38},{7,39},{8,9},{9,10},{... | collective-permute-start | bytes 1572872 | tf_op jit(solution)/shard_map/ppermute | solution.py:444
  60.1 20.7 %collective-permute-start.21 = (bf16[2,4,128,256]{3,2,1,0:T(8,128)(2,1)S(1)}, bf16[2,4,128,256]{3,2,1,0:T(8,128)(2,1)S(1)}, u32[]{:S(2)}, u32[]{:S(2)}) collective-permute-start(bf16[2,4,128,256]{3,2,1,0:T(8,128)(2,1)S(1)} %slice.17), channel_id=1, source_target_pairs={{0,3},{1,0},{2,1},{3,2},{4,100},{5,101},{6,102},{7,103},{8,11},{9,... | collective-permute-start | bytes 1572872 | tf_op jit(solution)/shard_map/ppermute | solution.py:444
  64.0 13.0 %collective-permute-start.13 = (bf16[4,128,256]{2,1,0:T(8,128)(2,1)S(1)}, bf16[4,128,256]{2,1,0:T(8,128)(2,1)S(1)}, u32[]{:S(2)}, u32[]{:S(2)}) collective-permute-start(bf16[4,128,256]{2,1,0:T(8,128)(2,1)S(1)} %shard_map.99.refs_0_), channel_id=1, source_target_pairs={{0,16},{1,17},{2,18},{3,19},{4,6},{5,7},{6,4},{7,5},{8,24},{9,25},... | collective-permute-start | bytes 786440 | tf_op jit(solution)/shard_map/ppermute | solution.py:444
  66.1 11.8 %collective-permute-start.12 = (bf16[4,128,256]{2,1,0:T(8,128)(2,1)S(1)}, bf16[4,128,256]{2,1,0:T(8,128)(2,1)S(1)}, u32[]{:S(2)}, u32[]{:S(2)}) collective-permute-start(bf16[4,128,256]{2,1,0:T(8,128)(2,1)S(1)} %shard_map.99.refs_0_), channel_id=1, source_target_pairs={{0,24},{1,25},{2,26},{3,27},{4,7},{5,4},{6,5},{7,6},{8,0},{9,1},{1... | collective-permute-start | bytes 786440 | tf_op jit(solution)/shard_map/ppermute | solution.py:444
  78.0 29.3 %collective-permute-start.19 = (bf16[4,4,128,256]{3,2,1,0:T(8,128)(2,1)S(1)}, bf16[4,4,128,256]{3,2,1,0:T(8,128)(2,1)S(1)}, u32[]{:S(2)}, u32[]{:S(2)}) collective-permute-start(bf16[4,4,128,256]{3,2,1,0:T(8,128)(2,1)S(1)} %shard_map.100.refs_0_), channel_id=1, source_target_pairs={{0,2},{1,3},{2,0},{3,1},{4,68},{5,69},{6,70},{7,71},{8,10},{9,11},... | collective-permute-start | bytes 3145736 | tf_op jit(solution)/shard_map/ppermute | solution.py:444
  78.1 31.7 %collective-permute-start.18 = (bf16[4,4,128,256]{3,2,1,0:T(8,128)(2,1)S(1)}, bf16[4,4,128,256]{3,2,1,0:T(8,128)(2,1)S(1)}, u32[]{:S(2)}, u32[]{:S(2)}) collective-permute-start(bf16[4,4,128,256]{3,2,1,0:T(8,128)(2,1)S(1)} %shard_map.100.refs_0_), channel_id=1, source_target_pairs={{0,1},{1,2},{2,3},{3,0},{4,36},{5,37},{6,38},{7,39},{8,9},{9,10},{... | collective-permute-start | bytes 3145736 | tf_op jit(solution)/shard_map/ppermute | solution.py:444
  79.6 30.5 %collective-permute-start.17 = (bf16[4,4,128,256]{3,2,1,0:T(8,128)(2,1)S(1)}, bf16[4,4,128,256]{3,2,1,0:T(8,128)(2,1)S(1)}, u32[]{:S(2)}, u32[]{:S(2)}) collective-permute-start(bf16[4,4,128,256]{3,2,1,0:T(8,128)(2,1)S(1)} %shard_map.100.refs_0_), channel_id=1, source_target_pairs={{0,3},{1,0},{2,1},{3,2},{4,100},{5,101},{6,102},{7,103},{8,11},{9,... | collective-permute-start | bytes 3145736 | tf_op jit(solution)/shard_map/ppermute | solution.py:444
  100.8 30.8 %collective-permute-start.23 = (bf16[2,176,512]{2,1,0:T(8,128)(2,1)S(1)}, bf16[2,176,512]{2,1,0:T(8,128)(2,1)S(1)}, u32[]{:S(2)}, u32[]{:S(2)}) collective-permute-start(bf16[2,176,512]{2,1,0:T(8,128)(2,1)S(1)} %get-tuple-element.57), channel_id=1, source_target_pairs={{0,8},{8,16},{16,24},{24,32},{32,40},{40,48},{48,56},{56,64},{64,7... | collective-permute-start | bytes 1081352 | tf_op jit(solution)/shard_map/ppermute | solution.py:500
  102.1 29.6 %collective-permute-start.24 = (bf16[2,176,512]{2,1,0:T(8,128)(2,1)S(1)}, bf16[2,176,512]{2,1,0:T(8,128)(2,1)S(1)}, u32[]{:S(2)}, u32[]{:S(2)}) collective-permute-start(bf16[2,176,512]{2,1,0:T(8,128)(2,1)S(1)} %get-tuple-element.58), channel_id=1, source_target_pairs={{4,8},{12,16},{20,24},{28,32},{36,40},{44,48},{52,56},{60,64},{68,... | collective-permute-start | bytes 1081352 | tf_op jit(solution)/shard_map/ppermute | solution.py:500
  107.3 26.5 %collective-permute-start.27 = (bf16[4,4,128,256]{3,2,1,0:T(8,128)(2,1)S(1)}, bf16[4,4,128,256]{3,2,1,0:T(8,128)(2,1)S(1)}, u32[]{:S(2)}, u32[]{:S(2)}) collective-permute-start(bf16[4,4,128,256]{3,2,1,0:T(8,128)(2,1)S(1)} %get-tuple-element.64), channel_id=1, source_target_pairs={{0,1},{1,2},{2,3},{3,0},{4,36},{5,37},{6,38},{7,39},{8,9},{9,10},{... | collective-permute-start | bytes 3145736 | tf_op jit(solution)/shard_map/ppermute | solution.py:401
  109.8 24.6 %collective-permute-start.28 = (bf16[4,4,128,256]{3,2,1,0:T(8,128)(2,1)S(1)}, bf16[4,4,128,256]{3,2,1,0:T(8,128)(2,1)S(1)}, u32[]{:S(2)}, u32[]{:S(2)}) collective-permute-start(bf16[4,4,128,256]{3,2,1,0:T(8,128)(2,1)S(1)} %get-tuple-element.65), channel_id=1, source_target_pairs={{0,3},{1,0},{2,1},{3,2},{4,100},{5,101},{6,102},{7,103},{8,11},{9,... | collective-permute-start | bytes 3145736 | tf_op jit(solution)/shard_map/ppermute | solution.py:401
  110.1 29.7 %collective-permute-start.29 = (bf16[4,4,128,256]{3,2,1,0:T(8,128)(2,1)S(1)}, bf16[4,4,128,256]{3,2,1,0:T(8,128)(2,1)S(1)}, u32[]{:S(2)}, u32[]{:S(2)}) collective-permute-start(bf16[4,4,128,256]{3,2,1,0:T(8,128)(2,1)S(1)} %get-tuple-element.66), channel_id=1, source_target_pairs={{0,2},{1,3},{2,0},{3,1},{4,68},{5,69},{6,70},{7,71},{8,10},{9,11},... | collective-permute-start | bytes 3145736 | tf_op jit(solution)/shard_map/ppermute | solution.py:401
  131.6 51.6 %collective-permute-start.22 = (bf16[2,512,1024]{2,1,0:T(8,128)(2,1)S(1)}, bf16[2,512,1024]{2,1,0:T(8,128)(2,1)S(1)}, u32[]{:S(2)}, u32[]{:S(2)}) collective-permute-start(bf16[2,512,1024]{2,1,0:T(8,128)(2,1)S(1)} %get-tuple-element.56), channel_id=1, source_target_pairs={{0,4},{4,0},{1,5},{5,1},{2,6},{6,2},{3,7},{7,3},{8,12},{12,8},{9,1... | collective-permute-start | bytes 6291464 | tf_op jit(solution)/shard_map/ppermute | solution.py:376
  131.7 9.5 %collective-permute-start.34 = (bf16[2,4,128,256]{3,2,1,0:T(8,128)(2,1)S(1)}, bf16[2,4,128,256]{3,2,1,0:T(8,128)(2,1)S(1)}, u32[]{:S(2)}, u32[]{:S(2)}) collective-permute-start(bf16[2,4,128,256]{3,2,1,0:T(8,128)(2,1)S(1)} %get-tuple-element.75), channel_id=1, source_target_pairs={{0,3},{1,0},{2,1},{3,2},{4,100},{5,101},{6,102},{7,103},{8,11},{9,... | collective-permute-start | bytes 1572872 | tf_op jit(solution)/shard_map/ppermute | solution.py:470
  133.8 11.5 %collective-permute-start.33 = (bf16[2,4,128,256]{3,2,1,0:T(8,128)(2,1)S(1)}, bf16[2,4,128,256]{3,2,1,0:T(8,128)(2,1)S(1)}, u32[]{:S(2)}, u32[]{:S(2)}) collective-permute-start(bf16[2,4,128,256]{3,2,1,0:T(8,128)(2,1)S(1)} %get-tuple-element.67.refs_4_), channel_id=1, source_target_pairs={{0,1},{1,2},{2,3},{3,0},{4,36},{5,37},{6,38},{7,39},{8,9},{9,10},{... | collective-permute-start | bytes 1572872 | tf_op jit(solution)/shard_map/ppermute | solution.py:469
  145.6 21.1 %collective-permute-start.35 = (bf16[4,4,128,256]{3,2,1,0:T(8,128)(2,1)S(1)}, bf16[4,4,128,256]{3,2,1,0:T(8,128)(2,1)S(1)}, u32[]{:S(2)}, u32[]{:S(2)}) collective-permute-start(bf16[4,4,128,256]{3,2,1,0:T(8,128)(2,1)S(1)} %get-tuple-element.76), channel_id=1, source_target_pairs={{0,1},{1,2},{2,3},{3,0},{4,36},{5,37},{6,38},{7,39},{8,9},{9,10},{... | collective-permute-start | bytes 3145736 | tf_op jit(solution)/shard_map/ppermute | solution.py:472
  146.4 20.3 %collective-permute-start.36 = (bf16[4,4,128,256]{3,2,1,0:T(8,128)(2,1)S(1)}, bf16[4,4,128,256]{3,2,1,0:T(8,128)(2,1)S(1)}, u32[]{:S(2)}, u32[]{:S(2)}) collective-permute-start(bf16[4,4,128,256]{3,2,1,0:T(8,128)(2,1)S(1)} %get-tuple-element.77), channel_id=1, source_target_pairs={{0,3},{1,0},{2,1},{3,2},{4,100},{5,101},{6,102},{7,103},{8,11},{9,... | collective-permute-start | bytes 3145736 | tf_op jit(solution)/shard_map/ppermute | solution.py:472
  148.4 9.6 %collective-permute-start.30 = (bf16[4,128,256]{2,1,0:T(8,128)(2,1)S(1)}, bf16[4,128,256]{2,1,0:T(8,128)(2,1)S(1)}, u32[]{:S(2)}, u32[]{:S(2)}) collective-permute-start(bf16[4,128,256]{2,1,0:T(8,128)(2,1)S(1)} %get-tuple-element.69), channel_id=1, source_target_pairs={{0,8},{1,9},{2,10},{3,11},{4,5},{5,6},{6,7},{7,4},{8,16},{9,17},{1... | collective-permute-start | bytes 786440 | tf_op jit(solution)/shard_map/ppermute | solution.py:401
  148.4 9.7 %collective-permute-start.31 = (bf16[4,128,256]{2,1,0:T(8,128)(2,1)S(1)}, bf16[4,128,256]{2,1,0:T(8,128)(2,1)S(1)}, u32[]{:S(2)}, u32[]{:S(2)}) collective-permute-start(bf16[4,128,256]{2,1,0:T(8,128)(2,1)S(1)} %get-tuple-element.70), channel_id=1, source_target_pairs={{0,24},{1,25},{2,26},{3,27},{4,7},{5,4},{6,5},{7,6},{8,0},{9,1},{1... | collective-permute-start | bytes 786440 | tf_op jit(solution)/shard_map/ppermute | solution.py:401
  158.1 12.1 %collective-permute-start.25 = (bf16[2,176,512]{2,1,0:T(8,128)(2,1)S(1)}, bf16[2,176,512]{2,1,0:T(8,128)(2,1)S(1)}, u32[]{:S(2)}, u32[]{:S(2)}) collective-permute-start(bf16[2,176,512]{2,1,0:T(8,128)(2,1)S(1)} %get-tuple-element.59), channel_id=1, source_target_pairs={{0,8},{8,16},{16,24},{24,32},{32,40},{40,48},{48,56},{56,64},{64,7... | collective-permute-start | bytes 1081352 | tf_op jit(solution)/shard_map/ppermute | solution.py:504
  164.8 9.0 %collective-permute-start.26 = (bf16[2,176,512]{2,1,0:T(8,128)(2,1)S(1)}, bf16[2,176,512]{2,1,0:T(8,128)(2,1)S(1)}, u32[]{:S(2)}, u32[]{:S(2)}) collective-permute-start(bf16[2,176,512]{2,1,0:T(8,128)(2,1)S(1)} %get-tuple-element.60), channel_id=1, source_target_pairs={{4,8},{12,16},{20,24},{28,32},{36,40},{44,48},{52,56},{60,64},{68,... | collective-permute-start | bytes 1081352 | tf_op jit(solution)/shard_map/ppermute | solution.py:504
  177.2 9.4 %collective-permute-start.40 = (bf16[128,512]{1,0:T(8,128)(2,1)S(1)}, bf16[128,512]{1,0:T(8,128)(2,1)S(1)}, u32[]{:S(2)}, u32[]{:S(2)}) collective-permute-start(bf16[128,512]{1,0:T(8,128)(2,1)S(1)} %get-tuple-element.83), channel_id=1, source_target_pairs={{0,32},{1,33},{2,34},{3,35},{4,12},{5,13},{6,14},{7,15},{8,40},{9,... | collective-permute-start | bytes 393224 | tf_op jit(solution)/shard_map/ppermute | solution.py:401
  (22 other events, 199.2 us)

commit v14 on v13

--- a/solution.py
+++ b/solution.py
@@ -398,7 +398,7 @@
 
 
 def exchange(parts, phase):
-    return [parts[0]] + [lax.ppermute(parts[r], ALL, shift(phase, r)) for r in (1, 3, 2)]
+    return [parts[0]] + [lax.ppermute(parts[r], ALL, shift(phase, r)) for r in (2, 1, 3)]
 
 
 def join_kernel(cols, *refs):

time: 194 us -> 192 us (0.990)
    ppermute x1, waiting for transfers between devices: 0.43 us -> 3.21 us  [scatter_ring(): got_b = lax.ppermute(far_b, ALL, shift(0, -1))]
    ppermute x1, waiting for transfers between devices: 4.18 us -> 1.79 us  [scatter_ring(): got_a = lax.ppermute(far_a, ALL, shift(0, 1))]
  transfers between devices with their start and end apart: 44 -> 44, of which waited for: 20 -> 19; matrix products, arithmetic and copies ran while one was open for 1% -> 1% of each run, Pallas kernels for 27% -> 27%
where the time goes in v14:
time: 192 us; the launch traced here: 191 us
  starting transfers between devices  67.1 us (35%)
  waiting for transfers between devices  65.9 us (34%)
  Pallas kernels  52.3 us (27%)
  local copies, waits for them, and re-layouts  2.68 us (1%)
  other arithmetic  2.21 us (1%)
    pallas_call x2, Pallas kernels, run_main(): pl.pallas_call(functools.partial(main_kernel, len(weights), len(before)),...  39.7 us
    ppermute x16, waiting for transfers between devices, ring(): return lax.ppermute(value, ALL, shift(phase, -amount))  31.1 us
    ppermute x16, starting transfers between devices, ring(): return lax.ppermute(value, ALL, shift(phase, -amount))  24.8 us
    ppermute x12, waiting for transfers between devices, exchange(): lax.ppermute(parts[r], ALL, shift(phase, r))  21.3 us
    ppermute x12, starting transfers between devices, exchange(): lax.ppermute(parts[r], ALL, shift(phase, r))  15.1 us
    ppermute x4, starting transfers between devices, body(): lax.ppermute(part, DP, pairs)  9.7 us
    ppermute x6, starting transfers between devices, swap(): return lax.ppermute(value, 'c', [(0, 1), (1, 0)])  5.8 us
    ppermute x1, waiting for transfers between devices, body(): sent_b = lax.ppermute(leave_b, DP, SEND_B)  5.47 us
  transfers between devices with their start and end apart: 44, of which 19 were waited for; matrix products, arithmetic and copies ran while one was open for 1% of the time, Pallas kernels for 27%

profile of v14, /device:TPU:1, one launch (start us, length us, event | category | flops | bytes accessed | tf_op | source)
XLA Modules:
  0.0 191.2 jit_solution(2760829448796478779)
XLA Ops:
  4.3 3.6 %shard_map.94 = (s32[8,4]{1,0:T(8,128)}, s32[4]{0:T(128)}, bf16[176,2048]{1,0:T(8,128)(2,1)}, bf16[176,2048]{1,0:T(8,128)(2,1)}) custom-call(s32[4]{0:T(128)} %pad_add_fusion.me, s32[4,128]{1,0:T(4,128)} %bitcast.7, s32[4,128]{1,0:T(4,128)} %bitcast.8, s32[4,128]{1,0:T(4,128)} %bitcast.9, bf16[512,2048]{1,0:T(8,128)(2,1)} %refs_4_.1, bf16[512,2048]{1,0:T(8,128)(2,1)} %refs_8_.1), custom_call_target="tpu_custom_call" | custom-call | tf_op jit(solution)/shard_map/pallas_call | solution.py:305
  7.9 3.3 %collective-permute-start.7 = (bf16[176,2048]{1,0:T(8,128)(2,1)}, bf16[176,2048]{1,0:T(8,128)(2,1)S(1)}, u32[]{:S(2)}, u32[]{:S(2)}) collective-permute-start(bf16[176,2048]{1,0:T(8,128)(2,1)} %get-tuple-element.51), channel_id=1, source_target_pairs={{8,0},{16,8},{24,16},{32,24},{40,32},{48,40},{56,48},{64,56},{72,6... | collective-permute-start | bytes 2162696 | tf_op jit(solution)/shard_map/ppermute | solution.py:480
  11.3 2.5 %collective-permute-start.8 = (bf16[176,2048]{1,0:T(8,128)(2,1)}, bf16[176,2048]{1,0:T(8,128)(2,1)S(1)}, u32[]{:S(2)}, u32[]{:S(2)}) collective-permute-start(bf16[176,2048]{1,0:T(8,128)(2,1)} %get-tuple-element.52), channel_id=1, source_target_pairs={{8,4},{16,12},{24,20},{32,28},{40,36},{48,44},{56,52},{64,60},{72,... | collective-permute-start | bytes 2162696 | tf_op jit(solution)/shard_map/ppermute | solution.py:481
  15.0 5.0 %collective-permute-start.4 = (bf16[128,512]{1,0:T(8,128)(2,1)S(1)}, bf16[128,512]{1,0:T(8,128)(2,1)S(1)}, u32[]{:S(2)}, u32[]{:S(2)}) collective-permute-start(bf16[128,512]{1,0:T(8,128)(2,1)S(1)} %shard_map.95.refs_0_), channel_id=1, source_target_pairs={{0,96},{1,97},{2,98},{3,99},{4,28},{5,29},{6,30},{7,31},{8,104},{9... | collective-permute-start | bytes 393224 | tf_op jit(solution)/shard_map/ppermute | solution.py:444
  22.0 2.1 %shard_map.96 = (bf16[1024,2048]{1,0:T(8,128)(2,1)S(1)}, bf16[2048,1024]{1,0:T(8,128)(2,1)S(1)}, f32[8,128]{1,0:T(8,128)S(1)}) custom-call(bf16[512,2048]{1,0:T(8,128)(2,1)S(1)} %copy-done.2, bf16[512,2048]{1,0:T(8,128)(2,1)S(1)} %collective-permute-done.refs_1_.b_ref, bf16[128,512]{1,0:T(8,128)(2,1)S(1)} %collective-permute-done.4.refs_0_.refs_1_), custom_call_target="tpu_custom_call" | custom-call | tf_op jit(solution)/shard_map/pallas_call | solution.py:327
  24.1 2.0 %copy-done.8 = bf16[2048,1024]{1,0:T(8,128)(2,1)} copy-done((bf16[2048,1024]{1,0:T(8,128)(2,1)}, bf16[2048,1024]{1,0:T(8,128)(2,1)S(1)}, u32[]{:S(2)}) %copy-start.8) | copy-done | bytes 4194328
  26.1 5.5 %collective-permute-done.8.refs_6_.refs_8_.refs_12_.refs_7_.refs_11_ = bf16[176,2048]{1,0:T(8,128)(2,1)S(1)} collective-permute-done((bf16[176,2048]{1,0:T(8,128)(2,1)}, bf16[176,2048]{1,0:T(8,128)(2,1)S(1)}, u32[]{:S(2)}, u32[]{:S(2)}) %collective-permute-start.8) | collective-permute-done | bytes 720928 | tf_op jit(solution)/shard_map/ppermute | solution.py:481
  31.6 1.8 collective-permute-done.6.refs_3_
  34.7 2.5 %collective-permute-start.10 = (bf16[4,128,256]{2,1,0:T(8,128)(2,1)S(1)}, bf16[4,128,256]{2,1,0:T(8,128)(2,1)S(1)}, u32[]{:S(2)}, u32[]{:S(2)}) collective-permute-start(bf16[4,128,256]{2,1,0:T(8,128)(2,1)S(1)} %shard_map.97.refs_0_), channel_id=1, source_target_pairs={{0,16},{1,17},{2,18},{3,19},{4,6},{5,7},{6,4},{7,5},{8,24},{9,25},... | collective-permute-start | bytes 786440 | tf_op jit(solution)/shard_map/ppermute | solution.py:444
  39.9 4.1 %collective-permute-done.10.refs_2_ = bf16[4,128,256]{2,1,0:T(8,128)(2,1)S(1)} collective-permute-done((bf16[4,128,256]{2,1,0:T(8,128)(2,1)S(1)}, bf16[4,128,256]{2,1,0:T(8,128)(2,1)S(1)}, u32[]{:S(2)}, u32[]{:S(2)}) %collective-permute-start.10) | collective-permute-done | bytes 262176 | tf_op jit(solution)/shard_map/ppermute | solution.py:444
  47.5 12.4 %collective-permute-done.16.refs_5_.refs_2_ = bf16[4,4,128,256]{3,2,1,0:T(8,128)(2,1)S(1)} collective-permute-done((bf16[4,4,128,256]{3,2,1,0:T(8,128)(2,1)S(1)}, bf16[4,4,128,256]{3,2,1,0:T(8,128)(2,1)S(1)}, u32[]{:S(2)}, u32[]{:S(2)}) %collective-permute-start.16) | collective-permute-done | bytes 1048608 | tf_op jit(solution)/shard_map/ppermute | solution.py:444
  60.1 2.7 %collective-permute-start.21 = (bf16[2,4,128,256]{3,2,1,0:T(8,128)(2,1)S(1)}, bf16[2,4,128,256]{3,2,1,0:T(8,128)(2,1)S(1)}, u32[]{:S(2)}, u32[]{:S(2)}) collective-permute-start(bf16[2,4,128,256]{3,2,1,0:T(8,128)(2,1)S(1)} %slice.17), channel_id=1, source_target_pairs={{0,3},{1,0},{2,1},{3,2},{4,100},{5,101},{6,102},{7,103},{8,11},{9,... | collective-permute-start | bytes 1572872 | tf_op jit(solution)/shard_map/ppermute | solution.py:444
  64.0 2.1 %collective-permute-start.13 = (bf16[4,128,256]{2,1,0:T(8,128)(2,1)S(1)}, bf16[4,128,256]{2,1,0:T(8,128)(2,1)S(1)}, u32[]{:S(2)}, u32[]{:S(2)}) collective-permute-start(bf16[4,128,256]{2,1,0:T(8,128)(2,1)S(1)} %shard_map.99.refs_0_), channel_id=1, source_target_pairs={{0,16},{1,17},{2,18},{3,19},{4,6},{5,7},{6,4},{7,5},{8,24},{9,25},... | collective-permute-start | bytes 786440 | tf_op jit(solution)/shard_map/ppermute | solution.py:444
  67.4 2.8 %collective-permute-done.14.refs_3_ = bf16[4,128,256]{2,1,0:T(8,128)(2,1)S(1)} collective-permute-done((bf16[4,128,256]{2,1,0:T(8,128)(2,1)S(1)}, bf16[4,128,256]{2,1,0:T(8,128)(2,1)S(1)}, u32[]{:S(2)}, u32[]{:S(2)}) %collective-permute-start.14) | collective-permute-done | bytes 262176 | tf_op jit(solution)/shard_map/ppermute | solution.py:444
  70.2 6.8 %collective-permute-done.13.refs_2_ = bf16[4,128,256]{2,1,0:T(8,128)(2,1)S(1)} collective-permute-done((bf16[4,128,256]{2,1,0:T(8,128)(2,1)S(1)}, bf16[4,128,256]{2,1,0:T(8,128)(2,1)S(1)}, u32[]{:S(2)}, u32[]{:S(2)}) %collective-permute-start.13) | collective-permute-done | bytes 262176 | tf_op jit(solution)/shard_map/ppermute | solution.py:444
  80.9 19.9 %shard_map.101 = (bf16[2,512,1024]{2,1,0:T(8,128)(2,1)S(1)}, bf16[2,512,1024]{2,1,0:T(8,128)(2,1)S(1)}, bf16[2,176,512]{2,1,0:T(8,128)(2,1)S(1)}, bf16[2,176,512...) custom-call(s32[8,4]{1,0:T(8,128)S(1)} %copy-done.9, ...), custom_call_target="tpu_custom_call" | custom-call | flops 12000000000 | bytes 24000000 | tf_op jit(solution)/shard_map/pallas_call | solution.py:160
  102.1 5.2 %collective-permute-start.24 = (bf16[2,176,512]{2,1,0:T(8,128)(2,1)S(1)}, bf16[2,176,512]{2,1,0:T(8,128)(2,1)S(1)}, u32[]{:S(2)}, u32[]{:S(2)}) collective-permute-start(bf16[2,176,512]{2,1,0:T(8,128)(2,1)S(1)} %get-tuple-element.58), channel_id=1, source_target_pairs={{4,8},{12,16},{20,24},{28,32},{36,40},{44,48},{52,56},{60,64},{68,... | collective-permute-start | bytes 1081352 | tf_op jit(solution)/shard_map/ppermute | solution.py:500
  109.9 2.6 %collective-permute-start.29 = (bf16[4,4,128,256]{3,2,1,0:T(8,128)(2,1)S(1)}, bf16[4,4,128,256]{3,2,1,0:T(8,128)(2,1)S(1)}, u32[]{:S(2)}, u32[]{:S(2)}) collective-permute-start(bf16[4,4,128,256]{3,2,1,0:T(8,128)(2,1)S(1)} %get-tuple-element.66), channel_id=1, source_target_pairs={{0,3},{1,0},{2,1},{3,2},{4,100},{5,101},{6,102},{7,103},{8,11},{9,... | collective-permute-start | bytes 3145736 | tf_op jit(solution)/shard_map/ppermute | solution.py:401
  112.5 19.8 %shard_map.102 = (bf16[2,512,1024]{2,1,0:T(8,128)(2,1)S(1)}, bf16[2,512,1024]{2,1,0:T(8,128)(2,1)S(1)}, bf16[2,176,512]{2,1,0:T(8,128)(2,1)S(1)}, bf16[2,176,512...) custom-call(s32[8,4]{1,0:T(8,128)S(1)} %copy-done.9, ...), custom_call_target="tpu_custom_call", output_to_operand_aliasing={{0}: (16, {}), {1}: (17, {})} | custom-call | flops 12000000000 | bytes 24000000 | tf_op jit(solution)/shard_map/pallas_call | solution.py:160
  132.5 2.5 %collective-permute-start.34 = (bf16[2,4,128,256]{3,2,1,0:T(8,128)(2,1)S(1)}, bf16[2,4,128,256]{3,2,1,0:T(8,128)(2,1)S(1)}, u32[]{:S(2)}, u32[]{:S(2)}) collective-permute-start(bf16[2,4,128,256]{3,2,1,0:T(8,128)(2,1)S(1)} %get-tuple-element.75), channel_id=1, source_target_pairs={{0,3},{1,0},{2,1},{3,2},{4,100},{5,101},{6,102},{7,103},{8,11},{9,... | collective-permute-start | bytes 1572872 | tf_op jit(solution)/shard_map/ppermute | solution.py:470
  135.6 2.7 %collective-permute-done.28.refs_2_ = bf16[4,4,128,256]{3,2,1,0:T(8,128)(2,1)S(1)} collective-permute-done((bf16[4,4,128,256]{3,2,1,0:T(8,128)(2,1)S(1)}, bf16[4,4,128,256]{3,2,1,0:T(8,128)(2,1)S(1)}, u32[]{:S(2)}, u32[]{:S(2)}) %collective-permute-start.28) | collective-permute-done | bytes 1048608 | tf_op jit(solution)/shard_map/ppermute | solution.py:401
  139.2 3.2 %collective-permute-done.34.got_b = bf16[2,4,128,256]{3,2,1,0:T(8,128)(2,1)S(1)} collective-permute-done((bf16[2,4,128,256]{3,2,1,0:T(8,128)(2,1)S(1)}, bf16[2,4,128,256]{3,2,1,0:T(8,128)(2,1)S(1)}, u32[]{:S(2)}, u32[]{:S(2)}) %collective-permute-start.34) | collective-permute-done | bytes 524320 | tf_op jit(solution)/shard_map/ppermute | solution.py:470
  148.3 8.5 %collective-permute-done.30.refs_3_.refs_1_ = bf16[4,128,256]{2,1,0:T(8,128)(2,1)S(1)} collective-permute-done((bf16[4,128,256]{2,1,0:T(8,128)(2,1)S(1)}, bf16[4,128,256]{2,1,0:T(8,128)(2,1)S(1)}, u32[]{:S(2)}, u32[]{:S(2)}) %collective-permute-start.30) | collective-permute-done | bytes 262176 | tf_op jit(solution)/shard_map/ppermute | solution.py:401
  156.8 3.5 %collective-permute-done.31.refs_4_.refs_2_ = bf16[4,128,256]{2,1,0:T(8,128)(2,1)S(1)} collective-permute-done((bf16[4,128,256]{2,1,0:T(8,128)(2,1)S(1)}, bf16[4,128,256]{2,1,0:T(8,128)(2,1)S(1)}, u32[]{:S(2)}, u32[]{:S(2)}) %collective-permute-start.31) | collective-permute-done | bytes 262176 | tf_op jit(solution)/shard_map/ppermute | solution.py:401
  161.6 3.0 %collective-permute-done.32.refs_5_.refs_3_ = bf16[4,128,256]{2,1,0:T(8,128)(2,1)S(1)} collective-permute-done((bf16[4,128,256]{2,1,0:T(8,128)(2,1)S(1)}, bf16[4,128,256]{2,1,0:T(8,128)(2,1)S(1)}, u32[]{:S(2)}, u32[]{:S(2)}) %collective-permute-start.32) | collective-permute-done | bytes 262176 | tf_op jit(solution)/shard_map/ppermute | solution.py:401
  164.7 1.9 collective-permute-start.26
  169.7 2.0 %collective-permute-start.39 = (bf16[4,128,256]{2,1,0:T(8,128)(2,1)S(1)}, bf16[4,128,256]{2,1,0:T(8,128)(2,1)S(1)}, u32[]{:S(2)}, u32[]{:S(2)}) collective-permute-start(bf16[4,128,256]{2,1,0:T(8,128)(2,1)S(1)} %get-tuple-element.81), channel_id=1, source_target_pairs={{0,24},{1,25},{2,26},{3,27},{4,7},{5,4},{6,5},{7,6},{8,0},{9,1},{1... | collective-permute-start | bytes 786440 | tf_op jit(solution)/shard_map/ppermute | solution.py:401
  171.7 2.0 %collective-permute-done.26.refs_5_.refs_9_ = bf16[2,176,512]{2,1,0:T(8,128)(2,1)S(1)} collective-permute-done((bf16[2,176,512]{2,1,0:T(8,128)(2,1)S(1)}, bf16[2,176,512]{2,1,0:T(8,128)(2,1)S(1)}, u32[]{:S(2)}, u32[]{:S(2)}) %collective-permute-start.26) | collective-permute-done | bytes 360480 | tf_op jit(solution)/shard_map/ppermute | solution.py:504
  174.4 2.8 %collective-permute-done.38.refs_6_ = bf16[4,128,256]{2,1,0:T(8,128)(2,1)S(1)} collective-permute-done((bf16[4,128,256]{2,1,0:T(8,128)(2,1)S(1)}, bf16[4,128,256]{2,1,0:T(8,128)(2,1)S(1)}, u32[]{:S(2)}, u32[]{:S(2)}) %collective-permute-start.38) | collective-permute-done | bytes 262176 | tf_op jit(solution)/shard_map/ppermute | solution.py:401
  179.2 2.0 %collective-permute-start.41 = (bf16[128,512]{1,0:T(8,128)(2,1)S(1)}, bf16[128,512]{1,0:T(8,128)(2,1)S(1)}, u32[]{:S(2)}, u32[]{:S(2)}) collective-permute-start(bf16[128,512]{1,0:T(8,128)(2,1)S(1)} %get-tuple-element.84), channel_id=1, source_target_pairs={{0,32},{1,33},{2,34},{3,35},{4,12},{5,13},{6,14},{7,15},{8,40},{9,... | collective-permute-start | bytes 393224 | tf_op jit(solution)/shard_map/ppermute | solution.py:401
  181.9 3.4 %shard_map.103 = (bf16[512,2048]{1,0:T(8,128)(2,1)}, bf16[512,2048]{1,0:T(8,128)(2,1)}, f32[8,128]{1,0:T(8,128)S(1)}) custom-call(s32[4]{0:T(128)S(1)} %copy-done.6, bf16[2,512,1024]{2,1,0:T(8,128)(2,1)S(1)} %get-tuple-element.55.refs_0_, bf16[2,512,1024]{2,1,0:T(8,128)(2,1)S(1)} %collective-permute-done.22.refs_1_, ...), custom_call_target="tpu_custom_call" | custom-call | tf_op jit(solution)/shard_map/pallas_call | solution.py:362
  185.9 3.5 %collective-permute-start.43 = (f32[64,512]{1,0:T(8,128)S(1)}, f32[64,512]{1,0:T(8,128)S(1)}, u32[]{:S(2)}, u32[]{:S(2)}) collective-permute-start(f32[64,512]{1,0:T(8,128)S(1)} %get-tuple-element.88), channel_id=1, source_target_pairs={{0,4},{4,0},{1,5},{5,1},{2,6},{6,2},{3,7},{7,3},{8,12},{12,8},{9,1... | collective-permute-start | bytes 393224 | tf_op jit(solution)/shard_map/ppermute | solution.py:376
  (97 shorter events, 42.4 us)
Async XLA Ops:
  0.6 13.2 %collective-permute-start = (bf16[512,2048]{1,0:T(8,128)(2,1)}, bf16[512,2048]{1,0:T(8,128)(2,1)S(1)}, u32[]{:S(2)}, u32[]{:S(2)}) collective-permute-start(bf16[512,2048]{1,0:T(8,128)(2,1)} %a_ref.1), channel_id=1, source_target_pairs={{0,4},{4,0},{1,5},{5,1},{2,6},{6,2},{3,7},{7,3},{8,12},{12,8},{9,1... | collective-permute-start | bytes 6291464 | tf_op jit(solution)/shard_map/ppermute | solution.py:376
  2.1 11.7 %collective-permute-start.2 = (bf16[512,2048]{1,0:T(8,128)(2,1)}, bf16[512,2048]{1,0:T(8,128)(2,1)}, u32[]{:S(2)}, u32[]{:S(2)}) collective-permute-start(bf16[512,2048]{1,0:T(8,128)(2,1)} %refs_4_.1), channel_id=1, source_target_pairs={{0,4},{4,0},{1,5},{5,1},{2,6},{6,2},{3,7},{7,3},{8,12},{12,8},{9,1... | collective-permute-start | bytes 6291464 | tf_op jit(solution)/shard_map/ppermute | solution.py:376
  2.2 11.6 %collective-permute-start.3 = (bf16[512,2048]{1,0:T(8,128)(2,1)}, bf16[512,2048]{1,0:T(8,128)(2,1)}, u32[]{:S(2)}, u32[]{:S(2)}) collective-permute-start(bf16[512,2048]{1,0:T(8,128)(2,1)} %refs_8_.1), channel_id=1, source_target_pairs={{0,4},{4,0},{1,5},{5,1},{2,6},{6,2},{3,7},{7,3},{8,12},{12,8},{9,1... | collective-permute-start | bytes 6291464 | tf_op jit(solution)/shard_map/ppermute | solution.py:376
  7.9 18.2 %collective-permute-start.7 = (bf16[176,2048]{1,0:T(8,128)(2,1)}, bf16[176,2048]{1,0:T(8,128)(2,1)S(1)}, u32[]{:S(2)}, u32[]{:S(2)}) collective-permute-start(bf16[176,2048]{1,0:T(8,128)(2,1)} %get-tuple-element.51), channel_id=1, source_target_pairs={{8,0},{16,8},{24,16},{32,24},{40,32},{48,40},{56,48},{64,56},{72,6... | collective-permute-start | bytes 2162696 | tf_op jit(solution)/shard_map/ppermute | solution.py:480
  11.3 20.3 %collective-permute-start.8 = (bf16[176,2048]{1,0:T(8,128)(2,1)}, bf16[176,2048]{1,0:T(8,128)(2,1)S(1)}, u32[]{:S(2)}, u32[]{:S(2)}) collective-permute-start(bf16[176,2048]{1,0:T(8,128)(2,1)} %get-tuple-element.52), channel_id=1, source_target_pairs={{8,4},{16,12},{24,20},{32,28},{40,36},{48,44},{56,52},{64,60},{72,... | collective-permute-start | bytes 2162696 | tf_op jit(solution)/shard_map/ppermute | solution.py:481
  20.0 13.4 %collective-permute-start.6 = (bf16[128,512]{1,0:T(8,128)(2,1)S(1)}, bf16[128,512]{1,0:T(8,128)(2,1)S(1)}, u32[]{:S(2)}, u32[]{:S(2)}) collective-permute-start(bf16[128,512]{1,0:T(8,128)(2,1)S(1)} %shard_map.95.refs_0_), channel_id=1, source_target_pairs={{0,32},{1,33},{2,34},{3,35},{4,12},{5,13},{6,14},{7,15},{8,40},{9,... | collective-permute-start | bytes 393224 | tf_op jit(solution)/shard_map/ppermute | solution.py:444
  20.0 13.4 %collective-permute-start.5 = (bf16[128,512]{1,0:T(8,128)(2,1)S(1)}, bf16[128,512]{1,0:T(8,128)(2,1)S(1)}, u32[]{:S(2)}, u32[]{:S(2)}) collective-permute-start(bf16[128,512]{1,0:T(8,128)(2,1)S(1)} %shard_map.95.refs_0_), channel_id=1, source_target_pairs={{0,64},{1,65},{2,66},{3,67},{4,20},{5,21},{6,22},{7,23},{8,72},{9,... | collective-permute-start | bytes 393224 | tf_op jit(solution)/shard_map/ppermute | solution.py:444
  34.7 9.3 %collective-permute-start.10 = (bf16[4,128,256]{2,1,0:T(8,128)(2,1)S(1)}, bf16[4,128,256]{2,1,0:T(8,128)(2,1)S(1)}, u32[]{:S(2)}, u32[]{:S(2)}) collective-permute-start(bf16[4,128,256]{2,1,0:T(8,128)(2,1)S(1)} %shard_map.97.refs_0_), channel_id=1, source_target_pairs={{0,16},{1,17},{2,18},{3,19},{4,6},{5,7},{6,4},{7,5},{8,24},{9,25},... | collective-permute-start | bytes 786440 | tf_op jit(solution)/shard_map/ppermute | solution.py:444
  44.1 15.9 %collective-permute-start.16 = (bf16[4,4,128,256]{3,2,1,0:T(8,128)(2,1)S(1)}, bf16[4,4,128,256]{3,2,1,0:T(8,128)(2,1)S(1)}, u32[]{:S(2)}, u32[]{:S(2)}) collective-permute-start(bf16[4,4,128,256]{3,2,1,0:T(8,128)(2,1)S(1)} %shard_map.98.refs_4_.refs_0_), channel_id=1, source_target_pairs={{0,1},{1,2},{2,3},{3,0},{4,36},{5,37},{6,38},{7,39},{8,9},{9,10},{... | collective-permute-start | bytes 3145736 | tf_op jit(solution)/shard_map/ppermute | solution.py:444
  45.8 14.3 %collective-permute-start.15 = (bf16[4,4,128,256]{3,2,1,0:T(8,128)(2,1)S(1)}, bf16[4,4,128,256]{3,2,1,0:T(8,128)(2,1)S(1)}, u32[]{:S(2)}, u32[]{:S(2)}) collective-permute-start(bf16[4,4,128,256]{3,2,1,0:T(8,128)(2,1)S(1)} %shard_map.98.refs_4_.refs_0_), channel_id=1, source_target_pairs={{0,3},{1,0},{2,1},{3,2},{4,100},{5,101},{6,102},{7,103},{8,11},{9,... | collective-permute-start | bytes 3145736 | tf_op jit(solution)/shard_map/ppermute | solution.py:444
  60.0 20.9 %collective-permute-start.20 = (bf16[2,4,128,256]{3,2,1,0:T(8,128)(2,1)S(1)}, bf16[2,4,128,256]{3,2,1,0:T(8,128)(2,1)S(1)}, u32[]{:S(2)}, u32[]{:S(2)}) collective-permute-start(bf16[2,4,128,256]{3,2,1,0:T(8,128)(2,1)S(1)} %slice.16), channel_id=1, source_target_pairs={{0,1},{1,2},{2,3},{3,0},{4,36},{5,37},{6,38},{7,39},{8,9},{9,10},{... | collective-permute-start | bytes 1572872 | tf_op jit(solution)/shard_map/ppermute | solution.py:444
  60.1 20.7 %collective-permute-start.21 = (bf16[2,4,128,256]{3,2,1,0:T(8,128)(2,1)S(1)}, bf16[2,4,128,256]{3,2,1,0:T(8,128)(2,1)S(1)}, u32[]{:S(2)}, u32[]{:S(2)}) collective-permute-start(bf16[2,4,128,256]{3,2,1,0:T(8,128)(2,1)S(1)} %slice.17), channel_id=1, source_target_pairs={{0,3},{1,0},{2,1},{3,2},{4,100},{5,101},{6,102},{7,103},{8,11},{9,... | collective-permute-start | bytes 1572872 | tf_op jit(solution)/shard_map/ppermute | solution.py:444
  64.0 13.0 %collective-permute-start.13 = (bf16[4,128,256]{2,1,0:T(8,128)(2,1)S(1)}, bf16[4,128,256]{2,1,0:T(8,128)(2,1)S(1)}, u32[]{:S(2)}, u32[]{:S(2)}) collective-permute-start(bf16[4,128,256]{2,1,0:T(8,128)(2,1)S(1)} %shard_map.99.refs_0_), channel_id=1, source_target_pairs={{0,16},{1,17},{2,18},{3,19},{4,6},{5,7},{6,4},{7,5},{8,24},{9,25},... | collective-permute-start | bytes 786440 | tf_op jit(solution)/shard_map/ppermute | solution.py:444
  66.1 11.8 %collective-permute-start.12 = (bf16[4,128,256]{2,1,0:T(8,128)(2,1)S(1)}, bf16[4,128,256]{2,1,0:T(8,128)(2,1)S(1)}, u32[]{:S(2)}, u32[]{:S(2)}) collective-permute-start(bf16[4,128,256]{2,1,0:T(8,128)(2,1)S(1)} %shard_map.99.refs_0_), channel_id=1, source_target_pairs={{0,24},{1,25},{2,26},{3,27},{4,7},{5,4},{6,5},{7,6},{8,0},{9,1},{1... | collective-permute-start | bytes 786440 | tf_op jit(solution)/shard_map/ppermute | solution.py:444
  78.0 29.3 %collective-permute-start.19 = (bf16[4,4,128,256]{3,2,1,0:T(8,128)(2,1)S(1)}, bf16[4,4,128,256]{3,2,1,0:T(8,128)(2,1)S(1)}, u32[]{:S(2)}, u32[]{:S(2)}) collective-permute-start(bf16[4,4,128,256]{3,2,1,0:T(8,128)(2,1)S(1)} %shard_map.100.refs_0_), channel_id=1, source_target_pairs={{0,2},{1,3},{2,0},{3,1},{4,68},{5,69},{6,70},{7,71},{8,10},{9,11},... | collective-permute-start | bytes 3145736 | tf_op jit(solution)/shard_map/ppermute | solution.py:444
  78.1 30.9 %collective-permute-start.18 = (bf16[4,4,128,256]{3,2,1,0:T(8,128)(2,1)S(1)}, bf16[4,4,128,256]{3,2,1,0:T(8,128)(2,1)S(1)}, u32[]{:S(2)}, u32[]{:S(2)}) collective-permute-start(bf16[4,4,128,256]{3,2,1,0:T(8,128)(2,1)S(1)} %shard_map.100.refs_0_), channel_id=1, source_target_pairs={{0,1},{1,2},{2,3},{3,0},{4,36},{5,37},{6,38},{7,39},{8,9},{9,10},{... | collective-permute-start | bytes 3145736 | tf_op jit(solution)/shard_map/ppermute | solution.py:444
  79.6 30.3 %collective-permute-start.17 = (bf16[4,4,128,256]{3,2,1,0:T(8,128)(2,1)S(1)}, bf16[4,4,128,256]{3,2,1,0:T(8,128)(2,1)S(1)}, u32[]{:S(2)}, u32[]{:S(2)}) collective-permute-start(bf16[4,4,128,256]{3,2,1,0:T(8,128)(2,1)S(1)} %shard_map.100.refs_0_), channel_id=1, source_target_pairs={{0,3},{1,0},{2,1},{3,2},{4,100},{5,101},{6,102},{7,103},{8,11},{9,... | collective-permute-start | bytes 3145736 | tf_op jit(solution)/shard_map/ppermute | solution.py:444
  100.8 31.6 %collective-permute-start.23 = (bf16[2,176,512]{2,1,0:T(8,128)(2,1)S(1)}, bf16[2,176,512]{2,1,0:T(8,128)(2,1)S(1)}, u32[]{:S(2)}, u32[]{:S(2)}) collective-permute-start(bf16[2,176,512]{2,1,0:T(8,128)(2,1)S(1)} %get-tuple-element.57), channel_id=1, source_target_pairs={{0,8},{8,16},{16,24},{24,32},{32,40},{40,48},{48,56},{56,64},{64,7... | collective-permute-start | bytes 1081352 | tf_op jit(solution)/shard_map/ppermute | solution.py:500
  102.1 30.4 %collective-permute-start.24 = (bf16[2,176,512]{2,1,0:T(8,128)(2,1)S(1)}, bf16[2,176,512]{2,1,0:T(8,128)(2,1)S(1)}, u32[]{:S(2)}, u32[]{:S(2)}) collective-permute-start(bf16[2,176,512]{2,1,0:T(8,128)(2,1)S(1)} %get-tuple-element.58), channel_id=1, source_target_pairs={{4,8},{12,16},{20,24},{28,32},{36,40},{44,48},{52,56},{60,64},{68,... | collective-permute-start | bytes 1081352 | tf_op jit(solution)/shard_map/ppermute | solution.py:500
  107.3 27.6 %collective-permute-start.27 = (bf16[4,4,128,256]{3,2,1,0:T(8,128)(2,1)S(1)}, bf16[4,4,128,256]{3,2,1,0:T(8,128)(2,1)S(1)}, u32[]{:S(2)}, u32[]{:S(2)}) collective-permute-start(bf16[4,4,128,256]{3,2,1,0:T(8,128)(2,1)S(1)} %get-tuple-element.64), channel_id=1, source_target_pairs={{0,2},{1,3},{2,0},{3,1},{4,68},{5,69},{6,70},{7,71},{8,10},{9,11},... | collective-permute-start | bytes 3145736 | tf_op jit(solution)/shard_map/ppermute | solution.py:401
  109.0 29.2 %collective-permute-start.28 = (bf16[4,4,128,256]{3,2,1,0:T(8,128)(2,1)S(1)}, bf16[4,4,128,256]{3,2,1,0:T(8,128)(2,1)S(1)}, u32[]{:S(2)}, u32[]{:S(2)}) collective-permute-start(bf16[4,4,128,256]{3,2,1,0:T(8,128)(2,1)S(1)} %get-tuple-element.65), channel_id=1, source_target_pairs={{0,1},{1,2},{2,3},{3,0},{4,36},{5,37},{6,38},{7,39},{8,9},{9,10},{... | collective-permute-start | bytes 3145736 | tf_op jit(solution)/shard_map/ppermute | solution.py:401
  109.9 28.3 %collective-permute-start.29 = (bf16[4,4,128,256]{3,2,1,0:T(8,128)(2,1)S(1)}, bf16[4,4,128,256]{3,2,1,0:T(8,128)(2,1)S(1)}, u32[]{:S(2)}, u32[]{:S(2)}) collective-permute-start(bf16[4,4,128,256]{3,2,1,0:T(8,128)(2,1)S(1)} %get-tuple-element.66), channel_id=1, source_target_pairs={{0,3},{1,0},{2,1},{3,2},{4,100},{5,101},{6,102},{7,103},{8,11},{9,... | collective-permute-start | bytes 3145736 | tf_op jit(solution)/shard_map/ppermute | solution.py:401
  132.4 49.5 %collective-permute-start.22 = (bf16[2,512,1024]{2,1,0:T(8,128)(2,1)S(1)}, bf16[2,512,1024]{2,1,0:T(8,128)(2,1)S(1)}, u32[]{:S(2)}, u32[]{:S(2)}) collective-permute-start(bf16[2,512,1024]{2,1,0:T(8,128)(2,1)S(1)} %get-tuple-element.56), channel_id=1, source_target_pairs={{0,4},{4,0},{1,5},{5,1},{2,6},{6,2},{3,7},{7,3},{8,12},{12,8},{9,1... | collective-permute-start | bytes 6291464 | tf_op jit(solution)/shard_map/ppermute | solution.py:376
  132.5 9.9 %collective-permute-start.34 = (bf16[2,4,128,256]{3,2,1,0:T(8,128)(2,1)S(1)}, bf16[2,4,128,256]{3,2,1,0:T(8,128)(2,1)S(1)}, u32[]{:S(2)}, u32[]{:S(2)}) collective-permute-start(bf16[2,4,128,256]{3,2,1,0:T(8,128)(2,1)S(1)} %get-tuple-element.75), channel_id=1, source_target_pairs={{0,3},{1,0},{2,1},{3,2},{4,100},{5,101},{6,102},{7,103},{8,11},{9,... | collective-permute-start | bytes 1572872 | tf_op jit(solution)/shard_map/ppermute | solution.py:470
  134.9 9.2 %collective-permute-start.33 = (bf16[2,4,128,256]{3,2,1,0:T(8,128)(2,1)S(1)}, bf16[2,4,128,256]{3,2,1,0:T(8,128)(2,1)S(1)}, u32[]{:S(2)}, u32[]{:S(2)}) collective-permute-start(bf16[2,4,128,256]{3,2,1,0:T(8,128)(2,1)S(1)} %get-tuple-element.67.refs_4_), channel_id=1, source_target_pairs={{0,1},{1,2},{2,3},{3,0},{4,36},{5,37},{6,38},{7,39},{8,9},{9,10},{... | collective-permute-start | bytes 1572872 | tf_op jit(solution)/shard_map/ppermute | solution.py:469
  144.5 22.1 %collective-permute-start.35 = (bf16[4,4,128,256]{3,2,1,0:T(8,128)(2,1)S(1)}, bf16[4,4,128,256]{3,2,1,0:T(8,128)(2,1)S(1)}, u32[]{:S(2)}, u32[]{:S(2)}) collective-permute-start(bf16[4,4,128,256]{3,2,1,0:T(8,128)(2,1)S(1)} %get-tuple-element.76), channel_id=1, source_target_pairs={{0,1},{1,2},{2,3},{3,0},{4,36},{5,37},{6,38},{7,39},{8,9},{9,10},{... | collective-permute-start | bytes 3145736 | tf_op jit(solution)/shard_map/ppermute | solution.py:472
  146.2 20.4 %collective-permute-start.36 = (bf16[4,4,128,256]{3,2,1,0:T(8,128)(2,1)S(1)}, bf16[4,4,128,256]{3,2,1,0:T(8,128)(2,1)S(1)}, u32[]{:S(2)}, u32[]{:S(2)}) collective-permute-start(bf16[4,4,128,256]{3,2,1,0:T(8,128)(2,1)S(1)} %get-tuple-element.77), channel_id=1, source_target_pairs={{0,3},{1,0},{2,1},{3,2},{4,100},{5,101},{6,102},{7,103},{8,11},{9,... | collective-permute-start | bytes 3145736 | tf_op jit(solution)/shard_map/ppermute | solution.py:472
  147.2 9.6 %collective-permute-start.30 = (bf16[4,128,256]{2,1,0:T(8,128)(2,1)S(1)}, bf16[4,128,256]{2,1,0:T(8,128)(2,1)S(1)}, u32[]{:S(2)}, u32[]{:S(2)}) collective-permute-start(bf16[4,128,256]{2,1,0:T(8,128)(2,1)S(1)} %get-tuple-element.69), channel_id=1, source_target_pairs={{0,16},{1,17},{2,18},{3,19},{4,6},{5,7},{6,4},{7,5},{8,24},{9,25},... | collective-permute-start | bytes 786440 | tf_op jit(solution)/shard_map/ppermute | solution.py:401
  148.3 12.0 %collective-permute-start.31 = (bf16[4,128,256]{2,1,0:T(8,128)(2,1)S(1)}, bf16[4,128,256]{2,1,0:T(8,128)(2,1)S(1)}, u32[]{:S(2)}, u32[]{:S(2)}) collective-permute-start(bf16[4,128,256]{2,1,0:T(8,128)(2,1)S(1)} %get-tuple-element.70), channel_id=1, source_target_pairs={{0,8},{1,9},{2,10},{3,11},{4,5},{5,6},{6,7},{7,4},{8,16},{9,17},{1... | collective-permute-start | bytes 786440 | tf_op jit(solution)/shard_map/ppermute | solution.py:401
  160.4 9.4 %collective-permute-start.25 = (bf16[2,176,512]{2,1,0:T(8,128)(2,1)S(1)}, bf16[2,176,512]{2,1,0:T(8,128)(2,1)S(1)}, u32[]{:S(2)}, u32[]{:S(2)}) collective-permute-start(bf16[2,176,512]{2,1,0:T(8,128)(2,1)S(1)} %get-tuple-element.59), channel_id=1, source_target_pairs={{0,8},{8,16},{16,24},{24,32},{32,40},{40,48},{48,56},{56,64},{64,7... | collective-permute-start | bytes 1081352 | tf_op jit(solution)/shard_map/ppermute | solution.py:504
  164.7 9.0 %collective-permute-start.26 = (bf16[2,176,512]{2,1,0:T(8,128)(2,1)S(1)}, bf16[2,176,512]{2,1,0:T(8,128)(2,1)S(1)}, u32[]{:S(2)}, u32[]{:S(2)}) collective-permute-start(bf16[2,176,512]{2,1,0:T(8,128)(2,1)S(1)} %get-tuple-element.60), channel_id=1, source_target_pairs={{4,8},{12,16},{20,24},{28,32},{36,40},{44,48},{52,56},{60,64},{68,... | collective-permute-start | bytes 1081352 | tf_op jit(solution)/shard_map/ppermute | solution.py:504
  169.0 8.2 %collective-permute-start.38 = (bf16[4,128,256]{2,1,0:T(8,128)(2,1)S(1)}, bf16[4,128,256]{2,1,0:T(8,128)(2,1)S(1)}, u32[]{:S(2)}, u32[]{:S(2)}) collective-permute-start(bf16[4,128,256]{2,1,0:T(8,128)(2,1)S(1)} %get-tuple-element.80), channel_id=1, source_target_pairs={{0,8},{1,9},{2,10},{3,11},{4,5},{5,6},{6,7},{7,4},{8,16},{9,17},{1... | collective-permute-start | bytes 786440 | tf_op jit(solution)/shard_map/ppermute | solution.py:401
  (22 other events, 196.0 us)

commit v15 on v14

--- a/solution.py
+++ b/solution.py
@@ -402,8 +402,8 @@
 
 
 def join_kernel(cols, *refs):
-    for n in range(4):
-        refs[-1][n] = refs[n][..., cols]
+    for n, place in enumerate((0, 1, 3, 2)):
+        refs[-1][place] = refs[n][..., cols]
 
 
 def join(parts, after, cols=slice(0, HEAD_DIM)):
@@ -482,14 +482,14 @@
 
     got = swap(jnp.where(c == 0, kv_weights[:, HALF:], kv_weights[:, :HALF]))
     own = pick(me, kv_weights, got, [info, *swapped])
-    first = [own] + [ring(own, 2, n) for n in (1, 2, 3)]
-    tokens, tokens_t, turned = turn(enc_hidden, swapped[0], [first[1]])
+    first = [own] + [ring(own, 2, n) for n in (1, 3, 2)]
+    tokens, tokens_t, turned = turn(enc_hidden, swapped[0], [first[3]])
     part = join(first, [turned, sent_a, sent_b])
-    part = join([part] + [ring(part, 1, n) for n in (1, 2, 3)], [])
+    part = join([part] + [ring(part, 1, n) for n in (1, 3, 2)], [])
     ahead, behind = ring(part, 0, 1), ring(part, 0, -1)
     weights = [[part, ahead, behind, ring(behind[:2], 0, -1), ring(ahead[2:], 0, 1)]]
     part = join(first, [part], slice(HEAD_DIM, HALF))
-    part = join([part] + [ring(part, 1, n) for n in (1, 2, 3)], [ahead, behind])
+    part = join([part] + [ring(part, 1, n) for n in (1, 3, 2)], [ahead, behind])
     weights.append([part, ring(part, 0, 1), ring(part, 0, -1), ring(part, 0, 2)])
 
     shared = (meta, me, tokens, tokens_t)

time: 192 us -> 192 us (level)
  starting transfers between devices: 67.1 us -> 65.1 us
  waiting for transfers between devices: 65.9 us -> 67.9 us
    ppermute x16, waiting for transfers between devices: 31.1 us -> 38.7 us  [ring(): return lax.ppermute(value, ALL, shift(phase, -amount))]
    ppermute x1, waiting for transfers between devices: 5.47 us -> 0.01 us  [body(): sent_b = lax.ppermute(leave_b, DP, SEND_B)]
where the time goes in v15:
time: 192 us; the launch traced here: 191 us
  waiting for transfers between devices  67.9 us (35%)
  starting transfers between devices  65.1 us (34%)
  Pallas kernels  52.3 us (27%)
  local copies, waits for them, and re-layouts  2.68 us (1%)
  other arithmetic  2.21 us (1%)
    pallas_call x2, Pallas kernels, run_main(): pl.pallas_call(functools.partial(main_kernel, len(weights), len(before)),...  39.7 us
    ppermute x16, waiting for transfers between devices, ring(): return lax.ppermute(value, ALL, shift(phase, -amount))  38.7 us
    ppermute x16, starting transfers between devices, ring(): return lax.ppermute(value, ALL, shift(phase, -amount))  25.3 us
    ppermute x12, waiting for transfers between devices, exchange(): lax.ppermute(parts[r], ALL, shift(phase, r))  21.7 us
    ppermute x12, starting transfers between devices, exchange(): lax.ppermute(parts[r], ALL, shift(phase, r))  14.1 us
    ppermute x4, starting transfers between devices, body(): lax.ppermute(part, DP, pairs)  8.08 us
    ppermute x6, starting transfers between devices, swap(): return lax.ppermute(value, 'c', [(0, 1), (1, 0)])  6.08 us
  transfers between devices with their start and end apart: 44, of which 19 were waited for; matrix products, arithmetic and copies ran while one was open for 1% of the time, Pallas kernels for 27%

profile of v15, /device:TPU:1, one launch (start us, length us, event | category | flops | bytes accessed | tf_op | source)
XLA Modules:
  0.0 191.1 jit_solution(16208598197242321704)
XLA Ops:
  4.3 3.6 %shard_map.94 = (s32[8,4]{1,0:T(8,128)}, s32[4]{0:T(128)}, bf16[176,2048]{1,0:T(8,128)(2,1)}, bf16[176,2048]{1,0:T(8,128)(2,1)}) custom-call(s32[4]{0:T(128)} %pad_add_fusion.me, s32[4,128]{1,0:T(4,128)} %bitcast.7, s32[4,128]{1,0:T(4,128)} %bitcast.8, s32[4,128]{1,0:T(4,128)} %bitcast.9, bf16[512,2048]{1,0:T(8,128)(2,1)} %refs_4_.1, bf16[512,2048]{1,0:T(8,128)(2,1)} %refs_8_.1), custom_call_target="tpu_custom_call" | custom-call | tf_op jit(solution)/shard_map/pallas_call | solution.py:305
  7.9 3.3 %collective-permute-start.7 = (bf16[176,2048]{1,0:T(8,128)(2,1)}, bf16[176,2048]{1,0:T(8,128)(2,1)S(1)}, u32[]{:S(2)}, u32[]{:S(2)}) collective-permute-start(bf16[176,2048]{1,0:T(8,128)(2,1)} %get-tuple-element.51), channel_id=1, source_target_pairs={{8,0},{16,8},{24,16},{32,24},{40,32},{48,40},{56,48},{64,56},{72,6... | collective-permute-start | bytes 2162696 | tf_op jit(solution)/shard_map/ppermute | solution.py:480
  11.3 2.5 %collective-permute-start.8 = (bf16[176,2048]{1,0:T(8,128)(2,1)}, bf16[176,2048]{1,0:T(8,128)(2,1)S(1)}, u32[]{:S(2)}, u32[]{:S(2)}) collective-permute-start(bf16[176,2048]{1,0:T(8,128)(2,1)} %get-tuple-element.52), channel_id=1, source_target_pairs={{8,4},{16,12},{24,20},{32,28},{40,36},{48,44},{56,52},{64,60},{72,... | collective-permute-start | bytes 2162696 | tf_op jit(solution)/shard_map/ppermute | solution.py:481
  15.0 3.1 %collective-permute-start.4 = (bf16[128,512]{1,0:T(8,128)(2,1)S(1)}, bf16[128,512]{1,0:T(8,128)(2,1)S(1)}, u32[]{:S(2)}, u32[]{:S(2)}) collective-permute-start(bf16[128,512]{1,0:T(8,128)(2,1)S(1)} %shard_map.95.refs_0_), channel_id=1, source_target_pairs={{0,64},{1,65},{2,66},{3,67},{4,20},{5,21},{6,22},{7,23},{8,72},{9,... | collective-permute-start | bytes 393224 | tf_op jit(solution)/shard_map/ppermute | solution.py:444
  18.1 2.5 %collective-permute-start.6 = (bf16[128,512]{1,0:T(8,128)(2,1)S(1)}, bf16[128,512]{1,0:T(8,128)(2,1)S(1)}, u32[]{:S(2)}, u32[]{:S(2)}) collective-permute-start(bf16[128,512]{1,0:T(8,128)(2,1)S(1)} %shard_map.95.refs_0_), channel_id=1, source_target_pairs={{0,32},{1,33},{2,34},{3,35},{4,12},{5,13},{6,14},{7,15},{8,40},{9,... | collective-permute-start | bytes 393224 | tf_op jit(solution)/shard_map/ppermute | solution.py:444
  20.8 11.4 %collective-permute-done.4.refs_0_.refs_3_ = bf16[128,512]{1,0:T(8,128)(2,1)S(1)} collective-permute-done((bf16[128,512]{1,0:T(8,128)(2,1)S(1)}, bf16[128,512]{1,0:T(8,128)(2,1)S(1)}, u32[]{:S(2)}, u32[]{:S(2)}) %collective-permute-start.4) | collective-permute-done | bytes 131104 | tf_op jit(solution)/shard_map/ppermute | solution.py:444
  32.2 2.1 %shard_map.96 = (bf16[1024,2048]{1,0:T(8,128)(2,1)S(1)}, bf16[2048,1024]{1,0:T(8,128)(2,1)S(1)}, f32[8,128]{1,0:T(8,128)S(1)}) custom-call(bf16[512,2048]{1,0:T(8,128)(2,1)S(1)} %copy-done.2, bf16[512,2048]{1,0:T(8,128)(2,1)S(1)} %collective-permute-done.refs_1_.b_ref, bf16[128,512]{1,0:T(8,128)(2,1)S(1)} %collective-permute-done.4.refs_0_.refs_3_), custom_call_target="tpu_custom_call" | custom-call | tf_op jit(solution)/shard_map/pallas_call | solution.py:327
  34.3 2.0 %copy-done.8 = bf16[2048,1024]{1,0:T(8,128)(2,1)} copy-done((bf16[2048,1024]{1,0:T(8,128)(2,1)}, bf16[2048,1024]{1,0:T(8,128)(2,1)S(1)}, u32[]{:S(2)}) %copy-start.8) | copy-done | bytes 4194328
  36.4 2.8 %collective-permute-start.11 = (bf16[4,128,256]{2,1,0:T(8,128)(2,1)S(1)}, bf16[4,128,256]{2,1,0:T(8,128)(2,1)S(1)}, u32[]{:S(2)}, u32[]{:S(2)}) collective-permute-start(bf16[4,128,256]{2,1,0:T(8,128)(2,1)S(1)} %shard_map.97.refs_0_), channel_id=1, source_target_pairs={{0,16},{1,17},{2,18},{3,19},{4,6},{5,7},{6,4},{7,5},{8,24},{9,25},... | collective-permute-start | bytes 786440 | tf_op jit(solution)/shard_map/ppermute | solution.py:444
  39.5 2.4 %collective-permute-start.9 = (bf16[4,128,256]{2,1,0:T(8,128)(2,1)S(1)}, bf16[4,128,256]{2,1,0:T(8,128)(2,1)S(1)}, u32[]{:S(2)}, u32[]{:S(2)}) collective-permute-start(bf16[4,128,256]{2,1,0:T(8,128)(2,1)S(1)} %shard_map.97.refs_0_), channel_id=1, source_target_pairs={{0,24},{1,25},{2,26},{3,27},{4,7},{5,4},{6,5},{7,6},{8,0},{9,1},{1... | collective-permute-start | bytes 786440 | tf_op jit(solution)/shard_map/ppermute | solution.py:444
  43.2 3.1 %collective-permute-done.10.refs_2_ = bf16[4,128,256]{2,1,0:T(8,128)(2,1)S(1)} collective-permute-done((bf16[4,128,256]{2,1,0:T(8,128)(2,1)S(1)}, bf16[4,128,256]{2,1,0:T(8,128)(2,1)S(1)}, u32[]{:S(2)}, u32[]{:S(2)}) %collective-permute-start.10) | collective-permute-done | bytes 262176 | tf_op jit(solution)/shard_map/ppermute | solution.py:444
  47.6 2.1 %collective-permute-start.15 = (bf16[4,4,128,256]{3,2,1,0:T(8,128)(2,1)S(1)}, bf16[4,4,128,256]{3,2,1,0:T(8,128)(2,1)S(1)}, u32[]{:S(2)}, u32[]{:S(2)}) collective-permute-start(bf16[4,4,128,256]{3,2,1,0:T(8,128)(2,1)S(1)} %shard_map.98.refs_4_.refs_0_), channel_id=1, source_target_pairs={{0,3},{1,0},{2,1},{3,2},{4,100},{5,101},{6,102},{7,103},{8,11},{9,... | collective-permute-start | bytes 3145736 | tf_op jit(solution)/shard_map/ppermute | solution.py:444
  49.7 12.4 %collective-permute-done.16.refs_5_.refs_2_ = bf16[4,4,128,256]{3,2,1,0:T(8,128)(2,1)S(1)} collective-permute-done((bf16[4,4,128,256]{3,2,1,0:T(8,128)(2,1)S(1)}, bf16[4,4,128,256]{3,2,1,0:T(8,128)(2,1)S(1)}, u32[]{:S(2)}, u32[]{:S(2)}) %collective-permute-start.16) | collective-permute-done | bytes 1048608 | tf_op jit(solution)/shard_map/ppermute | solution.py:444
  62.3 2.7 %collective-permute-start.21 = (bf16[2,4,128,256]{3,2,1,0:T(8,128)(2,1)S(1)}, bf16[2,4,128,256]{3,2,1,0:T(8,128)(2,1)S(1)}, u32[]{:S(2)}, u32[]{:S(2)}) collective-permute-start(bf16[2,4,128,256]{3,2,1,0:T(8,128)(2,1)S(1)} %slice.17), channel_id=1, source_target_pairs={{0,3},{1,0},{2,1},{3,2},{4,100},{5,101},{6,102},{7,103},{8,11},{9,... | collective-permute-start | bytes 1572872 | tf_op jit(solution)/shard_map/ppermute | solution.py:444
  69.3 3.8 %collective-permute-done.14.refs_3_ = bf16[4,128,256]{2,1,0:T(8,128)(2,1)S(1)} collective-permute-done((bf16[4,128,256]{2,1,0:T(8,128)(2,1)S(1)}, bf16[4,128,256]{2,1,0:T(8,128)(2,1)S(1)}, u32[]{:S(2)}, u32[]{:S(2)}) %collective-permute-start.14) | collective-permute-done | bytes 262176 | tf_op jit(solution)/shard_map/ppermute | solution.py:444
  73.2 4.8 %collective-permute-done.13.refs_2_ = bf16[4,128,256]{2,1,0:T(8,128)(2,1)S(1)} collective-permute-done((bf16[4,128,256]{2,1,0:T(8,128)(2,1)S(1)}, bf16[4,128,256]{2,1,0:T(8,128)(2,1)S(1)}, u32[]{:S(2)}, u32[]{:S(2)}) %collective-permute-start.13) | collective-permute-done | bytes 262176 | tf_op jit(solution)/shard_map/ppermute | solution.py:444
  80.9 2.7 %collective-permute-start.17 = (bf16[4,4,128,256]{3,2,1,0:T(8,128)(2,1)S(1)}, bf16[4,4,128,256]{3,2,1,0:T(8,128)(2,1)S(1)}, u32[]{:S(2)}, u32[]{:S(2)}) collective-permute-start(bf16[4,4,128,256]{3,2,1,0:T(8,128)(2,1)S(1)} %shard_map.100.refs_0_), channel_id=1, source_target_pairs={{0,3},{1,0},{2,1},{3,2},{4,100},{5,101},{6,102},{7,103},{8,11},{9,... | collective-permute-start | bytes 3145736 | tf_op jit(solution)/shard_map/ppermute | solution.py:444
  83.6 19.9 %shard_map.101 = (bf16[2,512,1024]{2,1,0:T(8,128)(2,1)S(1)}, bf16[2,512,1024]{2,1,0:T(8,128)(2,1)S(1)}, bf16[2,176,512]{2,1,0:T(8,128)(2,1)S(1)}, bf16[2,176,512...) custom-call(s32[8,4]{1,0:T(8,128)S(1)} %copy-done.9, ...), custom_call_target="tpu_custom_call" | custom-call | flops 12000000000 | bytes 24000000 | tf_op jit(solution)/shard_map/pallas_call | solution.py:160
  104.8 3.6 %collective-permute-start.24 = (bf16[2,176,512]{2,1,0:T(8,128)(2,1)S(1)}, bf16[2,176,512]{2,1,0:T(8,128)(2,1)S(1)}, u32[]{:S(2)}, u32[]{:S(2)}) collective-permute-start(bf16[2,176,512]{2,1,0:T(8,128)(2,1)S(1)} %get-tuple-element.58), channel_id=1, source_target_pairs={{4,8},{12,16},{20,24},{28,32},{36,40},{44,48},{52,56},{60,64},{68,... | collective-permute-start | bytes 1081352 | tf_op jit(solution)/shard_map/ppermute | solution.py:500
  109.0 2.6 %collective-permute-start.29 = (bf16[4,4,128,256]{3,2,1,0:T(8,128)(2,1)S(1)}, bf16[4,4,128,256]{3,2,1,0:T(8,128)(2,1)S(1)}, u32[]{:S(2)}, u32[]{:S(2)}) collective-permute-start(bf16[4,4,128,256]{3,2,1,0:T(8,128)(2,1)S(1)} %get-tuple-element.66), channel_id=1, source_target_pairs={{0,3},{1,0},{2,1},{3,2},{4,100},{5,101},{6,102},{7,103},{8,11},{9,... | collective-permute-start | bytes 3145736 | tf_op jit(solution)/shard_map/ppermute | solution.py:401
  111.6 19.8 %shard_map.102 = (bf16[2,512,1024]{2,1,0:T(8,128)(2,1)S(1)}, bf16[2,512,1024]{2,1,0:T(8,128)(2,1)S(1)}, bf16[2,176,512]{2,1,0:T(8,128)(2,1)S(1)}, bf16[2,176,512...) custom-call(s32[8,4]{1,0:T(8,128)S(1)} %copy-done.9, ...), custom_call_target="tpu_custom_call", output_to_operand_aliasing={{0}: (16, {}), {1}: (17, {})} | custom-call | flops 12000000000 | bytes 24000000 | tf_op jit(solution)/shard_map/pallas_call | solution.py:160
  131.7 2.2 %collective-permute-start.34 = (bf16[2,4,128,256]{3,2,1,0:T(8,128)(2,1)S(1)}, bf16[2,4,128,256]{3,2,1,0:T(8,128)(2,1)S(1)}, u32[]{:S(2)}, u32[]{:S(2)}) collective-permute-start(bf16[2,4,128,256]{3,2,1,0:T(8,128)(2,1)S(1)} %get-tuple-element.75), channel_id=1, source_target_pairs={{0,3},{1,0},{2,1},{3,2},{4,100},{5,101},{6,102},{7,103},{8,11},{9,... | collective-permute-start | bytes 1572872 | tf_op jit(solution)/shard_map/ppermute | solution.py:470
  134.6 3.8 %collective-permute-done.28.refs_2_ = bf16[4,4,128,256]{3,2,1,0:T(8,128)(2,1)S(1)} collective-permute-done((bf16[4,4,128,256]{3,2,1,0:T(8,128)(2,1)S(1)}, bf16[4,4,128,256]{3,2,1,0:T(8,128)(2,1)S(1)}, u32[]{:S(2)}, u32[]{:S(2)}) %collective-permute-start.28) | collective-permute-done | bytes 1048608 | tf_op jit(solution)/shard_map/ppermute | solution.py:401
  139.3 2.1 %collective-permute-done.34.got_b = bf16[2,4,128,256]{3,2,1,0:T(8,128)(2,1)S(1)} collective-permute-done((bf16[2,4,128,256]{3,2,1,0:T(8,128)(2,1)S(1)}, bf16[2,4,128,256]{3,2,1,0:T(8,128)(2,1)S(1)}, u32[]{:S(2)}, u32[]{:S(2)}) %collective-permute-start.34) | collective-permute-done | bytes 524320 | tf_op jit(solution)/shard_map/ppermute | solution.py:470
  141.4 2.6 %collective-permute-done.33.got_a = bf16[2,4,128,256]{3,2,1,0:T(8,128)(2,1)S(1)} collective-permute-done((bf16[2,4,128,256]{3,2,1,0:T(8,128)(2,1)S(1)}, bf16[2,4,128,256]{3,2,1,0:T(8,128)(2,1)S(1)}, u32[]{:S(2)}, u32[]{:S(2)}) %collective-permute-start.33) | collective-permute-done | bytes 524320 | tf_op jit(solution)/shard_map/ppermute | solution.py:469
  144.3 2.0 %collective-permute-start.35 = (bf16[4,4,128,256]{3,2,1,0:T(8,128)(2,1)S(1)}, bf16[4,4,128,256]{3,2,1,0:T(8,128)(2,1)S(1)}, u32[]{:S(2)}, u32[]{:S(2)}) collective-permute-start(bf16[4,4,128,256]{3,2,1,0:T(8,128)(2,1)S(1)} %get-tuple-element.76), channel_id=1, source_target_pairs={{0,1},{1,2},{2,3},{3,0},{4,36},{5,37},{6,38},{7,39},{8,9},{9,10},{... | collective-permute-start | bytes 3145736 | tf_op jit(solution)/shard_map/ppermute | solution.py:472
  148.6 8.0 %collective-permute-done.30.refs_3_.refs_1_ = bf16[4,128,256]{2,1,0:T(8,128)(2,1)S(1)} collective-permute-done((bf16[4,128,256]{2,1,0:T(8,128)(2,1)S(1)}, bf16[4,128,256]{2,1,0:T(8,128)(2,1)S(1)}, u32[]{:S(2)}, u32[]{:S(2)}) %collective-permute-start.30) | collective-permute-done | bytes 262176 | tf_op jit(solution)/shard_map/ppermute | solution.py:401
  156.7 3.7 %collective-permute-done.31.refs_4_.refs_2_ = bf16[4,128,256]{2,1,0:T(8,128)(2,1)S(1)} collective-permute-done((bf16[4,128,256]{2,1,0:T(8,128)(2,1)S(1)}, bf16[4,128,256]{2,1,0:T(8,128)(2,1)S(1)}, u32[]{:S(2)}, u32[]{:S(2)}) %collective-permute-start.31) | collective-permute-done | bytes 262176 | tf_op jit(solution)/shard_map/ppermute | solution.py:401
  166.3 2.1 %collective-permute-start.37 = (bf16[4,128,256]{2,1,0:T(8,128)(2,1)S(1)}, bf16[4,128,256]{2,1,0:T(8,128)(2,1)S(1)}, u32[]{:S(2)}, u32[]{:S(2)}) collective-permute-start(bf16[4,128,256]{2,1,0:T(8,128)(2,1)S(1)} %get-tuple-element.79), channel_id=1, source_target_pairs={{0,16},{1,17},{2,18},{3,19},{4,6},{5,7},{6,4},{7,5},{8,24},{9,25},... | collective-permute-start | bytes 786440 | tf_op jit(solution)/shard_map/ppermute | solution.py:401
  173.4 2.8 %collective-permute-done.38.refs_6_ = bf16[4,128,256]{2,1,0:T(8,128)(2,1)S(1)} collective-permute-done((bf16[4,128,256]{2,1,0:T(8,128)(2,1)S(1)}, bf16[4,128,256]{2,1,0:T(8,128)(2,1)S(1)}, u32[]{:S(2)}, u32[]{:S(2)}) %collective-permute-start.38) | collective-permute-done | bytes 262176 | tf_op jit(solution)/shard_map/ppermute | solution.py:401
  181.8 3.4 %shard_map.103 = (bf16[512,2048]{1,0:T(8,128)(2,1)}, bf16[512,2048]{1,0:T(8,128)(2,1)}, f32[8,128]{1,0:T(8,128)S(1)}) custom-call(s32[4]{0:T(128)S(1)} %copy-done.6, bf16[2,512,1024]{2,1,0:T(8,128)(2,1)S(1)} %get-tuple-element.55.refs_0_, bf16[2,512,1024]{2,1,0:T(8,128)(2,1)S(1)} %collective-permute-done.22.refs_1_, ...), custom_call_target="tpu_custom_call" | custom-call | tf_op jit(solution)/shard_map/pallas_call | solution.py:362
  185.8 3.6 %collective-permute-start.43 = (f32[64,512]{1,0:T(8,128)S(1)}, f32[64,512]{1,0:T(8,128)S(1)}, u32[]{:S(2)}, u32[]{:S(2)}) collective-permute-start(f32[64,512]{1,0:T(8,128)S(1)} %get-tuple-element.88), channel_id=1, source_target_pairs={{0,4},{4,0},{1,5},{5,1},{2,6},{6,2},{3,7},{7,3},{8,12},{12,8},{9,1... | collective-permute-start | bytes 393224 | tf_op jit(solution)/shard_map/ppermute | solution.py:376
  (97 shorter events, 40.6 us)
Async XLA Ops:
  0.6 13.2 %collective-permute-start = (bf16[512,2048]{1,0:T(8,128)(2,1)}, bf16[512,2048]{1,0:T(8,128)(2,1)S(1)}, u32[]{:S(2)}, u32[]{:S(2)}) collective-permute-start(bf16[512,2048]{1,0:T(8,128)(2,1)} %a_ref.1), channel_id=1, source_target_pairs={{0,4},{4,0},{1,5},{5,1},{2,6},{6,2},{3,7},{7,3},{8,12},{12,8},{9,1... | collective-permute-start | bytes 6291464 | tf_op jit(solution)/shard_map/ppermute | solution.py:376
  2.1 11.7 %collective-permute-start.2 = (bf16[512,2048]{1,0:T(8,128)(2,1)}, bf16[512,2048]{1,0:T(8,128)(2,1)}, u32[]{:S(2)}, u32[]{:S(2)}) collective-permute-start(bf16[512,2048]{1,0:T(8,128)(2,1)} %refs_4_.1), channel_id=1, source_target_pairs={{0,4},{4,0},{1,5},{5,1},{2,6},{6,2},{3,7},{7,3},{8,12},{12,8},{9,1... | collective-permute-start | bytes 6291464 | tf_op jit(solution)/shard_map/ppermute | solution.py:376
  2.2 11.6 %collective-permute-start.3 = (bf16[512,2048]{1,0:T(8,128)(2,1)}, bf16[512,2048]{1,0:T(8,128)(2,1)}, u32[]{:S(2)}, u32[]{:S(2)}) collective-permute-start(bf16[512,2048]{1,0:T(8,128)(2,1)} %refs_8_.1), channel_id=1, source_target_pairs={{0,4},{4,0},{1,5},{5,1},{2,6},{6,2},{3,7},{7,3},{8,12},{12,8},{9,1... | collective-permute-start | bytes 6291464 | tf_op jit(solution)/shard_map/ppermute | solution.py:376
  7.9 28.4 %collective-permute-start.7 = (bf16[176,2048]{1,0:T(8,128)(2,1)}, bf16[176,2048]{1,0:T(8,128)(2,1)S(1)}, u32[]{:S(2)}, u32[]{:S(2)}) collective-permute-start(bf16[176,2048]{1,0:T(8,128)(2,1)} %get-tuple-element.51), channel_id=1, source_target_pairs={{8,0},{16,8},{24,16},{32,24},{40,32},{48,40},{56,48},{64,56},{72,6... | collective-permute-start | bytes 2162696 | tf_op jit(solution)/shard_map/ppermute | solution.py:480
  11.3 25.0 %collective-permute-start.8 = (bf16[176,2048]{1,0:T(8,128)(2,1)}, bf16[176,2048]{1,0:T(8,128)(2,1)S(1)}, u32[]{:S(2)}, u32[]{:S(2)}) collective-permute-start(bf16[176,2048]{1,0:T(8,128)(2,1)} %get-tuple-element.52), channel_id=1, source_target_pairs={{8,4},{16,12},{24,20},{32,28},{40,36},{48,44},{56,52},{64,60},{72,... | collective-permute-start | bytes 2162696 | tf_op jit(solution)/shard_map/ppermute | solution.py:481
  15.0 17.2 %collective-permute-start.4 = (bf16[128,512]{1,0:T(8,128)(2,1)S(1)}, bf16[128,512]{1,0:T(8,128)(2,1)S(1)}, u32[]{:S(2)}, u32[]{:S(2)}) collective-permute-start(bf16[128,512]{1,0:T(8,128)(2,1)S(1)} %shard_map.95.refs_0_), channel_id=1, source_target_pairs={{0,64},{1,65},{2,66},{3,67},{4,20},{5,21},{6,22},{7,23},{8,72},{9,... | collective-permute-start | bytes 393224 | tf_op jit(solution)/shard_map/ppermute | solution.py:444
  18.1 18.2 %collective-permute-start.6 = (bf16[128,512]{1,0:T(8,128)(2,1)S(1)}, bf16[128,512]{1,0:T(8,128)(2,1)S(1)}, u32[]{:S(2)}, u32[]{:S(2)}) collective-permute-start(bf16[128,512]{1,0:T(8,128)(2,1)S(1)} %shard_map.95.refs_0_), channel_id=1, source_target_pairs={{0,32},{1,33},{2,34},{3,35},{4,12},{5,13},{6,14},{7,15},{8,40},{9,... | collective-permute-start | bytes 393224 | tf_op jit(solution)/shard_map/ppermute | solution.py:444
  20.6 15.7 %collective-permute-start.5 = (bf16[128,512]{1,0:T(8,128)(2,1)S(1)}, bf16[128,512]{1,0:T(8,128)(2,1)S(1)}, u32[]{:S(2)}, u32[]{:S(2)}) collective-permute-start(bf16[128,512]{1,0:T(8,128)(2,1)S(1)} %shard_map.95.refs_0_), channel_id=1, source_target_pairs={{0,96},{1,97},{2,98},{3,99},{4,28},{5,29},{6,30},{7,31},{8,104},{9... | collective-permute-start | bytes 393224 | tf_op jit(solution)/shard_map/ppermute | solution.py:444
  46.4 15.7 %collective-permute-start.16 = (bf16[4,4,128,256]{3,2,1,0:T(8,128)(2,1)S(1)}, bf16[4,4,128,256]{3,2,1,0:T(8,128)(2,1)S(1)}, u32[]{:S(2)}, u32[]{:S(2)}) collective-permute-start(bf16[4,4,128,256]{3,2,1,0:T(8,128)(2,1)S(1)} %shard_map.98.refs_4_.refs_0_), channel_id=1, source_target_pairs={{0,1},{1,2},{2,3},{3,0},{4,36},{5,37},{6,38},{7,39},{8,9},{9,10},{... | collective-permute-start | bytes 3145736 | tf_op jit(solution)/shard_map/ppermute | solution.py:444
  47.6 14.6 %collective-permute-start.15 = (bf16[4,4,128,256]{3,2,1,0:T(8,128)(2,1)S(1)}, bf16[4,4,128,256]{3,2,1,0:T(8,128)(2,1)S(1)}, u32[]{:S(2)}, u32[]{:S(2)}) collective-permute-start(bf16[4,4,128,256]{3,2,1,0:T(8,128)(2,1)S(1)} %shard_map.98.refs_4_.refs_0_), channel_id=1, source_target_pairs={{0,3},{1,0},{2,1},{3,2},{4,100},{5,101},{6,102},{7,103},{8,11},{9,... | collective-permute-start | bytes 3145736 | tf_op jit(solution)/shard_map/ppermute | solution.py:444
  62.2 21.4 %collective-permute-start.20 = (bf16[2,4,128,256]{3,2,1,0:T(8,128)(2,1)S(1)}, bf16[2,4,128,256]{3,2,1,0:T(8,128)(2,1)S(1)}, u32[]{:S(2)}, u32[]{:S(2)}) collective-permute-start(bf16[2,4,128,256]{3,2,1,0:T(8,128)(2,1)S(1)} %slice.16), channel_id=1, source_target_pairs={{0,1},{1,2},{2,3},{3,0},{4,36},{5,37},{6,38},{7,39},{8,9},{9,10},{... | collective-permute-start | bytes 1572872 | tf_op jit(solution)/shard_map/ppermute | solution.py:444
  62.3 21.3 %collective-permute-start.21 = (bf16[2,4,128,256]{3,2,1,0:T(8,128)(2,1)S(1)}, bf16[2,4,128,256]{3,2,1,0:T(8,128)(2,1)S(1)}, u32[]{:S(2)}, u32[]{:S(2)}) collective-permute-start(bf16[2,4,128,256]{3,2,1,0:T(8,128)(2,1)S(1)} %slice.17), channel_id=1, source_target_pairs={{0,3},{1,0},{2,1},{3,2},{4,100},{5,101},{6,102},{7,103},{8,11},{9,... | collective-permute-start | bytes 1572872 | tf_op jit(solution)/shard_map/ppermute | solution.py:444
  65.1 8.1 %collective-permute-start.14 = (bf16[4,128,256]{2,1,0:T(8,128)(2,1)S(1)}, bf16[4,128,256]{2,1,0:T(8,128)(2,1)S(1)}, u32[]{:S(2)}, u32[]{:S(2)}) collective-permute-start(bf16[4,128,256]{2,1,0:T(8,128)(2,1)S(1)} %shard_map.99.refs_0_), channel_id=1, source_target_pairs={{0,16},{1,17},{2,18},{3,19},{4,6},{5,7},{6,4},{7,5},{8,24},{9,25},... | collective-permute-start | bytes 786440 | tf_op jit(solution)/shard_map/ppermute | solution.py:444
  66.7 11.3 %collective-permute-start.13 = (bf16[4,128,256]{2,1,0:T(8,128)(2,1)S(1)}, bf16[4,128,256]{2,1,0:T(8,128)(2,1)S(1)}, u32[]{:S(2)}, u32[]{:S(2)}) collective-permute-start(bf16[4,128,256]{2,1,0:T(8,128)(2,1)S(1)} %shard_map.99.refs_0_), channel_id=1, source_target_pairs={{0,8},{1,9},{2,10},{3,11},{4,5},{5,6},{6,7},{7,4},{8,16},{9,17},{1... | collective-permute-start | bytes 786440 | tf_op jit(solution)/shard_map/ppermute | solution.py:444
  68.1 11.6 %collective-permute-start.12 = (bf16[4,128,256]{2,1,0:T(8,128)(2,1)S(1)}, bf16[4,128,256]{2,1,0:T(8,128)(2,1)S(1)}, u32[]{:S(2)}, u32[]{:S(2)}) collective-permute-start(bf16[4,128,256]{2,1,0:T(8,128)(2,1)S(1)} %shard_map.99.refs_0_), channel_id=1, source_target_pairs={{0,24},{1,25},{2,26},{3,27},{4,7},{5,4},{6,5},{7,6},{8,0},{9,1},{1... | collective-permute-start | bytes 786440 | tf_op jit(solution)/shard_map/ppermute | solution.py:444
  79.8 28.5 %collective-permute-start.19 = (bf16[4,4,128,256]{3,2,1,0:T(8,128)(2,1)S(1)}, bf16[4,4,128,256]{3,2,1,0:T(8,128)(2,1)S(1)}, u32[]{:S(2)}, u32[]{:S(2)}) collective-permute-start(bf16[4,4,128,256]{3,2,1,0:T(8,128)(2,1)S(1)} %shard_map.100.refs_0_), channel_id=1, source_target_pairs={{0,2},{1,3},{2,0},{3,1},{4,68},{5,69},{6,70},{7,71},{8,10},{9,11},... | collective-permute-start | bytes 3145736 | tf_op jit(solution)/shard_map/ppermute | solution.py:444
  80.9 27.6 %collective-permute-start.18 = (bf16[4,4,128,256]{3,2,1,0:T(8,128)(2,1)S(1)}, bf16[4,4,128,256]{3,2,1,0:T(8,128)(2,1)S(1)}, u32[]{:S(2)}, u32[]{:S(2)}) collective-permute-start(bf16[4,4,128,256]{3,2,1,0:T(8,128)(2,1)S(1)} %shard_map.100.refs_0_), channel_id=1, source_target_pairs={{0,1},{1,2},{2,3},{3,0},{4,36},{5,37},{6,38},{7,39},{8,9},{9,10},{... | collective-permute-start | bytes 3145736 | tf_op jit(solution)/shard_map/ppermute | solution.py:444
  80.9 28.1 %collective-permute-start.17 = (bf16[4,4,128,256]{3,2,1,0:T(8,128)(2,1)S(1)}, bf16[4,4,128,256]{3,2,1,0:T(8,128)(2,1)S(1)}, u32[]{:S(2)}, u32[]{:S(2)}) collective-permute-start(bf16[4,4,128,256]{3,2,1,0:T(8,128)(2,1)S(1)} %shard_map.100.refs_0_), channel_id=1, source_target_pairs={{0,3},{1,0},{2,1},{3,2},{4,100},{5,101},{6,102},{7,103},{8,11},{9,... | collective-permute-start | bytes 3145736 | tf_op jit(solution)/shard_map/ppermute | solution.py:444
  103.5 27.9 %collective-permute-start.23 = (bf16[2,176,512]{2,1,0:T(8,128)(2,1)S(1)}, bf16[2,176,512]{2,1,0:T(8,128)(2,1)S(1)}, u32[]{:S(2)}, u32[]{:S(2)}) collective-permute-start(bf16[2,176,512]{2,1,0:T(8,128)(2,1)S(1)} %get-tuple-element.57), channel_id=1, source_target_pairs={{0,8},{8,16},{16,24},{24,32},{32,40},{40,48},{48,56},{56,64},{64,7... | collective-permute-start | bytes 1081352 | tf_op jit(solution)/shard_map/ppermute | solution.py:500
  104.8 26.9 %collective-permute-start.24 = (bf16[2,176,512]{2,1,0:T(8,128)(2,1)S(1)}, bf16[2,176,512]{2,1,0:T(8,128)(2,1)S(1)}, u32[]{:S(2)}, u32[]{:S(2)}) collective-permute-start(bf16[2,176,512]{2,1,0:T(8,128)(2,1)S(1)} %get-tuple-element.58), channel_id=1, source_target_pairs={{4,8},{12,16},{20,24},{28,32},{36,40},{44,48},{52,56},{60,64},{68,... | collective-permute-start | bytes 1081352 | tf_op jit(solution)/shard_map/ppermute | solution.py:500
  108.4 25.5 %collective-permute-start.27 = (bf16[4,4,128,256]{3,2,1,0:T(8,128)(2,1)S(1)}, bf16[4,4,128,256]{3,2,1,0:T(8,128)(2,1)S(1)}, u32[]{:S(2)}, u32[]{:S(2)}) collective-permute-start(bf16[4,4,128,256]{3,2,1,0:T(8,128)(2,1)S(1)} %get-tuple-element.64), channel_id=1, source_target_pairs={{0,2},{1,3},{2,0},{3,1},{4,68},{5,69},{6,70},{7,71},{8,10},{9,11},... | collective-permute-start | bytes 3145736 | tf_op jit(solution)/shard_map/ppermute | solution.py:401
  108.5 29.9 %collective-permute-start.28 = (bf16[4,4,128,256]{3,2,1,0:T(8,128)(2,1)S(1)}, bf16[4,4,128,256]{3,2,1,0:T(8,128)(2,1)S(1)}, u32[]{:S(2)}, u32[]{:S(2)}) collective-permute-start(bf16[4,4,128,256]{3,2,1,0:T(8,128)(2,1)S(1)} %get-tuple-element.65), channel_id=1, source_target_pairs={{0,1},{1,2},{2,3},{3,0},{4,36},{5,37},{6,38},{7,39},{8,9},{9,10},{... | collective-permute-start | bytes 3145736 | tf_op jit(solution)/shard_map/ppermute | solution.py:401
  109.0 29.5 %collective-permute-start.29 = (bf16[4,4,128,256]{3,2,1,0:T(8,128)(2,1)S(1)}, bf16[4,4,128,256]{3,2,1,0:T(8,128)(2,1)S(1)}, u32[]{:S(2)}, u32[]{:S(2)}) collective-permute-start(bf16[4,4,128,256]{3,2,1,0:T(8,128)(2,1)S(1)} %get-tuple-element.66), channel_id=1, source_target_pairs={{0,3},{1,0},{2,1},{3,2},{4,100},{5,101},{6,102},{7,103},{8,11},{9,... | collective-permute-start | bytes 3145736 | tf_op jit(solution)/shard_map/ppermute | solution.py:401
  131.4 50.4 %collective-permute-start.22 = (bf16[2,512,1024]{2,1,0:T(8,128)(2,1)S(1)}, bf16[2,512,1024]{2,1,0:T(8,128)(2,1)S(1)}, u32[]{:S(2)}, u32[]{:S(2)}) collective-permute-start(bf16[2,512,1024]{2,1,0:T(8,128)(2,1)S(1)} %get-tuple-element.56), channel_id=1, source_target_pairs={{0,4},{4,0},{1,5},{5,1},{2,6},{6,2},{3,7},{7,3},{8,12},{12,8},{9,1... | collective-permute-start | bytes 6291464 | tf_op jit(solution)/shard_map/ppermute | solution.py:376
  131.7 9.7 %collective-permute-start.34 = (bf16[2,4,128,256]{3,2,1,0:T(8,128)(2,1)S(1)}, bf16[2,4,128,256]{3,2,1,0:T(8,128)(2,1)S(1)}, u32[]{:S(2)}, u32[]{:S(2)}) collective-permute-start(bf16[2,4,128,256]{3,2,1,0:T(8,128)(2,1)S(1)} %get-tuple-element.75), channel_id=1, source_target_pairs={{0,3},{1,0},{2,1},{3,2},{4,100},{5,101},{6,102},{7,103},{8,11},{9,... | collective-permute-start | bytes 1572872 | tf_op jit(solution)/shard_map/ppermute | solution.py:470
  133.8 10.2 %collective-permute-start.33 = (bf16[2,4,128,256]{3,2,1,0:T(8,128)(2,1)S(1)}, bf16[2,4,128,256]{3,2,1,0:T(8,128)(2,1)S(1)}, u32[]{:S(2)}, u32[]{:S(2)}) collective-permute-start(bf16[2,4,128,256]{3,2,1,0:T(8,128)(2,1)S(1)} %get-tuple-element.67.refs_4_), channel_id=1, source_target_pairs={{0,1},{1,2},{2,3},{3,0},{4,36},{5,37},{6,38},{7,39},{8,9},{9,10},{... | collective-permute-start | bytes 1572872 | tf_op jit(solution)/shard_map/ppermute | solution.py:469
  144.3 21.3 %collective-permute-start.35 = (bf16[4,4,128,256]{3,2,1,0:T(8,128)(2,1)S(1)}, bf16[4,4,128,256]{3,2,1,0:T(8,128)(2,1)S(1)}, u32[]{:S(2)}, u32[]{:S(2)}) collective-permute-start(bf16[4,4,128,256]{3,2,1,0:T(8,128)(2,1)S(1)} %get-tuple-element.76), channel_id=1, source_target_pairs={{0,1},{1,2},{2,3},{3,0},{4,36},{5,37},{6,38},{7,39},{8,9},{9,10},{... | collective-permute-start | bytes 3145736 | tf_op jit(solution)/shard_map/ppermute | solution.py:472
  146.3 19.3 %collective-permute-start.36 = (bf16[4,4,128,256]{3,2,1,0:T(8,128)(2,1)S(1)}, bf16[4,4,128,256]{3,2,1,0:T(8,128)(2,1)S(1)}, u32[]{:S(2)}, u32[]{:S(2)}) collective-permute-start(bf16[4,4,128,256]{3,2,1,0:T(8,128)(2,1)S(1)} %get-tuple-element.77), channel_id=1, source_target_pairs={{0,3},{1,0},{2,1},{3,2},{4,100},{5,101},{6,102},{7,103},{8,11},{9,... | collective-permute-start | bytes 3145736 | tf_op jit(solution)/shard_map/ppermute | solution.py:472
  147.1 9.6 %collective-permute-start.30 = (bf16[4,128,256]{2,1,0:T(8,128)(2,1)S(1)}, bf16[4,128,256]{2,1,0:T(8,128)(2,1)S(1)}, u32[]{:S(2)}, u32[]{:S(2)}) collective-permute-start(bf16[4,128,256]{2,1,0:T(8,128)(2,1)S(1)} %get-tuple-element.69), channel_id=1, source_target_pairs={{0,16},{1,17},{2,18},{3,19},{4,6},{5,7},{6,4},{7,5},{8,24},{9,25},... | collective-permute-start | bytes 786440 | tf_op jit(solution)/shard_map/ppermute | solution.py:401
  148.6 11.8 %collective-permute-start.31 = (bf16[4,128,256]{2,1,0:T(8,128)(2,1)S(1)}, bf16[4,128,256]{2,1,0:T(8,128)(2,1)S(1)}, u32[]{:S(2)}, u32[]{:S(2)}) collective-permute-start(bf16[4,128,256]{2,1,0:T(8,128)(2,1)S(1)} %get-tuple-element.70), channel_id=1, source_target_pairs={{0,8},{1,9},{2,10},{3,11},{4,5},{5,6},{6,7},{7,4},{8,16},{9,17},{1... | collective-permute-start | bytes 786440 | tf_op jit(solution)/shard_map/ppermute | solution.py:401
  160.4 9.2 %collective-permute-start.25 = (bf16[2,176,512]{2,1,0:T(8,128)(2,1)S(1)}, bf16[2,176,512]{2,1,0:T(8,128)(2,1)S(1)}, u32[]{:S(2)}, u32[]{:S(2)}) collective-permute-start(bf16[2,176,512]{2,1,0:T(8,128)(2,1)S(1)} %get-tuple-element.59), channel_id=1, source_target_pairs={{0,8},{8,16},{16,24},{24,32},{32,40},{40,48},{48,56},{56,64},{64,7... | collective-permute-start | bytes 1081352 | tf_op jit(solution)/shard_map/ppermute | solution.py:504
  163.7 9.1 %collective-permute-start.26 = (bf16[2,176,512]{2,1,0:T(8,128)(2,1)S(1)}, bf16[2,176,512]{2,1,0:T(8,128)(2,1)S(1)}, u32[]{:S(2)}, u32[]{:S(2)}) collective-permute-start(bf16[2,176,512]{2,1,0:T(8,128)(2,1)S(1)} %get-tuple-element.60), channel_id=1, source_target_pairs={{4,8},{12,16},{20,24},{28,32},{36,40},{44,48},{52,56},{60,64},{68,... | collective-permute-start | bytes 1081352 | tf_op jit(solution)/shard_map/ppermute | solution.py:504
  (22 other events, 201.5 us)
